TPU v7x, 32 devices: a whole 2x2x4 slice. The times are simulated.
32 devices in a mesh: sec: 2 (over x), gx: 8 (over z, y), gy: 2 (over core).
Axes of the slice: x: 2, y: 2, z: 4, core: 2. Of those that a mesh axis runs over, the one named last changes fastest.
Arguments:
- sections: float32 [2, 8, 128, 64, 128], P('sec', None, 'gx', 'gy'), may hold values from -4 to 8, as said below
- fiber_angles: float32 [8, 2], replicated, may hold values from -3.140625 to 3.140625
- fiber_class: int32 [128, 64, 8], P('gx', 'gy'), may hold values from 0 to 7
- row_map: int32 [8, 2, 512], P('gx', 'gy'), may hold values from 0 to 511, each once within a row
- interface_rows: int32 [2, 8, 2, 32], P(None, 'gx', 'gy'), may hold values from 0 to 31, each once within a row
Outputs:
- updated: float32 [2, 4, 128, 64, 128], P('sec', None, 'gx', 'gy')
Inputs may be any that keep to these rules, and one draw needn't show every extreme that they name: sections[0] holds calcium of 0.05 to 1, gates of 0 to 1, a bound buffer of 0 to 0.8 and tension of 0 to 1; sections[1] holds a stiffness of 0.5 to 2 and an activation coefficient of 2 to 8. `fiber_class`: the class of each column's block of 16 cells through the thickness. `row_map`: each block's list is a permutation of its 512 column places. `interface_rows`: for each side and block, a permutation of the 32 rows.
All inputs are finite; a program needn't handle non-finite values.
Results may differ from a plain program's by a relative error of at most 0.00002.
Values sent between devices are 32-bit elements; how exact they have to be, the bound alone decides.
No kernel may reach another device: no remote copies, remote signals or barrier semaphores. Data moves between devices by JAX's collectives and lax.ppermute only.
A program may use at most 64 MiB of HBM per device.

v0:
```python
import jax
import jax.numpy as jnp
from jax import lax
from jax.sharding import PartitionSpec as P

STEPS = 2
SWEEPS = 2


sigma_long = 1.0
sigma_cross = 0.25
time_step = 0.1
shear_modulus = 1.0
lame_first = 1.0
relax_weight = 0.6
tie_stiffness = 2.0
diagonal_coef = 10.0


def extended_2(block, sides, width):
    for axis, dim in sides:
        count = lax.axis_size(axis)
        forward = [(i, i + 1) for i in range(count - 1)]
        forward.append((count - 1, 0))
        backward = [(target, source) for source, target in forward]
        low = lax.ppermute(
            lax.slice_in_dim(block, block.shape[dim] - width, None, axis=dim), axis, forward
        )
        high = lax.ppermute(lax.slice_in_dim(block, 0, width, axis=dim), axis, backward)
        block = jnp.concatenate([low, block, high], axis=dim)
    return block


def from_behind(block, axis, distance):
    devices = range(lax.axis_size(axis))
    route = [(i - distance, i) for i in devices if i - distance in devices]
    return lax.ppermute(block, axis, route)


def fiber_table(fiber_angles):
    azimuth = fiber_angles[:, 0]
    elevation = fiber_angles[:, 1]
    fiber_dir = [
        jnp.cos(azimuth) * jnp.cos(elevation),
        jnp.sin(azimuth) * jnp.cos(elevation),
        jnp.sin(elevation),
    ]
    spread_gap = sigma_long - sigma_cross
    return jnp.stack(
        fiber_dir
        + [
            sigma_cross + spread_gap * fiber_dir[0] * fiber_dir[0],
            sigma_cross + spread_gap * fiber_dir[1] * fiber_dir[1],
            sigma_cross + spread_gap * fiber_dir[2] * fiber_dir[2],
            spread_gap * fiber_dir[0] * fiber_dir[1],
            spread_gap * fiber_dir[0] * fiber_dir[2],
            spread_gap * fiber_dir[1] * fiber_dir[2],
        ]
    )


def cell_values(fiber_class, fiber_rows, block_depth):
    class_count = fiber_rows.shape[1]
    onehot = (fiber_class[..., None] == jnp.arange(class_count, dtype=jnp.int32)).astype(
        jnp.float32
    )
    picked = jnp.sum(onehot[None] * fiber_rows[:, None, None, None, :], axis=-1)
    widened = jnp.broadcast_to(picked[..., None], picked.shape + (block_depth,))
    return widened.reshape(picked.shape[:-1] + (picked.shape[-1] * block_depth,))


def window(values, offset):
    size_x = values.shape[-3] - 2
    size_y = values.shape[-2] - 2
    size_z = values.shape[-1] - 2
    return values[
        ...,
        1 + offset[0] : 1 + offset[0] + size_x,
        1 + offset[1] : 1 + offset[1] + size_y,
        1 + offset[2] : 1 + offset[2] + size_z,
    ]


def unit_vec(axis_a, factor):
    return tuple((factor if place_a == axis_a else 0 for place_a in range(3)))


def add_offsets(first_off, second_off):
    return tuple((first_off[place_a] + second_off[place_a] for place_a in range(3)))


def second_diff(pick_cells, values, axis_a, centre):
    return (
        pick_cells(values, unit_vec(axis_a, 1))
        - 2.0 * centre
        + pick_cells(values, unit_vec(axis_a, -1))
    )


def cross_diff(pick_cells, values, axis_a, axis_b):
    plus_a, minus_a = (unit_vec(axis_a, 1), unit_vec(axis_a, -1))
    plus_b, minus_b = (unit_vec(axis_b, 1), unit_vec(axis_b, -1))
    return 0.25 * (
        pick_cells(values, add_offsets(plus_a, plus_b))
        - pick_cells(values, add_offsets(plus_a, minus_b))
        - pick_cells(values, add_offsets(minus_a, plus_b))
        + pick_cells(values, add_offsets(minus_a, minus_b))
    )


def diffuse(pick_cells, values, cell_fiber):
    centre = pick_cells(values, (0, 0, 0))
    result = jnp.zeros_like(centre)
    for axis_a in range(3):
        result = result + cell_fiber[3 + axis_a] * second_diff(pick_cells, values, axis_a, centre)
    for pair_axes, slot_index in (((0, 1), 6), ((0, 2), 7), ((1, 2), 8)):
        result = result + 2.0 * cell_fiber[slot_index] * cross_diff(
            pick_cells, values, pair_axes[0], pair_axes[1]
        )
    return result


def ionic_step(cell_state, diffusion):
    voltage, calcium, activation, inactivation, potassium, slow_gate, buffered, tension = cell_state
    bound_share = calcium * calcium / (calcium * calcium + 0.25)
    calcium_flow = 1.2 * activation * inactivation * (voltage - 2.0)
    current_sum = (
        calcium_flow
        + 0.8 * potassium * (voltage + 1.0)
        + 0.6 * bound_share * slow_gate * (voltage + 1.0)
        + 0.1 * voltage
    )
    binding = 2.0 * calcium * (1.0 - buffered) - 0.4 * buffered
    return [
        voltage + time_step * (diffusion - current_sum),
        calcium + time_step * (-0.3 * calcium_flow - 0.5 * calcium - binding),
        activation + time_step * (jax.nn.sigmoid(2.0 * voltage + 1.0) - activation) / 0.5,
        inactivation + time_step * (jax.nn.sigmoid(-2.0 * voltage) - inactivation) / 3.0,
        potassium + time_step * (jax.nn.sigmoid(2.0 * voltage) - potassium),
        slow_gate + time_step * (jax.nn.sigmoid(voltage - 0.5) - slow_gate) / 5.0,
        buffered + time_step * binding,
        tension + time_step * (bound_share - tension) / 2.0,
    ]


def navier(pick_cells, motion, stiffness):
    centre = pick_cells(motion, (0, 0, 0))
    laplace = jnp.zeros_like(centre)
    for axis_a in range(3):
        laplace = laplace + second_diff(pick_cells, motion, axis_a, centre)
    pieces = []
    for component in range(3):
        component_term = second_diff(pick_cells, motion[component], component, centre[component])
        for other_axis in range(3):
            if other_axis != component:
                component_term = component_term + cross_diff(
                    pick_cells, motion[other_axis], component, other_axis
                )
        pieces.append(component_term)
    graddiv = jnp.stack(pieces)
    return (centre, -stiffness * (shear_modulus * laplace + (lame_first + shear_modulus) * graddiv))


def tie_forces(partial_value, from_left, from_right, rows_first, rows_last):
    left_term = jnp.take(from_left, rows_first, axis=1) - partial_value[:, 0]
    right_term = jnp.take(from_right, rows_last, axis=1) - partial_value[:, -1]
    return jnp.zeros_like(partial_value).at[:, 0].add(left_term).at[:, -1].add(right_term)


def relax_sweep(motion, stiffness, drive, rows_first, rows_last):
    partial_value = tie_stiffness * stiffness * motion
    extended = extended_2(motion, (("gx", 1), ("gy", 2)), 1)
    face_pairs = jnp.stack([partial_value[:, 0], partial_value[:, -1]], axis=1)
    received_faces = extended_2(face_pairs, (("gx", 1),), 1)
    from_left = received_faces[:, 0]
    from_right = received_faces[:, 3]
    extended = jnp.pad(extended, ((0, 0), (0, 0), (0, 0), (1, 1)))
    centre, applied = navier(window, extended, stiffness)
    tie_force = tie_forces(partial_value, from_left, from_right, rows_first, rows_last)
    return centre + relax_weight * (drive + tie_force - applied) / (diagonal_coef * stiffness)


def local(sections, fiber_angles, fiber_class, row_map, interface_rows):
    own_data = sections[0]
    fiber_rows = fiber_table(fiber_angles)
    cell_fiber = cell_values(fiber_class, fiber_rows, own_data.shape[-1] // fiber_class.shape[-1])
    cell_state = [own_data[channel] for channel in range(8)]
    for repeat in range(STEPS):
        extended = extended_2(cell_state[0], (("gx", 0), ("gy", 1)), 1)
        extended = jnp.pad(extended, ((0, 0), (0, 0), (1, 1)))
        diffusion = diffuse(window, extended, cell_fiber)
        cell_state = ionic_step(cell_state, diffusion)
    tension_out = cell_state[7]
    received = from_behind(tension_out, "sec", 1)
    slab_shape = received.shape
    remapped = jnp.take(
        received.reshape(slab_shape[0] * slab_shape[1], slab_shape[2]), row_map[0, 0], axis=0
    )
    activity = own_data[7] * remapped.reshape(slab_shape)
    motion = own_data[0:3]
    stiffness = own_data[6]
    drive = own_data[3:6] + activity * cell_fiber[0:3]
    rows_first = interface_rows[0, 0, 0]
    rows_last = interface_rows[1, 0, 0]
    for repeat in range(SWEEPS):
        motion = relax_sweep(motion, stiffness, drive, rows_first, rows_last)
    electric_out = jnp.stack([cell_state[0], cell_state[1], cell_state[4], cell_state[7]])
    mechanic_out = jnp.concatenate([motion, activity[None]], axis=0)
    sec_place = lax.axis_index("sec")
    return jnp.where(sec_place == 0, electric_out, mechanic_out)[None]


def solution(mesh):
    in_specs = (
        P("sec", None, "gx", "gy", None),
        P(),
        P("gx", "gy", None),
        P("gx", "gy", None),
        P(None, "gx", "gy", None),
    )
    out_specs = P("sec", None, "gx", "gy", None)
    return jax.shard_map(local, mesh=mesh, in_specs=in_specs, out_specs=out_specs, check_vma=False)
```

profile of v0, /device:TPU:0, one launch (start us, length us, event | category | flops | bytes accessed | tf_op | source)
XLA Modules:
  0.0 114.3 jit_solution(16659895935848441153)
XLA Ops:
  1.4 3.0 %collective-permute-start.1 = (f32[1,32,128]{2,1,0:T(8,128)}, f32[1,32,128]{2,1,0:T(8,128)}, u32[]{:S(2)}, u32[]{:S(2)}) collective-permute-start(f32[1,32,128]{2,1,0:T(8,128)} %get-tuple-element.86), channel_id=1, source_target_pairs={{0,2},{2,4},{4,6},{6,8},{8,10},{10,12},{12,14},{14,0},{1,3},{3,5},... | collective-permute-start | bytes 49160 | tf_op jit(solution)/shard_map/ppermute | solution.py:26
  4.4 3.0 %collective-permute-start = (f32[1,32,128]{2,1,0:T(8,128)}, f32[1,32,128]{2,1,0:T(8,128)}, u32[]{:S(2)}, u32[]{:S(2)}) collective-permute-start(f32[1,32,128]{2,1,0:T(8,128)} %get-tuple-element.87), channel_id=1, source_target_pairs={{2,0},{4,2},{6,4},{8,6},{10,8},{12,10},{14,12},{0,14},{3,1},{5,3},... | collective-permute-start | bytes 49160 | tf_op jit(solution)/shard_map/ppermute | solution.py:29
  7.4 2.5 %fusion.158 = (f32[1,3,16,32,128]{4,3,2,1,0:T(8,128)}, f32[3,16,32,128]{3,2,1,0:T(8,128)S(1)}) fusion(f32[1,8,16,32,128]{4,3,2,1,0:T(8,128)} %param.15), kind=kLoop, calls=%fused_computation.386 | loop fusion | bytes 3145728 | tf_op jit(solution)/shard_map/slice | solution.py:202
  10.0 4.7 %collective-permute-start.11 = (f32[3,1,32,128]{3,2,1,0:T(8,128)S(1)}, f32[3,1,32,128]{3,2,1,0:T(8,128)S(1)}, u32[]{:S(2)}, u32[]{:S(2)}) collective-permute-start(f32[3,1,32,128]{3,2,1,0:T(8,128)S(1)} %get-tuple-element.99), channel_id=1, source_target_pairs={{2,0},{4,2},{6,4},{8,6},{10,8},{12,10},{14,12},{0,14},{3,1},{5,3},... | collective-permute-start | bytes 147464 | tf_op jit(solution)/shard_map/ppermute | solution.py:29
  25.4 3.6 %collective-permute-start.8 = (f32[16,32,128]{2,1,0:T(8,128)}, f32[16,32,128]{2,1,0:T(8,128)S(1)}, u32[]{:S(2)}, u32[]{:S(2)}) collective-permute-start(f32[16,32,128]{2,1,0:T(8,128)} %get-tuple-element.74), channel_id=1, source_target_pairs={{0,16},{1,17},{2,18},{3,19},{4,20},{5,21},{6,22},{7,23},{8,24},{9,... | collective-permute-start | bytes 786440 | tf_op jit(solution)/shard_map/ppermute | solution.py:37
  35.0 2.2 %copy.158 = f32[16,32,128]{2,1,0:T(8,128)} copy(f32[16,32,128]{1,2,0:T(8,128)} %bitcast.320) | data formatting | bytes 524288 | tf_op jit(solution)/shard_map/mul | solution.py:117
  38.3 2.2 %copy.157 = f32[16,32,128]{2,1,0:T(8,128)} copy(f32[16,32,128]{1,2,0:T(8,128)} %bitcast.321) | data formatting | bytes 524288 | tf_op jit(solution)/shard_map/mul | solution.py:117
  41.5 2.2 %copy.156 = f32[16,32,128]{2,1,0:T(8,128)} copy(f32[16,32,128]{1,2,0:T(8,128)} %bitcast.322) | data formatting | bytes 524288 | tf_op jit(solution)/shard_map/mul | solution.py:117
  43.8 1.9 %broadcast_in_dim.64 = f32[16,32,8,16]{1,3,2,0:T(8,128)} broadcast(f32[16,32,8]{1,2,0:T(8,128)} %get-tuple-element.104), dimensions={0,1,2} | broadcast | bytes 278528 | tf_op jit(solution)/shard_map/broadcast_in_dim | solution.py:68
  45.7 2.3 %copy.155 = f32[16,32,128]{2,1,0:T(8,128)} copy(f32[16,32,128]{1,2,0:T(8,128)} %bitcast.323) | data formatting | bytes 524288 | tf_op jit(solution)/shard_map/broadcast_in_dim | solution.py:68
  48.0 1.9 %broadcast_in_dim.62 = f32[16,32,8,16]{1,3,2,0:T(8,128)} broadcast(f32[16,32,8]{1,2,0:T(8,128)} %get-tuple-element.105), dimensions={0,1,2} | broadcast | bytes 278528 | tf_op jit(solution)/shard_map/broadcast_in_dim | solution.py:68
  49.9 2.3 %copy.154 = f32[16,32,128]{2,1,0:T(8,128)} copy(f32[16,32,128]{1,2,0:T(8,128)} %bitcast.324) | data formatting | bytes 524288 | tf_op jit(solution)/shard_map/broadcast_in_dim | solution.py:68
  52.1 1.9 %broadcast_in_dim.71 = f32[3,16,32,8,16]{2,4,3,1,0:T(8,128)} broadcast(f32[3,16,32,8]{2,3,1,0:T(8,128)S(1)} %slice-done), dimensions={0,1,2,3} | broadcast | bytes 835584 | tf_op jit(solution)/shard_map/broadcast_in_dim | solution.py:68
  54.0 3.1 %copy.166 = f32[3,16,32,128]{3,2,0,1:T(8,128)} copy(f32[3,16,32,128]{2,3,1,0:T(8,128)} %bitcast.318) | data formatting | bytes 1572864 | tf_op jit(solution)/shard_map/slice | solution.py:202
  58.8 2.1 %select_multiply_fusion = (f32[1,1,16,32,128]{4,3,2,1,0:T(8,128)}, f32[1,1,16,32,128]{4,3,2,1,0:T(8,128)}, f32[16,32,128]{2,1,0:T(8,128)S(1)}) fusion(f32[1,1,16,32,128]{4,3,2,1,0:T(8,128)} %bitcast.325, f32[1,8,16,32,128]{4,3,2,1,0:T(8,128)S(1)} %copy-done, pred[16,32]{1,0:T(8,128)(4,1)S(1)} %compare_and_fusion), kind=kLoop, calls=%fused_computation.320 | loop fusion | flops 1900544 | bytes 2621952 | tf_op jit(solution)/shard_map/mul | solution.py:199
  65.6 2.5 %add_bitcast_fusion = (f32[1,1,16,32,128]{4,3,2,1,0:T(8,128)}, f32[16,32,128]{2,1,0:T(8,128)S(1)}) fusion(f32[16,32,128]{2,1,0:T(8,128)S(1)} %copy-done.23, f32[1,8,16,32,128]{4,3,2,1,0:T(8,128)S(1)} %copy-done, f32[16,32,128]{2,1,0:T(8,128)S(1)} %get-tuple-element.85, f32[16,32,128]{2,1,0:T(8,128)S(1)} %copy-done.12, ...), kind=kLoop, calls=%fused_computation.322 | loop fusion | flops 5832704 | bytes 8683520 | tf_op jit(solution)/shard_map/stack | solution.py:207
  69.5 4.7 %collective-permute-start.4 = (f32[1,32,128]{2,1,0:T(8,128)S(1)}, f32[1,32,128]{2,1,0:T(8,128)S(1)}, u32[]{:S(2)}, u32[]{:S(2)}) collective-permute-start(f32[1,32,128]{2,1,0:T(8,128)S(1)} %get-tuple-element.115), channel_id=1, source_target_pairs={{2,0},{4,2},{6,4},{8,6},{10,8},{12,10},{14,12},{0,14},{3,1},{5,3},... | collective-permute-start | bytes 49160 | tf_op jit(solution)/shard_map/ppermute | solution.py:29
  76.6 4.8 %collective-permute-start.10 = (f32[3,1,32,128]{3,2,1,0:T(8,128)S(1)}, f32[3,1,32,128]{3,2,1,0:T(8,128)S(1)}, u32[]{:S(2)}, u32[]{:S(2)}) collective-permute-start(f32[3,1,32,128]{3,2,1,0:T(8,128)S(1)} %get-tuple-element.96), channel_id=1, source_target_pairs={{2,0},{4,2},{6,4},{8,6},{10,8},{12,10},{14,12},{0,14},{3,1},{5,3},... | collective-permute-start | bytes 147464 | tf_op jit(solution)/shard_map/ppermute | solution.py:29
  81.9 1.7 %fusion.75 = f32[1,1,16,32,128]{4,3,2,1,0:T(8,128)} fusion(f32[16,32,128]{2,1,0:T(8,128)S(1)} %get-tuple-element.61, f32[16,32,128]{2,1,0:T(8,128)S(1)} %copy-done.12, f32[18,34,130]{2,1,0:T(8,128)S(1)} %select_maximum_fusion.8, f32[16,32,128]{2,1,0:T(8,128)S(1)} %copy-done.13, f32[16,32,128]{2,1,0:T(8,128)S(1)} %copy-done.14, ...), kind=kLoop, calls=%fused_computation.194 | loop fusion | flops 5242880 | bytes 7897088 | tf_op jit(solution)/shard_map/stack | solution.py:207
  83.6 4.6 %collective-permute-done.9 = f32[3,1,32,128]{3,2,0,1:T(8,128)S(1)} collective-permute-done((f32[3,1,32,128]{3,2,0,1:T(8,128)S(1)}, f32[3,1,32,128]{3,2,0,1:T(8,128)S(1)}, u32[]{:S(2)}, u32[]{:S(2)}) %collective-permute-start.9) | collective-permute-done | bytes 49184 | tf_op jit(solution)/shard_map/ppermute | solution.py:26
  91.6 3.7 %fusion.18 = f32[3,16,32,128]{3,2,1,0:T(8,128)S(1)} fusion(f32[3,16,32,128]{3,2,1,0:T(8,128)S(1)} %copy-done.7, f32[3,18,34,130]{3,2,1,0:T(8,128)} %copy-done.1, f32[3,18,1,128]{3,2,1,0:T(1,128)S(1)} %copy-done.35, f32[3,1,32,128]{3,2,1,0:T(8,128)S(1)} %copy-done.33, f32[3,1,32,128]{3,2,1,0:T(8,128)S(1)} %copy-done.31, f32[3,18,1,128]{3,2,1,0:T(1,128)S(1)} %copy-done.37, ...), kind=kLoop, calls=%fused_computation.49 | loop fusion | flops 5701632 | bytes 7231488 | tf_op jit(solution)/shard_map/add | solution.py:180
  95.4 4.7 %collective-permute-start.17 = (f32[3,1,32,128]{3,2,1,0:T(8,128)S(1)}, f32[3,1,32,128]{3,2,1,0:T(8,128)S(1)}, u32[]{:S(2)}, u32[]{:S(2)}) collective-permute-start(f32[3,1,32,128]{3,2,1,0:T(8,128)S(1)} %get-tuple-element.95), channel_id=1, source_target_pairs={{2,0},{4,2},{6,4},{8,6},{10,8},{12,10},{14,12},{0,14},{3,1},{5,3},... | collective-permute-start | bytes 147464 | tf_op jit(solution)/shard_map/ppermute | solution.py:29
  100.2 2.0 %collective-permute-start.15 = (f32[3,1,32,128]{3,2,0,1:T(8,128)S(1)}, f32[3,1,32,128]{3,2,0,1:T(8,128)S(1)}, u32[]{:S(2)}, u32[]{:S(2)}) collective-permute-start(f32[3,1,32,128]{3,2,0,1:T(8,128)S(1)} %get-tuple-element.93), channel_id=1, source_target_pairs={{0,2},{2,4},{4,6},{6,8},{8,10},{10,12},{12,14},{14,0},{1,3},{3,5},... | collective-permute-start | bytes 147464 | tf_op jit(solution)/shard_map/ppermute | solution.py:26
  102.9 1.8 %collective-permute-done.16 = f32[3,1,32,128]{3,2,0,1:T(8,128)S(1)} collective-permute-done((f32[3,1,32,128]{3,2,0,1:T(8,128)S(1)}, f32[3,1,32,128]{3,2,0,1:T(8,128)S(1)}, u32[]{:S(2)}, u32[]{:S(2)}) %collective-permute-start.16) | collective-permute-done | bytes 49184 | tf_op jit(solution)/shard_map/ppermute | solution.py:29
  (190 shorter events, 44.2 us)
Async XLA Ops:
  0.0 14.8 %copy-start.45 = (s32[2,1,1,32]{3,2,1,0:T(1,128)S(1)}, s32[2,1,1,32]{3,2,1,0:T(1,128)}, u32[]{:S(2)}) copy-start(s32[2,1,1,32]{3,2,1,0:T(1,128)} %param.19) | copy-start | bytes 772
  0.0 15.4 %copy-start.38 = (s32[16,32,8]{1,2,0:T(8,128)S(1)}, s32[16,32,8]{1,2,0:T(8,128)}, u32[]{:S(2)}) copy-start(s32[16,32,8]{1,2,0:T(8,128)} %param.17) | copy-start | bytes 49156
  1.4 59.5 %collective-permute-start.1 = (f32[1,32,128]{2,1,0:T(8,128)}, f32[1,32,128]{2,1,0:T(8,128)}, u32[]{:S(2)}, u32[]{:S(2)}) collective-permute-start(f32[1,32,128]{2,1,0:T(8,128)} %get-tuple-element.86), channel_id=1, source_target_pairs={{0,2},{2,4},{4,6},{6,8},{8,10},{10,12},{12,14},{14,0},{1,3},{3,5},... | collective-permute-start | bytes 49160 | tf_op jit(solution)/shard_map/ppermute | solution.py:26
  4.4 56.6 %collective-permute-start = (f32[1,32,128]{2,1,0:T(8,128)}, f32[1,32,128]{2,1,0:T(8,128)}, u32[]{:S(2)}, u32[]{:S(2)}) collective-permute-start(f32[1,32,128]{2,1,0:T(8,128)} %get-tuple-element.87), channel_id=1, source_target_pairs={{2,0},{4,2},{6,4},{8,6},{10,8},{12,10},{14,12},{0,14},{3,1},{5,3},... | collective-permute-start | bytes 49160 | tf_op jit(solution)/shard_map/ppermute | solution.py:29
  9.9 8.5 %collective-permute-start.12 = (f32[3,1,32,128]{3,2,1,0:T(8,128)S(1)}, f32[3,1,32,128]{3,2,1,0:T(8,128)S(1)}, u32[]{:S(2)}, u32[]{:S(2)}) collective-permute-start(f32[3,1,32,128]{3,2,1,0:T(8,128)S(1)} %get-tuple-element.98), channel_id=1, source_target_pairs={{0,2},{2,4},{4,6},{6,8},{8,10},{10,12},{12,14},{14,0},{1,3},{3,5},... | collective-permute-start | bytes 147464 | tf_op jit(solution)/shard_map/ppermute | solution.py:26
  10.0 8.4 %collective-permute-start.11 = (f32[3,1,32,128]{3,2,1,0:T(8,128)S(1)}, f32[3,1,32,128]{3,2,1,0:T(8,128)S(1)}, u32[]{:S(2)}, u32[]{:S(2)}) collective-permute-start(f32[3,1,32,128]{3,2,1,0:T(8,128)S(1)} %get-tuple-element.99), channel_id=1, source_target_pairs={{2,0},{4,2},{6,4},{8,6},{10,8},{12,10},{14,12},{0,14},{3,1},{5,3},... | collective-permute-start | bytes 147464 | tf_op jit(solution)/shard_map/ppermute | solution.py:29
  18.4 1.3 %collective-permute-start.14 = (f32[3,18,1,128]{3,2,1,0:T(1,128)S(1)}, f32[3,18,1,128]{3,2,1,0:T(1,128)S(1)}, u32[]{:S(2)}, u32[]{:S(2)}) collective-permute-start(f32[3,18,1,128]{3,2,1,0:T(1,128)S(1)} %get-tuple-element.90), channel_id=1, source_target_pairs={{0,1},{1,0},{2,3},{3,2},{4,5},{5,4},{6,7},{7,6},{8,9},{9,8},{10,11... | collective-permute-start | bytes 82952 | tf_op jit(solution)/shard_map/ppermute | solution.py:26
  18.5 1.4 %collective-permute-start.13 = (f32[3,18,1,128]{3,2,1,0:T(1,128)S(1)}, f32[3,18,1,128]{3,2,1,0:T(1,128)S(1)}, u32[]{:S(2)}, u32[]{:S(2)}) collective-permute-start(f32[3,18,1,128]{3,2,1,0:T(1,128)S(1)} %get-tuple-element.91), channel_id=1, source_target_pairs={{1,0},{0,1},{3,2},{2,3},{5,4},{4,5},{7,6},{6,7},{9,8},{8,9},{11,10... | collective-permute-start | bytes 82952 | tf_op jit(solution)/shard_map/ppermute | solution.py:29
  25.4 31.8 %collective-permute-start.8 = (f32[16,32,128]{2,1,0:T(8,128)}, f32[16,32,128]{2,1,0:T(8,128)S(1)}, u32[]{:S(2)}, u32[]{:S(2)}) collective-permute-start(f32[16,32,128]{2,1,0:T(8,128)} %get-tuple-element.74), channel_id=1, source_target_pairs={{0,16},{1,17},{2,18},{3,19},{4,20},{5,21},{6,22},{7,23},{8,24},{9,... | collective-permute-start | bytes 786440 | tf_op jit(solution)/shard_map/ppermute | solution.py:37
  33.9 31.5 %copy-start.10 = (f32[16,32,128]{2,1,0:T(8,128)}, f32[16,32,128]{2,1,0:T(8,128)S(1)}, u32[]{:S(2)}) copy-start(f32[16,32,128]{2,1,0:T(8,128)S(1)} %copy.153) | copy-start | bytes 786436
  61.7 1.9 %collective-permute-start.3 = (f32[18,1,128]{2,1,0:T(1,128)S(1)}, f32[18,1,128]{2,1,0:T(1,128)S(1)}, u32[]{:S(2)}, u32[]{:S(2)}) collective-permute-start(f32[18,1,128]{2,1,0:T(1,128)S(1)} %get-tuple-element.112), channel_id=1, source_target_pairs={{0,1},{1,0},{2,3},{3,2},{4,5},{5,4},{6,7},{7,6},{8,9},{9,8},{10,11... | collective-permute-start | bytes 27656 | tf_op jit(solution)/shard_map/ppermute | solution.py:26
  61.8 1.7 %collective-permute-start.2 = (f32[18,1,128]{2,1,0:T(1,128)S(1)}, f32[18,1,128]{2,1,0:T(1,128)S(1)}, u32[]{:S(2)}, u32[]{:S(2)}) collective-permute-start(f32[18,1,128]{2,1,0:T(1,128)S(1)} %get-tuple-element.113), channel_id=1, source_target_pairs={{1,0},{0,1},{3,2},{2,3},{5,4},{4,5},{7,6},{6,7},{9,8},{8,9},{11,10... | collective-permute-start | bytes 27656 | tf_op jit(solution)/shard_map/ppermute | solution.py:29
  69.5 6.4 %collective-permute-start.5 = (f32[1,32,128]{2,1,0:T(8,128)S(1)}, f32[1,32,128]{2,1,0:T(8,128)S(1)}, u32[]{:S(2)}, u32[]{:S(2)}) collective-permute-start(f32[1,32,128]{2,1,0:T(8,128)S(1)} %get-tuple-element.114), channel_id=1, source_target_pairs={{0,2},{2,4},{4,6},{6,8},{8,10},{10,12},{12,14},{14,0},{1,3},{3,5},... | collective-permute-start | bytes 49160 | tf_op jit(solution)/shard_map/ppermute | solution.py:26
  69.5 6.4 %collective-permute-start.4 = (f32[1,32,128]{2,1,0:T(8,128)S(1)}, f32[1,32,128]{2,1,0:T(8,128)S(1)}, u32[]{:S(2)}, u32[]{:S(2)}) collective-permute-start(f32[1,32,128]{2,1,0:T(8,128)S(1)} %get-tuple-element.115), channel_id=1, source_target_pairs={{2,0},{4,2},{6,4},{8,6},{10,8},{12,10},{14,12},{0,14},{3,1},{5,3},... | collective-permute-start | bytes 49160 | tf_op jit(solution)/shard_map/ppermute | solution.py:29
  76.0 5.4 %collective-permute-start.7 = (f32[18,1,128]{2,1,0:T(1,128)S(1)}, f32[18,1,128]{2,1,0:T(1,128)S(1)}, u32[]{:S(2)}, u32[]{:S(2)}) collective-permute-start(f32[18,1,128]{2,1,0:T(1,128)S(1)} %get-tuple-element.108), channel_id=1, source_target_pairs={{0,1},{1,0},{2,3},{3,2},{4,5},{5,4},{6,7},{7,6},{8,9},{9,8},{10,11... | collective-permute-start | bytes 27656 | tf_op jit(solution)/shard_map/ppermute | solution.py:26
  76.1 5.3 %collective-permute-start.6 = (f32[18,1,128]{2,1,0:T(1,128)S(1)}, f32[18,1,128]{2,1,0:T(1,128)S(1)}, u32[]{:S(2)}, u32[]{:S(2)}) collective-permute-start(f32[18,1,128]{2,1,0:T(1,128)S(1)} %get-tuple-element.109), channel_id=1, source_target_pairs={{1,0},{0,1},{3,2},{2,3},{5,4},{4,5},{7,6},{6,7},{9,8},{8,9},{11,10... | collective-permute-start | bytes 27656 | tf_op jit(solution)/shard_map/ppermute | solution.py:29
  76.6 6.9 %collective-permute-start.10 = (f32[3,1,32,128]{3,2,1,0:T(8,128)S(1)}, f32[3,1,32,128]{3,2,1,0:T(8,128)S(1)}, u32[]{:S(2)}, u32[]{:S(2)}) collective-permute-start(f32[3,1,32,128]{3,2,1,0:T(8,128)S(1)} %get-tuple-element.96), channel_id=1, source_target_pairs={{2,0},{4,2},{6,4},{8,6},{10,8},{12,10},{14,12},{0,14},{3,1},{5,3},... | collective-permute-start | bytes 147464 | tf_op jit(solution)/shard_map/ppermute | solution.py:29
  81.3 6.8 %collective-permute-start.9 = (f32[3,1,32,128]{3,2,0,1:T(8,128)S(1)}, f32[3,1,32,128]{3,2,0,1:T(8,128)S(1)}, u32[]{:S(2)}, u32[]{:S(2)}) collective-permute-start(f32[3,1,32,128]{3,2,0,1:T(8,128)S(1)} %get-tuple-element.97), channel_id=1, source_target_pairs={{0,2},{2,4},{4,6},{6,8},{8,10},{10,12},{12,14},{14,0},{1,3},{3,5},... | collective-permute-start | bytes 147464 | tf_op jit(solution)/shard_map/ppermute | solution.py:26
  95.4 6.9 %collective-permute-start.18 = (f32[3,1,32,128]{3,2,1,0:T(8,128)S(1)}, f32[3,1,32,128]{3,2,1,0:T(8,128)S(1)}, u32[]{:S(2)}, u32[]{:S(2)}) collective-permute-start(f32[3,1,32,128]{3,2,1,0:T(8,128)S(1)} %get-tuple-element.94), channel_id=1, source_target_pairs={{0,2},{2,4},{4,6},{6,8},{8,10},{10,12},{12,14},{14,0},{1,3},{3,5},... | collective-permute-start | bytes 147464 | tf_op jit(solution)/shard_map/ppermute | solution.py:26
  95.4 6.8 %collective-permute-start.17 = (f32[3,1,32,128]{3,2,1,0:T(8,128)S(1)}, f32[3,1,32,128]{3,2,1,0:T(8,128)S(1)}, u32[]{:S(2)}, u32[]{:S(2)}) collective-permute-start(f32[3,1,32,128]{3,2,1,0:T(8,128)S(1)} %get-tuple-element.95), channel_id=1, source_target_pairs={{2,0},{4,2},{6,4},{8,6},{10,8},{12,10},{14,12},{0,14},{3,1},{5,3},... | collective-permute-start | bytes 147464 | tf_op jit(solution)/shard_map/ppermute | solution.py:29
  100.2 4.5 %collective-permute-start.16 = (f32[3,1,32,128]{3,2,0,1:T(8,128)S(1)}, f32[3,1,32,128]{3,2,0,1:T(8,128)S(1)}, u32[]{:S(2)}, u32[]{:S(2)}) collective-permute-start(f32[3,1,32,128]{3,2,0,1:T(8,128)S(1)} %get-tuple-element.92), channel_id=1, source_target_pairs={{2,0},{4,2},{6,4},{8,6},{10,8},{12,10},{14,12},{0,14},{3,1},{5,3},... | collective-permute-start | bytes 147464 | tf_op jit(solution)/shard_map/ppermute | solution.py:29
  100.2 6.8 %collective-permute-start.15 = (f32[3,1,32,128]{3,2,0,1:T(8,128)S(1)}, f32[3,1,32,128]{3,2,0,1:T(8,128)S(1)}, u32[]{:S(2)}, u32[]{:S(2)}) collective-permute-start(f32[3,1,32,128]{3,2,0,1:T(8,128)S(1)} %get-tuple-element.93), channel_id=1, source_target_pairs={{0,2},{2,4},{4,6},{6,8},{8,10},{10,12},{12,14},{14,0},{1,3},{3,5},... | collective-permute-start | bytes 147464 | tf_op jit(solution)/shard_map/ppermute | solution.py:26
  102.3 5.8 %collective-permute-start.20 = (f32[3,18,1,128]{3,2,1,0:T(1,128)S(1)}, f32[3,18,1,128]{3,2,1,0:T(1,128)S(1)}, u32[]{:S(2)}, u32[]{:S(2)}) collective-permute-start(f32[3,18,1,128]{3,2,1,0:T(1,128)S(1)} %get-tuple-element.88), channel_id=1, source_target_pairs={{0,1},{1,0},{2,3},{3,2},{4,5},{5,4},{6,7},{7,6},{8,9},{9,8},{10,11... | collective-permute-start | bytes 82952 | tf_op jit(solution)/shard_map/ppermute | solution.py:26
  102.4 5.7 %collective-permute-start.19 = (f32[3,18,1,128]{3,2,1,0:T(1,128)S(1)}, f32[3,18,1,128]{3,2,1,0:T(1,128)S(1)}, u32[]{:S(2)}, u32[]{:S(2)}) collective-permute-start(f32[3,18,1,128]{3,2,1,0:T(1,128)S(1)} %get-tuple-element.89), channel_id=1, source_target_pairs={{1,0},{0,1},{3,2},{2,3},{5,4},{4,5},{7,6},{6,7},{9,8},{8,9},{11,10... | collective-permute-start | bytes 82952 | tf_op jit(solution)/shard_map/ppermute | solution.py:29
  (44 other events, 225.6 us)
where the time goes:
time: 115 us; the launch traced here: 114 us
  local copies, waits for them, and re-layouts  40.1 us (35%)
  starting transfers between devices  33 us (29%)
  other arithmetic  30.6 us (27%)
  waiting for transfers between devices  9.91 us (9%)
    ppermute x10, starting transfers between devices, extended_2(): lax.ppermute(lax.slice_in_dim(block, 0, width, axis=dim), axis, backward)  24 us
    broadcast_in_dim x10, local copies, waits for them, and re-layouts, cell_values(): widened = jnp.broadcast_to(picked[..., None], picked.shape + (block_depth,))  15.9 us
    ppermute x10, waiting for transfers between devices, extended_2(): lax.ppermute(lax.slice_in_dim(block, block.shape[dim] - width, None, axis...  7.88 us
    mul x3, local copies, waits for them, and re-layouts, diffuse(): 2.0 * cell_fiber[slot_index]  6.68 us
    slice x4, local copies, waits for them, and re-layouts, local(): drive = own_data[3:6] + activity * cell_fiber[0:3]  5.59 us
    ppermute x10, starting transfers between devices, extended_2(): lax.ppermute(lax.slice_in_dim(block, block.shape[dim] - width, None, axis...  5.48 us
    concatenate x10, other arithmetic, extended_2(): block = jnp.concatenate([low, block, high], axis=dim)  4.92 us
    unnamed x93, local copies, waits for them, and re-layouts  4.48 us
  transfers between devices with their start and end apart: 21, of which 6 were waited for; matrix products, arithmetic and copies ran while one was open for 41% of the time, Pallas kernels for 0%

commit v1 on v0

v1 whole, which is shorter than its diff:
```python
import jax
import jax.numpy as jnp
from jax import lax
from jax.experimental import pallas as pl
from jax.experimental.pallas import tpu as pltpu
from jax.sharding import PartitionSpec as P

DT = 0.1
OMEGA = 0.06
F32 = jnp.float32
HIGHEST = lax.Precision.HIGHEST
VMEM_LIMIT = 24 * 1024 * 1024

ROW_NOW, ROW_NEXT, ROW_STIFF, ROW_COEF, ROW_SIDE, ROW_CLASS, ROW_LIST = 0, 96, 192, 224, 256, 280, 288
MESSAGE_ROWS = 296


def swap_pairs(pairs):
    return pairs + [(b, a) for a, b in pairs]


def sigmoid(v):
    return 1.0 / (1.0 + jnp.exp(-v))


def shift_y(w):
    rows = w.shape[0]
    return pltpu.roll(w, rows - 1, 0), pltpu.roll(w, 1, 0)


def shift_z(w):
    depth = w.shape[1]
    lane = lax.broadcasted_iota(jnp.int32, w.shape, 1)
    up = jnp.where(lane == depth - 1, 0.0, pltpu.roll(w, depth - 1, 1))
    down = jnp.where(lane == 0, 0.0, pltpu.roll(w, 1, 1))
    return up, down


def motion_parts(u, rows):
    sum_y, dif_y, sum_z, dif_z = [], [], [], []
    for w in u:
        yp, ym = shift_y(w)
        zp, zm = shift_z(w)
        sum_y.append(yp + ym)
        dif_y.append(yp - ym)
        sum_z.append(zp + zm)
        dif_z.append(zp - zm)
    cross = []
    for b in (1, 2):
        yp, ym = shift_y(dif_z[b])
        cross.append(0.5 * (yp - ym))
    inner = (
        sum_y[0] + sum_z[0],
        3.0 * sum_y[1] + sum_z[1] + cross[1],
        sum_y[2] + 3.0 * sum_z[2] + cross[0],
    )
    odd = (0.5 * (dif_y[1] + dif_z[2]), 0.5 * dif_y[0], 0.5 * dif_z[0])
    even = (3.0 * u[0], u[1], u[2])
    cut = lambda ws: [w[:rows] for w in ws]
    return cut(inner), cut(even), cut(odd)


def voltage_parts(v, rows):
    yp, ym = shift_y(v)
    zp, zm = shift_z(v)
    dif_z = zp - zm
    zyp, zym = shift_y(dif_z)
    return [w[:rows] for w in (yp + ym, zp + zm, yp - ym, dif_z, zyp - zym)]


def spread(classes, block_depth):
    blocks, _ = classes.shape
    cell = lax.broadcasted_iota(jnp.int32, (blocks, blocks * block_depth), 1) // block_depth
    block = lax.broadcasted_iota(jnp.int32, (blocks, blocks * block_depth), 0)
    pick = (cell == block).astype(F32)
    return lax.dot_general(
        classes.astype(F32), pick, (((0,), (0,)), ((), ())), preferred_element_type=F32
    )


def fiber_of(tab_ref, cls):
    out = [jnp.full(cls.shape, tab_ref[a, 0], F32) for a in range(3)]
    for k in range(1, tab_ref.shape[1]):
        hit = cls == float(k)
        out = [jnp.where(hit, tab_ref[a, k], out[a]) for a in range(3)]
    return out


def conduct(fib):
    d = {}
    for a in range(3):
        d[a, a] = 0.25 + 0.75 * fib[a] * fib[a]
    for a, b in ((0, 1), (0, 2), (1, 2)):
        d[a, b] = 0.75 * fib[a] * fib[b]
    return d


def plane_sum(d, v, parts):
    sum_y, sum_z, _, _, cross = parts
    return (
        d[1, 1] * sum_y + d[2, 2] * sum_z + 0.5 * d[1, 2] * cross - 2.0 * (d[0, 0] + d[1, 1] + d[2, 2]) * v
    )


def from_plane(d, v, dif_y, dif_z, sign):
    return d[0, 0] * v + (0.5 * sign) * (d[0, 1] * dif_y + d[0, 2] * dif_z)


def currents(v, c, d, f, n, r):
    q = c * c / (c * c + 0.25)
    calcium_flow = 1.2 * d * f * (v - 2.0)
    total = calcium_flow + 0.8 * n * (v + 1.0) + 0.6 * q * r * (v + 1.0) + 0.1 * v
    return q, calcium_flow, total


def permute_rows(listed, values):
    rows = values.shape[0]
    pick = (lax.broadcasted_iota(jnp.int32, (rows, rows), 0).astype(F32) == listed).astype(F32)
    return lax.dot_general(
        pick, values, (((0,), (0,)), ((), ())), precision=HIGHEST, preferred_element_type=F32
    )


def tie_rows(listed, stiff, u):
    joined = jnp.concatenate([2.0 * stiff * w for w in u], axis=1)
    moved = permute_rows(listed, joined)
    depth = u[0].shape[1]
    return [moved[:, a * depth : (a + 1) * depth] for a in range(3)]


def whole(main, side):
    return jnp.concatenate([main, side], axis=0)


def tension_kernel(pos_ref, map_ref, sec_ref, all_ref, a_ref, b_ref, plain):
    size_x, size_y = sec_ref.shape[1], sec_ref.shape[2]

    @pl.when(pos_ref[0] == 0)
    def _():
        def plane(x, carry):
            v, c, d, f, bound, s = [sec_ref[k, x] for k in (0, 1, 2, 3, 6, 7)]
            calcium_flow = 1.2 * d * f * (v - 2.0)
            q = c * c / (c * c + 0.25)
            flow = 2.0 * c * (1.0 - bound) - 0.4 * bound
            c1 = c + DT * (-0.3 * calcium_flow - 0.5 * c - flow)
            s1 = s + DT * (q - s) / 2.0
            q1 = c1 * c1 / (c1 * c1 + 0.25)
            plain[pl.ds(pl.multiple_of(x * size_y, size_y), size_y), :] = s1 + DT * (q1 - s1) / 2.0
            return carry

        lax.fori_loop(0, size_x, plane, 0)

        def rows(i, carry):
            for k in range(16):
                p = i * 16 + k
                all_ref[pl.ds(p, 1), :] = plain[pl.ds(map_ref[p], 1), :]
            return carry

        lax.fori_loop(0, size_x * size_y // 16, rows, 0)
        last = (size_x - 1) * size_y
        even = pos_ref[1] == 0
        a_ref[...] = all_ref[pl.ds(pl.multiple_of(jnp.where(even, last, 0), size_y), size_y), :]
        b_ref[...] = all_ref[pl.ds(pl.multiple_of(jnp.where(even, 0, last), size_y), size_y), :]


def message_kernel(pos_ref, tab_ref, sec_ref, side_ref, cls_ref, list_ref, a_ref, b_ref):
    size_x, size_y = sec_ref.shape[1], sec_ref.shape[2]
    block_depth = sec_ref.shape[3] // cls_ref.shape[1]
    for slot, out in enumerate((a_ref, b_ref)):
        right = (pos_ref[1] + slot) % 2 == 0
        edge = jnp.where(right, size_x - 1, 0)
        inner = jnp.where(right, size_x - 2, 1)
        sign = jnp.where(right, 1.0, -1.0).astype(F32)
        out[ROW_CLASS : ROW_CLASS + cls_ref.shape[1], 0:size_y] = cls_ref[edge].astype(F32)
        out[ROW_LIST : ROW_LIST + 8, 0:size_y] = jnp.broadcast_to(
            list_ref[jnp.where(right, 1, 0)].astype(F32), (8, size_y)
        )
        for a in range(3):
            out[ROW_NOW + a * size_y : ROW_NOW + (a + 1) * size_y, :] = sec_ref[a, edge]
            out[ROW_SIDE + a * 8 : ROW_SIDE + (a + 1) * 8, :] = side_ref[a, edge]

        @pl.when(pos_ref[0] == 0)
        def _():
            v, c, d, f, n, r = [sec_ref[k, edge] for k in range(6)]
            con = conduct(fiber_of(tab_ref, spread(cls_ref[edge], block_depth)))
            own = voltage_parts(whole(v, side_ref[0, edge]), size_y)
            near_v = sec_ref[0, inner]
            near = voltage_parts(whole(near_v, side_ref[0, inner]), size_y)
            _, _, total = currents(v, c, d, f, n, r)
            lap = plane_sum(con, v, own) + from_plane(con, near_v, near[2], near[3], -sign)
            out[ROW_NEXT : ROW_NEXT + size_y, :] = v + DT * (lap - total)

        @pl.when(pos_ref[0] != 0)
        def _():
            u = [sec_ref[a, edge] for a in range(3)]
            within, _, _ = motion_parts([whole(u[a], side_ref[a, edge]) for a in range(3)], size_y)
            _, even, odd = motion_parts(
                [whole(sec_ref[a, inner], side_ref[a, inner]) for a in range(3)], size_y
            )
            stiff = sec_ref[6, edge]
            beta = OMEGA / stiff
            out[ROW_STIFF : ROW_STIFF + size_y, :] = stiff
            out[ROW_COEF : ROW_COEF + size_y, :] = beta * sec_ref[7, edge]
            for a in range(3):
                out[ROW_NEXT + a * size_y : ROW_NEXT + (a + 1) * size_y, :] = (
                    0.28 * u[a]
                    + beta * sec_ref[3 + a, edge]
                    + OMEGA * (within[a] + even[a] - sign * odd[a])
                )


def first_kernel(
    pos_ref, tab_ref, sec_ref, side_ref, cls_ref, list_ref, got_a, got_b, ten_ref, ten_a, ten_b,
    next_ref, share_ref, rest_ref, wide, odds, evens
):
    size_x, size_y = sec_ref.shape[1], sec_ref.shape[2]
    block_depth = sec_ref.shape[3] // cls_ref.shape[1]
    slots = []
    for slot, got in enumerate((got_a, got_b)):
        right = (pos_ref[1] + slot) % 2 == 0
        slots.append(
            (
                got,
                (ten_a, ten_b)[slot],
                jnp.where(right, size_x + 1, 0),
                jnp.where(right, size_x - 1, 0),
                jnp.where(right, 1, 0),
                jnp.where(right, 1.0, -1.0).astype(F32),
            )
        )
    pick_last = lax.broadcasted_iota(jnp.int32, (8, sec_ref.shape[3]), 0) == 7

    def put(a, x, value):
        next_ref[a, x] = value
        share_ref[a, x] = jnp.where(pick_last, value[size_y - 8 :], value[:8])

    def got_plane(got, a):
        return whole(
            got[ROW_NOW + a * size_y : ROW_NOW + (a + 1) * size_y, :],
            got[ROW_SIDE + a * 8 : ROW_SIDE + (a + 1) * 8, :],
        )

    @pl.when(pos_ref[0] == 0)
    def _():
        for got, _, at, _, _, _ in slots:
            w = got_plane(got, 0)
            parts = voltage_parts(w, size_y)
            wide[0, at] = w[:size_y]
            odds[0, at] = parts[2]
            odds[1, at] = parts[3]

        def prepare(x, carry):
            v = sec_ref[0, x]
            parts = voltage_parts(whole(v, side_ref[0, x]), size_y)
            con = conduct(fiber_of(tab_ref, spread(cls_ref[x], block_depth)))
            wide[0, x + 1] = v
            odds[0, x + 1] = parts[2]
            odds[1, x + 1] = parts[3]
            evens[0, x + 1] = plane_sum(con, v, parts)
            return carry

        lax.fori_loop(0, size_x, prepare, 0)

        def step(x, carry):
            v, c, d, f, n, r, bound, s = [sec_ref[k, x] for k in range(8)]
            con = conduct(fiber_of(tab_ref, spread(cls_ref[x], block_depth)))
            lap = (
                evens[0, x + 1]
                + con[0, 0] * (wide[0, x + 2] + wide[0, x])
                + 0.5 * con[0, 1] * (odds[0, x + 2] - odds[0, x])
                + 0.5 * con[0, 2] * (odds[1, x + 2] - odds[1, x])
            )
            q, calcium_flow, total = currents(v, c, d, f, n, r)
            flow = 2.0 * c * (1.0 - bound) - 0.4 * bound
            put(0, x + 1, v + DT * (lap - total))
            rest_ref[0, x] = c + DT * (-0.3 * calcium_flow - 0.5 * c - flow)
            rest_ref[1, x] = d + DT * (sigmoid(2.0 * v + 1.0) - d) / 0.5
            rest_ref[2, x] = f + DT * (sigmoid(-2.0 * v) - f) / 3.0
            rest_ref[3, x] = n + DT * (sigmoid(2.0 * v) - n)
            rest_ref[4, x] = r + DT * (sigmoid(v - 0.5) - r) / 5.0
            rest_ref[5, x] = bound + DT * flow
            rest_ref[6, x] = s + DT * (q - s) / 2.0
            return carry

        lax.fori_loop(0, size_x, step, 0)
        for got, _, at, edge, _, sign in slots:
            con = conduct(
                fiber_of(tab_ref, spread(got[ROW_CLASS : ROW_CLASS + cls_ref.shape[1], 0:size_y], block_depth))
            )
            put(
                0,
                at,
                got[ROW_NEXT : ROW_NEXT + size_y, :]
                + DT * from_plane(con, wide[0, edge + 1], odds[0, edge + 1], odds[1, edge + 1], -sign),
            )

    @pl.when(pos_ref[0] != 0)
    def _():
        for got, _, at, _, _, _ in slots:
            _, even, odd = motion_parts([got_plane(got, a) for a in range(3)], size_y)
            for a in range(3):
                odds[a, at] = odd[a]
                evens[a, at] = even[a]

        def prepare(x, carry):
            u = [sec_ref[a, x] for a in range(3)]
            within, even, odd = motion_parts([whole(u[a], side_ref[a, x]) for a in range(3)], size_y)
            stiff = sec_ref[6, x]
            beta = OMEGA / stiff
            fib = fiber_of(tab_ref, spread(cls_ref[x], block_depth))
            act = sec_ref[7, x] * ten_ref[pl.ds(pl.multiple_of(x * size_y, size_y), size_y), :]
            rest_ref[6, x] = act
            for a in range(3):
                drive = beta * (sec_ref[3 + a, x] + act * fib[a])
                rest_ref[a, x] = drive
                wide[a, x + 1] = 0.4 * u[a] + drive + OMEGA * within[a]
                odds[a, x + 1] = odd[a]
                evens[a, x + 1] = even[a]
            return carry

        lax.fori_loop(0, size_x, prepare, 0)
        for got, _, _, edge, which, _ in slots:
            beta = OMEGA / sec_ref[6, edge]
            stiff = got[ROW_STIFF : ROW_STIFF + size_y, :]
            ties = tie_rows(
                list_ref[which].astype(F32),
                stiff,
                [got[ROW_NOW + a * size_y : ROW_NOW + (a + 1) * size_y, :] for a in range(3)],
            )
            for a in range(3):
                wide[a, edge + 1] = wide[a, edge + 1] + beta * ties[a] - 0.12 * sec_ref[a, edge]

        def sweep(x, carry):
            for a in range(3):
                put(
                    a,
                    x + 1,
                    wide[a, x + 1]
                    + OMEGA * (evens[a, x + 2] + evens[a, x] + odds[a, x + 2] - odds[a, x]),
                )
            return carry

        lax.fori_loop(0, size_x, sweep, 0)
        for got, ten, at, edge, _, sign in slots:
            fib = fiber_of(
                tab_ref, spread(got[ROW_CLASS : ROW_CLASS + cls_ref.shape[1], 0:size_y], block_depth)
            )
            beta = OMEGA / got[ROW_STIFF : ROW_STIFF + size_y, :]
            drive = got[ROW_COEF : ROW_COEF + size_y, :] * ten[...]
            ties = tie_rows(
                got[ROW_LIST : ROW_LIST + 1, 0:size_y], sec_ref[6, edge], [sec_ref[a, edge] for a in range(3)]
            )
            for a in range(3):
                put(
                    a,
                    at,
                    got[ROW_NEXT + a * size_y : ROW_NEXT + (a + 1) * size_y, :]
                    + OMEGA * (evens[a, edge + 1] - sign * odds[a, edge + 1])
                    + beta * ties[a]
                    + drive * fib[a],
                )


def second_kernel(
    pos_ref, tab_ref, sec_ref, cls_ref, list_ref, got_a, got_b, next_ref, share_ref, rest_ref,
    out_ref, wide, odds, evens
):
    size_x, size_y = sec_ref.shape[1], sec_ref.shape[2]
    block_depth = sec_ref.shape[3] // cls_ref.shape[1]

    @pl.when(pos_ref[0] == 0)
    def _():
        def prepare(x, carry):
            parts = voltage_parts(whole(next_ref[0, x], share_ref[0, x]), size_y)
            for k in range(5):
                (wide, wide, odds, odds, wide)[k][(0, 1, 0, 1, 2)[k], x] = parts[k]
            return carry

        lax.fori_loop(0, size_x + 2, prepare, 0)

        def step(x, carry):
            v = next_ref[0, x + 1]
            c, d, f, n, r, bound, s = [rest_ref[k, x] for k in range(7)]
            con = conduct(fiber_of(tab_ref, spread(cls_ref[x], block_depth)))
            lap = (
                plane_sum(con, v, (wide[0, x + 1], wide[1, x + 1], None, None, wide[2, x + 1]))
                + con[0, 0] * (next_ref[0, x + 2] + next_ref[0, x])
                + 0.5 * con[0, 1] * (odds[0, x + 2] - odds[0, x])
                + 0.5 * con[0, 2] * (odds[1, x + 2] - odds[1, x])
            )
            q, calcium_flow, total = currents(v, c, d, f, n, r)
            flow = 2.0 * c * (1.0 - bound) - 0.4 * bound
            out_ref[0, 0, x] = v + DT * (lap - total)
            out_ref[0, 1, x] = c + DT * (-0.3 * calcium_flow - 0.5 * c - flow)
            out_ref[0, 2, x] = n + DT * (sigmoid(2.0 * v) - n)
            out_ref[0, 3, x] = s + DT * (q - s) / 2.0
            return carry

        lax.fori_loop(0, size_x, step, 0)

    @pl.when(pos_ref[0] != 0)
    def _():
        def prepare(x, carry):
            u = [next_ref[a, x] for a in range(3)]
            within, even, odd = motion_parts([whole(u[a], share_ref[a, x]) for a in range(3)], size_y)
            own = jnp.clip(x - 1, 0, size_x - 1)
            for a in range(3):
                wide[a, x] = 0.4 * u[a] + rest_ref[a, own] + OMEGA * within[a]
                odds[a, x] = odd[a]
                evens[a, x] = even[a]
            return carry

        lax.fori_loop(0, size_x + 2, prepare, 0)
        for slot, got in enumerate((got_a, got_b)):
            right = (pos_ref[1] + slot) % 2 == 0
            at = jnp.where(right, size_x + 1, 0)
            edge = jnp.where(right, size_x - 1, 0)
            beta = OMEGA / sec_ref[6, edge]
            ties = tie_rows(
                list_ref[jnp.where(right, 1, 0)].astype(F32),
                got[ROW_STIFF : ROW_STIFF + size_y, :],
                [next_ref[a, at] for a in range(3)],
            )
            for a in range(3):
                wide[a, edge + 1] = wide[a, edge + 1] + beta * ties[a] - 0.12 * next_ref[a, edge + 1]

        def sweep(x, carry):
            for a in range(3):
                out_ref[0, a, x] = wide[a, x + 1] + OMEGA * (
                    evens[a, x + 2] + evens[a, x] + odds[a, x + 2] - odds[a, x]
                )
            out_ref[0, 3, x] = rest_ref[6, x]
            return carry

        lax.fori_loop(0, size_x, sweep, 0)


def fiber_table(fiber_angles):
    azimuth = fiber_angles[:, 0]
    elevation = fiber_angles[:, 1]
    return jnp.stack(
        [
            jnp.cos(azimuth) * jnp.cos(elevation),
            jnp.sin(azimuth) * jnp.cos(elevation),
            jnp.sin(elevation),
        ]
    )


def call(kernel, name, out_shape, operands, spaces, scratch=()):
    return pl.pallas_call(
        kernel,
        name=name,
        out_shape=out_shape,
        in_specs=[pl.BlockSpec(memory_space=space) for space in spaces],
        out_specs=jax.tree.map(lambda _: pl.BlockSpec(memory_space=pltpu.VMEM), out_shape),
        scratch_shapes=scratch,
        compiler_params=pltpu.CompilerParams(vmem_limit_bytes=VMEM_LIMIT),
    )(*operands)


def local(sections, fiber_angles, fiber_class, row_map, interface_rows):
    own = sections[0]
    _, size_x, size_y, depth = own.shape
    n_gx = lax.axis_size("gx")
    n_gy = lax.axis_size("gy")
    assert n_gx % 2 == 0 and n_gy == 2
    swap_a = swap_pairs([(i, i + 1) for i in range(0, n_gx, 2)])
    swap_b = swap_pairs([(i, (i + 1) % n_gx) for i in range(1, n_gx, 2)])
    cross_a = [(s * n_gx + i, (1 - s) * n_gx + j) for s in range(2) for i, j in swap_a]
    cross_b = [(s * n_gx + i, (1 - s) * n_gx + j) for s in range(2) for i, j in swap_b]
    both = swap_pairs([(0, 1)])
    S, V = pltpu.SMEM, pltpu.VMEM
    f32 = lambda *shape: jax.ShapeDtypeStruct(shape, F32)

    pos = jnp.stack([lax.axis_index("sec"), lax.axis_index("gx") % 2]).astype(jnp.int32)
    table = fiber_table(fiber_angles)
    classes = fiber_class.transpose(0, 2, 1)
    lists = interface_rows.reshape(2, 1, size_y)

    pick_last = jnp.arange(8)[:, None] == 7
    share = jnp.where(pick_last, own[:3, :, size_y - 8 :], own[:3, :, :8])
    side = lax.ppermute(share, "gy", both)
    tension, ten_a, ten_b = call(
        tension_kernel,
        "tension",
        (f32(size_x * size_y, depth), f32(size_y, depth), f32(size_y, depth)),
        (pos, row_map.reshape(-1), own),
        (S, S, V),
        [pltpu.VMEM((size_x * size_y, depth), F32)],
    )
    message_a, message_b = call(
        message_kernel,
        "message",
        (f32(MESSAGE_ROWS, depth), f32(MESSAGE_ROWS, depth)),
        (pos, table, own, side, classes, lists),
        (S, S, V, V, V, V),
    )
    got_b = lax.ppermute(message_b, "gx", swap_b)
    got_a = lax.ppermute(message_a, "gx", swap_a)
    ten_b = lax.ppermute(ten_b, ("sec", "gx"), cross_b)
    ten_a = lax.ppermute(ten_a, ("sec", "gx"), cross_a)
    tension = lax.ppermute(tension, "sec", both)
    fields = lambda n: pltpu.VMEM((n, size_x + 2, size_y, depth), F32)
    moved, share, rest = call(
        first_kernel,
        "first",
        (f32(3, size_x + 2, size_y, depth), f32(3, size_x + 2, 8, depth), f32(7, size_x, size_y, depth)),
        (pos, table, own, side, classes, lists, got_a, got_b, tension, ten_a, ten_b),
        (S, S, V, V, V, V, V, V, V, V, V),
        [fields(3), fields(3), fields(3)],
    )
    side = lax.ppermute(share, "gy", both)
    return call(
        second_kernel,
        "second",
        f32(1, 4, size_x, size_y, depth),
        (pos, table, own, classes, lists, got_a, got_b, moved, side, rest),
        (S, S, V, V, V, V, V, V, V, V),
        [fields(3), fields(3), fields(3)],
    )


def solution(mesh):
    in_specs = (
        P("sec", None, "gx", "gy", None),
        P(),
        P("gx", "gy", None),
        P("gx", "gy", None),
        P(None, "gx", "gy", None),
    )
    out_specs = P("sec", None, "gx", "gy", None)
    return jax.shard_map(local, mesh=mesh, in_specs=in_specs, out_specs=out_specs, check_vma=False)
```

time: 115 us -> 37.4 us (0.33)
  local copies, waits for them, and re-layouts: 40.1 us -> 2.29 us
  other arithmetic: 30.6 us -> 1.3 us
  starting transfers between devices: 33 us -> 10.1 us
  Pallas kernels: 0 us -> 17.2 us
  waiting for transfers between devices: 9.91 us -> 6.27 us
    ppermute x21 -> x7, starting transfers between devices: 33 us -> 10.1 us  [the longest x1 3.54 us: local(): got_b = lax.ppermute(message_b, 'gx', swap_b)]
    pallas_call x0 -> x4, Pallas kernels: none -> 17.2 us  [call(): pl.pallas_call(kernel, name=name, out_shape=out_shape, in_specs=[pl.Block...]
    broadcast_in_dim x10 -> x0, local copies, waits for them, and re-layouts: 15.9 us -> none  [cell_values(): widened = jnp.broadcast_to(picked[..., None], picked.shape + (block_depth,))]
    another operation x8 -> x2, other arithmetic: 8.1 us -> 0.09 us  [the longest x1 0.07 us: local(): jnp.stack([lax.axis_index('sec'), lax.axis_index('gx') % 2])]
    slice x10 -> x0, local copies, waits for them, and re-layouts: 7.02 us -> none  [the longest x4 5.59 us: local(): drive = own_data[3:6] + activity * cell_fiber[0:3]]
    mul x3 -> x0, local copies, waits for them, and re-layouts: 6.68 us -> none  [diffuse(): 2.0 * cell_fiber[slot_index]]
    concatenate x11 -> x0, other arithmetic: 5.88 us -> none  [the longest x10 4.92 us: extended_2(): block = jnp.concatenate([low, block, high], axis=dim)]
    gather x5 -> x0, local copies, waits for them, and re-layouts: 4.57 us -> none  [the longest x1 1.65 us: local(): jnp.take(received.reshape(slab_shape[0] * slab_shape[1], slab_shape[2]),...]
  transfers between devices with their start and end apart: 21 -> 7, of which waited for: 6 -> 3; matrix products, arithmetic and copies ran while one was open for 41% -> 0% of each run, Pallas kernels for 0% -> 7%
where the time goes in v1:
time: 37.4 us; the launch traced here: 37.2 us
  Pallas kernels  17.2 us (46%)
  starting transfers between devices  10.1 us (27%)
  waiting for transfers between devices  6.27 us (17%)
  local copies, waits for them, and re-layouts  2.29 us (6%)
  other arithmetic  1.3 us (3%)
    pallas_call x4, Pallas kernels, call(): pl.pallas_call(kernel, name=name, out_shape=out_shape, in_specs=[pl.Block...  17.2 us
    ppermute x1, starting transfers between devices, local(): got_b = lax.ppermute(message_b, 'gx', swap_b)  3.54 us
    ppermute x1, waiting for transfers between devices, local(): ten_b = lax.ppermute(ten_b, ('sec', 'gx'), cross_b)  2.68 us
    ppermute x1, starting transfers between devices, local(): ten_b = lax.ppermute(ten_b, ('sec', 'gx'), cross_b)  2.54 us
    unnamed x12, local copies, waits for them, and re-layouts  2.29 us
    ppermute x1, waiting for transfers between devices, local(): ten_a = lax.ppermute(ten_a, ('sec', 'gx'), cross_a)  2.12 us
    ppermute x1, starting transfers between devices, local(): got_a = lax.ppermute(message_a, 'gx', swap_a)  1.58 us
    ppermute x1, starting transfers between devices, local(): tension = lax.ppermute(tension, 'sec', both)  1.56 us
  transfers between devices with their start and end apart: 7, of which 3 were waited for; matrix products, arithmetic and copies ran while one was open for 0% of the time, Pallas kernels for 7%

profile of v1, /device:TPU:0, one launch (start us, length us, event | category | flops | bytes accessed | tf_op | source)
XLA Modules:
  0.0 37.2 jit_solution(13157301556642217980)
XLA Ops:
  0.0 1.2 %slice_select_fusion = f32[3,16,8,128]{3,2,1,0:T(8,128)S(1)} fusion(f32[8,16,32,128]{3,2,1,0:T(8,128)} %bitcast.14, pred[8]{0:T(512)(128)(4,1)S(1)} %iota_compare_fusion), kind=kLoop, calls=%fused_computation | loop fusion | flops 49152 | bytes 589832 | tf_op jit(solution)/shard_map/jit(_where)/select_n | solution.py:482
  1.2 0.5 %collective-permute-start = (f32[3,16,8,128]{3,2,1,0:T(8,128)S(1)}, f32[3,16,8,128]{3,2,1,0:T(8,128)S(1)}, u32[]{:S(2)}, u32[]{:S(2)}) collective-permute-start(f32[3,16,8,128]{3,2,1,0:T(8,128)S(1)} %slice_select_fusion), channel_id=1, source_target_pairs={{0,1},{1,0},{2,3},{3,2},{4,5},{5,4},{6,7},{7,6},{8,9},{9,8},{10,11... | collective-permute-start | bytes 589832 | tf_op jit(solution)/shard_map/ppermute | solution.py:483
  1.7 0.1 pad_add_fusion.pos_ref
  1.8 1.6 %copy-done = f32[1,8,16,32,128]{4,3,2,1,0:T(8,128)S(1)} copy-done((f32[1,8,16,32,128]{4,3,2,1,0:T(8,128)S(1)}, f32[1,8,16,32,128]{4,3,2,1,0:T(8,128)}, u32[]{:S(2)}) %copy-start) | copy-done | bytes 2097176
  3.4 0.7 %copy-done.4 = s32[1,1,512]{2,1,0:T(1,128)S(1)} copy-done((s32[1,1,512]{2,1,0:T(1,128)S(1)}, s32[1,1,512]{2,1,0:T(1,128)}, u32[]{:S(2)}) %copy-start.4) | copy-done | bytes 2072
  4.0 1.6 %tension.1 = (f32[512,128]{1,0:T(8,128)S(1)}, f32[32,128]{1,0:T(8,128)S(1)}, f32[32,128]{1,0:T(8,128)S(1)}) custom-call(s32[2]{0:T(128)S(1)} %pad_add_fusion.pos_ref, s32[512]{0:T(512)S(1)} %bitcast.25, f32[8,16,32,128]{3,2,1,0:T(8,128)S(1)} %bitcast.15), custom_call_target="tpu_custom_call" | custom-call | tf_op jit(solution)/shard_map/tension/pallas_call | solution.py:451
  5.6 1.6 %collective-permute-start.3 = (f32[512,128]{1,0:T(8,128)S(1)}, f32[512,128]{1,0:T(8,128)S(1)}, u32[]{:S(2)}, u32[]{:S(2)}) collective-permute-start(f32[512,128]{1,0:T(8,128)S(1)} %get-tuple-element.15), channel_id=1, source_target_pairs={{0,16},{16,0},{1,17},{17,1},{2,18},{18,2},{3,19},{19,3},{4,20},{20... | collective-permute-start | bytes 786440 | tf_op jit(solution)/shard_map/ppermute | solution.py:503
  7.2 0.0 copy-done.5
  7.2 0.1 multiply_bitcast_fusion.1
  7.3 0.0 collective-permute-done.side_ref
  7.3 1.1 %message.1 = (f32[296,128]{1,0:T(8,128)S(1)}, f32[296,128]{1,0:T(8,128)S(1)}) custom-call(s32[2]{0:T(128)S(1)} %pad_add_fusion.pos_ref, f32[3,8]{1,0:T(4,128)S(1)} %pad_maximum_fusion.tab_ref, f32[8,16,32,128]{3,2,1,0:T(8,128)S(1)} %bitcast.16, f32[3,16,8,128]{3,2,1,0:T(8,128)S(1)} %collective-permute-done.side_ref, s32[16,8,32]{2,1,0:T(8,128)S(1)} %bitcast.19, ...), custom_call_target="tpu_custom_call" | custom-call | tf_op jit(solution)/shard_map/message/pallas_call | solution.py:451
  8.4 1.6 %collective-permute-start.1 = (f32[296,128]{1,0:T(8,128)S(1)}, f32[296,128]{1,0:T(8,128)S(1)}, u32[]{:S(2)}, u32[]{:S(2)}) collective-permute-start(f32[296,128]{1,0:T(8,128)S(1)} %get-tuple-element.13), channel_id=1, source_target_pairs={{0,2},{4,6},{8,10},{12,14},{2,0},{6,4},{10,8},{14,12},{1,3},{5,7},... | collective-permute-start | bytes 454664 | tf_op jit(solution)/shard_map/ppermute | solution.py:500
  10.0 3.5 %collective-permute-start.2 = (f32[296,128]{1,0:T(8,128)S(1)}, f32[296,128]{1,0:T(8,128)S(1)}, u32[]{:S(2)}, u32[]{:S(2)}) collective-permute-start(f32[296,128]{1,0:T(8,128)S(1)} %get-tuple-element.14), channel_id=1, source_target_pairs={{2,4},{6,8},{10,12},{14,0},{4,2},{8,6},{12,10},{0,14},{3,5},{7,9},... | collective-permute-start | bytes 454664 | tf_op jit(solution)/shard_map/ppermute | solution.py:499
  13.5 0.3 collective-permute-start.4
  13.8 2.5 %collective-permute-start.5 = (f32[32,128]{1,0:T(8,128)S(1)}, f32[32,128]{1,0:T(8,128)S(1)}, u32[]{:S(2)}, u32[]{:S(2)}) collective-permute-start(f32[32,128]{1,0:T(8,128)S(1)} %get-tuple-element.17), channel_id=1, source_target_pairs={{2,20},{6,24},{10,28},{14,16},{4,18},{8,22},{12,26},{0,30},{18,4},... | collective-permute-start | bytes 49160 | tf_op jit(solution)/shard_map/ppermute | solution.py:501
  16.3 2.1 %collective-permute-done.4.ten_a = f32[32,128]{1,0:T(8,128)S(1)} collective-permute-done((f32[32,128]{1,0:T(8,128)S(1)}, f32[32,128]{1,0:T(8,128)S(1)}, u32[]{:S(2)}, u32[]{:S(2)}) %collective-permute-start.4) | collective-permute-done | bytes 16416 | tf_op jit(solution)/shard_map/ppermute | solution.py:502
  18.4 2.7 %collective-permute-done.5.ten_b = f32[32,128]{1,0:T(8,128)S(1)} collective-permute-done((f32[32,128]{1,0:T(8,128)S(1)}, f32[32,128]{1,0:T(8,128)S(1)}, u32[]{:S(2)}, u32[]{:S(2)}) %collective-permute-start.5) | collective-permute-done | bytes 16416 | tf_op jit(solution)/shard_map/ppermute | solution.py:501
  21.1 0.0 collective-permute-done.3.ten_ref
  21.1 0.0 collective-permute-done.1.got_a
  21.1 0.0 collective-permute-done.2.got_b
  21.1 7.8 %first.1 = (f32[3,18,32,128]{3,2,1,0:T(8,128)S(1)}, f32[3,18,8,128]{3,2,1,0:T(8,128)S(1)}, f32[7,16,32,128]{3,2,1,0:T(8,128)S(1)}) custom-call(s32[2]{0:T(128)S(1)} %pad_add_fusion.pos_ref, f32[3,8]{1,0:T(4,128)S(1)} %pad_maximum_fusion.tab_ref, f32[8,16,32,128]{3,2,1,0:T(8,128)S(1)} %bitcast.17, f32[3,16,8,128]{3,2,1,0:T(8,128)S(1)} %collective-permute-done.side_ref, ...), custom_call_target="tpu_custom_call" | custom-call | tf_op jit(solution)/shard_map/first/pallas_call | solution.py:451
  29.0 0.1 collective-permute-start.6
  29.1 1.5 %collective-permute-done.6.share_ref = f32[3,18,8,128]{3,2,1,0:T(8,128)S(1)} collective-permute-done((f32[3,18,8,128]{3,2,1,0:T(8,128)S(1)}, f32[3,18,8,128]{3,2,1,0:T(8,128)S(1)}, u32[]{:S(2)}, u32[]{:S(2)}) %collective-permute-start.6) | collective-permute-done | bytes 221216 | tf_op jit(solution)/shard_map/ppermute | solution.py:513
  30.5 6.7 %second.1 = f32[1,4,16,32,128]{4,3,2,1,0:T(8,128)} custom-call(s32[2]{0:T(128)S(1)} %pad_add_fusion.pos_ref, f32[3,8]{1,0:T(4,128)S(1)} %pad_maximum_fusion.tab_ref, f32[8,16,32,128]{3,2,1,0:T(8,128)S(1)} %bitcast.18, s32[16,8,32]{2,1,0:T(8,128)S(1)} %bitcast.21, s32[2,1,32]{2,1,0:T(1,128)S(1)} %bitcast.24, f32[296,128]{1,0:T(8,128)S(1)} %collective-permute-done.1.got_a, ...), custom_call_target="tpu_custom_call" | custom-call | tf_op jit(solution)/shard_map/second/pallas_call | solution.py:451
  (11 shorter events, 0.0 us)
Async XLA Ops:
  0.0 7.2 %copy-start.5 = (f32[8,2]{0,1:T(2,128)S(1)}, f32[8,2]{0,1:T(2,128)}, u32[]{:S(2)}) copy-start(f32[8,2]{0,1:T(2,128)} %param.6) | copy-start | bytes 196
  0.0 7.3 %copy-start.3 = (s32[2,1,1,32]{3,2,1,0:T(1,128)S(1)}, s32[2,1,1,32]{3,2,1,0:T(1,128)}, u32[]{:S(2)}) copy-start(s32[2,1,1,32]{3,2,1,0:T(1,128)} %param.9) | copy-start | bytes 772
  0.0 7.3 %copy-start.2 = (s32[16,32,8]{1,2,0:T(8,128)S(1)}, s32[16,32,8]{1,2,0:T(8,128)}, u32[]{:S(2)}) copy-start(s32[16,32,8]{1,2,0:T(8,128)} %param.7) | copy-start | bytes 49156
  1.2 6.1 %collective-permute-start = (f32[3,16,8,128]{3,2,1,0:T(8,128)S(1)}, f32[3,16,8,128]{3,2,1,0:T(8,128)S(1)}, u32[]{:S(2)}, u32[]{:S(2)}) collective-permute-start(f32[3,16,8,128]{3,2,1,0:T(8,128)S(1)} %slice_select_fusion), channel_id=1, source_target_pairs={{0,1},{1,0},{2,3},{3,2},{4,5},{5,4},{6,7},{7,6},{8,9},{9,8},{10,11... | collective-permute-start | bytes 589832 | tf_op jit(solution)/shard_map/ppermute | solution.py:483
  1.8 1.6 %copy-start = (f32[1,8,16,32,128]{4,3,2,1,0:T(8,128)S(1)}, f32[1,8,16,32,128]{4,3,2,1,0:T(8,128)}, u32[]{:S(2)}) copy-start(f32[1,8,16,32,128]{4,3,2,1,0:T(8,128)} %param.5) | copy-start | bytes 6291460
  3.4 0.7 %copy-start.4 = (s32[1,1,512]{2,1,0:T(1,128)S(1)}, s32[1,1,512]{2,1,0:T(1,128)}, u32[]{:S(2)}) copy-start(s32[1,1,512]{2,1,0:T(1,128)} %param.8) | copy-start | bytes 6148
  4.0 3.3 %copy-start.1 = (f32[1,8,16,32,128]{4,3,2,1,0:T(8,128)S(1)}, f32[1,8,16,32,128]{4,3,2,1,0:T(8,128)}, u32[]{:S(2)}) copy-start(f32[1,8,16,32,128]{4,3,2,1,0:T(8,128)} %param.5) | copy-start | bytes 6291460
  5.6 15.5 %collective-permute-start.3 = (f32[512,128]{1,0:T(8,128)S(1)}, f32[512,128]{1,0:T(8,128)S(1)}, u32[]{:S(2)}, u32[]{:S(2)}) collective-permute-start(f32[512,128]{1,0:T(8,128)S(1)} %get-tuple-element.15), channel_id=1, source_target_pairs={{0,16},{16,0},{1,17},{17,1},{2,18},{18,2},{3,19},{19,3},{4,20},{20... | collective-permute-start | bytes 786440 | tf_op jit(solution)/shard_map/ppermute | solution.py:503
  8.4 12.7 %collective-permute-start.1 = (f32[296,128]{1,0:T(8,128)S(1)}, f32[296,128]{1,0:T(8,128)S(1)}, u32[]{:S(2)}, u32[]{:S(2)}) collective-permute-start(f32[296,128]{1,0:T(8,128)S(1)} %get-tuple-element.13), channel_id=1, source_target_pairs={{0,2},{4,6},{8,10},{12,14},{2,0},{6,4},{10,8},{14,12},{1,3},{5,7},... | collective-permute-start | bytes 454664 | tf_op jit(solution)/shard_map/ppermute | solution.py:500
  10.0 11.2 %collective-permute-start.2 = (f32[296,128]{1,0:T(8,128)S(1)}, f32[296,128]{1,0:T(8,128)S(1)}, u32[]{:S(2)}, u32[]{:S(2)}) collective-permute-start(f32[296,128]{1,0:T(8,128)S(1)} %get-tuple-element.14), channel_id=1, source_target_pairs={{2,4},{6,8},{10,12},{14,0},{4,2},{8,6},{12,10},{0,14},{3,5},{7,9},... | collective-permute-start | bytes 454664 | tf_op jit(solution)/shard_map/ppermute | solution.py:499
  13.5 4.9 %collective-permute-start.4 = (f32[32,128]{1,0:T(8,128)S(1)}, f32[32,128]{1,0:T(8,128)S(1)}, u32[]{:S(2)}, u32[]{:S(2)}) collective-permute-start(f32[32,128]{1,0:T(8,128)S(1)} %get-tuple-element.16), channel_id=1, source_target_pairs={{0,18},{4,22},{8,26},{12,30},{2,16},{6,20},{10,24},{14,28},{16,2},... | collective-permute-start | bytes 49160 | tf_op jit(solution)/shard_map/ppermute | solution.py:502
  13.8 7.3 %collective-permute-start.5 = (f32[32,128]{1,0:T(8,128)S(1)}, f32[32,128]{1,0:T(8,128)S(1)}, u32[]{:S(2)}, u32[]{:S(2)}) collective-permute-start(f32[32,128]{1,0:T(8,128)S(1)} %get-tuple-element.17), channel_id=1, source_target_pairs={{2,20},{6,24},{10,28},{14,16},{4,18},{8,22},{12,26},{0,30},{18,4},... | collective-permute-start | bytes 49160 | tf_op jit(solution)/shard_map/ppermute | solution.py:501
  29.0 1.5 %collective-permute-start.6 = (f32[3,18,8,128]{3,2,1,0:T(8,128)S(1)}, f32[3,18,8,128]{3,2,1,0:T(8,128)S(1)}, u32[]{:S(2)}, u32[]{:S(2)}) collective-permute-start(f32[3,18,8,128]{3,2,1,0:T(8,128)S(1)} %get-tuple-element.19), channel_id=1, source_target_pairs={{0,1},{1,0},{2,3},{3,2},{4,5},{5,4},{6,7},{7,6},{8,9},{9,8},{10,11... | collective-permute-start | bytes 663560 | tf_op jit(solution)/shard_map/ppermute | solution.py:513

commit v2 on v1

v2 whole, which is shorter than its diff:
```python
import jax
import jax.numpy as jnp
from jax import lax
from jax.experimental import pallas as pl
from jax.experimental.pallas import tpu as pltpu
from jax.sharding import PartitionSpec as P

DT = 0.1
OMEGA = 0.06
F32 = jnp.float32
HIGHEST = lax.Precision.HIGHEST
VMEM_LIMIT = 32 * 1024 * 1024

PAD = 8

ROW_NOW, ROW_NEXT, ROW_STIFF, ROW_COEF, ROW_SIDE, ROW_CLASS, ROW_LIST = 0, 96, 192, 224, 256, 280, 288
MESSAGE_ROWS = 296


def swap_pairs(pairs):
    return pairs + [(b, a) for a, b in pairs]


def inverse(v):
    r = pl.reciprocal(v, approx=True)
    return r * (2.0 - v * r)


def rise(c):
    c2 = c * c
    return c2 * inverse(c2 + 0.25)


def ends(like):
    lane = lax.broadcasted_iota(jnp.int32, like, 1)
    return lane == like[1] - 1, lane == 0


def up_z(w, last):
    return jnp.where(last, 0.0, pltpu.roll(w, w.shape[1] - 1, 1))


def down_z(w, first):
    return jnp.where(first, 0.0, pltpu.roll(w, 1, 1))


def rows_of(pad, a, x, size_y, shift=0):
    return pad[a, x, PAD + shift : PAD + shift + size_y, :]


def motion_rate(pad, x, size_y):
    at = lambda a, dx=0, dy=0: rows_of(pad, a, x + dx, size_y, dy)
    u0, u1, u2 = at(0), at(1), at(2)
    last, first = ends(u0.shape)
    w0p, w0m, w1p, w1m = at(0, 1), at(0, -1), at(1, 1), at(1, -1)
    w2p, w2m = at(2, 1), at(2, -1)
    e0, e2 = 0.5 * (w0p - w0m), 0.5 * (w2p - w2m)
    e0y = (at(0, 1, 1) - at(0, -1, 1)) - (at(0, 1, -1) - at(0, -1, -1))
    e1y = (at(1, 1, 1) - at(1, -1, 1)) - (at(1, 1, -1) - at(1, -1, -1))
    v1p, v1m, v2p, v2m = at(1, 0, 1), at(1, 0, -1), at(2, 0, 1), at(2, 0, -1)
    d2 = 0.5 * (v2p - v2m)
    d1 = 0.5 * (v1p - v1m) + e0
    r0 = (
        up_z(u0 + e2, last) + down_z(u0 - e2, first)
        + (at(0, 0, 1) + at(0, 0, -1)) + 0.5 * e1y + 3.0 * (w0p + w0m)
    )
    r1 = (
        up_z(u1 + d2, last) + down_z(u1 - d2, first)
        + 3.0 * (v1p + v1m) + 0.5 * e0y + (w1p + w1m)
    )
    t2 = 3.0 * u2
    r2 = up_z(t2 + d1, last) + down_z(t2 - d1, first) + (v2p + v2m) + (w2p + w2m)
    return r0, r1, r2


def motion_from(pad, x, sign, size_y):
    u0, u1, u2 = [rows_of(pad, a, x, size_y) for a in range(3)]
    last, first = ends(u0.shape)
    half = 0.5 * sign
    dy0 = rows_of(pad, 0, x, size_y, 1) - rows_of(pad, 0, x, size_y, -1)
    dy1 = rows_of(pad, 1, x, size_y, 1) - rows_of(pad, 1, x, size_y, -1)
    dz0 = up_z(u0, last) - down_z(u0, first)
    dz2 = up_z(u2, last) - down_z(u2, first)
    return 3.0 * u0 + half * (dy1 + dz2), u1 + half * dy0, u2 + half * dz0


def volt_rate(pad, x, fib, size_y):
    at = lambda dx=0, dy=0: rows_of(pad, 0, x + dx, size_y, dy)
    v, wp, wm, yp, ym = at(), at(1), at(-1), at(0, 1), at(0, -1)
    last, first = ends(v.shape)
    e = wp - wm
    ey = (at(1, 1) - at(-1, 1)) - (at(1, -1) - at(-1, -1))
    dy = yp - ym
    sum_z = up_z(v, last) + down_z(v, first)
    ez = up_z(e, last) - down_z(e, first)
    dyz = up_z(dy, last) - down_z(dy, first)
    g = [0.75 * w for w in fib]
    d00, d11, d22 = [0.25 + a * b for a, b in zip(g, fib)]
    return (
        d00 * (wp + wm) + d11 * (yp + ym) + d22 * sum_z - 2.0 * (d00 + d11 + d22) * v
        + 0.5 * (fib[0] * (g[1] * ey + g[2] * ez) + g[1] * fib[2] * dyz)
    )


def volt_from(pad, x, fib, sign, size_y):
    v = rows_of(pad, 0, x, size_y)
    last, first = ends(v.shape)
    dy = rows_of(pad, 0, x, size_y, 1) - rows_of(pad, 0, x, size_y, -1)
    dz = up_z(v, last) - down_z(v, first)
    g = 0.75 * fib[0]
    return (0.25 + g * fib[0]) * v + (0.5 * sign) * g * (fib[1] * dy + fib[2] * dz)


def currents(v, c, d, f, n, r):
    q = rise(c)
    calcium_flow = 1.2 * d * f * (v - 2.0)
    return q, calcium_flow, calcium_flow + (0.8 * n + 0.6 * q * r) * (v + 1.0) + 0.1 * v


def spread(classes, block_depth):
    blocks, _ = classes.shape
    cell = lax.broadcasted_iota(jnp.int32, (blocks, blocks * block_depth), 1) // block_depth
    block = lax.broadcasted_iota(jnp.int32, (blocks, blocks * block_depth), 0)
    pick = (cell == block).astype(F32)
    return lax.dot_general(
        classes.astype(F32), pick, (((0,), (0,)), ((), ())), preferred_element_type=F32
    )


def fiber_of(tab_ref, cls):
    out = [jnp.full(cls.shape, tab_ref[a, 0], F32) for a in range(3)]
    for k in range(1, tab_ref.shape[1]):
        hit = cls == float(k)
        out = [jnp.where(hit, tab_ref[a, k], out[a]) for a in range(3)]
    return out


def permute_rows(listed, values):
    rows = values.shape[0]
    pick = (lax.broadcasted_iota(jnp.int32, (rows, rows), 0).astype(F32) == listed).astype(F32)
    return lax.dot_general(
        pick, values, (((0,), (0,)), ((), ())), precision=HIGHEST, preferred_element_type=F32
    )


def tie_rows(listed, stiff, u):
    joined = jnp.concatenate([2.0 * stiff * w for w in u], axis=1)
    moved = permute_rows(listed, joined)
    depth = u[0].shape[1]
    return [moved[:, a * depth : (a + 1) * depth] for a in range(3)]


def edges_tile(value):
    rows = value.shape[0]
    last = lax.broadcasted_iota(jnp.int32, (8, value.shape[1]), 0) == 7
    return jnp.where(last, value[rows - 8 :], value[:8])


def fill_sides(pad, a, x, tile, size_y):
    pad[a, x, 0:PAD, :] = tile
    pad[a, x, PAD + size_y :, :] = tile


def sides(pos_ref, size_x):
    out = []
    for slot in range(2):
        right = (pos_ref[1] + slot) % 2 == 0
        out.append(
            (
                jnp.where(right, size_x + 1, 0),
                jnp.where(right, size_x - 1, 0),
                jnp.where(right, 1, 0),
                jnp.where(right, 1.0, -1.0).astype(F32),
            )
        )
    return out


def load_kernel(sec_hbm, pad, rest, share, sems):
    size_x, size_y = sec_hbm.shape[1], sec_hbm.shape[2]
    inside = pl.ds(PAD, size_y)
    main = pltpu.make_async_copy(sec_hbm.at[0:3], pad.at[:, 1 : size_x + 1, inside, :], sems.at[0])
    other = pltpu.make_async_copy(sec_hbm.at[3:8], rest, sems.at[1])
    main.start()
    other.start()
    zeros = jnp.zeros(pad.shape[2:], F32)
    for a in range(3):
        pad[a, 0] = zeros
        pad[a, size_x + 1] = zeros
    main.wait()

    def plane(x, carry):
        for a in range(3):
            share[a, x] = edges_tile(rows_of(pad, a, x + 1, size_y))
        return carry

    lax.fori_loop(0, size_x, plane, 0, unroll=4)
    other.wait()


def local_kernel(pos_ref, map_ref, tab_ref, pad, rest, cls_ref, plain, all_ref, a_ref, b_ref, fib_ref, flat):
    size_x, size_y = rest.shape[1], rest.shape[2]
    blocks, classes = cls_ref.shape[1], tab_ref.shape[1]
    depth = rest.shape[3]

    @pl.when(pos_ref[0] == 0)
    def _():
        def plane(x, carry):
            v, c, d = [rows_of(pad, a, x + 1, size_y) for a in range(3)]
            f, bound, s = rest[0, x], rest[3, x], rest[4, x]
            calcium_flow = 1.2 * d * f * (v - 2.0)
            flow = 2.0 * c * (1.0 - bound) - 0.4 * bound
            c1 = c + DT * (-0.3 * calcium_flow - 0.5 * c - flow)
            s1 = s + (0.5 * DT) * (rise(c) - s)
            plain[pl.ds(pl.multiple_of(x * size_y, size_y), size_y), :] = s1 + (0.5 * DT) * (rise(c1) - s1)
            return carry

        lax.fori_loop(0, size_x, plane, 0, unroll=2)

        def rows(i, carry):
            for k in range(16):
                p = i * 16 + k
                all_ref[pl.ds(p, 1), :] = plain[pl.ds(map_ref[p], 1), :]
            return carry

        lax.fori_loop(0, size_x * size_y // 16, rows, 0)
        last = (size_x - 1) * size_y
        even = pos_ref[1] == 0
        a_ref[...] = all_ref[pl.ds(pl.multiple_of(jnp.where(even, last, 0), size_y), size_y), :]
        b_ref[...] = all_ref[pl.ds(pl.multiple_of(jnp.where(even, 0, last), size_y), size_y), :]

    for x in range(size_x):
        flat[:, x * size_y : (x + 1) * size_y] = cls_ref[x]
    cls = flat[...]
    hits = jnp.concatenate([(cls == k).astype(F32) for k in range(classes)], axis=0)
    own = lax.broadcasted_iota(jnp.int32, (blocks, depth), 1) // (depth // blocks)
    own = own == lax.broadcasted_iota(jnp.int32, (blocks, depth), 0)
    table = jnp.concatenate(
        [
            jnp.concatenate([jnp.where(own, tab_ref[a, k], 0.0) for a in range(3)], axis=1)
            for k in range(classes)
        ],
        axis=0,
    )
    fib = lax.dot_general(
        hits, table, (((0,), (0,)), ((), ())), precision=HIGHEST, preferred_element_type=F32
    )
    for a in range(3):
        fib_ref[a] = fib[:, a * depth : (a + 1) * depth]


def message_kernel(pos_ref, pad_in, rest, side_ref, fib_ref, cls_ref, list_ref, a_ref, b_ref, pad):
    size_x, size_y = rest.shape[1], rest.shape[2]

    def fill(x, carry):
        for a in range(3):
            fill_sides(pad, a, x + 1, side_ref[a, x], size_y)
        return carry

    lax.fori_loop(0, size_x, fill, 0, unroll=4)
    for (_, edge, which, _), out in zip(sides(pos_ref, size_x), (a_ref, b_ref)):
        out[ROW_CLASS : ROW_CLASS + cls_ref.shape[1], 0:size_y] = cls_ref[edge].astype(F32)
        out[ROW_LIST : ROW_LIST + 8, 0:size_y] = jnp.broadcast_to(list_ref[which].astype(F32), (8, size_y))
        for a in range(3):
            out[ROW_NOW + a * size_y : ROW_NOW + (a + 1) * size_y, :] = rows_of(pad, a, edge + 1, size_y)
            out[ROW_SIDE + a * 8 : ROW_SIDE + (a + 1) * 8, :] = side_ref[a, edge]

        @pl.when(pos_ref[0] == 0)
        def _():
            v, c, d = [rows_of(pad, a, edge + 1, size_y) for a in range(3)]
            f, n, r = [rest[k, edge] for k in range(3)]
            place = pl.ds(pl.multiple_of(edge * size_y, size_y), size_y)
            rate = volt_rate(pad, edge + 1, [fib_ref[a, place, :] for a in range(3)], size_y)
            _, _, total = currents(v, c, d, f, n, r)
            out[ROW_NEXT : ROW_NEXT + size_y, :] = v + DT * (rate - total)

        @pl.when(pos_ref[0] != 0)
        def _():
            rate = motion_rate(pad, edge + 1, size_y)
            stiff = rest[3, edge]
            beta = OMEGA * inverse(stiff)
            out[ROW_STIFF : ROW_STIFF + size_y, :] = stiff
            out[ROW_COEF : ROW_COEF + size_y, :] = beta * rest[4, edge]
            for a in range(3):
                out[ROW_NEXT + a * size_y : ROW_NEXT + (a + 1) * size_y, :] = (
                    0.28 * rows_of(pad, a, edge + 1, size_y) + beta * rest[a, edge] + OMEGA * rate[a]
                )


def inner_kernel(pos_ref, pad, rest, fib_ref, ten_ref, next_pad, share, keep):
    size_x, size_y = rest.shape[1], rest.shape[2]

    def put(a, x, value):
        next_pad[a, x, PAD : PAD + size_y, :] = value
        share[a, x] = edges_tile(value)

    @pl.when(pos_ref[0] == 0)
    def _():
        def plane(x, carry):
            place = pl.ds(pl.multiple_of(x * size_y, size_y), size_y)
            v, c, d = [rows_of(pad, a, x + 1, size_y) for a in range(3)]
            f, n, r, bound, _ = [rest[k, x] for k in range(5)]
            rate = volt_rate(pad, x + 1, [fib_ref[a, place, :] for a in range(3)], size_y)
            q, calcium_flow, total = currents(v, c, d, f, n, r)
            flow = 2.0 * c * (1.0 - bound) - 0.4 * bound
            put(0, x + 1, v + DT * (rate - total))
            c1 = c + DT * (-0.3 * calcium_flow - 0.5 * c - flow)
            tv = jnp.tanh(v)
            d1 = (1.0 - 2.0 * DT) * d + DT * (1.0 + jnp.tanh(v + 0.5))
            f1 = (1.0 - DT / 3.0) * f + (DT / 6.0) * (1.0 - tv)
            n1 = (1.0 - DT) * n + (0.5 * DT) * (1.0 + tv)
            r1 = (1.0 - DT / 5.0) * r + (DT / 10.0) * (1.0 + jnp.tanh(0.5 * v - 0.25))
            bound1 = bound + DT * flow
            flow1 = 2.0 * c1 * (1.0 - bound1) - 0.4 * bound1
            gate = 1.2 * d1 * f1
            leak = 0.8 * n1 + 0.6 * rise(c1) * r1
            keep[0, x] = n1
            keep[1, x] = gate
            keep[2, x] = leak
            keep[3, x] = c1 - DT * (0.5 * c1 + flow1)
            return carry

        lax.fori_loop(0, size_x, plane, 0, unroll=2)

    @pl.when(pos_ref[0] != 0)
    def _():
        def plane(x, carry):
            place = pl.ds(pl.multiple_of(x * size_y, size_y), size_y)
            rate = motion_rate(pad, x + 1, size_y)
            beta = OMEGA * inverse(rest[3, x])
            act = rest[4, x] * ten_ref[place, :]
            keep[3, x] = act
            for a in range(3):
                drive = beta * (rest[a, x] + act * fib_ref[a, place, :])
                keep[a, x] = drive
                put(a, x + 1, 0.4 * rows_of(pad, a, x + 1, size_y) + drive + OMEGA * rate[a])
            return carry

        lax.fori_loop(0, size_x, plane, 0, unroll=2)


def outer_kernel(
    pos_ref, tab_ref, pad_in, rest, fib_ref, cls_ref, list_ref, got_a, got_b, ten_a, ten_b, next_in, share_in,
    next_pad, share, wide
):
    size_x, size_y = rest.shape[1], rest.shape[2]
    block_depth = rest.shape[3] // cls_ref.shape[1]

    def put(a, x, value):
        next_pad[a, x, PAD : PAD + size_y, :] = value
        share[a, x] = edges_tile(value)

    work = list(zip(sides(pos_ref, size_x), (got_a, got_b), (ten_a, ten_b)))
    for slot, (_, got, _) in enumerate(work):
        for a in range(3):
            wide[a, slot, PAD : PAD + size_y, :] = got[ROW_NOW + a * size_y : ROW_NOW + (a + 1) * size_y, :]
            fill_sides(wide, a, slot, got[ROW_SIDE + a * 8 : ROW_SIDE + (a + 1) * 8, :], size_y)

    @pl.when(pos_ref[0] == 0)
    def _():
        for slot, ((halo, edge, _, sign), got, _) in enumerate(work):
            place = pl.ds(pl.multiple_of(edge * size_y, size_y), size_y)
            fib = [fib_ref[a, place, :] for a in range(3)]
            put(
                0,
                edge + 1,
                rows_of(next_pad, 0, edge + 1, size_y) + DT * volt_from(wide, slot, fib, sign, size_y),
            )
            fib = fiber_of(
                tab_ref, spread(got[ROW_CLASS : ROW_CLASS + cls_ref.shape[1], 0:size_y], block_depth)
            )
            put(
                0,
                halo,
                got[ROW_NEXT : ROW_NEXT + size_y, :] + DT * volt_from(pad_in, edge + 1, fib, -sign, size_y),
            )

    @pl.when(pos_ref[0] != 0)
    def _():
        for slot, ((halo, edge, which, sign), got, ten) in enumerate(work):
            stiff = got[ROW_STIFF : ROW_STIFF + size_y, :]
            own = rest[3, edge]
            now = [rows_of(pad_in, a, edge + 1, size_y) for a in range(3)]
            theirs = [rows_of(wide, a, slot, size_y) for a in range(3)]
            ties = tie_rows(list_ref[which].astype(F32), stiff, theirs)
            rate = motion_from(wide, slot, sign, size_y)
            beta = OMEGA * inverse(own)
            for a in range(3):
                put(
                    a,
                    edge + 1,
                    rows_of(next_pad, a, edge + 1, size_y) + OMEGA * rate[a] + beta * ties[a] - 0.12 * now[a],
                )
            fib = fiber_of(
                tab_ref, spread(got[ROW_CLASS : ROW_CLASS + cls_ref.shape[1], 0:size_y], block_depth)
            )
            ties = tie_rows(got[ROW_LIST : ROW_LIST + 1, 0:size_y], own, now)
            rate = motion_from(pad_in, edge + 1, -sign, size_y)
            beta = OMEGA * inverse(stiff)
            drive = got[ROW_COEF : ROW_COEF + size_y, :] * ten[...]
            for a in range(3):
                put(
                    a,
                    halo,
                    got[ROW_NEXT + a * size_y : ROW_NEXT + (a + 1) * size_y, :]
                    + OMEGA * rate[a] + beta * ties[a] + drive * fib[a],
                )


def last_kernel(
    pos_ref, rest, fib_ref, list_ref, plain, got_a, got_b, next_in, side_ref, keep, out_hbm, next_pad, out, sems
):
    size_x, size_y = rest.shape[1], rest.shape[2]
    chunk = size_x // sems.shape[0]

    def copy_out(i):
        return pltpu.make_async_copy(
            out.at[:, pl.ds(i * chunk, chunk)], out_hbm.at[0, :, pl.ds(i * chunk, chunk)], sems.at[i]
        )

    def fill(x, carry):
        for a in range(3):
            fill_sides(next_pad, a, x, side_ref[a, x], size_y)
        return carry

    @pl.when(pos_ref[0] == 0)
    def _():
        def fill_one(x, carry):
            fill_sides(next_pad, 0, x, side_ref[0, x], size_y)
            return carry

        lax.fori_loop(0, size_x + 2, fill_one, 0, unroll=3)

        def step(i, carry):
            for k in range(chunk):
                x = i * chunk + k
                place = pl.ds(pl.multiple_of(x * size_y, size_y), size_y)
                v = rows_of(next_pad, 0, x + 1, size_y)
                n, gate, leak, rest_c = [keep[k, x] for k in range(4)]
                rate = volt_rate(next_pad, x + 1, [fib_ref[a, place, :] for a in range(3)], size_y)
                flow = gate * (v - 2.0)
                out[0, x] = v + DT * (rate - flow - leak * (v + 1.0) - 0.1 * v)
                out[1, x] = rest_c - (0.3 * DT) * flow
                out[2, x] = (1.0 - DT) * n + (0.5 * DT) * (1.0 + jnp.tanh(v))
                out[3, x] = plain[place, :]
            copy_out(i).start()
            return carry

        lax.fori_loop(0, size_x // chunk, step, 0)

    @pl.when(pos_ref[0] != 0)
    def _():
        lax.fori_loop(0, size_x + 2, fill, 0, unroll=3)
        for (halo, edge, which, _), got in zip(sides(pos_ref, size_x), (got_a, got_b)):
            beta = OMEGA * inverse(rest[3, edge])
            tie = tie_rows(
                list_ref[which].astype(F32),
                got[ROW_STIFF : ROW_STIFF + size_y, :],
                [rows_of(next_pad, a, halo, size_y) for a in range(3)],
            )
            for a in range(3):
                out[a, edge] = beta * tie[a] - 0.12 * rows_of(next_pad, a, edge + 1, size_y)

        def sweep(i, carry):
            for k in range(chunk):
                x = i * chunk + k
                rate = motion_rate(next_pad, x + 1, size_y)
                tied = jnp.logical_or(x == 0, x == size_x - 1)
                for a in range(3):
                    value = 0.4 * rows_of(next_pad, a, x + 1, size_y) + keep[a, x] + OMEGA * rate[a]
                    out[a, x] = value + jnp.where(tied, out[a, x], 0.0)
                out[3, x] = keep[3, x]
            copy_out(i).start()
            return carry

        lax.fori_loop(0, size_x // chunk, sweep, 0)

    for i in range(size_x // chunk):
        copy_out(i).wait()


def fiber_table(fiber_angles):
    azimuth = fiber_angles[:, 0]
    elevation = fiber_angles[:, 1]
    return jnp.stack(
        [
            jnp.cos(azimuth) * jnp.cos(elevation),
            jnp.sin(azimuth) * jnp.cos(elevation),
            jnp.sin(elevation),
        ]
    )


def call(kernel, name, out_shape, operands, spaces, scratch=(), out_spaces=None, aliases=()):
    if out_spaces is None:
        out_spaces = [pltpu.VMEM] * len(out_shape)
    return pl.pallas_call(
        kernel,
        name=name,
        out_shape=tuple(out_shape),
        in_specs=[pl.BlockSpec(memory_space=space) for space in spaces],
        out_specs=tuple(pl.BlockSpec(memory_space=space) for space in out_spaces),
        scratch_shapes=scratch,
        input_output_aliases=dict(aliases),
        compiler_params=pltpu.CompilerParams(vmem_limit_bytes=VMEM_LIMIT),
    )(*operands)


def local(sections, fiber_angles, fiber_class, row_map, interface_rows):
    own = sections[0]
    channels, size_x, size_y, depth = own.shape
    n_gx = lax.axis_size("gx")
    n_gy = lax.axis_size("gy")
    assert n_gx % 2 == 0 and n_gy == 2
    swap_a = swap_pairs([(i, i + 1) for i in range(0, n_gx, 2)])
    swap_b = swap_pairs([(i, (i + 1) % n_gx) for i in range(1, n_gx, 2)])
    cross_a = [(s * n_gx + i, (1 - s) * n_gx + j) for s in range(2) for i, j in swap_a]
    cross_b = [(s * n_gx + i, (1 - s) * n_gx + j) for s in range(2) for i, j in swap_b]
    both = swap_pairs([(0, 1)])
    S, V, H = pltpu.SMEM, pltpu.VMEM, pltpu.HBM
    f32 = lambda *shape: jax.ShapeDtypeStruct(shape, F32)
    columns = size_x * size_y
    padded = f32(3, size_x + 2, size_y + 2 * PAD, depth)
    tiles = f32(3, size_x + 2, 8, depth)
    plane = f32(size_y, depth)

    pos = jnp.stack([lax.axis_index("sec"), lax.axis_index("gx") % 2]).astype(jnp.int32)
    table = fiber_table(fiber_angles)
    classes = fiber_class.transpose(0, 2, 1)
    lists = interface_rows.reshape(2, 1, size_y)

    pad, rest, share = call(
        load_kernel,
        "load",
        (padded, f32(channels - 3, size_x, size_y, depth), f32(3, size_x, 8, depth)),
        (pltpu.with_memory_space_constraint(own, H),),
        (H,),
        [pltpu.SemaphoreType.DMA((2,))],
    )
    side = lax.ppermute(share, "gy", both)
    plain, tension, ten_a, ten_b, fib = call(
        local_kernel,
        "local",
        (f32(columns, depth), f32(columns, depth), plane, plane, f32(3, columns, depth)),
        (pos, row_map.reshape(-1), table, pad, rest, classes),
        (S, S, S, V, V, V),
        [pltpu.VMEM((classes.shape[1], columns), jnp.int32)],
    )
    message = f32(MESSAGE_ROWS, depth)
    message_a, message_b, pad = call(
        message_kernel,
        "message",
        (message, message, padded),
        (pos, pad, rest, side, fib, classes, lists),
        (S, V, V, V, V, V, V),
        aliases={1: 2},
    )
    got_b = lax.ppermute(message_b, "gx", swap_b)
    got_a = lax.ppermute(message_a, "gx", swap_a)
    ten_b = lax.ppermute(ten_b, ("sec", "gx"), cross_b)
    ten_a = lax.ppermute(ten_a, ("sec", "gx"), cross_a)
    tension = lax.ppermute(tension, "sec", both)
    moved, share, keep = call(
        inner_kernel,
        "inner",
        (padded, tiles, f32(4, size_x, size_y, depth)),
        (pos, pad, rest, fib, tension),
        (S, V, V, V, V),
    )
    moved, share = call(
        outer_kernel,
        "outer",
        (padded, tiles),
        (pos, table, pad, rest, fib, classes, lists, got_a, got_b, ten_a, ten_b, moved, share),
        (S, S, V, V, V, V, V, V, V, V, V, V, V),
        [pltpu.VMEM((3, 2) + padded.shape[2:], F32)],
        aliases={11: 0, 12: 1},
    )
    side = lax.ppermute(share, "gy", both)
    return call(
        last_kernel,
        "last",
        (f32(1, 4, size_x, size_y, depth), padded),
        (pos, rest, fib, lists, plain, got_a, got_b, moved, side, keep),
        (S, V, V, V, V, V, V, V, V, V),
        [
            pltpu.VMEM((4, size_x, size_y, depth), F32),
            pltpu.SemaphoreType.DMA((4,)),
        ],
        out_spaces=(H, V),
        aliases={7: 1},
    )[0]


def solution(mesh):
    in_specs = (
        P("sec", None, "gx", "gy", None),
        P(),
        P("gx", "gy", None),
        P("gx", "gy", None),
        P(None, "gx", "gy", None),
    )
    out_specs = P("sec", None, "gx", "gy", None)
    return jax.shard_map(local, mesh=mesh, in_specs=in_specs, out_specs=out_specs, check_vma=False)
```

time: 37.4 us -> 24.8 us (0.66)
  Pallas kernels: 17.2 us -> 9.62 us
  local copies, waits for them, and re-layouts: 2.29 us -> 0.01 us
  waiting for transfers between devices: 6.27 us -> 4.65 us
  other arithmetic: 1.3 us -> 0.14 us
    pallas_call x4 -> x6, Pallas kernels: 17.2 us -> 9.62 us  [call(): pl.pallas_call(kernel, name=name, out_shape=tuple(out_shape), in_specs=[p...]
    unnamed x12 -> x8, local copies, waits for them, and re-layouts: 2.29 us -> 0.01 us
    ppermute x1, waiting for transfers between devices: 2.12 us -> 0.33 us  [local(): ten_a = lax.ppermute(ten_a, ('sec', 'gx'), cross_a)]
    select_n x1 -> x0, other arithmetic: 1.16 us -> none  [local(): share = jnp.where(pick_last, own[:3, :, size_y - 8:], own[:3, :, :8])]
  transfers between devices with their start and end apart: 7 -> 7, of which waited for: 3 -> 3; matrix products, arithmetic and copies ran while one was open for 0% -> 1% of each run, Pallas kernels for 7% -> 21%
where the time goes in v2:
time: 24.8 us; the launch traced here: 24.7 us
  starting transfers between devices  10.2 us (41%)
  Pallas kernels  9.62 us (39%)
  waiting for transfers between devices  4.65 us (19%)
    pallas_call x6, Pallas kernels, call(): pl.pallas_call(kernel, name=name, out_shape=tuple(out_shape), in_specs=[p...  9.62 us
    ppermute x1, starting transfers between devices, local(): got_b = lax.ppermute(message_b, 'gx', swap_b)  3.54 us
    ppermute x1, waiting for transfers between devices, local(): ten_b = lax.ppermute(ten_b, ('sec', 'gx'), cross_b)  2.84 us
    ppermute x1, starting transfers between devices, local(): ten_b = lax.ppermute(ten_b, ('sec', 'gx'), cross_b)  2.38 us
    ppermute x1, starting transfers between devices, local(): tension = lax.ppermute(tension, 'sec', both)  1.61 us
    ppermute x1, starting transfers between devices, local(): got_a = lax.ppermute(message_a, 'gx', swap_a)  1.59 us
    ppermute x2, waiting for transfers between devices, local(): side = lax.ppermute(share, 'gy', both)  1.47 us
    ppermute x2, starting transfers between devices, local(): side = lax.ppermute(share, 'gy', both)  0.61 us
  transfers between devices with their start and end apart: 7, of which 3 were waited for; matrix products, arithmetic and copies ran while one was open for 1% of the time, Pallas kernels for 21%

profile of v2, /device:TPU:0, one launch (start us, length us, event | category | flops | bytes accessed | tf_op | source)
XLA Modules:
  0.0 24.7 jit_solution(7596504694307712531)
XLA Ops:
  0.0 1.6 %load.1 = (f32[3,18,48,128]{3,2,1,0:T(8,128)S(1)}, f32[5,16,32,128]{3,2,1,0:T(8,128)S(1)}, f32[3,16,8,128]{3,2,1,0:T(8,128)S(1)}) custom-call(f32[8,16,32,128]{3,2,1,0:T(8,128)} %bitcast.21), custom_call_target="tpu_custom_call" | custom-call | tf_op jit(solution)/shard_map/load/pallas_call | solution.py:497
  1.6 0.5 %collective-permute-start = (f32[3,16,8,128]{3,2,1,0:T(8,128)S(1)}, f32[3,16,8,128]{3,2,1,0:T(8,128)S(1)}, u32[]{:S(2)}, u32[]{:S(2)}) collective-permute-start(f32[3,16,8,128]{3,2,1,0:T(8,128)S(1)} %get-tuple-element.26), channel_id=1, source_target_pairs={{0,1},{1,0},{2,3},{3,2},{4,5},{5,4},{6,7},{7,6},{8,9},{9,8},{10,11... | collective-permute-start | bytes 589832 | tf_op jit(solution)/shard_map/ppermute | solution.py:540
  2.2 0.0 copy-done.3
  2.2 0.1 multiply_bitcast_fusion.1
  2.2 0.1 pad_add_fusion.pos_ref
  2.3 0.0 copy-done
  2.3 2.5 %local.1 = (f32[512,128]{1,0:T(8,128)S(1)}, f32[512,128]{1,0:T(8,128)S(1)}, f32[32,128]{1,0:T(8,128)S(1)}, f32[32,128]{1,0:T(8,128)S(1)}, f32[3,512,128]{2,1,0:T(8,128)S(1)}) custom-call(s32[2]{0:T(128)S(1)} %pad_add_fusion.pos_ref, s32[512]{0:T(512)S(1)} %bitcast.20, f32[3,8]{1,0:T(4,128)S(1)} %pad_maximum_fusion.tab_ref, ...), custom_call_target="tpu_custom_call" | custom-call | tf_op jit(solution)/shard_map/local/pallas_call | solution.py:497
  4.8 1.6 %collective-permute-start.5 = (f32[512,128]{1,0:T(8,128)S(1)}, f32[512,128]{1,0:T(8,128)S(1)}, u32[]{:S(2)}, u32[]{:S(2)}) collective-permute-start(f32[512,128]{1,0:T(8,128)S(1)} %get-tuple-element.32), channel_id=1, source_target_pairs={{0,16},{16,0},{1,17},{17,1},{2,18},{18,2},{3,19},{19,3},{4,20},{20... | collective-permute-start | bytes 786440 | tf_op jit(solution)/shard_map/ppermute | solution.py:562
  6.4 0.0 collective-permute-done.side_ref
  6.4 0.8 %message.1 = (f32[296,128]{1,0:T(8,128)S(1)}, f32[296,128]{1,0:T(8,128)S(1)}, f32[3,18,48,128]{3,2,1,0:T(8,128)S(1)}) custom-call(s32[2]{0:T(128)S(1)} %pad_add_fusion.pos_ref, f32[3,18,48,128]{3,2,1,0:T(8,128)S(1)} %get-tuple-element.23.pad.pad_in, f32[5,16,32,128]{3,2,1,0:T(8,128)S(1)} %get-tuple-element.22.rest, ...), custom_call_target="tpu_custom_call", output_to_operand_aliasing={{2}: (1, {})} | custom-call | tf_op jit(solution)/shard_map/message/pallas_call | solution.py:497
  7.3 1.6 %collective-permute-start.1 = (f32[296,128]{1,0:T(8,128)S(1)}, f32[296,128]{1,0:T(8,128)S(1)}, u32[]{:S(2)}, u32[]{:S(2)}) collective-permute-start(f32[296,128]{1,0:T(8,128)S(1)} %get-tuple-element.27), channel_id=1, source_target_pairs={{0,2},{4,6},{8,10},{12,14},{2,0},{6,4},{10,8},{14,12},{1,3},{5,7},... | collective-permute-start | bytes 454664 | tf_op jit(solution)/shard_map/ppermute | solution.py:559
  8.8 3.5 %collective-permute-start.2 = (f32[296,128]{1,0:T(8,128)S(1)}, f32[296,128]{1,0:T(8,128)S(1)}, u32[]{:S(2)}, u32[]{:S(2)}) collective-permute-start(f32[296,128]{1,0:T(8,128)S(1)} %get-tuple-element.28), channel_id=1, source_target_pairs={{2,4},{6,8},{10,12},{14,0},{4,2},{8,6},{12,10},{0,14},{3,5},{7,9},... | collective-permute-start | bytes 454664 | tf_op jit(solution)/shard_map/ppermute | solution.py:558
  12.4 0.4 %collective-permute-start.3 = (f32[32,128]{1,0:T(8,128)S(1)}, f32[32,128]{1,0:T(8,128)S(1)}, u32[]{:S(2)}, u32[]{:S(2)}) collective-permute-start(f32[32,128]{1,0:T(8,128)S(1)} %get-tuple-element.30), channel_id=1, source_target_pairs={{0,18},{4,22},{8,26},{12,30},{2,16},{6,20},{10,24},{14,28},{16,2},... | collective-permute-start | bytes 49160 | tf_op jit(solution)/shard_map/ppermute | solution.py:561
  12.8 2.4 %collective-permute-start.4 = (f32[32,128]{1,0:T(8,128)S(1)}, f32[32,128]{1,0:T(8,128)S(1)}, u32[]{:S(2)}, u32[]{:S(2)}) collective-permute-start(f32[32,128]{1,0:T(8,128)S(1)} %get-tuple-element.31), channel_id=1, source_target_pairs={{2,20},{6,24},{10,28},{14,16},{4,18},{8,22},{12,26},{0,30},{18,4},... | collective-permute-start | bytes 49160 | tf_op jit(solution)/shard_map/ppermute | solution.py:560
  15.2 0.0 collective-permute-done.5.ten_ref
  15.2 1.8 %inner.1 = (f32[3,18,48,128]{3,2,1,0:T(8,128)S(1)}, f32[3,18,8,128]{3,2,1,0:T(8,128)S(1)}, f32[4,16,32,128]{3,2,1,0:T(8,128)S(1)}) custom-call(s32[2]{0:T(128)S(1)} %pad_add_fusion.pos_ref, f32[3,18,48,128]{3,2,1,0:T(8,128)S(1)} %get-tuple-element.29.pad.pad_in, f32[5,16,32,128]{3,2,1,0:T(8,128)S(1)} %get-tuple-element.22.rest, ...), custom_call_target="tpu_custom_call" | custom-call | tf_op jit(solution)/shard_map/inner/pallas_call | solution.py:497
  17.0 0.3 %collective-permute-done.3.ten_a = f32[32,128]{1,0:T(8,128)S(1)} collective-permute-done((f32[32,128]{1,0:T(8,128)S(1)}, f32[32,128]{1,0:T(8,128)S(1)}, u32[]{:S(2)}, u32[]{:S(2)}) %collective-permute-start.3) | collective-permute-done | bytes 16416 | tf_op jit(solution)/shard_map/ppermute | solution.py:561
  17.3 2.8 %collective-permute-done.4.ten_b = f32[32,128]{1,0:T(8,128)S(1)} collective-permute-done((f32[32,128]{1,0:T(8,128)S(1)}, f32[32,128]{1,0:T(8,128)S(1)}, u32[]{:S(2)}, u32[]{:S(2)}) %collective-permute-start.4) | collective-permute-done | bytes 16416 | tf_op jit(solution)/shard_map/ppermute | solution.py:560
  20.1 0.0 collective-permute-done.1.got_a
  20.2 0.0 collective-permute-done.2.got_b
  20.2 0.8 %outer.1 = (f32[3,18,48,128]{3,2,1,0:T(8,128)S(1)}, f32[3,18,8,128]{3,2,1,0:T(8,128)S(1)}) custom-call(s32[2]{0:T(128)S(1)} %pad_add_fusion.pos_ref, f32[3,8]{1,0:T(4,128)S(1)} %pad_maximum_fusion.tab_ref, f32[3,18,48,128]{3,2,1,0:T(8,128)S(1)} %get-tuple-element.29.pad.pad_in, ...), custom_call_target="tpu_custom_call", output_to_operand_aliasing={{0}: (11, {}), {1}: (12, {})} | custom-call | tf_op jit(solution)/shard_map/outer/pallas_call | solution.py:497
  21.0 0.1 collective-permute-start.6
  21.1 1.5 %collective-permute-done.6.side_ref = f32[3,18,8,128]{3,2,1,0:T(8,128)S(1)} collective-permute-done((f32[3,18,8,128]{3,2,1,0:T(8,128)S(1)}, f32[3,18,8,128]{3,2,1,0:T(8,128)S(1)}, u32[]{:S(2)}, u32[]{:S(2)}) %collective-permute-start.6) | collective-permute-done | bytes 221216 | tf_op jit(solution)/shard_map/ppermute | solution.py:579
  22.5 2.1 %last.1 = (f32[1,4,16,32,128]{4,3,2,1,0:T(8,128)}, f32[3,18,48,128]{3,2,1,0:T(8,128)S(1)}) custom-call(s32[2]{0:T(128)S(1)} %pad_add_fusion.pos_ref, f32[5,16,32,128]{3,2,1,0:T(8,128)S(1)} %get-tuple-element.22.rest, f32[3,512,128]{2,1,0:T(8,128)S(1)} %get-tuple-element.24.fib_ref, s32[2,1,32]{2,1,0:T(1,128)S(1)} %bitcast.19, ...), custom_call_target="tpu_custom_call", output_to_operand_aliasing={{1}: (7, {})} | custom-call | tf_op jit(solution)/shard_map/last/pallas_call | solution.py:497
  (7 shorter events, 0.0 us)
Async XLA Ops:
  0.0 2.2 %copy-start.3 = (f32[8,2]{0,1:T(2,128)S(1)}, f32[8,2]{0,1:T(2,128)}, u32[]{:S(2)}) copy-start(f32[8,2]{0,1:T(2,128)} %param.6) | copy-start | bytes 196
  0.0 2.3 %copy-start.2 = (s32[1,1,512]{2,1,0:T(1,128)S(1)}, s32[1,1,512]{2,1,0:T(1,128)}, u32[]{:S(2)}) copy-start(s32[1,1,512]{2,1,0:T(1,128)} %param.8) | copy-start | bytes 6148
  0.0 2.3 %copy-start = (s32[16,32,8]{1,2,0:T(8,128)S(1)}, s32[16,32,8]{1,2,0:T(8,128)}, u32[]{:S(2)}) copy-start(s32[16,32,8]{1,2,0:T(8,128)} %param.7) | copy-start | bytes 49156
  1.6 4.8 %collective-permute-start = (f32[3,16,8,128]{3,2,1,0:T(8,128)S(1)}, f32[3,16,8,128]{3,2,1,0:T(8,128)S(1)}, u32[]{:S(2)}, u32[]{:S(2)}) collective-permute-start(f32[3,16,8,128]{3,2,1,0:T(8,128)S(1)} %get-tuple-element.26), channel_id=1, source_target_pairs={{0,1},{1,0},{2,3},{3,2},{4,5},{5,4},{6,7},{7,6},{8,9},{9,8},{10,11... | collective-permute-start | bytes 589832 | tf_op jit(solution)/shard_map/ppermute | solution.py:540
  2.3 4.1 %copy-start.1 = (s32[2,1,1,32]{3,2,1,0:T(1,128)S(1)}, s32[2,1,1,32]{3,2,1,0:T(1,128)}, u32[]{:S(2)}) copy-start(s32[2,1,1,32]{3,2,1,0:T(1,128)} %param.9) | copy-start | bytes 772
  4.8 10.4 %collective-permute-start.5 = (f32[512,128]{1,0:T(8,128)S(1)}, f32[512,128]{1,0:T(8,128)S(1)}, u32[]{:S(2)}, u32[]{:S(2)}) collective-permute-start(f32[512,128]{1,0:T(8,128)S(1)} %get-tuple-element.32), channel_id=1, source_target_pairs={{0,16},{16,0},{1,17},{17,1},{2,18},{18,2},{3,19},{19,3},{4,20},{20... | collective-permute-start | bytes 786440 | tf_op jit(solution)/shard_map/ppermute | solution.py:562
  7.3 12.9 %collective-permute-start.1 = (f32[296,128]{1,0:T(8,128)S(1)}, f32[296,128]{1,0:T(8,128)S(1)}, u32[]{:S(2)}, u32[]{:S(2)}) collective-permute-start(f32[296,128]{1,0:T(8,128)S(1)} %get-tuple-element.27), channel_id=1, source_target_pairs={{0,2},{4,6},{8,10},{12,14},{2,0},{6,4},{10,8},{14,12},{1,3},{5,7},... | collective-permute-start | bytes 454664 | tf_op jit(solution)/shard_map/ppermute | solution.py:559
  8.8 11.3 %collective-permute-start.2 = (f32[296,128]{1,0:T(8,128)S(1)}, f32[296,128]{1,0:T(8,128)S(1)}, u32[]{:S(2)}, u32[]{:S(2)}) collective-permute-start(f32[296,128]{1,0:T(8,128)S(1)} %get-tuple-element.28), channel_id=1, source_target_pairs={{2,4},{6,8},{10,12},{14,0},{4,2},{8,6},{12,10},{0,14},{3,5},{7,9},... | collective-permute-start | bytes 454664 | tf_op jit(solution)/shard_map/ppermute | solution.py:558
  12.4 4.9 %collective-permute-start.3 = (f32[32,128]{1,0:T(8,128)S(1)}, f32[32,128]{1,0:T(8,128)S(1)}, u32[]{:S(2)}, u32[]{:S(2)}) collective-permute-start(f32[32,128]{1,0:T(8,128)S(1)} %get-tuple-element.30), channel_id=1, source_target_pairs={{0,18},{4,22},{8,26},{12,30},{2,16},{6,20},{10,24},{14,28},{16,2},... | collective-permute-start | bytes 49160 | tf_op jit(solution)/shard_map/ppermute | solution.py:561
  12.8 7.3 %collective-permute-start.4 = (f32[32,128]{1,0:T(8,128)S(1)}, f32[32,128]{1,0:T(8,128)S(1)}, u32[]{:S(2)}, u32[]{:S(2)}) collective-permute-start(f32[32,128]{1,0:T(8,128)S(1)} %get-tuple-element.31), channel_id=1, source_target_pairs={{2,20},{6,24},{10,28},{14,16},{4,18},{8,22},{12,26},{0,30},{18,4},... | collective-permute-start | bytes 49160 | tf_op jit(solution)/shard_map/ppermute | solution.py:560
  21.0 1.5 %collective-permute-start.6 = (f32[3,18,8,128]{3,2,1,0:T(8,128)S(1)}, f32[3,18,8,128]{3,2,1,0:T(8,128)S(1)}, u32[]{:S(2)}, u32[]{:S(2)}) collective-permute-start(f32[3,18,8,128]{3,2,1,0:T(8,128)S(1)} %get-tuple-element.36), channel_id=1, source_target_pairs={{0,1},{1,0},{2,3},{3,2},{4,5},{5,4},{6,7},{7,6},{8,9},{9,8},{10,11... | collective-permute-start | bytes 663560 | tf_op jit(solution)/shard_map/ppermute | solution.py:579

commit v3 on v2

v3 whole, which is shorter than its diff:
```python
import jax
import jax.numpy as jnp
from jax import lax
from jax.experimental import pallas as pl
from jax.experimental.pallas import tpu as pltpu
from jax.sharding import PartitionSpec as P

DT = 0.1
OMEGA = 0.06
F32 = jnp.float32
HIGHEST = lax.Precision.HIGHEST
VMEM_LIMIT = 32 * 1024 * 1024

PAD = 8

ROW_NOW, ROW_NEXT, ROW_STIFF, ROW_SIDE, ROW_LIST = 0, 96, 192, 224, 248
MESSAGE_ROWS = 256


def swap_pairs(pairs):
    return pairs + [(b, a) for a, b in pairs]


def inverse(v):
    r = pl.reciprocal(v, approx=True)
    return r * (2.0 - v * r)


def rise(c):
    c2 = c * c
    return c2 * inverse(c2 + 0.25)


def ends(like):
    lane = lax.broadcasted_iota(jnp.int32, like, 1)
    return lane == like[1] - 1, lane == 0


def up_z(w, last):
    return jnp.where(last, 0.0, pltpu.roll(w, w.shape[1] - 1, 1))


def down_z(w, first):
    return jnp.where(first, 0.0, pltpu.roll(w, 1, 1))


def rows_of(pad, a, x, size_y, shift=0):
    return pad[a, x, PAD + shift : PAD + shift + size_y, :]


def motion_rate(pad, x, size_y):
    at = lambda a, dx=0, dy=0: rows_of(pad, a, x + dx, size_y, dy)
    u0, u1, u2 = at(0), at(1), at(2)
    last, first = ends(u0.shape)
    w0p, w0m, w1p, w1m = at(0, 1), at(0, -1), at(1, 1), at(1, -1)
    w2p, w2m = at(2, 1), at(2, -1)
    e0, e2 = 0.5 * (w0p - w0m), 0.5 * (w2p - w2m)
    e0y = (at(0, 1, 1) - at(0, -1, 1)) - (at(0, 1, -1) - at(0, -1, -1))
    e1y = (at(1, 1, 1) - at(1, -1, 1)) - (at(1, 1, -1) - at(1, -1, -1))
    v1p, v1m, v2p, v2m = at(1, 0, 1), at(1, 0, -1), at(2, 0, 1), at(2, 0, -1)
    d2 = 0.5 * (v2p - v2m)
    d1 = 0.5 * (v1p - v1m) + e0
    r0 = (
        up_z(u0 + e2, last) + down_z(u0 - e2, first)
        + (at(0, 0, 1) + at(0, 0, -1)) + 0.5 * e1y + 3.0 * (w0p + w0m)
    )
    r1 = (
        up_z(u1 + d2, last) + down_z(u1 - d2, first)
        + 3.0 * (v1p + v1m) + 0.5 * e0y + (w1p + w1m)
    )
    t2 = 3.0 * u2
    r2 = up_z(t2 + d1, last) + down_z(t2 - d1, first) + (v2p + v2m) + (w2p + w2m)
    return r0, r1, r2


def motion_from(pad, x, sign, size_y):
    u0, u1, u2 = [rows_of(pad, a, x, size_y) for a in range(3)]
    last, first = ends(u0.shape)
    half = 0.5 * sign
    dy0 = rows_of(pad, 0, x, size_y, 1) - rows_of(pad, 0, x, size_y, -1)
    dy1 = rows_of(pad, 1, x, size_y, 1) - rows_of(pad, 1, x, size_y, -1)
    dz0 = up_z(u0, last) - down_z(u0, first)
    dz2 = up_z(u2, last) - down_z(u2, first)
    return 3.0 * u0 + half * (dy1 + dz2), u1 + half * dy0, u2 + half * dz0


def volt_rate(pad, x, fib, size_y):
    at = lambda dx=0, dy=0: rows_of(pad, 0, x + dx, size_y, dy)
    v, wp, wm, yp, ym = at(), at(1), at(-1), at(0, 1), at(0, -1)
    last, first = ends(v.shape)
    e = wp - wm
    ey = (at(1, 1) - at(-1, 1)) - (at(1, -1) - at(-1, -1))
    dy = yp - ym
    sum_z = up_z(v, last) + down_z(v, first)
    ez = up_z(e, last) - down_z(e, first)
    dyz = up_z(dy, last) - down_z(dy, first)
    g = [0.75 * w for w in fib]
    d00, d11, d22 = [0.25 + a * b for a, b in zip(g, fib)]
    return (
        d00 * (wp + wm) + d11 * (yp + ym) + d22 * sum_z - 2.0 * (d00 + d11 + d22) * v
        + 0.5 * (fib[0] * (g[1] * ey + g[2] * ez) + g[1] * fib[2] * dyz)
    )


def couplings(fib):
    g = 0.75 * fib[0]
    return 0.25 + g * fib[0], 0.5 * g * fib[1], 0.5 * g * fib[2]


def volt_from(pad, x, coupled, sign, size_y):
    v = rows_of(pad, 0, x, size_y)
    last, first = ends(v.shape)
    dy = rows_of(pad, 0, x, size_y, 1) - rows_of(pad, 0, x, size_y, -1)
    dz = up_z(v, last) - down_z(v, first)
    return coupled[0] * v + sign * (coupled[1] * dy + coupled[2] * dz)


def currents(v, c, d, f, n, r):
    q = rise(c)
    calcium_flow = 1.2 * d * f * (v - 2.0)
    return q, calcium_flow, calcium_flow + (0.8 * n + 0.6 * q * r) * (v + 1.0) + 0.1 * v


def permute_rows(listed, values):
    rows = values.shape[0]
    pick = (lax.broadcasted_iota(jnp.int32, (rows, rows), 0).astype(F32) == listed).astype(F32)
    return lax.dot_general(
        pick, values, (((0,), (0,)), ((), ())), precision=HIGHEST, preferred_element_type=F32
    )


def tie_rows(listed, stiff, u):
    joined = jnp.concatenate([2.0 * stiff * w for w in u], axis=1)
    moved = permute_rows(listed, joined)
    depth = u[0].shape[1]
    return [moved[:, a * depth : (a + 1) * depth] for a in range(3)]


def edges_tile(value):
    rows = value.shape[0]
    last = lax.broadcasted_iota(jnp.int32, (8, value.shape[1]), 0) == 7
    return jnp.where(last, value[rows - 8 :], value[:8])


def fill_sides(pad, a, x, tile, size_y):
    pad[a, x, 0:PAD, :] = tile
    pad[a, x, PAD + size_y :, :] = tile


def sides(size_x):
    out = []
    for slot in range(2):
        right = (lax.axis_index("gx") + slot) % 2 == 0
        out.append(
            (
                jnp.where(right, size_x + 1, 0),
                jnp.where(right, size_x - 1, 0),
                jnp.where(right, 1, 0),
                jnp.where(right, 1.0, -1.0).astype(F32),
            )
        )
    return out


def place_of(x, size_y):
    return pl.ds(pl.multiple_of(x * size_y, size_y), size_y)


def electric():
    return lax.axis_index("sec") == 0


def fiber_fields(angles, cls, flat, fib_ref, size_x, size_y):
    blocks, classes, depth = cls.shape[1], angles.shape[1], fib_ref.shape[2]
    azimuth, elevation = angles[0:1, :], angles[1:2, :]
    flat_part = jnp.cos(elevation)
    fib = [jnp.cos(azimuth) * flat_part, jnp.sin(azimuth) * flat_part, jnp.sin(elevation)]
    for x in range(size_x):
        flat[:, x * size_y : (x + 1) * size_y] = cls[x]
    own = lax.broadcasted_iota(jnp.int32, (blocks, depth), 1) // (depth // blocks)
    own = own == lax.broadcasted_iota(jnp.int32, (blocks, depth), 0)
    hits = jnp.concatenate([(flat[...] == k).astype(F32) for k in range(classes)], axis=0)
    table = jnp.concatenate(
        [
            jnp.concatenate(
                [jnp.where(own, jnp.broadcast_to(w[:, k : k + 1], own.shape), 0.0) for w in fib], axis=1
            )
            for k in range(classes)
        ],
        axis=0,
    )
    high = table.astype(jnp.bfloat16).astype(F32)
    mid = (table - high).astype(jnp.bfloat16).astype(F32)
    parts = jnp.concatenate([high, mid, table - high - mid], axis=0)
    found = lax.dot_general(
        jnp.concatenate([hits] * 3, axis=0), parts, (((0,), (0,)), ((), ())), preferred_element_type=F32
    )
    for a in range(3):
        fib_ref[a] = found[:, a * depth : (a + 1) * depth]


def load_kernel(
    sec_hbm, cls_hbm, ang_hbm, map_hbm, pad, rest, share, plain, edge_ten, fib_ref, cls, ang, map_ref, flat, sems
):
    size_x, size_y = sec_hbm.shape[1], sec_hbm.shape[2]
    small = [
        pltpu.make_async_copy(src, dst, sems.at[i])
        for i, (src, dst) in enumerate(((cls_hbm, cls), (ang_hbm, ang), (map_hbm, map_ref)))
    ]
    pieces = (sems.shape[0] - 3) // 2
    chunk = size_x // pieces
    main = []
    for i in range(pieces):
        here, there = pl.ds(i * chunk, chunk), pl.ds(i * chunk + 1, chunk)
        main.append(
            (
                pltpu.make_async_copy(
                    sec_hbm.at[0:3, here], pad.at[:, there, pl.ds(PAD, size_y), :], sems.at[3 + 2 * i]
                ),
                pltpu.make_async_copy(sec_hbm.at[3:8, here], rest.at[:, here], sems.at[4 + 2 * i]),
            )
        )
    for copy in small:
        copy.start()
    for pair in main:
        for copy in pair:
            copy.start()
    zeros = jnp.zeros(pad.shape[2:], F32)
    for a in range(3):
        pad[a, 0] = zeros
        pad[a, size_x + 1] = zeros
    small[0].wait()
    small[1].wait()
    fiber_fields(ang[...], cls, flat, fib_ref, size_x, size_y)

    def tension(x, carry):
        v, c, d = [rows_of(pad, a, x + 1, size_y) for a in range(3)]
        f, bound, s = rest[0, x], rest[3, x], rest[4, x]
        calcium_flow = 1.2 * d * f * (v - 2.0)
        flow = 2.0 * c * (1.0 - bound) - 0.4 * bound
        c1 = c + DT * (-0.3 * calcium_flow - 0.5 * c - flow)
        s1 = s + (0.5 * DT) * (rise(c) - s)
        plain[place_of(x, size_y), :] = s1 + (0.5 * DT) * (rise(c1) - s1)
        return carry

    def pack(x, carry):
        for a in range(3):
            share[a, x] = edges_tile(rows_of(pad, a, x + 1, size_y))
        return carry

    for i, pair in enumerate(main):
        for copy in pair:
            copy.wait()
        lax.fori_loop(i * chunk, (i + 1) * chunk, pack, 0, unroll=True)

        @pl.when(electric())
        def _():
            lax.fori_loop(i * chunk, (i + 1) * chunk, tension, 0, unroll=2)

    small[2].wait()

    @pl.when(electric())
    def _():
        last = (size_x - 1) * size_y
        for p in range(size_y):
            edge_ten[0, p : p + 1, :] = plain[pl.ds(map_ref[p], 1), :]
            edge_ten[1, p : p + 1, :] = plain[pl.ds(map_ref[last + p], 1), :]


def gather_kernel(map_ref, plain, all_ref):
    @pl.when(electric())
    def _():
        def rows(i, carry):
            for k in range(32):
                p = i * 32 + k
                all_ref[pl.ds(p, 1), :] = plain[pl.ds(map_ref[p], 1), :]
            return carry

        lax.fori_loop(0, all_ref.shape[0] // 32, rows, 0)


def message_kernel(pad_in, rest, side_ref, fib_ref, ten_ref, list_ref, a_ref, b_ref, pad):
    size_x, size_y = rest.shape[1], rest.shape[2]

    def fill(x, carry):
        for a in range(3):
            fill_sides(pad, a, x + 1, side_ref[a, x], size_y)
        return carry

    lax.fori_loop(0, size_x, fill, 0, unroll=4)
    for (_, edge, which, _), out in zip(sides(size_x), (a_ref, b_ref)):
        fib = [fib_ref[a, place_of(edge, size_y), :] for a in range(3)]
        out[ROW_LIST : ROW_LIST + 8, 0:size_y] = jnp.broadcast_to(list_ref[which].astype(F32), (8, size_y))
        for a in range(3):
            out[ROW_SIDE + a * 8 : ROW_SIDE + (a + 1) * 8, :] = side_ref[a, edge]

        @pl.when(electric())
        def _():
            v, c, d = [rows_of(pad, a, edge + 1, size_y) for a in range(3)]
            f, n, r = [rest[k, edge] for k in range(3)]
            rate = volt_rate(pad, edge + 1, fib, size_y)
            _, _, total = currents(v, c, d, f, n, r)
            for at, value in zip(
                (ROW_NOW, ROW_NOW + size_y, ROW_NOW + 2 * size_y, ROW_NEXT, ROW_NEXT + size_y),
                (v,) + couplings(fib)[:2] + (v + DT * (rate - total), couplings(fib)[2]),
            ):
                out[at : at + size_y, :] = value

        @pl.when(jnp.logical_not(electric()))
        def _():
            rate = motion_rate(pad, edge + 1, size_y)
            stiff = rest[3, edge]
            beta = OMEGA * inverse(stiff)
            act = rest[4, edge] * ten_ref[which]
            out[ROW_STIFF : ROW_STIFF + size_y, :] = stiff
            for a in range(3):
                u = rows_of(pad, a, edge + 1, size_y)
                out[ROW_NOW + a * size_y : ROW_NOW + (a + 1) * size_y, :] = u
                out[ROW_NEXT + a * size_y : ROW_NEXT + (a + 1) * size_y, :] = (
                    0.28 * u + beta * (rest[a, edge] + act * fib[a]) + OMEGA * rate[a]
                )


def inner_kernel(pad, rest, fib_ref, ten_ref, next_pad, share, keep):
    size_x, size_y = rest.shape[1], rest.shape[2]

    def put(a, x, value):
        next_pad[a, x, PAD : PAD + size_y, :] = value
        share[a, x] = edges_tile(value)

    @pl.when(electric())
    def _():
        def plane(x, carry):
            place = place_of(x, size_y)
            v, c, d = [rows_of(pad, a, x + 1, size_y) for a in range(3)]
            f, n, r, bound, _ = [rest[k, x] for k in range(5)]
            rate = volt_rate(pad, x + 1, [fib_ref[a, place, :] for a in range(3)], size_y)
            q, calcium_flow, total = currents(v, c, d, f, n, r)
            flow = 2.0 * c * (1.0 - bound) - 0.4 * bound
            put(0, x + 1, v + DT * (rate - total))
            c1 = c + DT * (-0.3 * calcium_flow - 0.5 * c - flow)
            tv = jnp.tanh(v)
            d1 = (1.0 - 2.0 * DT) * d + DT * (1.0 + jnp.tanh(v + 0.5))
            f1 = (1.0 - DT / 3.0) * f + (DT / 6.0) * (1.0 - tv)
            n1 = (1.0 - DT) * n + (0.5 * DT) * (1.0 + tv)
            r1 = (1.0 - DT / 5.0) * r + (DT / 10.0) * (1.0 + jnp.tanh(0.5 * v - 0.25))
            bound1 = bound + DT * flow
            flow1 = 2.0 * c1 * (1.0 - bound1) - 0.4 * bound1
            keep[0, x] = n1
            keep[1, x] = 1.2 * d1 * f1
            keep[2, x] = 0.8 * n1 + 0.6 * rise(c1) * r1
            keep[3, x] = c1 - DT * (0.5 * c1 + flow1)
            return carry

        lax.fori_loop(0, size_x, plane, 0, unroll=2)

    @pl.when(jnp.logical_not(electric()))
    def _():
        def plane(x, carry):
            place = place_of(x, size_y)
            rate = motion_rate(pad, x + 1, size_y)
            beta = OMEGA * inverse(rest[3, x])
            act = rest[4, x] * ten_ref[place, :]
            keep[3, x] = act
            for a in range(3):
                drive = beta * (rest[a, x] + act * fib_ref[a, place, :])
                keep[a, x] = drive
                put(a, x + 1, 0.4 * rows_of(pad, a, x + 1, size_y) + drive + OMEGA * rate[a])
            return carry

        lax.fori_loop(0, size_x, plane, 0, unroll=2)


def outer_kernel(pad, rest, fib_ref, list_ref, got_a, got_b, next_in, next_pad, share, wide):
    size_x, size_y = rest.shape[1], rest.shape[2]
    work = list(zip(sides(size_x), (got_a, got_b)))
    for slot, (_, got) in enumerate(work):
        for a in range(3):
            wide[a, slot, PAD : PAD + size_y, :] = got[ROW_NOW + a * size_y : ROW_NOW + (a + 1) * size_y, :]
            fill_sides(wide, a, slot, got[ROW_SIDE + a * 8 : ROW_SIDE + (a + 1) * 8, :], size_y)

    def put(a, x, slot, value):
        next_pad[a, x, PAD : PAD + size_y, :] = value
        share[a, slot] = edges_tile(value)

    @pl.when(electric())
    def _():
        for slot, ((halo, edge, which, sign), got) in enumerate(work):
            fib = [fib_ref[a, place_of(edge, size_y), :] for a in range(3)]
            put(
                0,
                edge + 1,
                1 + which,
                rows_of(next_pad, 0, edge + 1, size_y) + DT * volt_from(wide, slot, couplings(fib), sign, size_y),
            )
            theirs = [
                got[at : at + size_y, :] for at in (ROW_NOW + size_y, ROW_NOW + 2 * size_y, ROW_NEXT + size_y)
            ]
            put(
                0,
                halo,
                3 * which,
                got[ROW_NEXT : ROW_NEXT + size_y, :] + DT * volt_from(pad, edge + 1, theirs, -sign, size_y),
            )

    @pl.when(jnp.logical_not(electric()))
    def _():
        for slot, ((halo, edge, which, sign), got) in enumerate(work):
            stiff = got[ROW_STIFF : ROW_STIFF + size_y, :]
            own = rest[3, edge]
            now = [rows_of(pad, a, edge + 1, size_y) for a in range(3)]
            theirs = [rows_of(wide, a, slot, size_y) for a in range(3)]
            ties = tie_rows(list_ref[which].astype(F32), stiff, theirs)
            rate = motion_from(wide, slot, sign, size_y)
            beta = OMEGA * inverse(own)
            for a in range(3):
                put(
                    a,
                    edge + 1,
                    1 + which,
                    rows_of(next_pad, a, edge + 1, size_y) + OMEGA * rate[a] + beta * ties[a] - 0.12 * now[a],
                )
            ties = tie_rows(got[ROW_LIST : ROW_LIST + 1, 0:size_y], own, now)
            rate = motion_from(pad, edge + 1, -sign, size_y)
            beta = OMEGA * inverse(stiff)
            for a in range(3):
                put(
                    a,
                    halo,
                    3 * which,
                    got[ROW_NEXT + a * size_y : ROW_NEXT + (a + 1) * size_y, :] + OMEGA * rate[a] + beta * ties[a],
                )


def electric_end(x, next_pad, fib_ref, plain, keep, out):
    size_y = fib_ref.shape[1] // keep.shape[1]
    place = place_of(x, size_y)
    v = rows_of(next_pad, 0, x + 1, size_y)
    n, gate, leak, rest_c = [keep[k, x] for k in range(4)]
    rate = volt_rate(next_pad, x + 1, [fib_ref[a, place, :] for a in range(3)], size_y)
    flow = gate * (v - 2.0)
    out[0, x] = v + DT * (rate - flow - leak * (v + 1.0) - 0.1 * v)
    out[1, x] = rest_c - (0.3 * DT) * flow
    out[2, x] = (1.0 - DT) * n + (0.5 * DT) * (1.0 + jnp.tanh(v))
    out[3, x] = plain[place, :]


def mechanic_end(x, next_pad, keep, out, size_y, ties=None):
    rate = motion_rate(next_pad, x + 1, size_y)
    for a in range(3):
        u = rows_of(next_pad, a, x + 1, size_y)
        value = 0.4 * u + keep[a, x] + OMEGA * rate[a]
        out[a, x] = value if ties is None else value + ties[a] - 0.12 * u
    out[3, x] = keep[3, x]


def middle_kernel(fib_ref, plain, next_in, side_ref, keep, out_hbm, next_pad, out, sems):
    size_x = keep.shape[1]
    size_y = fib_ref.shape[1] // size_x
    pieces = sems.shape[0]
    chunk = (size_x - 4) // pieces

    def copy_out(i):
        here = pl.ds(2 + i * chunk, chunk)
        return pltpu.make_async_copy(out.at[:, here], out_hbm.at[0, :, here], sems.at[i])

    def fill(count):
        def one(x, carry):
            for a in range(count):
                fill_sides(next_pad, a, x, side_ref[a, x], size_y)
            return carry

        lax.fori_loop(2, size_x, one, 0, unroll=2)

    @pl.when(electric())
    def _():
        fill(1)

        def step(i, carry):
            for k in range(chunk):
                electric_end(2 + i * chunk + k, next_pad, fib_ref, plain, keep, out)
            copy_out(i).start()
            return carry

        lax.fori_loop(0, pieces, step, 0)

    @pl.when(jnp.logical_not(electric()))
    def _():
        fill(3)

        def sweep(i, carry):
            for k in range(chunk):
                mechanic_end(2 + i * chunk + k, next_pad, keep, out, size_y)
            copy_out(i).start()
            return carry

        lax.fori_loop(0, pieces, sweep, 0)

    for i in range(pieces):
        copy_out(i).wait()


def last_kernel(
    rest, fib_ref, list_ref, plain, got_a, got_b, next_in, side_ref, keep, out_in, out_hbm, next_pad, out, sems
):
    size_x, size_y = rest.shape[1], rest.shape[2]

    def copy_out(slot, first):
        here = pl.ds(first, 2)
        return pltpu.make_async_copy(out.at[:, here], out_hbm.at[0, :, here], sems.at[slot])

    work = []
    for slot, ((halo, edge, which, _), got) in enumerate(zip(sides(size_x), (got_a, got_b))):
        near = jnp.where(which == 1, size_x - 2, 1)
        work.append((halo, edge, near, which, got, copy_out(slot, jnp.minimum(edge, near))))

    @pl.when(electric())
    def _():
        for halo, edge, near, which, _, copy in work:
            fill_sides(next_pad, 0, halo, side_ref[0, 3 * which], size_y)
            fill_sides(next_pad, 0, edge + 1, side_ref[0, 1 + which], size_y)
            for x in (near, edge):
                electric_end(x, next_pad, fib_ref, plain, keep, out)
            copy.start()

    @pl.when(jnp.logical_not(electric()))
    def _():
        for halo, edge, near, which, got, copy in work:
            for a in range(3):
                fill_sides(next_pad, a, halo, side_ref[a, 3 * which], size_y)
                fill_sides(next_pad, a, edge + 1, side_ref[a, 1 + which], size_y)
            beta = OMEGA * inverse(rest[3, edge])
            ties = tie_rows(
                list_ref[which].astype(F32),
                got[ROW_STIFF : ROW_STIFF + size_y, :],
                [rows_of(next_pad, a, halo, size_y) for a in range(3)],
            )
            mechanic_end(near, next_pad, keep, out, size_y)
            mechanic_end(edge, next_pad, keep, out, size_y, [beta * w for w in ties])
            copy.start()

    for item in work:
        item[-1].wait()


def call(kernel, name, out_shape, operands, spaces, scratch=(), out_spaces=None, aliases=()):
    if out_spaces is None:
        out_spaces = [pltpu.VMEM] * len(out_shape)
    return pl.pallas_call(
        kernel,
        name=name,
        out_shape=tuple(out_shape),
        in_specs=[pl.BlockSpec(memory_space=space) for space in spaces],
        out_specs=tuple(pl.BlockSpec(memory_space=space) for space in out_spaces),
        scratch_shapes=scratch,
        input_output_aliases=dict(aliases),
        compiler_params=pltpu.CompilerParams(vmem_limit_bytes=VMEM_LIMIT),
    )(*operands)


def local(sections, fiber_angles, fiber_class, row_map, interface_rows):
    own = sections[0]
    channels, size_x, size_y, depth = own.shape
    n_gx = lax.axis_size("gx")
    n_gy = lax.axis_size("gy")
    assert n_gx % 2 == 0 and n_gy == 2
    swap_a = swap_pairs([(i, i + 1) for i in range(0, n_gx, 2)])
    swap_b = swap_pairs([(i, (i + 1) % n_gx) for i in range(1, n_gx, 2)])
    both = swap_pairs([(0, 1)])
    S, V, H = pltpu.SMEM, pltpu.VMEM, pltpu.HBM
    f32 = lambda *shape: jax.ShapeDtypeStruct(shape, F32)
    hbm = lambda w: pltpu.with_memory_space_constraint(w, H)
    columns = size_x * size_y
    padded = f32(3, size_x + 2, size_y + 2 * PAD, depth)
    classes = fiber_class.transpose(0, 2, 1)
    lists = interface_rows.reshape(2, 1, size_y)
    places = row_map.reshape(-1)

    pad, rest, share, plain, edge_ten, fib = call(
        load_kernel,
        "load",
        (
            padded,
            f32(channels - 3, size_x, size_y, depth),
            f32(3, size_x, 8, depth),
            f32(columns, depth),
            f32(2, size_y, depth),
            f32(3, columns, depth),
        ),
        (hbm(own), hbm(classes), hbm(fiber_angles.T), hbm(places)),
        (H, H, H, H),
        [
            pltpu.VMEM(classes.shape, jnp.int32),
            pltpu.VMEM(fiber_angles.shape[::-1], F32),
            pltpu.SMEM((columns,), jnp.int32),
            pltpu.VMEM((classes.shape[1], columns), jnp.int32),
            pltpu.SemaphoreType.DMA((3 + 2 * 4,)),
        ],
    )
    edge_ten = lax.ppermute(edge_ten, "sec", both)
    side = lax.ppermute(share, "gy", both)
    (tension,) = call(gather_kernel, "gather", (f32(columns, depth),), (places, plain), (S, V))
    tension = lax.ppermute(tension, "sec", both)
    message = f32(MESSAGE_ROWS, depth)
    message_a, message_b, pad = call(
        message_kernel,
        "message",
        (message, message, padded),
        (pad, rest, side, fib, edge_ten, lists),
        (V,) * 6,
        aliases={0: 2},
    )
    got_a = lax.ppermute(message_a, "gx", swap_a)
    got_b = lax.ppermute(message_b, "gx", swap_b)
    moved, share, keep = call(
        inner_kernel,
        "inner",
        (padded, f32(3, size_x + 2, 8, depth), f32(4, size_x, size_y, depth)),
        (pad, rest, fib, tension),
        (V,) * 4,
    )
    side = lax.ppermute(share, "gy", both)
    moved, share = call(
        outer_kernel,
        "outer",
        (padded, f32(3, 4, 8, depth)),
        (pad, rest, fib, lists, got_a, got_b, moved),
        (V,) * 7,
        [pltpu.VMEM((3, 2) + padded.shape[2:], F32)],
        aliases={6: 0},
    )
    end_side = lax.ppermute(share, "gy", both)
    fields = pltpu.VMEM((4, size_x, size_y, depth), F32)
    result = f32(1, 4, size_x, size_y, depth)
    result, moved = call(
        middle_kernel,
        "middle",
        (result, padded),
        (fib, plain, moved, side, keep),
        (V,) * 5,
        [fields, pltpu.SemaphoreType.DMA((3,))],
        out_spaces=(H, V),
        aliases={2: 1},
    )
    return call(
        last_kernel,
        "last",
        (f32(1, 4, size_x, size_y, depth), padded),
        (rest, fib, lists, plain, got_a, got_b, moved, end_side, keep, result),
        (V,) * 9 + (H,),
        [fields, pltpu.SemaphoreType.DMA((2,))],
        out_spaces=(H, V),
        aliases={6: 1, 9: 0},
    )[0]


def solution(mesh):
    in_specs = (
        P("sec", None, "gx", "gy", None),
        P(),
        P("gx", "gy", None),
        P("gx", "gy", None),
        P(None, "gx", "gy", None),
    )
    out_specs = P("sec", None, "gx", "gy", None)
    return jax.shard_map(local, mesh=mesh, in_specs=in_specs, out_specs=out_specs, check_vma=False)
```

time: 24.8 us -> 27.5 us (1.11)
  the two profiles are of different devices: /device:TPU:0 before, /device:TPU:1 now
where the time goes in v3:
time: 27.5 us; the launch traced here: 27.4 us
  waiting for transfers between devices  10.3 us (37%)
  starting transfers between devices  9.98 us (36%)
  Pallas kernels  6.97 us (25%)
    pallas_call x7, Pallas kernels, call(): pl.pallas_call(kernel, name=name, out_shape=tuple(out_shape), in_specs=[p...  6.97 us
    ppermute x1, waiting for transfers between devices, local(): edge_ten = lax.ppermute(edge_ten, 'sec', both)  6.16 us
    ppermute x1, starting transfers between devices, local(): got_b = lax.ppermute(message_b, 'gx', swap_b)  3.26 us
    ppermute x1, waiting for transfers between devices, local(): got_a = lax.ppermute(message_a, 'gx', swap_a)  2.41 us
    ppermute x1, starting transfers between devices, local(): got_a = lax.ppermute(message_a, 'gx', swap_a)  2.08 us
    ppermute x2, starting transfers between devices, local(): side = lax.ppermute(share, 'gy', both)  2.05 us
    ppermute x1, waiting for transfers between devices, local(): got_b = lax.ppermute(message_b, 'gx', swap_b)  1.76 us
    ppermute x1, starting transfers between devices, local(): tension = lax.ppermute(tension, 'sec', both)  1.35 us
  transfers between devices with their start and end apart: 7, of which 3 were waited for; matrix products, arithmetic and copies ran while one was open for 0% of the time, Pallas kernels for 6%

profile of v3, /device:TPU:1, one launch (start us, length us, event | category | flops | bytes accessed | tf_op | source)
XLA Modules:
  0.0 27.4 jit_solution(9847514838092375093)
XLA Ops:
  0.0 0.0 copy-start.1
  0.0 2.0 %load.1 = (f32[3,18,48,128]{3,2,1,0:T(8,128)S(1)}, f32[5,16,32,128]{3,2,1,0:T(8,128)S(1)}, f32[3,16,8,128]{3,2,1,0:T(8,128)S(1)}, f32[512,128]{1,0:T(8,128)S(1)}...) custom-call(f32[8,16,32,128]{3,2,1,0:T(8,128)} %bitcast.12, s32[16,8,32]{2,1,0:T(8,128)} %bitcast.13, ...), custom_call_target="tpu_custom_call" | custom-call | tf_op jit(solution)/shard_map/load/pallas_call | solution.py:549
  2.0 0.0 copy-done.1
  2.1 1.1 %gather.1 = f32[512,128]{1,0:T(8,128)S(1)} custom-call(s32[512]{0:T(512)S(1)} %bitcast.11, f32[512,128]{1,0:T(8,128)S(1)} %get-tuple-element.24.plain), custom_call_target="tpu_custom_call" | custom-call | tf_op jit(solution)/shard_map/gather/pallas_call | solution.py:549
  3.1 1.3 %collective-permute-start.4 = (f32[512,128]{1,0:T(8,128)S(1)}, f32[512,128]{1,0:T(8,128)S(1)}, u32[]{:S(2)}, u32[]{:S(2)}) collective-permute-start(f32[512,128]{1,0:T(8,128)S(1)} %gather.1), channel_id=1, source_target_pairs={{0,16},{16,0},{1,17},{17,1},{2,18},{18,2},{3,19},{19,3},{4,20},{20... | collective-permute-start | bytes 786440 | tf_op jit(solution)/shard_map/ppermute | solution.py:603
  4.5 1.0 %collective-permute-start = (f32[3,16,8,128]{3,2,1,0:T(8,128)S(1)}, f32[3,16,8,128]{3,2,1,0:T(8,128)S(1)}, u32[]{:S(2)}, u32[]{:S(2)}) collective-permute-start(f32[3,16,8,128]{3,2,1,0:T(8,128)S(1)} %get-tuple-element.26), channel_id=1, source_target_pairs={{0,1},{1,0},{2,3},{3,2},{4,5},{5,4},{6,7},{7,6},{8,9},{9,8},{10,11... | collective-permute-start | bytes 589832 | tf_op jit(solution)/shard_map/ppermute | solution.py:601
  5.4 0.0 collective-permute-start.1
  5.4 6.2 %collective-permute-done.1.ten_ref = f32[2,32,128]{2,1,0:T(8,128)S(1)} collective-permute-done((f32[2,32,128]{2,1,0:T(8,128)S(1)}, f32[2,32,128]{2,1,0:T(8,128)S(1)}, u32[]{:S(2)}, u32[]{:S(2)}) %collective-permute-start.1) | collective-permute-done | bytes 32800 | tf_op jit(solution)/shard_map/ppermute | solution.py:600
  11.6 0.0 collective-permute-done.side_ref
  11.6 0.0 copy-done
  11.6 0.3 message.1
  11.8 0.0 collective-permute-done.4.ten_ref
  11.9 1.2 %inner.1 = (f32[3,18,48,128]{3,2,1,0:T(8,128)S(1)}, f32[3,18,8,128]{3,2,1,0:T(8,128)S(1)}, f32[4,16,32,128]{3,2,1,0:T(8,128)S(1)}) custom-call(f32[3,18,48,128]{3,2,1,0:T(8,128)S(1)} %get-tuple-element.30.pad, f32[5,16,32,128]{3,2,1,0:T(8,128)S(1)} %get-tuple-element.22.rest, f32[3,512,128]{2,1,0:T(8,128)S(1)} %get-tuple-element.23.fib_ref, ...), custom_call_target="tpu_custom_call" | custom-call | tf_op jit(solution)/shard_map/inner/pallas_call | solution.py:549
  13.1 1.1 %collective-permute-start.5 = (f32[3,18,8,128]{3,2,1,0:T(8,128)S(1)}, f32[3,18,8,128]{3,2,1,0:T(8,128)S(1)}, u32[]{:S(2)}, u32[]{:S(2)}) collective-permute-start(f32[3,18,8,128]{3,2,1,0:T(8,128)S(1)} %get-tuple-element.33), channel_id=1, source_target_pairs={{0,1},{1,0},{2,3},{3,2},{4,5},{5,4},{6,7},{7,6},{8,9},{9,8},{10,11... | collective-permute-start | bytes 663560 | tf_op jit(solution)/shard_map/ppermute | solution.py:622
  14.2 2.1 %collective-permute-start.2 = (f32[256,128]{1,0:T(8,128)S(1)}, f32[256,128]{1,0:T(8,128)S(1)}, u32[]{:S(2)}, u32[]{:S(2)}) collective-permute-start(f32[256,128]{1,0:T(8,128)S(1)} %get-tuple-element.28), channel_id=1, source_target_pairs={{0,2},{4,6},{8,10},{12,14},{2,0},{6,4},{10,8},{14,12},{1,3},{5,7},... | collective-permute-start | bytes 393224 | tf_op jit(solution)/shard_map/ppermute | solution.py:613
  16.3 3.3 %collective-permute-start.3 = (f32[256,128]{1,0:T(8,128)S(1)}, f32[256,128]{1,0:T(8,128)S(1)}, u32[]{:S(2)}, u32[]{:S(2)}) collective-permute-start(f32[256,128]{1,0:T(8,128)S(1)} %get-tuple-element.29), channel_id=1, source_target_pairs={{2,4},{6,8},{10,12},{14,0},{4,2},{8,6},{12,10},{0,14},{3,5},{7,9},... | collective-permute-start | bytes 393224 | tf_op jit(solution)/shard_map/ppermute | solution.py:614
  19.5 2.4 %collective-permute-done.2.got_a = f32[256,128]{1,0:T(8,128)S(1)} collective-permute-done((f32[256,128]{1,0:T(8,128)S(1)}, f32[256,128]{1,0:T(8,128)S(1)}, u32[]{:S(2)}, u32[]{:S(2)}) %collective-permute-start.2) | collective-permute-done | bytes 131104 | tf_op jit(solution)/shard_map/ppermute | solution.py:613
  22.0 1.8 %collective-permute-done.3.got_b = f32[256,128]{1,0:T(8,128)S(1)} collective-permute-done((f32[256,128]{1,0:T(8,128)S(1)}, f32[256,128]{1,0:T(8,128)S(1)}, u32[]{:S(2)}, u32[]{:S(2)}) %collective-permute-start.3) | collective-permute-done | bytes 131104 | tf_op jit(solution)/shard_map/ppermute | solution.py:614
  23.7 0.1 outer.1
  23.9 1.2 %collective-permute-start.6 = (f32[3,4,8,128]{3,2,1,0:T(8,128)S(1)}, f32[3,4,8,128]{3,2,1,0:T(8,128)S(1)}, u32[]{:S(2)}, u32[]{:S(2)}) collective-permute-start(f32[3,4,8,128]{3,2,1,0:T(8,128)S(1)} %get-tuple-element.36), channel_id=1, source_target_pairs={{0,1},{1,0},{2,3},{3,2},{4,5},{5,4},{6,7},{7,6},{8,9},{9,8},{10,11... | collective-permute-start | bytes 147464 | tf_op jit(solution)/shard_map/ppermute | solution.py:632
  25.1 0.0 collective-permute-done.5.side_ref
  25.1 1.3 %middle.1 = (f32[1,4,16,32,128]{4,3,2,1,0:T(8,128)}, f32[3,18,48,128]{3,2,1,0:T(8,128)S(1)}) custom-call(f32[3,512,128]{2,1,0:T(8,128)S(1)} %get-tuple-element.23.fib_ref, f32[512,128]{1,0:T(8,128)S(1)} %get-tuple-element.24.plain, f32[3,18,48,128]{3,2,1,0:T(8,128)S(1)} %get-tuple-element.32.next_in, ...), custom_call_target="tpu_custom_call", output_to_operand_aliasing={{1}: (2, {})} | custom-call | tf_op jit(solution)/shard_map/middle/pallas_call | solution.py:549
  26.5 0.0 collective-permute-done.6.side_ref
  26.5 0.9 %last.1 = (f32[1,4,16,32,128]{4,3,2,1,0:T(8,128)}, f32[3,18,48,128]{3,2,1,0:T(8,128)S(1)}) custom-call(f32[5,16,32,128]{3,2,1,0:T(8,128)S(1)} %get-tuple-element.22.rest, f32[3,512,128]{2,1,0:T(8,128)S(1)} %get-tuple-element.23.fib_ref, s32[2,1,32]{2,1,0:T(1,128)S(1)} %bitcast.9, ...), custom_call_target="tpu_custom_call", output_to_operand_aliasing={{1}: (6, {}), {0}: (9, {})} | custom-call | tf_op jit(solution)/shard_map/last/pallas_call | solution.py:549
  (1 shorter events, 0.0 us)
Async XLA Ops:
  0.0 2.0 %copy-start.1 = (s32[1,1,512]{2,1,0:T(1,128)S(1)}, s32[1,1,512]{2,1,0:T(1,128)}, u32[]{:S(2)}) copy-start(s32[1,1,512]{2,1,0:T(1,128)} %param.8) | copy-start | bytes 6148
  0.0 11.6 %copy-start = (s32[2,1,1,32]{3,2,1,0:T(1,128)S(1)}, s32[2,1,1,32]{3,2,1,0:T(1,128)}, u32[]{:S(2)}) copy-start(s32[2,1,1,32]{3,2,1,0:T(1,128)} %param.9) | copy-start | bytes 772
  3.1 8.7 %collective-permute-start.4 = (f32[512,128]{1,0:T(8,128)S(1)}, f32[512,128]{1,0:T(8,128)S(1)}, u32[]{:S(2)}, u32[]{:S(2)}) collective-permute-start(f32[512,128]{1,0:T(8,128)S(1)} %gather.1), channel_id=1, source_target_pairs={{0,16},{16,0},{1,17},{17,1},{2,18},{18,2},{3,19},{19,3},{4,20},{20... | collective-permute-start | bytes 786440 | tf_op jit(solution)/shard_map/ppermute | solution.py:603
  4.5 7.1 %collective-permute-start = (f32[3,16,8,128]{3,2,1,0:T(8,128)S(1)}, f32[3,16,8,128]{3,2,1,0:T(8,128)S(1)}, u32[]{:S(2)}, u32[]{:S(2)}) collective-permute-start(f32[3,16,8,128]{3,2,1,0:T(8,128)S(1)} %get-tuple-element.26), channel_id=1, source_target_pairs={{0,1},{1,0},{2,3},{3,2},{4,5},{5,4},{6,7},{7,6},{8,9},{9,8},{10,11... | collective-permute-start | bytes 589832 | tf_op jit(solution)/shard_map/ppermute | solution.py:601
  5.4 6.2 %collective-permute-start.1 = (f32[2,32,128]{2,1,0:T(8,128)S(1)}, f32[2,32,128]{2,1,0:T(8,128)S(1)}, u32[]{:S(2)}, u32[]{:S(2)}) collective-permute-start(f32[2,32,128]{2,1,0:T(8,128)S(1)} %get-tuple-element.27), channel_id=1, source_target_pairs={{0,16},{16,0},{1,17},{17,1},{2,18},{18,2},{3,19},{19,3},{4,20},{20... | collective-permute-start | bytes 98312 | tf_op jit(solution)/shard_map/ppermute | solution.py:600
  13.1 12.0 %collective-permute-start.5 = (f32[3,18,8,128]{3,2,1,0:T(8,128)S(1)}, f32[3,18,8,128]{3,2,1,0:T(8,128)S(1)}, u32[]{:S(2)}, u32[]{:S(2)}) collective-permute-start(f32[3,18,8,128]{3,2,1,0:T(8,128)S(1)} %get-tuple-element.33), channel_id=1, source_target_pairs={{0,1},{1,0},{2,3},{3,2},{4,5},{5,4},{6,7},{7,6},{8,9},{9,8},{10,11... | collective-permute-start | bytes 663560 | tf_op jit(solution)/shard_map/ppermute | solution.py:622
  14.2 7.8 %collective-permute-start.2 = (f32[256,128]{1,0:T(8,128)S(1)}, f32[256,128]{1,0:T(8,128)S(1)}, u32[]{:S(2)}, u32[]{:S(2)}) collective-permute-start(f32[256,128]{1,0:T(8,128)S(1)} %get-tuple-element.28), channel_id=1, source_target_pairs={{0,2},{4,6},{8,10},{12,14},{2,0},{6,4},{10,8},{14,12},{1,3},{5,7},... | collective-permute-start | bytes 393224 | tf_op jit(solution)/shard_map/ppermute | solution.py:613
  16.3 7.4 %collective-permute-start.3 = (f32[256,128]{1,0:T(8,128)S(1)}, f32[256,128]{1,0:T(8,128)S(1)}, u32[]{:S(2)}, u32[]{:S(2)}) collective-permute-start(f32[256,128]{1,0:T(8,128)S(1)} %get-tuple-element.29), channel_id=1, source_target_pairs={{2,4},{6,8},{10,12},{14,0},{4,2},{8,6},{12,10},{0,14},{3,5},{7,9},... | collective-permute-start | bytes 393224 | tf_op jit(solution)/shard_map/ppermute | solution.py:614
  23.9 2.6 %collective-permute-start.6 = (f32[3,4,8,128]{3,2,1,0:T(8,128)S(1)}, f32[3,4,8,128]{3,2,1,0:T(8,128)S(1)}, u32[]{:S(2)}, u32[]{:S(2)}) collective-permute-start(f32[3,4,8,128]{3,2,1,0:T(8,128)S(1)} %get-tuple-element.36), channel_id=1, source_target_pairs={{0,1},{1,0},{2,3},{3,2},{4,5},{5,4},{6,7},{7,6},{8,9},{9,8},{10,11... | collective-permute-start | bytes 147464 | tf_op jit(solution)/shard_map/ppermute | solution.py:632

commit v4 on v3

--- a/solution.py
+++ b/solution.py
@@ -10,6 +10,7 @@
 F32 = jnp.float32
 HIGHEST = lax.Precision.HIGHEST
 VMEM_LIMIT = 32 * 1024 * 1024
+COST = (10**10, 10**7)
 
 PAD = 8
 
@@ -543,7 +544,7 @@
         item[-1].wait()
 
 
-def call(kernel, name, out_shape, operands, spaces, scratch=(), out_spaces=None, aliases=()):
+def call(kernel, name, out_shape, operands, spaces, scratch=(), out_spaces=None, aliases=(), weight=1):
     if out_spaces is None:
         out_spaces = [pltpu.VMEM] * len(out_shape)
     return pl.pallas_call(
@@ -554,6 +555,9 @@
         out_specs=tuple(pl.BlockSpec(memory_space=space) for space in out_spaces),
         scratch_shapes=scratch,
         input_output_aliases=dict(aliases),
+        cost_estimate=pl.CostEstimate(
+            flops=weight * COST[0], bytes_accessed=weight * COST[1], transcendentals=0
+        ),
         compiler_params=pltpu.CompilerParams(vmem_limit_bytes=VMEM_LIMIT),
     )(*operands)
 
@@ -599,7 +603,9 @@
     )
     edge_ten = lax.ppermute(edge_ten, "sec", both)
     side = lax.ppermute(share, "gy", both)
-    (tension,) = call(gather_kernel, "gather", (f32(columns, depth),), (places, plain), (S, V))
+    (tension,) = call(
+        gather_kernel, "gather", (f32(columns, depth),), (places, plain), (S, V), weight=6
+    )
     tension = lax.ppermute(tension, "sec", both)
     message = f32(MESSAGE_ROWS, depth)
     message_a, message_b, pad = call(
@@ -618,6 +624,7 @@
         (padded, f32(3, size_x + 2, 8, depth), f32(4, size_x, size_y, depth)),
         (pad, rest, fib, tension),
         (V,) * 4,
+        weight=6,
     )
     side = lax.ppermute(share, "gy", both)
     moved, share = call(
@@ -641,6 +648,7 @@
         [fields, pltpu.SemaphoreType.DMA((3,))],
         out_spaces=(H, V),
         aliases={2: 1},
+        weight=6,
     )
     return call(
         last_kernel,

time: 27.5 us -> 19.8 us (0.72)
  the two profiles are of different devices: /device:TPU:1 before, /device:TPU:0 now
where the time goes in v4:
time: 19.8 us; the launch traced here: 19.6 us
  starting transfers between devices  8.88 us (45%)
  Pallas kernels  6.93 us (35%)
  waiting for transfers between devices  3.72 us (19%)
    pallas_call x7, Pallas kernels, call(): pl.pallas_call(kernel, name=name, out_shape=tuple(out_shape), in_specs=[p...  6.93 us
    ppermute x1, starting transfers between devices, local(): got_b = lax.ppermute(message_b, 'gx', swap_b)  3.54 us
    ppermute x1, starting transfers between devices, local(): edge_ten = lax.ppermute(edge_ten, 'sec', both)  2.71 us
    ppermute x1, starting transfers between devices, local(): got_a = lax.ppermute(message_a, 'gx', swap_a)  2.41 us
    ppermute x1, waiting for transfers between devices, local(): tension = lax.ppermute(tension, 'sec', both)  1.73 us
    ppermute x1, waiting for transfers between devices, local(): got_b = lax.ppermute(message_b, 'gx', swap_b)  1.06 us
    ppermute x1, waiting for transfers between devices, local(): edge_ten = lax.ppermute(edge_ten, 'sec', both)  0.75 us
  transfers between devices with their start and end apart: 7, of which 4 were waited for; matrix products, arithmetic and copies ran while one was open for 0% of the time, Pallas kernels for 20%

profile of v4, /device:TPU:0, one launch (start us, length us, event | category | flops | bytes accessed | tf_op | source)
XLA Modules:
  0.0 19.6 jit_solution(12488574187676132169)
XLA Ops:
  0.0 0.0 copy-start
  0.0 2.0 %load.1 = (f32[3,18,48,128]{3,2,1,0:T(8,128)S(1)}, f32[5,16,32,128]{3,2,1,0:T(8,128)S(1)}, f32[3,16,8,128]{3,2,1,0:T(8,128)S(1)}, f32[512,128]{1,0:T(8,128)S(1)}...) custom-call(f32[8,16,32,128]{3,2,1,0:T(8,128)} %bitcast.12, s32[16,8,32]{2,1,0:T(8,128)} %bitcast.13, ...), custom_call_target="tpu_custom_call" | custom-call | flops 10000000000 | bytes 10000000 | tf_op jit(solution)/shard_map/load/pallas_call | solution.py:550
  2.0 2.7 %collective-permute-start.1 = (f32[2,32,128]{2,1,0:T(8,128)S(1)}, f32[2,32,128]{2,1,0:T(8,128)S(1)}, u32[]{:S(2)}, u32[]{:S(2)}) collective-permute-start(f32[2,32,128]{2,1,0:T(8,128)S(1)} %get-tuple-element.27), channel_id=1, source_target_pairs={{0,16},{16,0},{1,17},{17,1},{2,18},{18,2},{3,19},{19,3},{4,20},{20... | collective-permute-start | bytes 98312 | tf_op jit(solution)/shard_map/ppermute | solution.py:604
  4.7 0.0 collective-permute-start
  4.7 0.0 copy-done
  4.7 1.0 %gather.1 = f32[512,128]{1,0:T(8,128)S(1)} custom-call(s32[512]{0:T(512)S(1)} %bitcast.8, f32[512,128]{1,0:T(8,128)S(1)} %get-tuple-element.24.plain), custom_call_target="tpu_custom_call" | custom-call | flops 60000002048 | bytes 60000000 | tf_op jit(solution)/shard_map/gather/pallas_call | solution.py:550
  5.8 0.1 collective-permute-start.4
  5.9 0.8 %collective-permute-done.1.ten_ref = f32[2,32,128]{2,1,0:T(8,128)S(1)} collective-permute-done((f32[2,32,128]{2,1,0:T(8,128)S(1)}, f32[2,32,128]{2,1,0:T(8,128)S(1)}, u32[]{:S(2)}, u32[]{:S(2)}) %collective-permute-start.1) | collective-permute-done | bytes 32800 | tf_op jit(solution)/shard_map/ppermute | solution.py:604
  6.6 0.0 collective-permute-done.side_ref
  6.6 0.0 copy-done.1
  6.6 0.3 %message.1 = (f32[256,128]{1,0:T(8,128)S(1)}, f32[256,128]{1,0:T(8,128)S(1)}, f32[3,18,48,128]{3,2,1,0:T(8,128)S(1)}) custom-call(f32[3,18,48,128]{3,2,1,0:T(8,128)S(1)} %get-tuple-element.25.pad_in, f32[5,16,32,128]{3,2,1,0:T(8,128)S(1)} %get-tuple-element.22.rest, ...), custom_call_target="tpu_custom_call", output_to_operand_aliasing={{2}: (0, {})} | custom-call | flops 10000000000 | bytes 10000000 | tf_op jit(solution)/shard_map/message/pallas_call | solution.py:550
  6.9 2.4 %collective-permute-start.2 = (f32[256,128]{1,0:T(8,128)S(1)}, f32[256,128]{1,0:T(8,128)S(1)}, u32[]{:S(2)}, u32[]{:S(2)}) collective-permute-start(f32[256,128]{1,0:T(8,128)S(1)} %get-tuple-element.28), channel_id=1, source_target_pairs={{0,2},{4,6},{8,10},{12,14},{2,0},{6,4},{10,8},{14,12},{1,3},{5,7},... | collective-permute-start | bytes 393224 | tf_op jit(solution)/shard_map/ppermute | solution.py:619
  9.3 3.5 %collective-permute-start.3 = (f32[256,128]{1,0:T(8,128)S(1)}, f32[256,128]{1,0:T(8,128)S(1)}, u32[]{:S(2)}, u32[]{:S(2)}) collective-permute-start(f32[256,128]{1,0:T(8,128)S(1)} %get-tuple-element.29), channel_id=1, source_target_pairs={{2,4},{6,8},{10,12},{14,0},{4,2},{8,6},{12,10},{0,14},{3,5},{7,9},... | collective-permute-start | bytes 393224 | tf_op jit(solution)/shard_map/ppermute | solution.py:620
  12.9 1.7 %collective-permute-done.4.ten_ref = f32[512,128]{1,0:T(8,128)S(1)} collective-permute-done((f32[512,128]{1,0:T(8,128)S(1)}, f32[512,128]{1,0:T(8,128)S(1)}, u32[]{:S(2)}, u32[]{:S(2)}) %collective-permute-start.4) | collective-permute-done | bytes 262176 | tf_op jit(solution)/shard_map/ppermute | solution.py:609
  14.6 1.2 %inner.1 = (f32[3,18,48,128]{3,2,1,0:T(8,128)S(1)}, f32[3,18,8,128]{3,2,1,0:T(8,128)S(1)}, f32[4,16,32,128]{3,2,1,0:T(8,128)S(1)}) custom-call(f32[3,18,48,128]{3,2,1,0:T(8,128)S(1)} %get-tuple-element.30.pad, f32[5,16,32,128]{3,2,1,0:T(8,128)S(1)} %get-tuple-element.22.rest, f32[3,512,128]{2,1,0:T(8,128)S(1)} %get-tuple-element.23.fib_ref, ...), custom_call_target="tpu_custom_call" | custom-call | flops 60000002048 | bytes 60000000 | tf_op jit(solution)/shard_map/inner/pallas_call | solution.py:550
  15.8 0.1 collective-permute-start.5
  15.9 0.0 collective-permute-done.2.got_a
  15.9 1.1 %collective-permute-done.3.got_b = f32[256,128]{1,0:T(8,128)S(1)} collective-permute-done((f32[256,128]{1,0:T(8,128)S(1)}, f32[256,128]{1,0:T(8,128)S(1)}, u32[]{:S(2)}, u32[]{:S(2)}) %collective-permute-start.3) | collective-permute-done | bytes 131104 | tf_op jit(solution)/shard_map/ppermute | solution.py:620
  17.0 0.1 outer.1
  17.1 0.1 collective-permute-start.6
  17.2 0.2 collective-permute-done.5.side_ref
  17.4 1.3 %middle.1 = (f32[1,4,16,32,128]{4,3,2,1,0:T(8,128)}, f32[3,18,48,128]{3,2,1,0:T(8,128)S(1)}) custom-call(f32[3,512,128]{2,1,0:T(8,128)S(1)} %get-tuple-element.23.fib_ref, f32[512,128]{1,0:T(8,128)S(1)} %get-tuple-element.24.plain, f32[3,18,48,128]{3,2,1,0:T(8,128)S(1)} %get-tuple-element.32.next_in, ...), custom_call_target="tpu_custom_call", output_to_operand_aliasing={{1}: (2, {})} | custom-call | flops 60000002048 | bytes 60000000 | tf_op jit(solution)/shard_map/middle/pallas_call | solution.py:550
  18.7 0.0 collective-permute-done.6.side_ref
  18.7 0.9 %last.1 = (f32[1,4,16,32,128]{4,3,2,1,0:T(8,128)}, f32[3,18,48,128]{3,2,1,0:T(8,128)S(1)}) custom-call(f32[5,16,32,128]{3,2,1,0:T(8,128)S(1)} %get-tuple-element.22.rest, f32[3,512,128]{2,1,0:T(8,128)S(1)} %get-tuple-element.23.fib_ref, s32[2,1,32]{2,1,0:T(1,128)S(1)} %bitcast.11, ...), custom_call_target="tpu_custom_call", output_to_operand_aliasing={{1}: (6, {}), {0}: (9, {})} | custom-call | flops 10000000000 | bytes 10000000 | tf_op jit(solution)/shard_map/last/pallas_call | solution.py:550
  (1 shorter events, 0.0 us)
Async XLA Ops:
  0.0 4.7 %copy-start = (s32[1,1,512]{2,1,0:T(1,128)S(1)}, s32[1,1,512]{2,1,0:T(1,128)}, u32[]{:S(2)}) copy-start(s32[1,1,512]{2,1,0:T(1,128)} %param.8) | copy-start | bytes 6148
  2.0 4.6 %collective-permute-start.1 = (f32[2,32,128]{2,1,0:T(8,128)S(1)}, f32[2,32,128]{2,1,0:T(8,128)S(1)}, u32[]{:S(2)}, u32[]{:S(2)}) collective-permute-start(f32[2,32,128]{2,1,0:T(8,128)S(1)} %get-tuple-element.27), channel_id=1, source_target_pairs={{0,16},{16,0},{1,17},{17,1},{2,18},{18,2},{3,19},{19,3},{4,20},{20... | collective-permute-start | bytes 98312 | tf_op jit(solution)/shard_map/ppermute | solution.py:604
  4.7 1.9 %collective-permute-start = (f32[3,16,8,128]{3,2,1,0:T(8,128)S(1)}, f32[3,16,8,128]{3,2,1,0:T(8,128)S(1)}, u32[]{:S(2)}, u32[]{:S(2)}) collective-permute-start(f32[3,16,8,128]{3,2,1,0:T(8,128)S(1)} %get-tuple-element.26), channel_id=1, source_target_pairs={{0,1},{1,0},{2,3},{3,2},{4,5},{5,4},{6,7},{7,6},{8,9},{9,8},{10,11... | collective-permute-start | bytes 589832 | tf_op jit(solution)/shard_map/ppermute | solution.py:605
  4.7 1.9 %copy-start.1 = (s32[2,1,1,32]{3,2,1,0:T(1,128)S(1)}, s32[2,1,1,32]{3,2,1,0:T(1,128)}, u32[]{:S(2)}) copy-start(s32[2,1,1,32]{3,2,1,0:T(1,128)} %param.9) | copy-start | bytes 772
  5.8 8.8 %collective-permute-start.4 = (f32[512,128]{1,0:T(8,128)S(1)}, f32[512,128]{1,0:T(8,128)S(1)}, u32[]{:S(2)}, u32[]{:S(2)}) collective-permute-start(f32[512,128]{1,0:T(8,128)S(1)} %gather.1), channel_id=1, source_target_pairs={{0,16},{16,0},{1,17},{17,1},{2,18},{18,2},{3,19},{19,3},{4,20},{20... | collective-permute-start | bytes 786440 | tf_op jit(solution)/shard_map/ppermute | solution.py:609
  6.9 9.0 %collective-permute-start.2 = (f32[256,128]{1,0:T(8,128)S(1)}, f32[256,128]{1,0:T(8,128)S(1)}, u32[]{:S(2)}, u32[]{:S(2)}) collective-permute-start(f32[256,128]{1,0:T(8,128)S(1)} %get-tuple-element.28), channel_id=1, source_target_pairs={{0,2},{4,6},{8,10},{12,14},{2,0},{6,4},{10,8},{14,12},{1,3},{5,7},... | collective-permute-start | bytes 393224 | tf_op jit(solution)/shard_map/ppermute | solution.py:619
  9.3 7.7 %collective-permute-start.3 = (f32[256,128]{1,0:T(8,128)S(1)}, f32[256,128]{1,0:T(8,128)S(1)}, u32[]{:S(2)}, u32[]{:S(2)}) collective-permute-start(f32[256,128]{1,0:T(8,128)S(1)} %get-tuple-element.29), channel_id=1, source_target_pairs={{2,4},{6,8},{10,12},{14,0},{4,2},{8,6},{12,10},{0,14},{3,5},{7,9},... | collective-permute-start | bytes 393224 | tf_op jit(solution)/shard_map/ppermute | solution.py:620
  15.8 1.5 %collective-permute-start.5 = (f32[3,18,8,128]{3,2,1,0:T(8,128)S(1)}, f32[3,18,8,128]{3,2,1,0:T(8,128)S(1)}, u32[]{:S(2)}, u32[]{:S(2)}) collective-permute-start(f32[3,18,8,128]{3,2,1,0:T(8,128)S(1)} %get-tuple-element.33), channel_id=1, source_target_pairs={{0,1},{1,0},{2,3},{3,2},{4,5},{5,4},{6,7},{7,6},{8,9},{9,8},{10,11... | collective-permute-start | bytes 663560 | tf_op jit(solution)/shard_map/ppermute | solution.py:629
  17.1 1.6 %collective-permute-start.6 = (f32[3,4,8,128]{3,2,1,0:T(8,128)S(1)}, f32[3,4,8,128]{3,2,1,0:T(8,128)S(1)}, u32[]{:S(2)}, u32[]{:S(2)}) collective-permute-start(f32[3,4,8,128]{3,2,1,0:T(8,128)S(1)} %get-tuple-element.36), channel_id=1, source_target_pairs={{0,1},{1,0},{2,3},{3,2},{4,5},{5,4},{6,7},{7,6},{8,9},{9,8},{10,11... | collective-permute-start | bytes 147464 | tf_op jit(solution)/shard_map/ppermute | solution.py:639

commit v5 on v4

v5 whole, which is shorter than its diff:
```python
import jax
import jax.numpy as jnp
from jax import lax
from jax.experimental import pallas as pl
from jax.experimental.pallas import tpu as pltpu
from jax.sharding import PartitionSpec as P

DT = 0.1
OMEGA = 0.06
F32 = jnp.float32
HIGHEST = lax.Precision.HIGHEST
VMEM_LIMIT = 16 * 1024 * 1024
COST = (10**10, 10**7)

PAD = 8

ROW_NOW, ROW_NEXT, ROW_STIFF, ROW_SIDE = 0, 96, 192, 224
ROW_LIST = ROW_SIDE + 6
MESSAGE_ROWS = 232


def inverse(v):
    r = pl.reciprocal(v, approx=True)
    return r * (2.0 - v * r)


def rise(c):
    c2 = c * c
    return c2 * inverse(c2 + 0.25)


def ends(like):
    lane = lax.broadcasted_iota(jnp.int32, like, 1)
    return lane == like[1] - 1, lane == 0


def up_z(w, last):
    return jnp.where(last, 0.0, pltpu.roll(w, w.shape[1] - 1, 1))


def down_z(w, first):
    return jnp.where(first, 0.0, pltpu.roll(w, 1, 1))


def rows_of(pad, a, x, size_y, shift=0):
    return pad[a, x, PAD + shift : PAD + shift + size_y, :]


def motion_rate(pad, x, size_y):
    at = lambda a, dx=0, dy=0: rows_of(pad, a, x + dx, size_y, dy)
    u0, u1, u2 = at(0), at(1), at(2)
    last, first = ends(u0.shape)
    w0p, w0m, w1p, w1m = at(0, 1), at(0, -1), at(1, 1), at(1, -1)
    w2p, w2m = at(2, 1), at(2, -1)
    e0, e2 = 0.5 * (w0p - w0m), 0.5 * (w2p - w2m)
    e0y = (at(0, 1, 1) - at(0, -1, 1)) - (at(0, 1, -1) - at(0, -1, -1))
    e1y = (at(1, 1, 1) - at(1, -1, 1)) - (at(1, 1, -1) - at(1, -1, -1))
    v1p, v1m, v2p, v2m = at(1, 0, 1), at(1, 0, -1), at(2, 0, 1), at(2, 0, -1)
    d2 = 0.5 * (v2p - v2m)
    d1 = 0.5 * (v1p - v1m) + e0
    r0 = (
        up_z(u0 + e2, last) + down_z(u0 - e2, first)
        + (at(0, 0, 1) + at(0, 0, -1)) + 0.5 * e1y + 3.0 * (w0p + w0m)
    )
    r1 = (
        up_z(u1 + d2, last) + down_z(u1 - d2, first)
        + 3.0 * (v1p + v1m) + 0.5 * e0y + (w1p + w1m)
    )
    t2 = 3.0 * u2
    r2 = up_z(t2 + d1, last) + down_z(t2 - d1, first) + (v2p + v2m) + (w2p + w2m)
    return r0, r1, r2


def motion_from(pad, x, sign, size_y):
    u0, u1, u2 = [rows_of(pad, a, x, size_y) for a in range(3)]
    last, first = ends(u0.shape)
    half = 0.5 * sign
    dy0 = rows_of(pad, 0, x, size_y, 1) - rows_of(pad, 0, x, size_y, -1)
    dy1 = rows_of(pad, 1, x, size_y, 1) - rows_of(pad, 1, x, size_y, -1)
    dz0 = up_z(u0, last) - down_z(u0, first)
    dz2 = up_z(u2, last) - down_z(u2, first)
    return 3.0 * u0 + half * (dy1 + dz2), u1 + half * dy0, u2 + half * dz0


def volt_rate(pad, x, fib, size_y):
    at = lambda dx=0, dy=0: rows_of(pad, 0, x + dx, size_y, dy)
    v, wp, wm, yp, ym = at(), at(1), at(-1), at(0, 1), at(0, -1)
    last, first = ends(v.shape)
    e = wp - wm
    ey = (at(1, 1) - at(-1, 1)) - (at(1, -1) - at(-1, -1))
    dy = yp - ym
    sum_z = up_z(v, last) + down_z(v, first)
    ez = up_z(e, last) - down_z(e, first)
    dyz = up_z(dy, last) - down_z(dy, first)
    g = [0.75 * w for w in fib]
    d00, d11, d22 = [0.25 + a * b for a, b in zip(g, fib)]
    return (
        d00 * (wp + wm) + d11 * (yp + ym) + d22 * sum_z - 2.0 * (d00 + d11 + d22) * v
        + 0.5 * (fib[0] * (g[1] * ey + g[2] * ez) + g[1] * fib[2] * dyz)
    )


def couplings(fib):
    g = 0.75 * fib[0]
    return 0.25 + g * fib[0], 0.5 * g * fib[1], 0.5 * g * fib[2]


def volt_from(pad, x, coupled, sign, size_y):
    v = rows_of(pad, 0, x, size_y)
    last, first = ends(v.shape)
    dy = rows_of(pad, 0, x, size_y, 1) - rows_of(pad, 0, x, size_y, -1)
    dz = up_z(v, last) - down_z(v, first)
    return coupled[0] * v + sign * (coupled[1] * dy + coupled[2] * dz)


def currents(v, c, d, f, n, r):
    q = rise(c)
    calcium_flow = 1.2 * d * f * (v - 2.0)
    return q, calcium_flow, calcium_flow + (0.8 * n + 0.6 * q * r) * (v + 1.0) + 0.1 * v


def permute_rows(listed, values):
    rows = values.shape[0]
    pick = (lax.broadcasted_iota(jnp.int32, (rows, rows), 0).astype(F32) == listed).astype(F32)
    return lax.dot_general(
        pick, values, (((0,), (0,)), ((), ())), precision=HIGHEST, preferred_element_type=F32
    )


def tie_rows(listed, stiff, u):
    joined = jnp.concatenate([2.0 * stiff * w for w in u], axis=1)
    moved = permute_rows(listed, joined)
    depth = u[0].shape[1]
    return [moved[:, a * depth : (a + 1) * depth] for a in range(3)]


def edges_tile(value):
    rows = value.shape[0]
    last = lax.broadcasted_iota(jnp.int32, (8, value.shape[1]), 0) == 7
    return jnp.where(last, value[rows - 8 :], value[:8])


def fill_sides(pad, a, x, tile, size_y):
    pad[a, x, 0:PAD, :] = tile
    pad[a, x, PAD + size_y :, :] = tile


def sides(size_x):
    return (0, 0, -1.0), (size_x + 1, size_x - 1, 1.0)


def place_of(x, size_y):
    return pl.ds(pl.multiple_of(x * size_y, size_y), size_y)


def electric():
    return lax.axis_index("sec") == 0


def fiber_fields(angles, cls, flat, fib_ref, size_x, size_y):
    blocks, classes, depth = cls.shape[1], angles.shape[1], fib_ref.shape[2]
    azimuth, elevation = angles[0:1, :], angles[1:2, :]
    flat_part = jnp.cos(elevation)
    fib = [jnp.cos(azimuth) * flat_part, jnp.sin(azimuth) * flat_part, jnp.sin(elevation)]
    for x in range(size_x):
        flat[:, x * size_y : (x + 1) * size_y] = cls[x]
    own = lax.broadcasted_iota(jnp.int32, (blocks, depth), 1) // (depth // blocks)
    own = own == lax.broadcasted_iota(jnp.int32, (blocks, depth), 0)
    hits = jnp.concatenate([(flat[...] == k).astype(F32) for k in range(classes)], axis=0)
    table = jnp.concatenate(
        [
            jnp.concatenate(
                [jnp.where(own, jnp.broadcast_to(w[:, k : k + 1], own.shape), 0.0) for w in fib], axis=1
            )
            for k in range(classes)
        ],
        axis=0,
    )
    high = table.astype(jnp.bfloat16).astype(F32)
    mid = (table - high).astype(jnp.bfloat16).astype(F32)
    parts = jnp.concatenate([high, mid, table - high - mid], axis=0)
    found = lax.dot_general(
        jnp.concatenate([hits] * 3, axis=0), parts, (((0,), (0,)), ((), ())), preferred_element_type=F32
    )
    for a in range(3):
        fib_ref[a] = found[:, a * depth : (a + 1) * depth]


def tension_kernel(sec_hbm, map_hbm, plain, edge_ten, main, gate, late, map_ref, sems):
    size_x, size_y = sec_hbm.shape[1], sec_hbm.shape[2]
    pieces = (sems.shape[0] - 1) // 3
    chunk = size_x // pieces

    def plane(x, carry):
        v, c, d, f, bound, s = main[0, x], main[1, x], main[2, x], gate[0, x], late[0, x], late[1, x]
        calcium_flow = 1.2 * d * f * (v - 2.0)
        flow = 2.0 * c * (1.0 - bound) - 0.4 * bound
        c1 = c + DT * (-0.3 * calcium_flow - 0.5 * c - flow)
        s1 = s + (0.5 * DT) * (rise(c) - s)
        plain[place_of(x, size_y), :] = s1 + (0.5 * DT) * (rise(c1) - s1)
        return carry

    @pl.when(electric())
    def _():
        places = pltpu.make_async_copy(map_hbm, map_ref, sems.at[0])
        copies = []
        for i in range(pieces):
            here = pl.ds(i * chunk, chunk)
            copies.append(
                [
                    pltpu.make_async_copy(sec_hbm.at[src, here], dst.at[:, here], sems.at[1 + 3 * i + k])
                    for k, (src, dst) in enumerate(
                        ((pl.ds(0, 3), main), (pl.ds(3, 1), gate), (pl.ds(6, 2), late))
                    )
                ]
            )
            for copy in copies[-1]:
                copy.start()
        places.start()
        for i in range(pieces):
            for copy in copies[i]:
                copy.wait()
            lax.fori_loop(i * chunk, (i + 1) * chunk, plane, 0, unroll=2)
        places.wait()
        last = (size_x - 1) * size_y
        for p in range(size_y):
            edge_ten[0, p : p + 1, :] = plain[pl.ds(map_ref[p], 1), :]
            edge_ten[1, p : p + 1, :] = plain[pl.ds(map_ref[last + p], 1), :]


def share_kernel(own, pad, share):
    size_x, size_y = own.shape[1], own.shape[2]
    zeros = jnp.zeros(pad.shape[2:], F32)
    for a in range(3):
        pad[a, 0] = zeros
        pad[a, size_x + 1] = zeros

    def plane(x, carry):
        for a in range(3):
            value = own[a, x]
            pad[a, x + 1, PAD : PAD + size_y, :] = value
            share[a, x] = edges_tile(value)
        return carry

    lax.fori_loop(0, size_x, plane, 0, unroll=4)


def gather_kernel(map_hbm, plain, cls_ref, ang_ref, all_ref, fib_ref, out_hbm, map_ref, flat, sems):
    size_x = cls_ref.shape[0]
    size_y = all_ref.shape[0] // size_x
    places = pltpu.make_async_copy(map_hbm, map_ref, sems.at[0])
    copies = [
        pltpu.make_async_copy(plain.at[x * size_y : (x + 1) * size_y], out_hbm.at[0, 3, x], sems.at[1 + x])
        for x in range(size_x)
    ]

    @pl.when(electric())
    def _():
        places.start()
        for copy in copies:
            copy.start()

    fiber_fields(ang_ref[...], cls_ref, flat, fib_ref, size_x, size_y)

    @pl.when(electric())
    def _():
        places.wait()

        def rows(i, carry):
            for k in range(32):
                p = i * 32 + k
                all_ref[pl.ds(p, 1), :] = plain[pl.ds(map_ref[p], 1), :]
            return carry

        lax.fori_loop(0, all_ref.shape[0] // 32, rows, 0)
        for copy in copies:
            copy.wait()


def message_electric(pad_in, own, side_ref, fib_ref, list_ref, high_ref, low_ref, pad):
    size_x, size_y = own.shape[1], own.shape[2]

    def fill(x, carry):
        for a in range(3):
            fill_sides(pad, a, x + 1, side_ref[a, x], size_y)
        return carry

    lax.fori_loop(0, size_x, fill, 0, unroll=4)
    for which, ((_, edge, _), out) in enumerate(zip(sides(size_x), (low_ref, high_ref))):
        for a in range(3):
            row = ROW_SIDE + 2 * a
            out[row : row + 1, :] = side_ref[a, edge, 7:8, :]
            out[row + 1 : row + 2, :] = side_ref[a, edge, 0:1, :]
        out[ROW_LIST : ROW_LIST + 1, 0:size_y] = list_ref[which].astype(F32)

        @pl.when(electric())
        def _():
            fib = [fib_ref[a, place_of(edge, size_y), :] for a in range(3)]
            v, c, d = [rows_of(pad, a, edge + 1, size_y) for a in range(3)]
            f, n, r = [own[k, edge] for k in range(3, 6)]
            rate = volt_rate(pad, edge + 1, fib, size_y)
            _, _, total = currents(v, c, d, f, n, r)
            for at, value in zip(
                (ROW_NOW, ROW_NOW + size_y, ROW_NOW + 2 * size_y, ROW_NEXT, ROW_NEXT + size_y),
                (v,) + couplings(fib)[:2] + (v + DT * (rate - total), couplings(fib)[2]),
            ):
                out[at : at + size_y, :] = value

        @pl.when(jnp.logical_not(electric()))
        def _():
            rate = motion_rate(pad, edge + 1, size_y)
            stiff = own[6, edge]
            beta = OMEGA * inverse(stiff)
            out[ROW_STIFF : ROW_STIFF + size_y, :] = stiff
            for a in range(3):
                u = rows_of(pad, a, edge + 1, size_y)
                out[ROW_NOW + a * size_y : ROW_NOW + (a + 1) * size_y, :] = u
                out[ROW_NEXT + a * size_y : ROW_NEXT + (a + 1) * size_y, :] = (
                    0.28 * u + beta * own[3 + a, edge] + OMEGA * rate[a]
                )


def message_mechanic(own, fib_ref, ten_ref, high_in, low_in, high_ref, low_ref):
    size_x, size_y = own.shape[1], own.shape[2]

    @pl.when(jnp.logical_not(electric()))
    def _():
        for which, ((_, edge, _), out) in enumerate(zip(sides(size_x), (low_ref, high_ref))):
            act = OMEGA * inverse(own[6, edge]) * own[7, edge] * ten_ref[which]
            for a in range(3):
                rows = slice(ROW_NEXT + a * size_y, ROW_NEXT + (a + 1) * size_y)
                out[rows, :] = out[rows, :] + act * fib_ref[a, place_of(edge, size_y), :]


def put_inner(next_pad, share, a, x, value):
    next_pad[a, x, PAD : PAD + value.shape[0], :] = value
    share[a, x] = edges_tile(value)


def inner_electric(pad, own, fib_ref, next_pad, share, keep):
    size_x, size_y = own.shape[1], own.shape[2]

    @pl.when(electric())
    def _():
        def plane(x, carry):
            place = place_of(x, size_y)
            v, c, d = [rows_of(pad, a, x + 1, size_y) for a in range(3)]
            f, n, r, bound, _ = [own[k, x] for k in range(3, 8)]
            rate = volt_rate(pad, x + 1, [fib_ref[a, place, :] for a in range(3)], size_y)
            q, calcium_flow, total = currents(v, c, d, f, n, r)
            flow = 2.0 * c * (1.0 - bound) - 0.4 * bound
            put_inner(next_pad, share, 0, x + 1, v + DT * (rate - total))
            c1 = c + DT * (-0.3 * calcium_flow - 0.5 * c - flow)
            tv = jnp.tanh(v)
            d1 = (1.0 - 2.0 * DT) * d + DT * (1.0 + jnp.tanh(v + 0.5))
            f1 = (1.0 - DT / 3.0) * f + (DT / 6.0) * (1.0 - tv)
            n1 = (1.0 - DT) * n + (0.5 * DT) * (1.0 + tv)
            r1 = (1.0 - DT / 5.0) * r + (DT / 10.0) * (1.0 + jnp.tanh(0.5 * v - 0.25))
            bound1 = bound + DT * flow
            flow1 = 2.0 * c1 * (1.0 - bound1) - 0.4 * bound1
            keep[0, x] = n1
            keep[1, x] = 1.2 * d1 * f1
            keep[2, x] = 0.8 * n1 + 0.6 * rise(c1) * r1
            keep[3, x] = c1 - DT * (0.5 * c1 + flow1)
            return carry

        lax.fori_loop(0, size_x, plane, 0, unroll=2)


def inner_mechanic(pad, own, fib_ref, ten_ref, next_in, share_in, keep_in, next_pad, share, keep):
    size_x, size_y = own.shape[1], own.shape[2]

    @pl.when(jnp.logical_not(electric()))
    def _():
        def plane(x, carry):
            place = place_of(x, size_y)
            rate = motion_rate(pad, x + 1, size_y)
            beta = OMEGA * inverse(own[6, x])
            act = own[7, x] * ten_ref[place, :]
            keep[3, x] = act
            for a in range(3):
                drive = beta * (own[3 + a, x] + act * fib_ref[a, place, :])
                keep[a, x] = drive
                value = 0.4 * rows_of(pad, a, x + 1, size_y) + drive + OMEGA * rate[a]
                put_inner(next_pad, share, a, x + 1, value)
            return carry

        lax.fori_loop(0, size_x, plane, 0, unroll=2)


def outer_kernel(pad, own, fib_ref, list_ref, got_low, got_high, next_in, next_pad, share, wide):
    size_x, size_y = own.shape[1], own.shape[2]
    work = list(zip(sides(size_x), (got_low, got_high)))
    for slot, (_, got) in enumerate(work):
        for a in range(3):
            wide[a, slot, PAD : PAD + size_y, :] = got[ROW_NOW + a * size_y : ROW_NOW + (a + 1) * size_y, :]
            row = ROW_SIDE + 2 * a
            wide[a, slot, PAD - 1 : PAD, :] = got[row : row + 1, :]
            wide[a, slot, PAD + size_y : PAD + size_y + 1, :] = got[row + 1 : row + 2, :]

    def put(a, x, slot, value):
        next_pad[a, x, PAD : PAD + size_y, :] = value
        share[a, slot] = edges_tile(value)

    @pl.when(electric())
    def _():
        for which, ((halo, edge, sign), got) in enumerate(work):
            fib = [fib_ref[a, place_of(edge, size_y), :] for a in range(3)]
            put(
                0,
                edge + 1,
                1 + which,
                rows_of(next_pad, 0, edge + 1, size_y) + DT * volt_from(wide, which, couplings(fib), sign, size_y),
            )
            theirs = [
                got[at : at + size_y, :] for at in (ROW_NOW + size_y, ROW_NOW + 2 * size_y, ROW_NEXT + size_y)
            ]
            put(
                0,
                halo,
                3 * which,
                got[ROW_NEXT : ROW_NEXT + size_y, :] + DT * volt_from(pad, edge + 1, theirs, -sign, size_y),
            )

    @pl.when(jnp.logical_not(electric()))
    def _():
        for which, ((halo, edge, sign), got) in enumerate(work):
            stiff = got[ROW_STIFF : ROW_STIFF + size_y, :]
            stiff_own = own[6, edge]
            now = [rows_of(pad, a, edge + 1, size_y) for a in range(3)]
            theirs = [rows_of(wide, a, which, size_y) for a in range(3)]
            ties = tie_rows(list_ref[which].astype(F32), stiff, theirs)
            rate = motion_from(wide, which, sign, size_y)
            beta = OMEGA * inverse(stiff_own)
            for a in range(3):
                put(
                    a,
                    edge + 1,
                    1 + which,
                    rows_of(next_pad, a, edge + 1, size_y) + OMEGA * rate[a] + beta * ties[a] - 0.12 * now[a],
                )
            ties = tie_rows(got[ROW_LIST : ROW_LIST + 1, 0:size_y], stiff_own, now)
            rate = motion_from(pad, edge + 1, -sign, size_y)
            beta = OMEGA * inverse(stiff)
            for a in range(3):
                put(
                    a,
                    halo,
                    3 * which,
                    got[ROW_NEXT + a * size_y : ROW_NEXT + (a + 1) * size_y, :] + OMEGA * rate[a] + beta * ties[a],
                )


def electric_end(x, next_pad, fib_ref):
    size_y = next_pad.shape[2] - 2 * PAD
    place = place_of(x, size_y)
    return rows_of(next_pad, 0, x + 1, size_y) + DT * volt_rate(
        next_pad, x + 1, [fib_ref[a, place, :] for a in range(3)], size_y
    )


def electric_rest(x, next_pad, keep, out):
    size_y = next_pad.shape[2] - 2 * PAD
    v = rows_of(next_pad, 0, x + 1, size_y)
    n, gate, leak, rest_c = [keep[k, x] for k in range(4)]
    flow = gate * (v - 2.0)
    out[0, x] = -DT * (flow + leak * (v + 1.0) + 0.1 * v)
    out[1, x] = rest_c - (0.3 * DT) * flow
    out[2, x] = (1.0 - DT) * n + (0.5 * DT) * (1.0 + jnp.tanh(v))


def mechanic_end(x, next_pad, keep, out, size_y, ties=None):
    rate = motion_rate(next_pad, x + 1, size_y)
    for a in range(3):
        u = rows_of(next_pad, a, x + 1, size_y)
        value = 0.4 * u + keep[a, x] + OMEGA * rate[a]
        out[a, x] = value if ties is None else value + ties[a] - 0.12 * u


def middle_kernel(fib_ref, next_in, side_ref, keep, out_in, out_hbm, next_pad, held, out, sems):
    size_x = keep.shape[1]
    size_y = fib_ref.shape[1] // size_x
    pieces = sems.shape[0] - 1
    chunk = (size_x - 4) // pieces

    def copy_out(i, fields):
        here = pl.ds(2 + i * chunk, chunk)
        return pltpu.make_async_copy(out.at[0:fields, here], out_hbm.at[0, 0:fields, here], sems.at[i])

    def fill(count):
        def one(x, carry):
            for a in range(count):
                fill_sides(next_pad, a, x, side_ref[a, x], size_y)
            return carry

        lax.fori_loop(2, size_x, one, 0, unroll=2)

    @pl.when(electric())
    def _():
        fill(1)

        def rest(x, carry):
            electric_rest(x, next_pad, keep, out)
            return carry

        lax.fori_loop(0, size_x, rest, 0, unroll=2)
        copy = pltpu.make_async_copy(out.at[1:3], out_hbm.at[0, 1:3], sems.at[pieces])
        copy.start()
        for i, x in enumerate((0, 1, size_x - 2, size_x - 1)):
            held[i] = out[0, x]

        def step(i, carry):
            for k in range(chunk):
                x = 2 + i * chunk + k
                out[0, x] = out[0, x] + electric_end(x, next_pad, fib_ref)
            copy_out(i, 1).start()
            return carry

        lax.fori_loop(0, pieces, step, 0)
        copy.wait()
        for i in range(pieces):
            copy_out(i, 1).wait()

    @pl.when(jnp.logical_not(electric()))
    def _():
        fill(3)
        copy = pltpu.make_async_copy(keep.at[3:4], out_hbm.at[0, 3:4], sems.at[pieces])
        copy.start()

        def sweep(i, carry):
            for k in range(chunk):
                mechanic_end(2 + i * chunk + k, next_pad, keep, out, size_y)
            copy_out(i, 3).start()
            return carry

        lax.fori_loop(0, pieces, sweep, 0)
        copy.wait()
        for i in range(pieces):
            copy_out(i, 3).wait()


def last_kernel(
    own, fib_ref, list_ref, got_low, got_high, next_in, side_ref, keep, held, out_in, out_hbm, next_pad, out, sems
):
    size_x, size_y = own.shape[1], own.shape[2]

    def copy_out(which, first, fields):
        here = pl.ds(first, 2)
        return pltpu.make_async_copy(out.at[0:fields, here], out_hbm.at[0, 0:fields, here], sems.at[which])

    work = []
    for which, ((halo, edge, _), got) in enumerate(zip(sides(size_x), (got_low, got_high))):
        near = abs(edge - 1)
        work.append((halo, edge, near, which, got, min(edge, near)))

    @pl.when(electric())
    def _():
        for halo, edge, near, which, _, first in work:
            fill_sides(next_pad, 0, halo, side_ref[0, 3 * which], size_y)
            fill_sides(next_pad, 0, edge + 1, side_ref[0, 1 + which], size_y)
            for x in (near, edge):
                out[0, x] = held[2 * which + x - first] + electric_end(x, next_pad, fib_ref)
            copy_out(which, first, 1).start()
        for item in work:
            copy_out(item[3], item[-1], 1).wait()

    @pl.when(jnp.logical_not(electric()))
    def _():
        for halo, edge, near, which, got, first in work:
            for a in range(3):
                fill_sides(next_pad, a, halo, side_ref[a, 3 * which], size_y)
                fill_sides(next_pad, a, edge + 1, side_ref[a, 1 + which], size_y)
            beta = OMEGA * inverse(own[6, edge])
            ties = tie_rows(
                list_ref[which].astype(F32),
                got[ROW_STIFF : ROW_STIFF + size_y, :],
                [rows_of(next_pad, a, halo, size_y) for a in range(3)],
            )
            mechanic_end(near, next_pad, keep, out, size_y)
            mechanic_end(edge, next_pad, keep, out, size_y, [beta * w for w in ties])
            copy_out(which, first, 3).start()
        for item in work:
            copy_out(item[3], item[-1], 3).wait()


def call(kernel, name, out_shape, operands, spaces, scratch=(), out_spaces=None, aliases=(), weight=1):
    if out_spaces is None:
        out_spaces = [pltpu.VMEM] * len(out_shape)
    return pl.pallas_call(
        kernel,
        name=name,
        out_shape=tuple(out_shape),
        in_specs=[pl.BlockSpec(memory_space=space) for space in spaces],
        out_specs=tuple(pl.BlockSpec(memory_space=space) for space in out_spaces),
        scratch_shapes=scratch,
        input_output_aliases=dict(aliases),
        cost_estimate=pl.CostEstimate(
            flops=weight * COST[0], bytes_accessed=weight * COST[1], transcendentals=0
        ),
        compiler_params=pltpu.CompilerParams(vmem_limit_bytes=VMEM_LIMIT),
    )(*operands)


def local(sections, fiber_angles, fiber_class, row_map, interface_rows):
    own = sections[0]
    channels, size_x, size_y, depth = own.shape
    n_gx = lax.axis_size("gx")
    n_gy = lax.axis_size("gy")
    assert lax.axis_size("sec") == 2 and n_gy == 2
    upward = [(i, (i + 1) % n_gx) for i in range(n_gx)]
    downward = [(j, i) for i, j in upward]
    both = [(0, 1), (1, 0)]
    S, V, H = pltpu.SMEM, pltpu.VMEM, pltpu.HBM
    f32 = lambda *shape: jax.ShapeDtypeStruct(shape, F32)
    hbm = lambda w: pltpu.with_memory_space_constraint(w, H)
    columns = size_x * size_y
    padded = f32(3, size_x + 2, size_y + 2 * PAD, depth)
    classes = fiber_class.transpose(0, 2, 1)
    lists = interface_rows.reshape(2, 1, size_y)
    places = row_map.reshape(-1)

    field = lambda n: pltpu.VMEM((n, size_x, size_y, depth), F32)
    plain, edge_ten = call(
        tension_kernel,
        "tension",
        (f32(columns, depth), f32(2, size_y, depth)),
        (hbm(own), hbm(places)),
        (H, H),
        [
            field(3),
            field(1),
            field(2),
            pltpu.SMEM((columns,), jnp.int32),
            pltpu.SemaphoreType.DMA((1 + 3 * 4,)),
        ],
    )
    edge_ten = lax.ppermute(edge_ten, "sec", both)
    pad, share = call(share_kernel, "share", (padded, f32(3, size_x, 8, depth)), (own,), (V,))
    side = lax.ppermute(share, "gy", both)
    result = f32(1, 4, size_x, size_y, depth)
    tension, fib, result = call(
        gather_kernel,
        "gather",
        (f32(columns, depth), f32(3, columns, depth), result),
        (hbm(places), plain, classes, fiber_angles.T),
        (H, V, V, V),
        [
            pltpu.SMEM((columns,), jnp.int32),
            pltpu.VMEM((classes.shape[1], columns), jnp.int32),
            pltpu.SemaphoreType.DMA((1 + size_x,)),
        ],
        out_spaces=(V, V, H),
        weight=6,
    )
    tension = lax.ppermute(tension, "sec", both)
    message = f32(MESSAGE_ROWS, depth)
    high, low, pad = call(
        message_electric,
        "message_electric",
        (message, message, padded),
        (pad, own, side, fib, lists),
        (V,) * 5,
        aliases={0: 2},
    )
    high, low = call(
        message_mechanic,
        "message_mechanic",
        (message, message),
        (own, fib, edge_ten, high, low),
        (V,) * 5,
        aliases={3: 0, 4: 1},
    )
    got_low = lax.ppermute(high, "gx", upward)
    got_high = lax.ppermute(low, "gx", downward)
    moved, share, keep = call(
        inner_electric,
        "inner_electric",
        (padded, f32(3, size_x + 2, 8, depth), f32(4, size_x, size_y, depth)),
        (pad, own, fib),
        (V,) * 3,
        weight=6,
    )
    moved, share, keep = call(
        inner_mechanic,
        "inner_mechanic",
        (padded, f32(3, size_x + 2, 8, depth), f32(4, size_x, size_y, depth)),
        (pad, own, fib, tension, moved, share, keep),
        (V,) * 7,
        aliases={4: 0, 5: 1, 6: 2},
        weight=6,
    )
    side = lax.ppermute(share, "gy", both)
    moved, share = call(
        outer_kernel,
        "outer",
        (padded, f32(3, 4, 8, depth)),
        (pad, own, fib, lists, got_low, got_high, moved),
        (V,) * 7,
        [pltpu.VMEM((3, 2) + padded.shape[2:], F32)],
        aliases={6: 0},
    )
    end_side = lax.ppermute(share, "gy", both)
    fields = pltpu.VMEM((3, size_x, size_y, depth), F32)
    result, moved, held = call(
        middle_kernel,
        "middle",
        (f32(1, 4, size_x, size_y, depth), padded, f32(4, size_y, depth)),
        (fib, moved, side, keep, result),
        (V,) * 4 + (H,),
        [fields, pltpu.SemaphoreType.DMA((4,))],
        out_spaces=(H, V, V),
        aliases={1: 1, 4: 0},
        weight=6,
    )
    return call(
        last_kernel,
        "last",
        (f32(1, 4, size_x, size_y, depth), padded),
        (own, fib, lists, got_low, got_high, moved, end_side, keep, held, result),
        (V,) * 9 + (H,),
        [fields, pltpu.SemaphoreType.DMA((2,))],
        out_spaces=(H, V),
        aliases={5: 1, 9: 0},
    )[0]


def solution(mesh):
    in_specs = (
        P("sec", None, "gx", "gy", None),
        P(),
        P("gx", "gy", None),
        P("gx", "gy", None),
        P(None, "gx", "gy", None),
    )
    out_specs = P("sec", None, "gx", "gy", None)
    return jax.shard_map(local, mesh=mesh, in_specs=in_specs, out_specs=out_specs, check_vma=False)
```

time: 19.8 us -> 18.9 us (0.955)
  the two profiles are of different devices: /device:TPU:0 before, /device:TPU:1 now
where the time goes in v5:
time: 18.9 us; the launch traced here: 18.7 us
  starting transfers between devices  10.4 us (55%)
  Pallas kernels  7.35 us (39%)
  waiting for transfers between devices  0.81 us (4%)
    pallas_call x10, Pallas kernels, call(): pl.pallas_call(kernel, name=name, out_shape=tuple(out_shape), in_specs=[p...  7.35 us
    ppermute x1, starting transfers between devices, local(): got_high = lax.ppermute(low, 'gx', downward)  3.1 us
    ppermute x1, starting transfers between devices, local(): end_side = lax.ppermute(share, 'gy', both)  2.59 us
    ppermute x1, starting transfers between devices, local(): got_low = lax.ppermute(high, 'gx', upward)  2.19 us
    ppermute x2, starting transfers between devices, local(): side = lax.ppermute(share, 'gy', both)  1.85 us
    ppermute x1, waiting for transfers between devices, local(): tension = lax.ppermute(tension, 'sec', both)  0.8 us
  transfers between devices with their start and end apart: 7, of which 1 were waited for; matrix products, arithmetic and copies ran while one was open for 0% of the time, Pallas kernels for 25%

profile of v5, /device:TPU:1, one launch (start us, length us, event | category | flops | bytes accessed | tf_op | source)
XLA Modules:
  0.0 18.7 jit_solution(12142938352699929387)
XLA Ops:
  0.0 1.9 %tension.1 = (f32[512,128]{1,0:T(8,128)S(1)}, f32[2,32,128]{2,1,0:T(8,128)S(1)}) custom-call(f32[8,16,32,128]{3,2,1,0:T(8,128)} %bitcast.7, s32[512]{0:T(512)} %bitcast.20), custom_call_target="tpu_custom_call" | custom-call | flops 10000000000 | bytes 10000000 | tf_op jit(solution)/shard_map/tension/pallas_call | solution.py:589
  1.9 0.0 copy-start.1
  1.9 0.0 copy-start.2
  1.9 0.4 %collective-permute-start = (f32[2,32,128]{2,1,0:T(8,128)S(1)}, f32[2,32,128]{2,1,0:T(8,128)S(1)}, u32[]{:S(2)}, u32[]{:S(2)}) collective-permute-start(f32[2,32,128]{2,1,0:T(8,128)S(1)} %get-tuple-element.31), channel_id=1, source_target_pairs={{0,16},{16,0},{1,17},{17,1},{2,18},{18,2},{3,19},{19,3},{4,20},{20... | collective-permute-start | bytes 98312 | tf_op jit(solution)/shard_map/ppermute | solution.py:637
  2.3 0.1 share.1
  2.3 1.0 %collective-permute-start.1 = (f32[3,16,8,128]{3,2,1,0:T(8,128)S(1)}, f32[3,16,8,128]{3,2,1,0:T(8,128)S(1)}, u32[]{:S(2)}, u32[]{:S(2)}) collective-permute-start(f32[3,16,8,128]{3,2,1,0:T(8,128)S(1)} %get-tuple-element.33), channel_id=1, source_target_pairs={{0,1},{1,0},{2,3},{3,2},{4,5},{5,4},{6,7},{7,6},{8,9},{9,8},{10,11... | collective-permute-start | bytes 589832 | tf_op jit(solution)/shard_map/ppermute | solution.py:639
  3.4 1.5 %gather.1 = (f32[512,128]{1,0:T(8,128)S(1)}, f32[3,512,128]{2,1,0:T(8,128)S(1)}, f32[1,4,16,32,128]{4,3,2,1,0:T(8,128)}) custom-call(s32[512]{0:T(512)} %bitcast.21, f32[512,128]{1,0:T(8,128)S(1)} %get-tuple-element.29.plain, s32[16,8,32]{2,1,0:T(8,128)S(1)} %bitcast.15, f32[2,8]{1,0:T(2,128)S(1)} %bitcast.16), custom_call_target="tpu_custom_call" | custom-call | flops 60000002048 | bytes 60000000 | tf_op jit(solution)/shard_map/gather/pallas_call | solution.py:589
  4.9 0.3 %collective-permute-start.4 = (f32[512,128]{1,0:T(8,128)S(1)}, f32[512,128]{1,0:T(8,128)S(1)}, u32[]{:S(2)}, u32[]{:S(2)}) collective-permute-start(f32[512,128]{1,0:T(8,128)S(1)} %get-tuple-element.39), channel_id=1, source_target_pairs={{0,16},{16,0},{1,17},{17,1},{2,18},{18,2},{3,19},{19,3},{4,20},{20... | collective-permute-start | bytes 786440 | tf_op jit(solution)/shard_map/ppermute | solution.py:655
  5.3 0.0 collective-permute-done.1.side_ref
  5.3 0.2 %message_electric.1 = (f32[232,128]{1,0:T(8,128)S(1)}, f32[232,128]{1,0:T(8,128)S(1)}, f32[3,18,48,128]{3,2,1,0:T(8,128)S(1)}) custom-call(f32[3,18,48,128]{3,2,1,0:T(8,128)S(1)} %get-tuple-element.32.pad_in, f32[8,16,32,128]{3,2,1,0:T(8,128)S(1)} %bitcast.9, f32[3,16,8,128]{3,2,1,0:T(8,128)S(1)} %collective-permute-done.1.side_ref, ...), custom_call_target="tpu_custom_call", output_to_operand_aliasing={{2}: (0, {})} | custom-call | flops 10000000000 | bytes 10000000 | tf_op jit(solution)/shard_map/message_electric/pallas_call | solution.py:589
  5.5 0.0 collective-permute-done.ten_ref
  5.6 2.2 %collective-permute-start.2 = (f32[232,128]{1,0:T(8,128)S(1)}, f32[232,128]{1,0:T(8,128)S(1)}, u32[]{:S(2)}, u32[]{:S(2)}) collective-permute-start(f32[232,128]{1,0:T(8,128)S(1)} %get-tuple-element.36), channel_id=1, source_target_pairs={{0,2},{2,4},{4,6},{6,8},{8,10},{10,12},{12,14},{14,0},{1,3},{3,5},... | collective-permute-start | bytes 356360 | tf_op jit(solution)/shard_map/ppermute | solution.py:673
  7.7 3.1 %collective-permute-start.3 = (f32[232,128]{1,0:T(8,128)S(1)}, f32[232,128]{1,0:T(8,128)S(1)}, u32[]{:S(2)}, u32[]{:S(2)}) collective-permute-start(f32[232,128]{1,0:T(8,128)S(1)} %get-tuple-element.37), channel_id=1, source_target_pairs={{2,0},{4,2},{6,4},{8,6},{10,8},{12,10},{14,12},{0,14},{3,1},{5,3},... | collective-permute-start | bytes 356360 | tf_op jit(solution)/shard_map/ppermute | solution.py:674
  10.8 1.2 %inner_electric.1 = (f32[3,18,48,128]{3,2,1,0:T(8,128)S(1)}, f32[3,18,8,128]{3,2,1,0:T(8,128)S(1)}, f32[4,16,32,128]{3,2,1,0:T(8,128)S(1)}) custom-call(f32[3,18,48,128]{3,2,1,0:T(8,128)S(1)} %get-tuple-element.38.pad, f32[8,16,32,128]{3,2,1,0:T(8,128)S(1)} %bitcast.11, f32[3,512,128]{2,1,0:T(8,128)S(1)} %get-tuple-element.30.fib_ref), custom_call_target="tpu_custom_call" | custom-call | flops 60000002048 | bytes 60000000 | tf_op jit(solution)/shard_map/inner_electric/pallas_call | solution.py:589
  12.1 0.8 %collective-permute-done.4.ten_ref = f32[512,128]{1,0:T(8,128)S(1)} collective-permute-done((f32[512,128]{1,0:T(8,128)S(1)}, f32[512,128]{1,0:T(8,128)S(1)}, u32[]{:S(2)}, u32[]{:S(2)}) %collective-permute-start.4) | collective-permute-done | bytes 262176 | tf_op jit(solution)/shard_map/ppermute | solution.py:655
  12.9 0.8 %collective-permute-start.5 = (f32[3,18,8,128]{3,2,1,0:T(8,128)S(1)}, f32[3,18,8,128]{3,2,1,0:T(8,128)S(1)}, u32[]{:S(2)}, u32[]{:S(2)}) collective-permute-start(f32[3,18,8,128]{3,2,1,0:T(8,128)S(1)} %get-tuple-element.45), channel_id=1, source_target_pairs={{0,1},{1,0},{2,3},{3,2},{4,5},{5,4},{6,7},{7,6},{8,9},{9,8},{10,11... | collective-permute-start | bytes 663560 | tf_op jit(solution)/shard_map/ppermute | solution.py:692
  13.7 0.0 collective-permute-done.2.got_low
  13.7 0.0 collective-permute-done.3.got_high
  13.7 0.1 outer.1
  13.8 2.6 %collective-permute-start.6 = (f32[3,4,8,128]{3,2,1,0:T(8,128)S(1)}, f32[3,4,8,128]{3,2,1,0:T(8,128)S(1)}, u32[]{:S(2)}, u32[]{:S(2)}) collective-permute-start(f32[3,4,8,128]{3,2,1,0:T(8,128)S(1)} %get-tuple-element.49), channel_id=1, source_target_pairs={{0,1},{1,0},{2,3},{3,2},{4,5},{5,4},{6,7},{7,6},{8,9},{9,8},{10,11... | collective-permute-start | bytes 147464 | tf_op jit(solution)/shard_map/ppermute | solution.py:702
  16.4 0.0 collective-permute-done.5.side_ref
  16.4 1.4 %middle.1 = (f32[1,4,16,32,128]{4,3,2,1,0:T(8,128)}, f32[3,18,48,128]{3,2,1,0:T(8,128)S(1)}, f32[4,32,128]{2,1,0:T(8,128)S(1)}) custom-call(f32[3,512,128]{2,1,0:T(8,128)S(1)} %get-tuple-element.30.fib_ref, f32[3,18,48,128]{3,2,1,0:T(8,128)S(1)} %get-tuple-element.44.next_in, ...), custom_call_target="tpu_custom_call", output_to_operand_aliasing={{1}: (1, {}), {0}: (4, {})} | custom-call | flops 60000002048 | bytes 60000000 | tf_op jit(solution)/shard_map/middle/pallas_call | solution.py:589
  17.9 0.0 collective-permute-done.6.side_ref
  17.9 0.8 %last.1 = (f32[1,4,16,32,128]{4,3,2,1,0:T(8,128)}, f32[3,18,48,128]{3,2,1,0:T(8,128)S(1)}) custom-call(f32[8,16,32,128]{3,2,1,0:T(8,128)S(1)} %bitcast.14, f32[3,512,128]{2,1,0:T(8,128)S(1)} %get-tuple-element.30.fib_ref, s32[2,1,32]{2,1,0:T(1,128)S(1)} %bitcast.19, ...), custom_call_target="tpu_custom_call", output_to_operand_aliasing={{1}: (5, {}), {0}: (9, {})} | custom-call | flops 10000000000 | bytes 10000000 | tf_op jit(solution)/shard_map/last/pallas_call | solution.py:589
  (8 shorter events, 0.0 us)
Async XLA Ops:
  0.0 2.3 %copy-start = (f32[1,8,16,32,128]{4,3,2,1,0:T(8,128)S(1)}, f32[1,8,16,32,128]{4,3,2,1,0:T(8,128)}, u32[]{:S(2)}) copy-start(f32[1,8,16,32,128]{4,3,2,1,0:T(8,128)} %param.5) | copy-start | bytes 6291460
  1.9 1.5 %copy-start.1 = (s32[16,32,8]{1,2,0:T(8,128)S(1)}, s32[16,32,8]{1,2,0:T(8,128)}, u32[]{:S(2)}) copy-start(s32[16,32,8]{1,2,0:T(8,128)} %param.7) | copy-start | bytes 49156
  1.9 1.5 %copy-start.2 = (f32[8,2]{0,1:T(2,128)S(1)}, f32[8,2]{0,1:T(2,128)}, u32[]{:S(2)}) copy-start(f32[8,2]{0,1:T(2,128)} %param.6) | copy-start | bytes 196
  1.9 3.6 %collective-permute-start = (f32[2,32,128]{2,1,0:T(8,128)S(1)}, f32[2,32,128]{2,1,0:T(8,128)S(1)}, u32[]{:S(2)}, u32[]{:S(2)}) collective-permute-start(f32[2,32,128]{2,1,0:T(8,128)S(1)} %get-tuple-element.31), channel_id=1, source_target_pairs={{0,16},{16,0},{1,17},{17,1},{2,18},{18,2},{3,19},{19,3},{4,20},{20... | collective-permute-start | bytes 98312 | tf_op jit(solution)/shard_map/ppermute | solution.py:637
  2.3 2.9 %collective-permute-start.1 = (f32[3,16,8,128]{3,2,1,0:T(8,128)S(1)}, f32[3,16,8,128]{3,2,1,0:T(8,128)S(1)}, u32[]{:S(2)}, u32[]{:S(2)}) collective-permute-start(f32[3,16,8,128]{3,2,1,0:T(8,128)S(1)} %get-tuple-element.33), channel_id=1, source_target_pairs={{0,1},{1,0},{2,3},{3,2},{4,5},{5,4},{6,7},{7,6},{8,9},{9,8},{10,11... | collective-permute-start | bytes 589832 | tf_op jit(solution)/shard_map/ppermute | solution.py:639
  3.4 1.9 %copy-start.3 = (s32[2,1,1,32]{3,2,1,0:T(1,128)S(1)}, s32[2,1,1,32]{3,2,1,0:T(1,128)}, u32[]{:S(2)}) copy-start(s32[2,1,1,32]{3,2,1,0:T(1,128)} %param.9) | copy-start | bytes 772
  4.9 8.0 %collective-permute-start.4 = (f32[512,128]{1,0:T(8,128)S(1)}, f32[512,128]{1,0:T(8,128)S(1)}, u32[]{:S(2)}, u32[]{:S(2)}) collective-permute-start(f32[512,128]{1,0:T(8,128)S(1)} %get-tuple-element.39), channel_id=1, source_target_pairs={{0,16},{16,0},{1,17},{17,1},{2,18},{18,2},{3,19},{19,3},{4,20},{20... | collective-permute-start | bytes 786440 | tf_op jit(solution)/shard_map/ppermute | solution.py:655
  5.6 8.2 %collective-permute-start.2 = (f32[232,128]{1,0:T(8,128)S(1)}, f32[232,128]{1,0:T(8,128)S(1)}, u32[]{:S(2)}, u32[]{:S(2)}) collective-permute-start(f32[232,128]{1,0:T(8,128)S(1)} %get-tuple-element.36), channel_id=1, source_target_pairs={{0,2},{2,4},{4,6},{6,8},{8,10},{10,12},{12,14},{14,0},{1,3},{3,5},... | collective-permute-start | bytes 356360 | tf_op jit(solution)/shard_map/ppermute | solution.py:673
  7.7 6.0 %collective-permute-start.3 = (f32[232,128]{1,0:T(8,128)S(1)}, f32[232,128]{1,0:T(8,128)S(1)}, u32[]{:S(2)}, u32[]{:S(2)}) collective-permute-start(f32[232,128]{1,0:T(8,128)S(1)} %get-tuple-element.37), channel_id=1, source_target_pairs={{2,0},{4,2},{6,4},{8,6},{10,8},{12,10},{14,12},{0,14},{3,1},{5,3},... | collective-permute-start | bytes 356360 | tf_op jit(solution)/shard_map/ppermute | solution.py:674
  12.9 3.6 %collective-permute-start.5 = (f32[3,18,8,128]{3,2,1,0:T(8,128)S(1)}, f32[3,18,8,128]{3,2,1,0:T(8,128)S(1)}, u32[]{:S(2)}, u32[]{:S(2)}) collective-permute-start(f32[3,18,8,128]{3,2,1,0:T(8,128)S(1)} %get-tuple-element.45), channel_id=1, source_target_pairs={{0,1},{1,0},{2,3},{3,2},{4,5},{5,4},{6,7},{7,6},{8,9},{9,8},{10,11... | collective-permute-start | bytes 663560 | tf_op jit(solution)/shard_map/ppermute | solution.py:692
  13.8 4.0 %collective-permute-start.6 = (f32[3,4,8,128]{3,2,1,0:T(8,128)S(1)}, f32[3,4,8,128]{3,2,1,0:T(8,128)S(1)}, u32[]{:S(2)}, u32[]{:S(2)}) collective-permute-start(f32[3,4,8,128]{3,2,1,0:T(8,128)S(1)} %get-tuple-element.49), channel_id=1, source_target_pairs={{0,1},{1,0},{2,3},{3,2},{4,5},{5,4},{6,7},{7,6},{8,9},{9,8},{10,11... | collective-permute-start | bytes 147464 | tf_op jit(solution)/shard_map/ppermute | solution.py:702

commit v6 on v5

--- a/solution.py
+++ b/solution.py
@@ -10,13 +10,27 @@
 F32 = jnp.float32
 HIGHEST = lax.Precision.HIGHEST
 VMEM_LIMIT = 16 * 1024 * 1024
-COST = (10**10, 10**7)
+COST = {
+    "tension": 0.001,
+    "share": 0.001,
+    "gather": 6,
+    "message_electric": 1,
+    "message_mechanic": 1,
+    "inner_electric": 6,
+    "inner_mechanic": 6,
+    "outer_electric": 1,
+    "outer_mechanic": 1,
+    "middle": 6,
+    "last": 1,
+}
 
 PAD = 8
 
 ROW_NOW, ROW_NEXT, ROW_STIFF, ROW_SIDE = 0, 96, 192, 224
 ROW_LIST = ROW_SIDE + 6
 MESSAGE_ROWS = 232
+ROW_VOLT, ROW_VOLT_NEXT, ROW_COUPLED, ROW_VOLT_SIDE = 0, 32, 64, 160
+VOLT_ROWS = 168
 
 
 def inverse(v):
@@ -228,7 +242,7 @@
             edge_ten[1, p : p + 1, :] = plain[pl.ds(map_ref[last + p], 1), :]
 
 
-def share_kernel(own, pad, share):
+def share_kernel(own, after, pad, share):
     size_x, size_y = own.shape[1], own.shape[2]
     zeros = jnp.zeros(pad.shape[2:], F32)
     for a in range(3):
@@ -277,7 +291,7 @@
             copy.wait()
 
 
-def message_electric(pad_in, own, side_ref, fib_ref, list_ref, high_ref, low_ref, pad):
+def message_electric(pad_in, own, side_ref, fib_ref, high_ref, low_ref, pad):
     size_x, size_y = own.shape[1], own.shape[2]
 
     def fill(x, carry):
@@ -286,50 +300,44 @@
         return carry
 
     lax.fori_loop(0, size_x, fill, 0, unroll=4)
-    for which, ((_, edge, _), out) in enumerate(zip(sides(size_x), (low_ref, high_ref))):
-        for a in range(3):
-            row = ROW_SIDE + 2 * a
-            out[row : row + 1, :] = side_ref[a, edge, 7:8, :]
-            out[row + 1 : row + 2, :] = side_ref[a, edge, 0:1, :]
-        out[ROW_LIST : ROW_LIST + 1, 0:size_y] = list_ref[which].astype(F32)
-
-        @pl.when(electric())
-        def _():
+
+    @pl.when(electric())
+    def _():
+        for which, ((_, edge, _), out) in enumerate(zip(sides(size_x), (low_ref, high_ref))):
+            out[ROW_VOLT_SIDE : ROW_VOLT_SIDE + 1, :] = side_ref[0, edge, 7:8, :]
+            out[ROW_VOLT_SIDE + 1 : ROW_VOLT_SIDE + 2, :] = side_ref[0, edge, 0:1, :]
             fib = [fib_ref[a, place_of(edge, size_y), :] for a in range(3)]
             v, c, d = [rows_of(pad, a, edge + 1, size_y) for a in range(3)]
             f, n, r = [own[k, edge] for k in range(3, 6)]
             rate = volt_rate(pad, edge + 1, fib, size_y)
             _, _, total = currents(v, c, d, f, n, r)
-            for at, value in zip(
-                (ROW_NOW, ROW_NOW + size_y, ROW_NOW + 2 * size_y, ROW_NEXT, ROW_NEXT + size_y),
-                (v,) + couplings(fib)[:2] + (v + DT * (rate - total), couplings(fib)[2]),
-            ):
-                out[at : at + size_y, :] = value
-
-        @pl.when(jnp.logical_not(electric()))
-        def _():
+            out[ROW_VOLT : ROW_VOLT + size_y, :] = v
+            out[ROW_VOLT_NEXT : ROW_VOLT_NEXT + size_y, :] = v + DT * (rate - total)
+            for k, value in enumerate(couplings(fib)):
+                out[ROW_COUPLED + k * size_y : ROW_COUPLED + (k + 1) * size_y, :] = value
+
+def message_mechanic(pad_in, own, side_ref, fib_ref, ten_ref, list_ref, high_ref, low_ref, pad):
+    size_x, size_y = own.shape[1], own.shape[2]
+
+    @pl.when(jnp.logical_not(electric()))
+    def _():
+        for which, ((_, edge, _), out) in enumerate(zip(sides(size_x), (low_ref, high_ref))):
+            out[ROW_LIST : ROW_LIST + 1, 0:size_y] = list_ref[which].astype(F32)
             rate = motion_rate(pad, edge + 1, size_y)
             stiff = own[6, edge]
             beta = OMEGA * inverse(stiff)
+            act = own[7, edge] * ten_ref[which]
             out[ROW_STIFF : ROW_STIFF + size_y, :] = stiff
             for a in range(3):
+                row = ROW_SIDE + 2 * a
+                out[row : row + 1, :] = side_ref[a, edge, 7:8, :]
+                out[row + 1 : row + 2, :] = side_ref[a, edge, 0:1, :]
                 u = rows_of(pad, a, edge + 1, size_y)
                 out[ROW_NOW + a * size_y : ROW_NOW + (a + 1) * size_y, :] = u
+                drive = own[3 + a, edge] + act * fib_ref[a, place_of(edge, size_y), :]
                 out[ROW_NEXT + a * size_y : ROW_NEXT + (a + 1) * size_y, :] = (
-                    0.28 * u + beta * own[3 + a, edge] + OMEGA * rate[a]
+                    0.28 * u + beta * drive + OMEGA * rate[a]
                 )
-
-
-def message_mechanic(own, fib_ref, ten_ref, high_in, low_in, high_ref, low_ref):
-    size_x, size_y = own.shape[1], own.shape[2]
-
-    @pl.when(jnp.logical_not(electric()))
-    def _():
-        for which, ((_, edge, _), out) in enumerate(zip(sides(size_x), (low_ref, high_ref))):
-            act = OMEGA * inverse(own[6, edge]) * own[7, edge] * ten_ref[which]
-            for a in range(3):
-                rows = slice(ROW_NEXT + a * size_y, ROW_NEXT + (a + 1) * size_y)
-                out[rows, :] = out[rows, :] + act * fib_ref[a, place_of(edge, size_y), :]
 
 
 def put_inner(next_pad, share, a, x, value):
@@ -388,23 +396,22 @@
         lax.fori_loop(0, size_x, plane, 0, unroll=2)
 
 
-def outer_kernel(pad, own, fib_ref, list_ref, got_low, got_high, next_in, next_pad, share, wide):
+def outer_electric(pad, own, fib_ref, volt_low, volt_high, next_in, next_pad, share, wide):
     size_x, size_y = own.shape[1], own.shape[2]
-    work = list(zip(sides(size_x), (got_low, got_high)))
-    for slot, (_, got) in enumerate(work):
-        for a in range(3):
-            wide[a, slot, PAD : PAD + size_y, :] = got[ROW_NOW + a * size_y : ROW_NOW + (a + 1) * size_y, :]
-            row = ROW_SIDE + 2 * a
-            wide[a, slot, PAD - 1 : PAD, :] = got[row : row + 1, :]
-            wide[a, slot, PAD + size_y : PAD + size_y + 1, :] = got[row + 1 : row + 2, :]
-
     def put(a, x, slot, value):
         next_pad[a, x, PAD : PAD + size_y, :] = value
         share[a, slot] = edges_tile(value)
 
+    def put_side(a, which, low, high):
+        wide[a, which, PAD - 1 : PAD, :] = low
+        wide[a, which, PAD + size_y : PAD + size_y + 1, :] = high
+
     @pl.when(electric())
     def _():
-        for which, ((halo, edge, sign), got) in enumerate(work):
+        for which, ((halo, edge, sign), got) in enumerate(zip(sides(size_x), (volt_low, volt_high))):
+            wide[0, which, PAD : PAD + size_y, :] = got[ROW_VOLT : ROW_VOLT + size_y, :]
+            row = ROW_VOLT_SIDE
+            put_side(0, which, got[row : row + 1, :], got[row + 1 : row + 2, :])
             fib = [fib_ref[a, place_of(edge, size_y), :] for a in range(3)]
             put(
                 0,
@@ -412,19 +419,32 @@
                 1 + which,
                 rows_of(next_pad, 0, edge + 1, size_y) + DT * volt_from(wide, which, couplings(fib), sign, size_y),
             )
-            theirs = [
-                got[at : at + size_y, :] for at in (ROW_NOW + size_y, ROW_NOW + 2 * size_y, ROW_NEXT + size_y)
-            ]
+            theirs = [got[ROW_COUPLED + k * size_y : ROW_COUPLED + (k + 1) * size_y, :] for k in range(3)]
             put(
                 0,
                 halo,
                 3 * which,
-                got[ROW_NEXT : ROW_NEXT + size_y, :] + DT * volt_from(pad, edge + 1, theirs, -sign, size_y),
+                got[ROW_VOLT_NEXT : ROW_VOLT_NEXT + size_y, :] + DT * volt_from(pad, edge + 1, theirs, -sign, size_y),
             )
 
+
+def outer_mechanic(pad, own, list_ref, got_low, got_high, next_in, share_in, next_pad, share, wide):
+    size_x, size_y = own.shape[1], own.shape[2]
+    def put(a, x, slot, value):
+        next_pad[a, x, PAD : PAD + size_y, :] = value
+        share[a, slot] = edges_tile(value)
+
+    def put_side(a, which, low, high):
+        wide[a, which, PAD - 1 : PAD, :] = low
+        wide[a, which, PAD + size_y : PAD + size_y + 1, :] = high
+
     @pl.when(jnp.logical_not(electric()))
     def _():
-        for which, ((halo, edge, sign), got) in enumerate(work):
+        for which, ((halo, edge, sign), got) in enumerate(zip(sides(size_x), (got_low, got_high))):
+            for a in range(3):
+                wide[a, which, PAD : PAD + size_y, :] = got[ROW_NOW + a * size_y : ROW_NOW + (a + 1) * size_y, :]
+                row = ROW_SIDE + 2 * a
+                put_side(a, which, got[row : row + 1, :], got[row + 1 : row + 2, :])
             stiff = got[ROW_STIFF : ROW_STIFF + size_y, :]
             stiff_own = own[6, edge]
             now = [rows_of(pad, a, edge + 1, size_y) for a in range(3)]
@@ -583,7 +603,7 @@
             copy_out(item[3], item[-1], 3).wait()
 
 
-def call(kernel, name, out_shape, operands, spaces, scratch=(), out_spaces=None, aliases=(), weight=1):
+def call(kernel, name, out_shape, operands, spaces, scratch=(), out_spaces=None, aliases=()):
     if out_spaces is None:
         out_spaces = [pltpu.VMEM] * len(out_shape)
     return pl.pallas_call(
@@ -595,7 +615,7 @@
         scratch_shapes=scratch,
         input_output_aliases=dict(aliases),
         cost_estimate=pl.CostEstimate(
-            flops=weight * COST[0], bytes_accessed=weight * COST[1], transcendentals=0
+            flops=int(COST[name] * 10**10), bytes_accessed=int(COST[name] * 10**7), transcendentals=0
         ),
         compiler_params=pltpu.CompilerParams(vmem_limit_bytes=VMEM_LIMIT),
     )(*operands)
@@ -607,8 +627,15 @@
     n_gx = lax.axis_size("gx")
     n_gy = lax.axis_size("gy")
     assert lax.axis_size("sec") == 2 and n_gy == 2
-    upward = [(i, (i + 1) % n_gx) for i in range(n_gx)]
-    downward = [(j, i) for i, j in upward]
+    axes = ("sec", "gx", "gy")
+    place = lambda sec, i, j: (sec * n_gx + i % n_gx) * n_gy + j
+    blocks = [(i, j) for i in range(n_gx) for j in range(n_gy)]
+
+    def ring(section, step):
+        return [(place(section, i, j), place(section, i + step, j)) for i, j in blocks] + [
+            (place(1 - section, i, j), place(1 - section, i, 1 - j)) for i, j in blocks
+        ]
+
     both = [(0, 1), (1, 0)]
     S, V, H = pltpu.SMEM, pltpu.VMEM, pltpu.HBM
     f32 = lambda *shape: jax.ShapeDtypeStruct(shape, F32)
@@ -635,7 +662,7 @@
         ],
     )
     edge_ten = lax.ppermute(edge_ten, "sec", both)
-    pad, share = call(share_kernel, "share", (padded, f32(3, size_x, 8, depth)), (own,), (V,))
+    pad, share = call(share_kernel, "share", (padded, f32(3, size_x, 8, depth)), (own, plain), (V, V))
     side = lax.ppermute(share, "gy", both)
     result = f32(1, 4, size_x, size_y, depth)
     tension, fib, result = call(
@@ -650,35 +677,36 @@
             pltpu.SemaphoreType.DMA((1 + size_x,)),
         ],
         out_spaces=(V, V, H),
-        weight=6,
     )
     tension = lax.ppermute(tension, "sec", both)
-    message = f32(MESSAGE_ROWS, depth)
+    message = f32(VOLT_ROWS, depth)
     high, low, pad = call(
         message_electric,
         "message_electric",
         (message, message, padded),
-        (pad, own, side, fib, lists),
-        (V,) * 5,
+        (pad, own, side, fib),
+        (V,) * 4,
         aliases={0: 2},
     )
-    high, low = call(
+    volt_low = lax.ppermute(high, axes, ring(0, 1))
+    volt_high = lax.ppermute(low, axes, ring(0, -1))
+    message = f32(MESSAGE_ROWS, depth)
+    high, low, pad = call(
         message_mechanic,
         "message_mechanic",
-        (message, message),
-        (own, fib, edge_ten, high, low),
-        (V,) * 5,
-        aliases={3: 0, 4: 1},
-    )
-    got_low = lax.ppermute(high, "gx", upward)
-    got_high = lax.ppermute(low, "gx", downward)
+        (message, message, padded),
+        (pad, own, side, fib, edge_ten, lists),
+        (V,) * 6,
+        aliases={0: 2},
+    )
+    got_low = lax.ppermute(high, axes, ring(1, 1))
+    got_high = lax.ppermute(low, axes, ring(1, -1))
     moved, share, keep = call(
         inner_electric,
         "inner_electric",
         (padded, f32(3, size_x + 2, 8, depth), f32(4, size_x, size_y, depth)),
         (pad, own, fib),
         (V,) * 3,
-        weight=6,
     )
     moved, share, keep = call(
         inner_mechanic,
@@ -687,17 +715,26 @@
         (pad, own, fib, tension, moved, share, keep),
         (V,) * 7,
         aliases={4: 0, 5: 1, 6: 2},
-        weight=6,
     )
     side = lax.ppermute(share, "gy", both)
+    wide = pltpu.VMEM((3, 2) + padded.shape[2:], F32)
     moved, share = call(
-        outer_kernel,
-        "outer",
+        outer_electric,
+        "outer_electric",
         (padded, f32(3, 4, 8, depth)),
-        (pad, own, fib, lists, got_low, got_high, moved),
+        (pad, own, fib, volt_low, volt_high, moved),
+        (V,) * 6,
+        [wide],
+        aliases={5: 0},
+    )
+    moved, share = call(
+        outer_mechanic,
+        "outer_mechanic",
+        (padded, f32(3, 4, 8, depth)),
+        (pad, own, lists, got_low, got_high, moved, share),
         (V,) * 7,
-        [pltpu.VMEM((3, 2) + padded.shape[2:], F32)],
-        aliases={6: 0},
+        [wide],
+        aliases={5: 0, 6: 1},
     )
     end_side = lax.ppermute(share, "gy", both)
     fields = pltpu.VMEM((3, size_x, size_y, depth), F32)
@@ -710,7 +747,6 @@
         [fields, pltpu.SemaphoreType.DMA((4,))],
         out_spaces=(H, V, V),
         aliases={1: 1, 4: 0},
-        weight=6,
     )
     return call(
         last_kernel,

time: 18.9 us -> 18.4 us (0.974)
  the two profiles are of different devices: /device:TPU:1 before, /device:TPU:3 now
where the time goes in v6:
time: 18.4 us; the launch traced here: 18.2 us
  starting transfers between devices  11.8 us (64%)
  Pallas kernels  4.86 us (26%)
  waiting for transfers between devices  1.14 us (6%)
  local copies, waits for them, and re-layouts  0.3 us (2%)
    pallas_call x11, Pallas kernels, call(): pl.pallas_call(kernel, name=name, out_shape=tuple(out_shape), in_specs=[p...  4.86 us
    ppermute x1, starting transfers between devices, local(): got_high = lax.ppermute(low, axes, ring(1, -1))  3.1 us
    ppermute x1, starting transfers between devices, local(): end_side = lax.ppermute(share, 'gy', both)  2.07 us
    ppermute x1, starting transfers between devices, local(): got_low = lax.ppermute(high, axes, ring(1, 1))  1.97 us
    ppermute x2, starting transfers between devices, local(): side = lax.ppermute(share, 'gy', both)  1.61 us
    ppermute x1, starting transfers between devices, local(): tension = lax.ppermute(tension, 'sec', both)  1.26 us
    ppermute x1, starting transfers between devices, local(): edge_ten = lax.ppermute(edge_ten, 'sec', both)  1.23 us
    ppermute x1, waiting for transfers between devices, local(): tension = lax.ppermute(tension, 'sec', both)  0.82 us
  transfers between devices with their start and end apart: 9, of which 2 were waited for; matrix products, arithmetic and copies ran while one was open for 0% of the time, Pallas kernels for 21%

profile of v6, /device:TPU:3, one launch (start us, length us, event | category | flops | bytes accessed | tf_op | source)
XLA Modules:
  0.0 18.2 jit_solution(2944831652406428570)
XLA Ops:
  0.0 0.1 tension.1
  0.1 0.0 copy-start.1
  0.1 0.0 copy-start.2
  0.2 1.2 %collective-permute-start.1 = (f32[2,32,128]{2,1,0:T(8,128)S(1)}, f32[2,32,128]{2,1,0:T(8,128)S(1)}, u32[]{:S(2)}, u32[]{:S(2)}) collective-permute-start(f32[2,32,128]{2,1,0:T(8,128)S(1)} %get-tuple-element.37), channel_id=1, source_target_pairs={{0,16},{16,0},{1,17},{17,1},{2,18},{18,2},{3,19},{19,3},{4,20},{20... | collective-permute-start | bytes 98312 | tf_op jit(solution)/shard_map/ppermute | solution.py:664
  1.4 0.2 %copy-done = f32[1,8,16,32,128]{4,3,2,1,0:T(8,128)S(1)} copy-done((f32[1,8,16,32,128]{4,3,2,1,0:T(8,128)S(1)}, f32[1,8,16,32,128]{4,3,2,1,0:T(8,128)}, u32[]{:S(2)}) %copy-start) | copy-done | bytes 2097176
  1.6 0.1 share.1
  1.7 0.7 %collective-permute-start = (f32[3,16,8,128]{3,2,1,0:T(8,128)S(1)}, f32[3,16,8,128]{3,2,1,0:T(8,128)S(1)}, u32[]{:S(2)}, u32[]{:S(2)}) collective-permute-start(f32[3,16,8,128]{3,2,1,0:T(8,128)S(1)} %get-tuple-element.35), channel_id=1, source_target_pairs={{0,1},{1,0},{2,3},{3,2},{4,5},{5,4},{6,7},{7,6},{8,9},{9,8},{10,11... | collective-permute-start | bytes 589832 | tf_op jit(solution)/shard_map/ppermute | solution.py:666
  2.4 0.7 %gather.1 = (f32[512,128]{1,0:T(8,128)S(1)}, f32[3,512,128]{2,1,0:T(8,128)S(1)}, f32[1,4,16,32,128]{4,3,2,1,0:T(8,128)}) custom-call(s32[512]{0:T(512)} %bitcast.22, f32[512,128]{1,0:T(8,128)S(1)} %get-tuple-element.32.plain.after, s32[16,8,32]{2,1,0:T(8,128)S(1)} %bitcast.16, f32[2,8]{1,0:T(2,128)S(1)} %bitcast.17), custom_call_target="tpu_custom_call" | custom-call | flops 60000002048 | bytes 60000000 | tf_op jit(solution)/shard_map/gather/pallas_call | solution.py:609
  3.2 1.3 %collective-permute-start.6 = (f32[512,128]{1,0:T(8,128)S(1)}, f32[512,128]{1,0:T(8,128)S(1)}, u32[]{:S(2)}, u32[]{:S(2)}) collective-permute-start(f32[512,128]{1,0:T(8,128)S(1)} %get-tuple-element.43), channel_id=1, source_target_pairs={{0,16},{16,0},{1,17},{17,1},{2,18},{18,2},{3,19},{19,3},{4,20},{20... | collective-permute-start | bytes 786440 | tf_op jit(solution)/shard_map/ppermute | solution.py:681
  4.4 0.0 collective-permute-done.side_ref
  4.5 0.4 %collective-permute-start.4 = (f32[168,128]{1,0:T(8,128)S(1)}, f32[168,128]{1,0:T(8,128)S(1)}, u32[]{:S(2)}, u32[]{:S(2)}) collective-permute-start(f32[168,128]{1,0:T(8,128)S(1)} %get-tuple-element.41), channel_id=1, source_target_pairs={{0,2},{1,3},{2,4},{3,5},{4,6},{5,7},{6,8},{7,9},{8,10},{9,11},{10,... | collective-permute-start | bytes 258056 | tf_op jit(solution)/shard_map/ppermute | solution.py:691
  4.8 0.2 %collective-permute-start.5 = (f32[168,128]{1,0:T(8,128)S(1)}, f32[168,128]{1,0:T(8,128)S(1)}, u32[]{:S(2)}, u32[]{:S(2)}) collective-permute-start(f32[168,128]{1,0:T(8,128)S(1)} %get-tuple-element.42), channel_id=1, source_target_pairs={{0,14},{1,15},{2,0},{3,1},{4,2},{5,3},{6,4},{7,5},{8,6},{9,7},{10,... | collective-permute-start | bytes 258056 | tf_op jit(solution)/shard_map/ppermute | solution.py:692
  5.0 0.1 copy-done.3
  5.1 0.1 message_mechanic.1
  5.2 2.0 %collective-permute-start.2 = (f32[232,128]{1,0:T(8,128)S(1)}, f32[232,128]{1,0:T(8,128)S(1)}, u32[]{:S(2)}, u32[]{:S(2)}) collective-permute-start(f32[232,128]{1,0:T(8,128)S(1)} %get-tuple-element.38), channel_id=1, source_target_pairs={{16,18},{17,19},{18,20},{19,21},{20,22},{21,23},{22,24},{23,25},{2... | collective-permute-start | bytes 356360 | tf_op jit(solution)/shard_map/ppermute | solution.py:702
  7.2 3.1 %collective-permute-start.3 = (f32[232,128]{1,0:T(8,128)S(1)}, f32[232,128]{1,0:T(8,128)S(1)}, u32[]{:S(2)}, u32[]{:S(2)}) collective-permute-start(f32[232,128]{1,0:T(8,128)S(1)} %get-tuple-element.39), channel_id=1, source_target_pairs={{16,30},{17,31},{18,16},{19,17},{20,18},{21,19},{22,20},{23,21},{2... | collective-permute-start | bytes 356360 | tf_op jit(solution)/shard_map/ppermute | solution.py:703
  10.3 0.8 %collective-permute-done.6.ten_ref = f32[512,128]{1,0:T(8,128)S(1)} collective-permute-done((f32[512,128]{1,0:T(8,128)S(1)}, f32[512,128]{1,0:T(8,128)S(1)}, u32[]{:S(2)}, u32[]{:S(2)}) %collective-permute-start.6) | collective-permute-done | bytes 262176 | tf_op jit(solution)/shard_map/ppermute | solution.py:681
  11.1 1.1 %inner_mechanic.1 = (f32[3,18,48,128]{3,2,1,0:T(8,128)S(1)}, f32[3,18,8,128]{3,2,1,0:T(8,128)S(1)}, f32[4,16,32,128]{3,2,1,0:T(8,128)S(1)}) custom-call(f32[3,18,48,128]{3,2,1,0:T(8,128)S(1)} %get-tuple-element.40.pad, f32[8,16,32,128]{3,2,1,0:T(8,128)S(1)} %bitcast.12, ...), custom_call_target="tpu_custom_call", output_to_operand_aliasing={{0}: (4, {}), {1}: (5, {}), {2}: (6, {})} | custom-call | flops 60000002048 | bytes 60000000 | tf_op jit(solution)/shard_map/inner_mechanic/pallas_call | solution.py:609
  12.2 0.9 %collective-permute-start.7 = (f32[3,18,8,128]{3,2,1,0:T(8,128)S(1)}, f32[3,18,8,128]{3,2,1,0:T(8,128)S(1)}, u32[]{:S(2)}, u32[]{:S(2)}) collective-permute-start(f32[3,18,8,128]{3,2,1,0:T(8,128)S(1)} %get-tuple-element.51), channel_id=1, source_target_pairs={{0,1},{1,0},{2,3},{3,2},{4,5},{5,4},{6,7},{7,6},{8,9},{9,8},{10,11... | collective-permute-start | bytes 663560 | tf_op jit(solution)/shard_map/ppermute | solution.py:719
  13.1 0.3 %collective-permute-done.2.got_low = f32[232,128]{1,0:T(8,128)S(1)} collective-permute-done((f32[232,128]{1,0:T(8,128)S(1)}, f32[232,128]{1,0:T(8,128)S(1)}, u32[]{:S(2)}, u32[]{:S(2)}) %collective-permute-start.2) | collective-permute-done | bytes 118816 | tf_op jit(solution)/shard_map/ppermute | solution.py:702
  13.4 0.4 %outer_mechanic.1 = (f32[3,18,48,128]{3,2,1,0:T(8,128)S(1)}, f32[3,4,8,128]{3,2,1,0:T(8,128)S(1)}) custom-call(f32[3,18,48,128]{3,2,1,0:T(8,128)S(1)} %get-tuple-element.40.pad, f32[8,16,32,128]{3,2,1,0:T(8,128)S(1)} %bitcast.14, s32[2,1,32]{2,1,0:T(1,128)S(1)} %bitcast.19, ...), custom_call_target="tpu_custom_call", output_to_operand_aliasing={{0}: (5, {}), {1}: (6, {})} | custom-call | flops 10000000000 | bytes 10000000 | tf_op jit(solution)/shard_map/outer_mechanic/pallas_call | solution.py:609
  13.8 2.1 %collective-permute-start.8 = (f32[3,4,8,128]{3,2,1,0:T(8,128)S(1)}, f32[3,4,8,128]{3,2,1,0:T(8,128)S(1)}, u32[]{:S(2)}, u32[]{:S(2)}) collective-permute-start(f32[3,4,8,128]{3,2,1,0:T(8,128)S(1)} %get-tuple-element.55), channel_id=1, source_target_pairs={{0,1},{1,0},{2,3},{3,2},{4,5},{5,4},{6,7},{7,6},{8,9},{9,8},{10,11... | collective-permute-start | bytes 147464 | tf_op jit(solution)/shard_map/ppermute | solution.py:739
  15.9 1.3 %middle.1 = (f32[1,4,16,32,128]{4,3,2,1,0:T(8,128)}, f32[3,18,48,128]{3,2,1,0:T(8,128)S(1)}, f32[4,32,128]{2,1,0:T(8,128)S(1)}) custom-call(f32[3,512,128]{2,1,0:T(8,128)S(1)} %get-tuple-element.33.fib_ref, f32[3,18,48,128]{3,2,1,0:T(8,128)S(1)} %get-tuple-element.50.next_in, ...), custom_call_target="tpu_custom_call", output_to_operand_aliasing={{1}: (1, {}), {0}: (4, {})} | custom-call | flops 60000002048 | bytes 60000000 | tf_op jit(solution)/shard_map/middle/pallas_call | solution.py:609
  17.2 1.0 %last.1 = (f32[1,4,16,32,128]{4,3,2,1,0:T(8,128)}, f32[3,18,48,128]{3,2,1,0:T(8,128)S(1)}) custom-call(f32[8,16,32,128]{3,2,1,0:T(8,128)S(1)} %bitcast.15, f32[3,512,128]{2,1,0:T(8,128)S(1)} %get-tuple-element.33.fib_ref, s32[2,1,32]{2,1,0:T(1,128)S(1)} %bitcast.20, ...), custom_call_target="tpu_custom_call", output_to_operand_aliasing={{1}: (5, {}), {0}: (9, {})} | custom-call | flops 10000000000 | bytes 10000000 | tf_op jit(solution)/shard_map/last/pallas_call | solution.py:609
  (13 shorter events, 0.1 us)
Async XLA Ops:
  0.0 1.6 %copy-start = (f32[1,8,16,32,128]{4,3,2,1,0:T(8,128)S(1)}, f32[1,8,16,32,128]{4,3,2,1,0:T(8,128)}, u32[]{:S(2)}) copy-start(f32[1,8,16,32,128]{4,3,2,1,0:T(8,128)} %param.5) | copy-start | bytes 6291460
  0.1 2.3 %copy-start.1 = (s32[16,32,8]{1,2,0:T(8,128)S(1)}, s32[16,32,8]{1,2,0:T(8,128)}, u32[]{:S(2)}) copy-start(s32[16,32,8]{1,2,0:T(8,128)} %param.7) | copy-start | bytes 49156
  0.1 2.3 %copy-start.2 = (f32[8,2]{0,1:T(2,128)S(1)}, f32[8,2]{0,1:T(2,128)}, u32[]{:S(2)}) copy-start(f32[8,2]{0,1:T(2,128)} %param.6) | copy-start | bytes 196
  0.2 4.9 %collective-permute-start.1 = (f32[2,32,128]{2,1,0:T(8,128)S(1)}, f32[2,32,128]{2,1,0:T(8,128)S(1)}, u32[]{:S(2)}, u32[]{:S(2)}) collective-permute-start(f32[2,32,128]{2,1,0:T(8,128)S(1)} %get-tuple-element.37), channel_id=1, source_target_pairs={{0,16},{16,0},{1,17},{17,1},{2,18},{18,2},{3,19},{19,3},{4,20},{20... | collective-permute-start | bytes 98312 | tf_op jit(solution)/shard_map/ppermute | solution.py:664
  1.7 2.7 %collective-permute-start = (f32[3,16,8,128]{3,2,1,0:T(8,128)S(1)}, f32[3,16,8,128]{3,2,1,0:T(8,128)S(1)}, u32[]{:S(2)}, u32[]{:S(2)}) collective-permute-start(f32[3,16,8,128]{3,2,1,0:T(8,128)S(1)} %get-tuple-element.35), channel_id=1, source_target_pairs={{0,1},{1,0},{2,3},{3,2},{4,5},{5,4},{6,7},{7,6},{8,9},{9,8},{10,11... | collective-permute-start | bytes 589832 | tf_op jit(solution)/shard_map/ppermute | solution.py:666
  3.2 8.0 %collective-permute-start.6 = (f32[512,128]{1,0:T(8,128)S(1)}, f32[512,128]{1,0:T(8,128)S(1)}, u32[]{:S(2)}, u32[]{:S(2)}) collective-permute-start(f32[512,128]{1,0:T(8,128)S(1)} %get-tuple-element.43), channel_id=1, source_target_pairs={{0,16},{16,0},{1,17},{17,1},{2,18},{18,2},{3,19},{19,3},{4,20},{20... | collective-permute-start | bytes 786440 | tf_op jit(solution)/shard_map/ppermute | solution.py:681
  4.4 0.7 %copy-start.3 = (s32[2,1,1,32]{3,2,1,0:T(1,128)S(1)}, s32[2,1,1,32]{3,2,1,0:T(1,128)}, u32[]{:S(2)}) copy-start(s32[2,1,1,32]{3,2,1,0:T(1,128)} %param.9) | copy-start | bytes 772
  4.5 8.6 %collective-permute-start.4 = (f32[168,128]{1,0:T(8,128)S(1)}, f32[168,128]{1,0:T(8,128)S(1)}, u32[]{:S(2)}, u32[]{:S(2)}) collective-permute-start(f32[168,128]{1,0:T(8,128)S(1)} %get-tuple-element.41), channel_id=1, source_target_pairs={{0,2},{1,3},{2,4},{3,5},{4,6},{5,7},{6,8},{7,9},{8,10},{9,11},{10,... | collective-permute-start | bytes 258056 | tf_op jit(solution)/shard_map/ppermute | solution.py:691
  4.8 8.3 %collective-permute-start.5 = (f32[168,128]{1,0:T(8,128)S(1)}, f32[168,128]{1,0:T(8,128)S(1)}, u32[]{:S(2)}, u32[]{:S(2)}) collective-permute-start(f32[168,128]{1,0:T(8,128)S(1)} %get-tuple-element.42), channel_id=1, source_target_pairs={{0,14},{1,15},{2,0},{3,1},{4,2},{5,3},{6,4},{7,5},{8,6},{9,7},{10,... | collective-permute-start | bytes 258056 | tf_op jit(solution)/shard_map/ppermute | solution.py:692
  5.2 8.2 %collective-permute-start.2 = (f32[232,128]{1,0:T(8,128)S(1)}, f32[232,128]{1,0:T(8,128)S(1)}, u32[]{:S(2)}, u32[]{:S(2)}) collective-permute-start(f32[232,128]{1,0:T(8,128)S(1)} %get-tuple-element.38), channel_id=1, source_target_pairs={{16,18},{17,19},{18,20},{19,21},{20,22},{21,23},{22,24},{23,25},{2... | collective-permute-start | bytes 356360 | tf_op jit(solution)/shard_map/ppermute | solution.py:702
  7.2 6.2 %collective-permute-start.3 = (f32[232,128]{1,0:T(8,128)S(1)}, f32[232,128]{1,0:T(8,128)S(1)}, u32[]{:S(2)}, u32[]{:S(2)}) collective-permute-start(f32[232,128]{1,0:T(8,128)S(1)} %get-tuple-element.39), channel_id=1, source_target_pairs={{16,30},{17,31},{18,16},{19,17},{20,18},{21,19},{22,20},{23,21},{2... | collective-permute-start | bytes 356360 | tf_op jit(solution)/shard_map/ppermute | solution.py:703
  12.2 3.7 %collective-permute-start.7 = (f32[3,18,8,128]{3,2,1,0:T(8,128)S(1)}, f32[3,18,8,128]{3,2,1,0:T(8,128)S(1)}, u32[]{:S(2)}, u32[]{:S(2)}) collective-permute-start(f32[3,18,8,128]{3,2,1,0:T(8,128)S(1)} %get-tuple-element.51), channel_id=1, source_target_pairs={{0,1},{1,0},{2,3},{3,2},{4,5},{5,4},{6,7},{7,6},{8,9},{9,8},{10,11... | collective-permute-start | bytes 663560 | tf_op jit(solution)/shard_map/ppermute | solution.py:719
  13.8 3.4 %collective-permute-start.8 = (f32[3,4,8,128]{3,2,1,0:T(8,128)S(1)}, f32[3,4,8,128]{3,2,1,0:T(8,128)S(1)}, u32[]{:S(2)}, u32[]{:S(2)}) collective-permute-start(f32[3,4,8,128]{3,2,1,0:T(8,128)S(1)} %get-tuple-element.55), channel_id=1, source_target_pairs={{0,1},{1,0},{2,3},{3,2},{4,5},{5,4},{6,7},{7,6},{8,9},{9,8},{10,11... | collective-permute-start | bytes 147464 | tf_op jit(solution)/shard_map/ppermute | solution.py:739

commit v7 on v6

--- a/solution.py
+++ b/solution.py
@@ -8,7 +8,6 @@
 DT = 0.1
 OMEGA = 0.06
 F32 = jnp.float32
-HIGHEST = lax.Precision.HIGHEST
 VMEM_LIMIT = 16 * 1024 * 1024
 COST = {
     "tension": 0.001,
@@ -23,6 +22,8 @@
     "middle": 6,
     "last": 1,
 }
+
+CELLS = 16
 
 PAD = 8
 
@@ -133,18 +134,19 @@
     return q, calcium_flow, calcium_flow + (0.8 * n + 0.6 * q * r) * (v + 1.0) + 0.1 * v
 
 
-def permute_rows(listed, values):
-    rows = values.shape[0]
+def in_three(values):
+    high = values.astype(jnp.bfloat16).astype(F32)
+    mid = (values - high).astype(jnp.bfloat16).astype(F32)
+    return jnp.concatenate([high, mid, values - high - mid], axis=0)
+
+
+def tie_rows(listed, stiff, u):
+    rows, depth = u[0].shape
+    joined = in_three(jnp.concatenate([2.0 * stiff * w for w in u], axis=1))
     pick = (lax.broadcasted_iota(jnp.int32, (rows, rows), 0).astype(F32) == listed).astype(F32)
-    return lax.dot_general(
-        pick, values, (((0,), (0,)), ((), ())), precision=HIGHEST, preferred_element_type=F32
-    )
-
-
-def tie_rows(listed, stiff, u):
-    joined = jnp.concatenate([2.0 * stiff * w for w in u], axis=1)
-    moved = permute_rows(listed, joined)
-    depth = u[0].shape[1]
+    moved = lax.dot_general(
+        jnp.concatenate([pick] * 3, axis=0), joined, (((0,), (0,)), ((), ())), preferred_element_type=F32
+    )
     return [moved[:, a * depth : (a + 1) * depth] for a in range(3)]
 
 
@@ -171,16 +173,15 @@
     return lax.axis_index("sec") == 0
 
 
-def fiber_fields(angles, cls, flat, fib_ref, size_x, size_y):
-    blocks, classes, depth = cls.shape[1], angles.shape[1], fib_ref.shape[2]
+def fiber_fields(angles, cls):
+    blocks, classes = cls.shape[0], angles.shape[1]
+    depth = CELLS * blocks
     azimuth, elevation = angles[0:1, :], angles[1:2, :]
     flat_part = jnp.cos(elevation)
     fib = [jnp.cos(azimuth) * flat_part, jnp.sin(azimuth) * flat_part, jnp.sin(elevation)]
-    for x in range(size_x):
-        flat[:, x * size_y : (x + 1) * size_y] = cls[x]
-    own = lax.broadcasted_iota(jnp.int32, (blocks, depth), 1) // (depth // blocks)
+    own = lax.broadcasted_iota(jnp.int32, (blocks, depth), 1) // CELLS
     own = own == lax.broadcasted_iota(jnp.int32, (blocks, depth), 0)
-    hits = jnp.concatenate([(flat[...] == k).astype(F32) for k in range(classes)], axis=0)
+    hits = jnp.concatenate([(cls == k).astype(F32) for k in range(classes)], axis=0)
     table = jnp.concatenate(
         [
             jnp.concatenate(
@@ -190,12 +191,17 @@
         ],
         axis=0,
     )
-    high = table.astype(jnp.bfloat16).astype(F32)
-    mid = (table - high).astype(jnp.bfloat16).astype(F32)
-    parts = jnp.concatenate([high, mid, table - high - mid], axis=0)
-    found = lax.dot_general(
-        jnp.concatenate([hits] * 3, axis=0), parts, (((0,), (0,)), ((), ())), preferred_element_type=F32
-    )
+    return lax.dot_general(
+        jnp.concatenate([hits] * 3, axis=0), in_three(table), (((0,), (0,)), ((), ())), preferred_element_type=F32
+    )
+
+
+def all_fibers(ang_ref, cls_ref, flat, fib_ref):
+    size_x, _, size_y = cls_ref.shape
+    depth = fib_ref.shape[2]
+    for x in range(size_x):
+        flat[:, x * size_y : (x + 1) * size_y] = cls_ref[x]
+    found = fiber_fields(ang_ref[...], flat[...])
     for a in range(3):
         fib_ref[a] = found[:, a * depth : (a + 1) * depth]
 
@@ -259,25 +265,18 @@
     lax.fori_loop(0, size_x, plane, 0, unroll=4)
 
 
-def gather_kernel(map_hbm, plain, cls_ref, ang_ref, all_ref, fib_ref, out_hbm, map_ref, flat, sems):
-    size_x = cls_ref.shape[0]
-    size_y = all_ref.shape[0] // size_x
-    places = pltpu.make_async_copy(map_hbm, map_ref, sems.at[0])
-    copies = [
-        pltpu.make_async_copy(plain.at[x * size_y : (x + 1) * size_y], out_hbm.at[0, 3, x], sems.at[1 + x])
-        for x in range(size_x)
-    ]
-
+def gather_kernel(map_hbm, plain, all_ref, out_hbm, map_ref, sems):
     @pl.when(electric())
     def _():
+        size_x, size_y = out_hbm.shape[2], out_hbm.shape[3]
+        places = pltpu.make_async_copy(map_hbm, map_ref, sems.at[0])
         places.start()
+        copies = [
+            pltpu.make_async_copy(plain.at[x * size_y : (x + 1) * size_y], out_hbm.at[0, 3, x], sems.at[1 + x])
+            for x in range(size_x)
+        ]
         for copy in copies:
             copy.start()
-
-    fiber_fields(ang_ref[...], cls_ref, flat, fib_ref, size_x, size_y)
-
-    @pl.when(electric())
-    def _():
         places.wait()
 
         def rows(i, carry):
@@ -291,7 +290,7 @@
             copy.wait()
 
 
-def message_electric(pad_in, own, side_ref, fib_ref, high_ref, low_ref, pad):
+def message_electric(pad_in, own, side_ref, cls_ref, ang_ref, after, high_ref, low_ref, pad, fib_ref, flat):
     size_x, size_y = own.shape[1], own.shape[2]
 
     def fill(x, carry):
@@ -303,6 +302,7 @@
 
     @pl.when(electric())
     def _():
+        all_fibers(ang_ref, cls_ref, flat, fib_ref)
         for which, ((_, edge, _), out) in enumerate(zip(sides(size_x), (low_ref, high_ref))):
             out[ROW_VOLT_SIDE : ROW_VOLT_SIDE + 1, :] = side_ref[0, edge, 7:8, :]
             out[ROW_VOLT_SIDE + 1 : ROW_VOLT_SIDE + 2, :] = side_ref[0, edge, 0:1, :]
@@ -316,11 +316,17 @@
             for k, value in enumerate(couplings(fib)):
                 out[ROW_COUPLED + k * size_y : ROW_COUPLED + (k + 1) * size_y, :] = value
 
-def message_mechanic(pad_in, own, side_ref, fib_ref, ten_ref, list_ref, high_ref, low_ref, pad):
+def message_mechanic(
+    pad_in, own, side_ref, cls_ref, ang_ref, ten_ref, list_ref, high_ref, low_ref, pad, flat
+):
     size_x, size_y = own.shape[1], own.shape[2]
 
     @pl.when(jnp.logical_not(electric()))
     def _():
+        depth = own.shape[3]
+        for which, (_, edge, _) in enumerate(sides(size_x)):
+            flat[:, which * size_y : (which + 1) * size_y] = cls_ref[edge]
+        fibers = fiber_fields(ang_ref[...], flat[...])
         for which, ((_, edge, _), out) in enumerate(zip(sides(size_x), (low_ref, high_ref))):
             out[ROW_LIST : ROW_LIST + 1, 0:size_y] = list_ref[which].astype(F32)
             rate = motion_rate(pad, edge + 1, size_y)
@@ -334,7 +340,7 @@
                 out[row + 1 : row + 2, :] = side_ref[a, edge, 0:1, :]
                 u = rows_of(pad, a, edge + 1, size_y)
                 out[ROW_NOW + a * size_y : ROW_NOW + (a + 1) * size_y, :] = u
-                drive = own[3 + a, edge] + act * fib_ref[a, place_of(edge, size_y), :]
+                drive = own[3 + a, edge] + act * fibers[which * size_y : (which + 1) * size_y, a * depth : (a + 1) * depth]
                 out[ROW_NEXT + a * size_y : ROW_NEXT + (a + 1) * size_y, :] = (
                     0.28 * u + beta * drive + OMEGA * rate[a]
                 )
@@ -375,11 +381,15 @@
         lax.fori_loop(0, size_x, plane, 0, unroll=2)
 
 
-def inner_mechanic(pad, own, fib_ref, ten_ref, next_in, share_in, keep_in, next_pad, share, keep):
+def inner_mechanic(
+    pad, own, cls_ref, ang_ref, ten_ref, next_in, share_in, keep_in, next_pad, share, keep, fib_ref, flat
+):
     size_x, size_y = own.shape[1], own.shape[2]
 
     @pl.when(jnp.logical_not(electric()))
     def _():
+        all_fibers(ang_ref, cls_ref, flat, fib_ref)
+
         def plane(x, carry):
             place = place_of(x, size_y)
             rate = motion_rate(pad, x + 1, size_y)
@@ -494,10 +504,12 @@
     for a in range(3):
         u = rows_of(next_pad, a, x + 1, size_y)
         value = 0.4 * u + keep[a, x] + OMEGA * rate[a]
-        out[a, x] = value if ties is None else value + ties[a] - 0.12 * u
-
-
-def middle_kernel(fib_ref, next_in, side_ref, keep, out_in, out_hbm, next_pad, held, out, sems):
+        out[a, x] = value if ties is None else value + ties[a]
+
+
+def middle_kernel(
+    fib_ref, own, list_ref, got_low, got_high, next_in, side_ref, keep, out_in, out_hbm, next_pad, held, out, sems
+):
     size_x = keep.shape[1]
     size_y = fib_ref.shape[1] // size_x
     pieces = sems.shape[0] - 1
@@ -554,28 +566,38 @@
             return carry
 
         lax.fori_loop(0, pieces, sweep, 0)
+        for which, ((halo, edge, _), got) in enumerate(zip(sides(size_x), (got_low, got_high))):
+            beta = OMEGA * inverse(own[6, edge])
+            ties = tie_rows(
+                list_ref[which].astype(F32),
+                got[ROW_STIFF : ROW_STIFF + size_y, :],
+                [rows_of(next_pad, a, halo, size_y) for a in range(3)],
+            )
+            for a in range(3):
+                held[3 * which + a] = beta * ties[a] - 0.12 * rows_of(next_pad, a, edge + 1, size_y)
         copy.wait()
         for i in range(pieces):
             copy_out(i, 3).wait()
 
 
 def last_kernel(
-    own, fib_ref, list_ref, got_low, got_high, next_in, side_ref, keep, held, out_in, out_hbm, next_pad, out, sems
+    fib_ref, next_in, side_ref, keep, held, out_in, out_hbm, next_pad, out, sems
 ):
-    size_x, size_y = own.shape[1], own.shape[2]
+    size_x = keep.shape[1]
+    size_y = fib_ref.shape[1] // size_x
 
     def copy_out(which, first, fields):
         here = pl.ds(first, 2)
         return pltpu.make_async_copy(out.at[0:fields, here], out_hbm.at[0, 0:fields, here], sems.at[which])
 
     work = []
-    for which, ((halo, edge, _), got) in enumerate(zip(sides(size_x), (got_low, got_high))):
+    for which, (halo, edge, _) in enumerate(sides(size_x)):
         near = abs(edge - 1)
-        work.append((halo, edge, near, which, got, min(edge, near)))
+        work.append((halo, edge, near, which, min(edge, near)))
 
     @pl.when(electric())
     def _():
-        for halo, edge, near, which, _, first in work:
+        for halo, edge, near, which, first in work:
             fill_sides(next_pad, 0, halo, side_ref[0, 3 * which], size_y)
             fill_sides(next_pad, 0, edge + 1, side_ref[0, 1 + which], size_y)
             for x in (near, edge):
@@ -586,18 +608,12 @@
 
     @pl.when(jnp.logical_not(electric()))
     def _():
-        for halo, edge, near, which, got, first in work:
+        for halo, edge, near, which, first in work:
             for a in range(3):
                 fill_sides(next_pad, a, halo, side_ref[a, 3 * which], size_y)
                 fill_sides(next_pad, a, edge + 1, side_ref[a, 1 + which], size_y)
-            beta = OMEGA * inverse(own[6, edge])
-            ties = tie_rows(
-                list_ref[which].astype(F32),
-                got[ROW_STIFF : ROW_STIFF + size_y, :],
-                [rows_of(next_pad, a, halo, size_y) for a in range(3)],
-            )
             mechanic_end(near, next_pad, keep, out, size_y)
-            mechanic_end(edge, next_pad, keep, out, size_y, [beta * w for w in ties])
+            mechanic_end(edge, next_pad, keep, out, size_y, [held[3 * which + a] for a in range(3)])
             copy_out(which, first, 3).start()
         for item in work:
             copy_out(item[3], item[-1], 3).wait()
@@ -665,27 +681,27 @@
     pad, share = call(share_kernel, "share", (padded, f32(3, size_x, 8, depth)), (own, plain), (V, V))
     side = lax.ppermute(share, "gy", both)
     result = f32(1, 4, size_x, size_y, depth)
-    tension, fib, result = call(
+    gathered, result = call(
         gather_kernel,
         "gather",
-        (f32(columns, depth), f32(3, columns, depth), result),
-        (hbm(places), plain, classes, fiber_angles.T),
-        (H, V, V, V),
-        [
-            pltpu.SMEM((columns,), jnp.int32),
-            pltpu.VMEM((classes.shape[1], columns), jnp.int32),
-            pltpu.SemaphoreType.DMA((1 + size_x,)),
-        ],
-        out_spaces=(V, V, H),
-    )
-    tension = lax.ppermute(tension, "sec", both)
+        (f32(columns, depth), result),
+        (hbm(places), plain),
+        (H, V),
+        [pltpu.SMEM((columns,), jnp.int32), pltpu.SemaphoreType.DMA((1 + size_x,))],
+        out_spaces=(V, H),
+    )
+    tension = lax.ppermute(gathered, "sec", both)
+    assert depth == CELLS * classes.shape[1]
+    angles = fiber_angles.T
+    flat = lambda count: pltpu.VMEM((classes.shape[1], count), jnp.int32)
     message = f32(VOLT_ROWS, depth)
-    high, low, pad = call(
+    high, low, pad, fib = call(
         message_electric,
         "message_electric",
-        (message, message, padded),
-        (pad, own, side, fib),
-        (V,) * 4,
+        (message, message, padded, f32(3, columns, depth)),
+        (pad, own, side, classes, angles, gathered),
+        (V,) * 6,
+        [flat(columns)],
         aliases={0: 2},
     )
     volt_low = lax.ppermute(high, axes, ring(0, 1))
@@ -695,8 +711,9 @@
         message_mechanic,
         "message_mechanic",
         (message, message, padded),
-        (pad, own, side, fib, edge_ten, lists),
-        (V,) * 6,
+        (pad, own, side, classes, angles, edge_ten, lists),
+        (V,) * 7,
+        [flat(2 * size_y)],
         aliases={0: 2},
     )
     got_low = lax.ppermute(high, axes, ring(1, 1))
@@ -712,9 +729,10 @@
         inner_mechanic,
         "inner_mechanic",
         (padded, f32(3, size_x + 2, 8, depth), f32(4, size_x, size_y, depth)),
-        (pad, own, fib, tension, moved, share, keep),
-        (V,) * 7,
-        aliases={4: 0, 5: 1, 6: 2},
+        (pad, own, classes, angles, tension, moved, share, keep),
+        (V,) * 8,
+        [pltpu.VMEM((3, columns, depth), F32), flat(columns)],
+        aliases={5: 0, 6: 1, 7: 2},
     )
     side = lax.ppermute(share, "gy", both)
     wide = pltpu.VMEM((3, 2) + padded.shape[2:], F32)
@@ -741,22 +759,22 @@
     result, moved, held = call(
         middle_kernel,
         "middle",
-        (f32(1, 4, size_x, size_y, depth), padded, f32(4, size_y, depth)),
-        (fib, moved, side, keep, result),
-        (V,) * 4 + (H,),
+        (f32(1, 4, size_x, size_y, depth), padded, f32(6, size_y, depth)),
+        (fib, own, lists, got_low, got_high, moved, side, keep, result),
+        (V,) * 8 + (H,),
         [fields, pltpu.SemaphoreType.DMA((4,))],
         out_spaces=(H, V, V),
-        aliases={1: 1, 4: 0},
+        aliases={5: 1, 8: 0},
     )
     return call(
         last_kernel,
         "last",
         (f32(1, 4, size_x, size_y, depth), padded),
-        (own, fib, lists, got_low, got_high, moved, end_side, keep, held, result),
-        (V,) * 9 + (H,),
+        (fib, moved, end_side, keep, held, result),
+        (V,) * 5 + (H,),
         [fields, pltpu.SemaphoreType.DMA((2,))],
         out_spaces=(H, V),
-        aliases={5: 1, 9: 0},
+        aliases={1: 1, 5: 0},
     )[0]
 
 

time: 18.4 us -> 17.9 us (0.973)
  waiting for transfers between devices: 1.14 us -> 0.89 us
  starting transfers between devices: 11.8 us -> 11.6 us
    ppermute x1, starting transfers between devices: 1.26 us -> 1.6 us  [local(): tension = lax.ppermute(gathered, 'sec', both)]
    ppermute x1, starting transfers between devices: 2.07 us -> 1.83 us  [local(): end_side = lax.ppermute(share, 'gy', both)]
    ppermute x1, waiting for transfers between devices: 0.82 us -> 0.6 us  [local(): tension = lax.ppermute(gathered, 'sec', both)]
    ppermute x1, starting transfers between devices: 1.97 us -> 1.77 us  [local(): got_low = lax.ppermute(high, axes, ring(1, 1))]
  transfers between devices with their start and end apart: 9 -> 9, of which waited for: 2 -> 2; matrix products, arithmetic and copies ran while one was open for 0% -> 0% of each run, Pallas kernels for 21% -> 22%
where the time goes in v7:
time: 17.9 us; the launch traced here: 17.8 us
  starting transfers between devices  11.6 us (65%)
  Pallas kernels  4.85 us (27%)
  waiting for transfers between devices  0.89 us (5%)
  local copies, waits for them, and re-layouts  0.31 us (2%)
    pallas_call x11, Pallas kernels, call(): pl.pallas_call(kernel, name=name, out_shape=tuple(out_shape), in_specs=[p...  4.85 us
    ppermute x1, starting transfers between devices, local(): got_high = lax.ppermute(low, axes, ring(1, -1))  3.1 us
    ppermute x1, starting transfers between devices, local(): end_side = lax.ppermute(share, 'gy', both)  1.83 us
    ppermute x1, starting transfers between devices, local(): got_low = lax.ppermute(high, axes, ring(1, 1))  1.77 us
    ppermute x1, starting transfers between devices, local(): tension = lax.ppermute(gathered, 'sec', both)  1.6 us
    ppermute x2, starting transfers between devices, local(): side = lax.ppermute(share, 'gy', both)  1.54 us
    ppermute x1, starting transfers between devices, local(): edge_ten = lax.ppermute(edge_ten, 'sec', both)  1.23 us
    ppermute x1, waiting for transfers between devices, local(): tension = lax.ppermute(gathered, 'sec', both)  0.6 us
  transfers between devices with their start and end apart: 9, of which 2 were waited for; matrix products, arithmetic and copies ran while one was open for 0% of the time, Pallas kernels for 22%

profile of v7, /device:TPU:3, one launch (start us, length us, event | category | flops | bytes accessed | tf_op | source)
XLA Modules:
  0.0 17.8 jit_solution(15484168130735263482)
XLA Ops:
  0.0 0.1 tension.1
  0.1 1.2 %collective-permute-start.1 = (f32[2,32,128]{2,1,0:T(8,128)S(1)}, f32[2,32,128]{2,1,0:T(8,128)S(1)}, u32[]{:S(2)}, u32[]{:S(2)}) collective-permute-start(f32[2,32,128]{2,1,0:T(8,128)S(1)} %get-tuple-element.38), channel_id=1, source_target_pairs={{0,16},{16,0},{1,17},{17,1},{2,18},{18,2},{3,19},{19,3},{4,20},{20... | collective-permute-start | bytes 98312 | tf_op jit(solution)/shard_map/ppermute | solution.py:680
  1.4 0.2 %copy-done = f32[1,8,16,32,128]{4,3,2,1,0:T(8,128)S(1)} copy-done((f32[1,8,16,32,128]{4,3,2,1,0:T(8,128)S(1)}, f32[1,8,16,32,128]{4,3,2,1,0:T(8,128)}, u32[]{:S(2)}) %copy-start) | copy-done | bytes 2097176
  1.6 0.1 share.1
  1.7 0.0 copy-start.1
  1.7 0.0 copy-start.2
  1.7 0.7 %collective-permute-start = (f32[3,16,8,128]{3,2,1,0:T(8,128)S(1)}, f32[3,16,8,128]{3,2,1,0:T(8,128)S(1)}, u32[]{:S(2)}, u32[]{:S(2)}) collective-permute-start(f32[3,16,8,128]{3,2,1,0:T(8,128)S(1)} %get-tuple-element.34), channel_id=1, source_target_pairs={{0,1},{1,0},{2,3},{3,2},{4,5},{5,4},{6,7},{7,6},{8,9},{9,8},{10,11... | collective-permute-start | bytes 589832 | tf_op jit(solution)/shard_map/ppermute | solution.py:682
  2.4 0.2 gather.1
  2.6 1.6 %collective-permute-start.6 = (f32[512,128]{1,0:T(8,128)S(1)}, f32[512,128]{1,0:T(8,128)S(1)}, u32[]{:S(2)}, u32[]{:S(2)}) collective-permute-start(f32[512,128]{1,0:T(8,128)S(1)} %get-tuple-element.35.after), channel_id=1, source_target_pairs={{0,16},{16,0},{1,17},{17,1},{2,18},{18,2},{3,19},{19,3},{4,20},{20... | collective-permute-start | bytes 786440 | tf_op jit(solution)/shard_map/ppermute | solution.py:693
  4.2 0.0 copy-start.3
  4.3 0.4 %collective-permute-start.4 = (f32[168,128]{1,0:T(8,128)S(1)}, f32[168,128]{1,0:T(8,128)S(1)}, u32[]{:S(2)}, u32[]{:S(2)}) collective-permute-start(f32[168,128]{1,0:T(8,128)S(1)} %get-tuple-element.42), channel_id=1, source_target_pairs={{0,2},{1,3},{2,4},{3,5},{4,6},{5,7},{6,8},{7,9},{8,10},{9,11},{10,... | collective-permute-start | bytes 258056 | tf_op jit(solution)/shard_map/ppermute | solution.py:707
  4.6 0.2 %collective-permute-start.5 = (f32[168,128]{1,0:T(8,128)S(1)}, f32[168,128]{1,0:T(8,128)S(1)}, u32[]{:S(2)}, u32[]{:S(2)}) collective-permute-start(f32[168,128]{1,0:T(8,128)S(1)} %get-tuple-element.43), channel_id=1, source_target_pairs={{0,14},{1,15},{2,0},{3,1},{4,2},{5,3},{6,4},{7,5},{8,6},{9,7},{10,... | collective-permute-start | bytes 258056 | tf_op jit(solution)/shard_map/ppermute | solution.py:708
  4.8 0.1 copy-done.3
  4.9 0.4 %message_mechanic.1 = (f32[232,128]{1,0:T(8,128)S(1)}, f32[232,128]{1,0:T(8,128)S(1)}, f32[3,18,48,128]{3,2,1,0:T(8,128)S(1)}) custom-call(f32[3,18,48,128]{3,2,1,0:T(8,128)S(1)} %get-tuple-element.37.pad_in, f32[8,16,32,128]{3,2,1,0:T(8,128)S(1)} %bitcast.10, f32[3,16,8,128]{3,2,1,0:T(8,128)S(1)} %collective-permute-done.side_ref, ...), custom_call_target="tpu_custom_call", output_to_operand_aliasing={{2}: (0, {})} | custom-call | flops 10000000000 | bytes 10000000 | tf_op jit(solution)/shard_map/message_mechanic/pallas_call | solution.py:625
  5.3 1.8 %collective-permute-start.2 = (f32[232,128]{1,0:T(8,128)S(1)}, f32[232,128]{1,0:T(8,128)S(1)}, u32[]{:S(2)}, u32[]{:S(2)}) collective-permute-start(f32[232,128]{1,0:T(8,128)S(1)} %get-tuple-element.39), channel_id=1, source_target_pairs={{16,18},{17,19},{18,20},{19,21},{20,22},{21,23},{22,24},{23,25},{2... | collective-permute-start | bytes 356360 | tf_op jit(solution)/shard_map/ppermute | solution.py:719
  7.0 3.1 %collective-permute-start.3 = (f32[232,128]{1,0:T(8,128)S(1)}, f32[232,128]{1,0:T(8,128)S(1)}, u32[]{:S(2)}, u32[]{:S(2)}) collective-permute-start(f32[232,128]{1,0:T(8,128)S(1)} %get-tuple-element.40), channel_id=1, source_target_pairs={{16,30},{17,31},{18,16},{19,17},{20,18},{21,19},{22,20},{23,21},{2... | collective-permute-start | bytes 356360 | tf_op jit(solution)/shard_map/ppermute | solution.py:720
  10.1 0.6 %collective-permute-done.6.ten_ref = f32[512,128]{1,0:T(8,128)S(1)} collective-permute-done((f32[512,128]{1,0:T(8,128)S(1)}, f32[512,128]{1,0:T(8,128)S(1)}, u32[]{:S(2)}, u32[]{:S(2)}) %collective-permute-start.6) | collective-permute-done | bytes 262176 | tf_op jit(solution)/shard_map/ppermute | solution.py:693
  10.7 1.6 %inner_mechanic.1 = (f32[3,18,48,128]{3,2,1,0:T(8,128)S(1)}, f32[3,18,8,128]{3,2,1,0:T(8,128)S(1)}, f32[4,16,32,128]{3,2,1,0:T(8,128)S(1)}) custom-call(f32[3,18,48,128]{3,2,1,0:T(8,128)S(1)} %get-tuple-element.41.pad, f32[8,16,32,128]{3,2,1,0:T(8,128)S(1)} %bitcast.12, ...), custom_call_target="tpu_custom_call", output_to_operand_aliasing={{0}: (5, {}), {1}: (6, {}), {2}: (7, {})} | custom-call | flops 60000002048 | bytes 60000000 | tf_op jit(solution)/shard_map/inner_mechanic/pallas_call | solution.py:625
  12.4 0.8 %collective-permute-start.7 = (f32[3,18,8,128]{3,2,1,0:T(8,128)S(1)}, f32[3,18,8,128]{3,2,1,0:T(8,128)S(1)}, u32[]{:S(2)}, u32[]{:S(2)}) collective-permute-start(f32[3,18,8,128]{3,2,1,0:T(8,128)S(1)} %get-tuple-element.51), channel_id=1, source_target_pairs={{0,1},{1,0},{2,3},{3,2},{4,5},{5,4},{6,7},{7,6},{8,9},{9,8},{10,11... | collective-permute-start | bytes 663560 | tf_op jit(solution)/shard_map/ppermute | solution.py:737
  13.2 0.3 %collective-permute-done.2.got_low = f32[232,128]{1,0:T(8,128)S(1)} collective-permute-done((f32[232,128]{1,0:T(8,128)S(1)}, f32[232,128]{1,0:T(8,128)S(1)}, u32[]{:S(2)}, u32[]{:S(2)}) %collective-permute-start.2) | collective-permute-done | bytes 118816 | tf_op jit(solution)/shard_map/ppermute | solution.py:719
  13.5 0.3 %outer_mechanic.1 = (f32[3,18,48,128]{3,2,1,0:T(8,128)S(1)}, f32[3,4,8,128]{3,2,1,0:T(8,128)S(1)}) custom-call(f32[3,18,48,128]{3,2,1,0:T(8,128)S(1)} %get-tuple-element.41.pad, f32[8,16,32,128]{3,2,1,0:T(8,128)S(1)} %bitcast.14, s32[2,1,32]{2,1,0:T(1,128)S(1)} %bitcast.23, ...), custom_call_target="tpu_custom_call", output_to_operand_aliasing={{0}: (5, {}), {1}: (6, {})} | custom-call | flops 10000000000 | bytes 10000000 | tf_op jit(solution)/shard_map/outer_mechanic/pallas_call | solution.py:625
  13.7 1.8 %collective-permute-start.8 = (f32[3,4,8,128]{3,2,1,0:T(8,128)S(1)}, f32[3,4,8,128]{3,2,1,0:T(8,128)S(1)}, u32[]{:S(2)}, u32[]{:S(2)}) collective-permute-start(f32[3,4,8,128]{3,2,1,0:T(8,128)S(1)} %get-tuple-element.55), channel_id=1, source_target_pairs={{0,1},{1,0},{2,3},{3,2},{4,5},{5,4},{6,7},{7,6},{8,9},{9,8},{10,11... | collective-permute-start | bytes 147464 | tf_op jit(solution)/shard_map/ppermute | solution.py:757
  15.6 1.3 %middle.1 = (f32[1,4,16,32,128]{4,3,2,1,0:T(8,128)}, f32[3,18,48,128]{3,2,1,0:T(8,128)S(1)}, f32[6,32,128]{2,1,0:T(8,128)S(1)}) custom-call(f32[3,512,128]{2,1,0:T(8,128)S(1)} %get-tuple-element.36.fib_ref, f32[8,16,32,128]{3,2,1,0:T(8,128)S(1)} %bitcast.15, s32[2,1,32]{2,1,0:T(1,128)S(1)} %bitcast.24, ...), custom_call_target="tpu_custom_call", output_to_operand_aliasing={{1}: (5, {}), {0}: (8, {})} | custom-call | flops 60000002048 | bytes 60000000 | tf_op jit(solution)/shard_map/middle/pallas_call | solution.py:625
  16.9 0.9 %last.1 = (f32[1,4,16,32,128]{4,3,2,1,0:T(8,128)}, f32[3,18,48,128]{3,2,1,0:T(8,128)S(1)}) custom-call(f32[3,512,128]{2,1,0:T(8,128)S(1)} %get-tuple-element.36.fib_ref, f32[3,18,48,128]{3,2,1,0:T(8,128)S(1)} %get-tuple-element.54.next_in, f32[3,4,8,128]{3,2,1,0:T(8,128)S(1)} %collective-permute-done.8.side_ref, ...), custom_call_target="tpu_custom_call", output_to_operand_aliasing={{1}: (1, {}), {0}: (5, {})} | custom-call | flops 10000000000 | bytes 10000000 | tf_op jit(solution)/shard_map/last/pallas_call | solution.py:625
  (13 shorter events, 0.1 us)
Async XLA Ops:
  0.0 1.6 %copy-start = (f32[1,8,16,32,128]{4,3,2,1,0:T(8,128)S(1)}, f32[1,8,16,32,128]{4,3,2,1,0:T(8,128)}, u32[]{:S(2)}) copy-start(f32[1,8,16,32,128]{4,3,2,1,0:T(8,128)} %param.5) | copy-start | bytes 6291460
  0.1 4.7 %collective-permute-start.1 = (f32[2,32,128]{2,1,0:T(8,128)S(1)}, f32[2,32,128]{2,1,0:T(8,128)S(1)}, u32[]{:S(2)}, u32[]{:S(2)}) collective-permute-start(f32[2,32,128]{2,1,0:T(8,128)S(1)} %get-tuple-element.38), channel_id=1, source_target_pairs={{0,16},{16,0},{1,17},{17,1},{2,18},{18,2},{3,19},{19,3},{4,20},{20... | collective-permute-start | bytes 98312 | tf_op jit(solution)/shard_map/ppermute | solution.py:680
  1.7 2.5 %copy-start.1 = (s32[16,32,8]{1,2,0:T(8,128)S(1)}, s32[16,32,8]{1,2,0:T(8,128)}, u32[]{:S(2)}) copy-start(s32[16,32,8]{1,2,0:T(8,128)} %param.7) | copy-start | bytes 49156
  1.7 2.5 %copy-start.2 = (f32[8,2]{0,1:T(2,128)S(1)}, f32[8,2]{0,1:T(2,128)}, u32[]{:S(2)}) copy-start(f32[8,2]{0,1:T(2,128)} %param.6) | copy-start | bytes 196
  1.7 2.5 %collective-permute-start = (f32[3,16,8,128]{3,2,1,0:T(8,128)S(1)}, f32[3,16,8,128]{3,2,1,0:T(8,128)S(1)}, u32[]{:S(2)}, u32[]{:S(2)}) collective-permute-start(f32[3,16,8,128]{3,2,1,0:T(8,128)S(1)} %get-tuple-element.34), channel_id=1, source_target_pairs={{0,1},{1,0},{2,3},{3,2},{4,5},{5,4},{6,7},{7,6},{8,9},{9,8},{10,11... | collective-permute-start | bytes 589832 | tf_op jit(solution)/shard_map/ppermute | solution.py:682
  2.6 8.1 %collective-permute-start.6 = (f32[512,128]{1,0:T(8,128)S(1)}, f32[512,128]{1,0:T(8,128)S(1)}, u32[]{:S(2)}, u32[]{:S(2)}) collective-permute-start(f32[512,128]{1,0:T(8,128)S(1)} %get-tuple-element.35.after), channel_id=1, source_target_pairs={{0,16},{16,0},{1,17},{17,1},{2,18},{18,2},{3,19},{19,3},{4,20},{20... | collective-permute-start | bytes 786440 | tf_op jit(solution)/shard_map/ppermute | solution.py:693
  4.2 0.7 %copy-start.3 = (s32[2,1,1,32]{3,2,1,0:T(1,128)S(1)}, s32[2,1,1,32]{3,2,1,0:T(1,128)}, u32[]{:S(2)}) copy-start(s32[2,1,1,32]{3,2,1,0:T(1,128)} %param.9) | copy-start | bytes 772
  4.3 8.9 %collective-permute-start.4 = (f32[168,128]{1,0:T(8,128)S(1)}, f32[168,128]{1,0:T(8,128)S(1)}, u32[]{:S(2)}, u32[]{:S(2)}) collective-permute-start(f32[168,128]{1,0:T(8,128)S(1)} %get-tuple-element.42), channel_id=1, source_target_pairs={{0,2},{1,3},{2,4},{3,5},{4,6},{5,7},{6,8},{7,9},{8,10},{9,11},{10,... | collective-permute-start | bytes 258056 | tf_op jit(solution)/shard_map/ppermute | solution.py:707
  4.6 8.5 %collective-permute-start.5 = (f32[168,128]{1,0:T(8,128)S(1)}, f32[168,128]{1,0:T(8,128)S(1)}, u32[]{:S(2)}, u32[]{:S(2)}) collective-permute-start(f32[168,128]{1,0:T(8,128)S(1)} %get-tuple-element.43), channel_id=1, source_target_pairs={{0,14},{1,15},{2,0},{3,1},{4,2},{5,3},{6,4},{7,5},{8,6},{9,7},{10,... | collective-permute-start | bytes 258056 | tf_op jit(solution)/shard_map/ppermute | solution.py:708
  5.3 8.2 %collective-permute-start.2 = (f32[232,128]{1,0:T(8,128)S(1)}, f32[232,128]{1,0:T(8,128)S(1)}, u32[]{:S(2)}, u32[]{:S(2)}) collective-permute-start(f32[232,128]{1,0:T(8,128)S(1)} %get-tuple-element.39), channel_id=1, source_target_pairs={{16,18},{17,19},{18,20},{19,21},{20,22},{21,23},{22,24},{23,25},{2... | collective-permute-start | bytes 356360 | tf_op jit(solution)/shard_map/ppermute | solution.py:719
  7.0 6.4 %collective-permute-start.3 = (f32[232,128]{1,0:T(8,128)S(1)}, f32[232,128]{1,0:T(8,128)S(1)}, u32[]{:S(2)}, u32[]{:S(2)}) collective-permute-start(f32[232,128]{1,0:T(8,128)S(1)} %get-tuple-element.40), channel_id=1, source_target_pairs={{16,30},{17,31},{18,16},{19,17},{20,18},{21,19},{22,20},{23,21},{2... | collective-permute-start | bytes 356360 | tf_op jit(solution)/shard_map/ppermute | solution.py:720
  12.4 3.2 %collective-permute-start.7 = (f32[3,18,8,128]{3,2,1,0:T(8,128)S(1)}, f32[3,18,8,128]{3,2,1,0:T(8,128)S(1)}, u32[]{:S(2)}, u32[]{:S(2)}) collective-permute-start(f32[3,18,8,128]{3,2,1,0:T(8,128)S(1)} %get-tuple-element.51), channel_id=1, source_target_pairs={{0,1},{1,0},{2,3},{3,2},{4,5},{5,4},{6,7},{7,6},{8,9},{9,8},{10,11... | collective-permute-start | bytes 663560 | tf_op jit(solution)/shard_map/ppermute | solution.py:737
  13.7 3.2 %collective-permute-start.8 = (f32[3,4,8,128]{3,2,1,0:T(8,128)S(1)}, f32[3,4,8,128]{3,2,1,0:T(8,128)S(1)}, u32[]{:S(2)}, u32[]{:S(2)}) collective-permute-start(f32[3,4,8,128]{3,2,1,0:T(8,128)S(1)} %get-tuple-element.55), channel_id=1, source_target_pairs={{0,1},{1,0},{2,3},{3,2},{4,5},{5,4},{6,7},{7,6},{8,9},{9,8},{10,11... | collective-permute-start | bytes 147464 | tf_op jit(solution)/shard_map/ppermute | solution.py:757

commit v8 on v7

--- a/solution.py
+++ b/solution.py
@@ -206,9 +206,11 @@
         fib_ref[a] = found[:, a * depth : (a + 1) * depth]
 
 
-def tension_kernel(sec_hbm, map_hbm, plain, edge_ten, main, gate, late, map_ref, sems):
+def tension_kernel(
+    sec_hbm, map_hbm, list_hbm, plain, edge_ten, list_ref, main, gate, late, map_ref, sems
+):
     size_x, size_y = sec_hbm.shape[1], sec_hbm.shape[2]
-    pieces = (sems.shape[0] - 1) // 3
+    pieces = (sems.shape[0] - 2) // 3
     chunk = size_x // pieces
 
     def plane(x, carry):
@@ -222,13 +224,16 @@
 
     @pl.when(electric())
     def _():
-        places = pltpu.make_async_copy(map_hbm, map_ref, sems.at[0])
+        small = [
+            pltpu.make_async_copy(src, dst, sems.at[i])
+            for i, (src, dst) in enumerate(((map_hbm, map_ref), (list_hbm, list_ref)))
+        ]
         copies = []
         for i in range(pieces):
             here = pl.ds(i * chunk, chunk)
             copies.append(
                 [
-                    pltpu.make_async_copy(sec_hbm.at[src, here], dst.at[:, here], sems.at[1 + 3 * i + k])
+                    pltpu.make_async_copy(sec_hbm.at[src, here], dst.at[:, here], sems.at[2 + 3 * i + k])
                     for k, (src, dst) in enumerate(
                         ((pl.ds(0, 3), main), (pl.ds(3, 1), gate), (pl.ds(6, 2), late))
                     )
@@ -236,12 +241,14 @@
             )
             for copy in copies[-1]:
                 copy.start()
-        places.start()
+        for copy in small:
+            copy.start()
         for i in range(pieces):
             for copy in copies[i]:
                 copy.wait()
             lax.fori_loop(i * chunk, (i + 1) * chunk, plane, 0, unroll=2)
-        places.wait()
+        for copy in small:
+            copy.wait()
         last = (size_x - 1) * size_y
         for p in range(size_y):
             edge_ten[0, p : p + 1, :] = plain[pl.ds(map_ref[p], 1), :]
@@ -265,29 +272,21 @@
     lax.fori_loop(0, size_x, plane, 0, unroll=4)
 
 
-def gather_kernel(map_hbm, plain, all_ref, out_hbm, map_ref, sems):
+def gather_kernel(plain, list_ref, all_ref):
     @pl.when(electric())
     def _():
-        size_x, size_y = out_hbm.shape[2], out_hbm.shape[3]
-        places = pltpu.make_async_copy(map_hbm, map_ref, sems.at[0])
-        places.start()
-        copies = [
-            pltpu.make_async_copy(plain.at[x * size_y : (x + 1) * size_y], out_hbm.at[0, 3, x], sems.at[1 + x])
-            for x in range(size_x)
-        ]
-        for copy in copies:
-            copy.start()
-        places.wait()
-
-        def rows(i, carry):
-            for k in range(32):
-                p = i * 32 + k
-                all_ref[pl.ds(p, 1), :] = plain[pl.ds(map_ref[p], 1), :]
-            return carry
-
-        lax.fori_loop(0, all_ref.shape[0] // 32, rows, 0)
-        for copy in copies:
-            copy.wait()
+        columns, depth = plain.shape
+        pick = (lax.broadcasted_iota(jnp.int32, (columns, columns), 0) == list_ref[...]).astype(F32)
+        values = plain[...]
+        high = values.astype(jnp.bfloat16).astype(F32)
+        mid = (values - high).astype(jnp.bfloat16).astype(F32)
+        moved = lax.dot_general(
+            pick,
+            jnp.concatenate([high, mid, values - high - mid], axis=1),
+            (((0,), (0,)), ((), ())),
+            preferred_element_type=F32,
+        )
+        all_ref[...] = moved[:, :depth] + moved[:, depth : 2 * depth] + moved[:, 2 * depth :]
 
 
 def message_electric(pad_in, own, side_ref, cls_ref, ang_ref, after, high_ref, low_ref, pad, fib_ref, flat):
@@ -351,11 +350,18 @@
     share[a, x] = edges_tile(value)
 
 
-def inner_electric(pad, own, fib_ref, next_pad, share, keep):
+def inner_electric(pad, own, fib_ref, plain, next_pad, share, keep, out_hbm, sems):
     size_x, size_y = own.shape[1], own.shape[2]
 
     @pl.when(electric())
     def _():
+        copies = [
+            pltpu.make_async_copy(plain.at[x * size_y : (x + 1) * size_y], out_hbm.at[0, 3, x], sems.at[x])
+            for x in range(size_x)
+        ]
+        for copy in copies:
+            copy.start()
+
         def plane(x, carry):
             place = place_of(x, size_y)
             v, c, d = [rows_of(pad, a, x + 1, size_y) for a in range(3)]
@@ -379,6 +385,8 @@
             return carry
 
         lax.fori_loop(0, size_x, plane, 0, unroll=2)
+        for copy in copies:
+            copy.wait()
 
 
 def inner_mechanic(
@@ -663,37 +671,29 @@
     places = row_map.reshape(-1)
 
     field = lambda n: pltpu.VMEM((n, size_x, size_y, depth), F32)
-    plain, edge_ten = call(
+    angles = fiber_angles.T
+    plain, edge_ten, own_list = call(
         tension_kernel,
         "tension",
-        (f32(columns, depth), f32(2, size_y, depth)),
-        (hbm(own), hbm(places)),
-        (H, H),
+        (f32(columns, depth), f32(2, size_y, depth), jax.ShapeDtypeStruct((1, columns), jnp.int32)),
+        (hbm(own), hbm(places), hbm(row_map.reshape(1, columns))),
+        (H,) * 3,
         [
             field(3),
             field(1),
             field(2),
             pltpu.SMEM((columns,), jnp.int32),
-            pltpu.SemaphoreType.DMA((1 + 3 * 4,)),
+            pltpu.SemaphoreType.DMA((2 + 3 * 4,)),
         ],
     )
     edge_ten = lax.ppermute(edge_ten, "sec", both)
     pad, share = call(share_kernel, "share", (padded, f32(3, size_x, 8, depth)), (own, plain), (V, V))
     side = lax.ppermute(share, "gy", both)
     result = f32(1, 4, size_x, size_y, depth)
-    gathered, result = call(
-        gather_kernel,
-        "gather",
-        (f32(columns, depth), result),
-        (hbm(places), plain),
-        (H, V),
-        [pltpu.SMEM((columns,), jnp.int32), pltpu.SemaphoreType.DMA((1 + size_x,))],
-        out_spaces=(V, H),
-    )
+    flat = lambda count: pltpu.VMEM((classes.shape[1], count), jnp.int32)
+    (gathered,) = call(gather_kernel, "gather", (f32(columns, depth),), (plain, own_list), (V, V))
     tension = lax.ppermute(gathered, "sec", both)
     assert depth == CELLS * classes.shape[1]
-    angles = fiber_angles.T
-    flat = lambda count: pltpu.VMEM((classes.shape[1], count), jnp.int32)
     message = f32(VOLT_ROWS, depth)
     high, low, pad, fib = call(
         message_electric,
@@ -718,12 +718,14 @@
     )
     got_low = lax.ppermute(high, axes, ring(1, 1))
     got_high = lax.ppermute(low, axes, ring(1, -1))
-    moved, share, keep = call(
+    moved, share, keep, result = call(
         inner_electric,
         "inner_electric",
-        (padded, f32(3, size_x + 2, 8, depth), f32(4, size_x, size_y, depth)),
-        (pad, own, fib),
-        (V,) * 3,
+        (padded, f32(3, size_x + 2, 8, depth), f32(4, size_x, size_y, depth), result),
+        (pad, own, fib, plain),
+        (V,) * 4,
+        [pltpu.SemaphoreType.DMA((size_x,))],
+        out_spaces=(V, V, V, H),
     )
     moved, share, keep = call(
         inner_mechanic,

time: 17.9 us -> 17.6 us (0.983)
  waiting for transfers between devices: 0.89 us -> 0.59 us
    ppermute x1, starting transfers between devices: 1.6 us -> 0.92 us  [local(): tension = lax.ppermute(gathered, 'sec', both)]
    ppermute x1, starting transfers between devices: 1.77 us -> 2.17 us  [local(): got_low = lax.ppermute(high, axes, ring(1, 1))]
    ppermute x1, waiting for transfers between devices: 0.6 us -> 0.23 us  [local(): tension = lax.ppermute(gathered, 'sec', both)]
    ppermute x2, starting transfers between devices: 1.54 us -> 1.75 us  [local(): side = lax.ppermute(share, 'gy', both)]
  transfers between devices with their start and end apart: 9 -> 9, of which waited for: 2 -> 3; matrix products, arithmetic and copies ran while one was open for 0% -> 0% of each run, Pallas kernels for 22% -> 22%
where the time goes in v8:
time: 17.6 us; the launch traced here: 17.5 us
  starting transfers between devices  11.6 us (66%)
  Pallas kernels  4.84 us (27%)
  waiting for transfers between devices  0.59 us (3%)
  local copies, waits for them, and re-layouts  0.31 us (2%)
    pallas_call x11, Pallas kernels, call(): pl.pallas_call(kernel, name=name, out_shape=tuple(out_shape), in_specs=[p...  4.84 us
    ppermute x1, starting transfers between devices, local(): got_high = lax.ppermute(low, axes, ring(1, -1))  3.1 us
    ppermute x1, starting transfers between devices, local(): got_low = lax.ppermute(high, axes, ring(1, 1))  2.17 us
    ppermute x1, starting transfers between devices, local(): end_side = lax.ppermute(share, 'gy', both)  1.91 us
    ppermute x2, starting transfers between devices, local(): side = lax.ppermute(share, 'gy', both)  1.75 us
    ppermute x1, starting transfers between devices, local(): edge_ten = lax.ppermute(edge_ten, 'sec', both)  1.23 us
    ppermute x1, starting transfers between devices, local(): tension = lax.ppermute(gathered, 'sec', both)  0.92 us
    ppermute x1, starting transfers between devices, local(): volt_low = lax.ppermute(high, axes, ring(0, 1))  0.43 us
  transfers between devices with their start and end apart: 9, of which 3 were waited for; matrix products, arithmetic and copies ran while one was open for 0% of the time, Pallas kernels for 22%

profile of v8, /device:TPU:3, one launch (start us, length us, event | category | flops | bytes accessed | tf_op | source)
XLA Modules:
  0.0 17.5 jit_solution(13844940438939050722)
XLA Ops:
  0.0 0.1 tension.1
  0.1 1.2 %collective-permute-start.1 = (f32[2,32,128]{2,1,0:T(8,128)S(1)}, f32[2,32,128]{2,1,0:T(8,128)S(1)}, u32[]{:S(2)}, u32[]{:S(2)}) collective-permute-start(f32[2,32,128]{2,1,0:T(8,128)S(1)} %get-tuple-element.38), channel_id=1, source_target_pairs={{0,16},{16,0},{1,17},{17,1},{2,18},{18,2},{3,19},{19,3},{4,20},{20... | collective-permute-start | bytes 98312 | tf_op jit(solution)/shard_map/ppermute | solution.py:689
  1.4 0.2 %copy-done = f32[1,8,16,32,128]{4,3,2,1,0:T(8,128)S(1)} copy-done((f32[1,8,16,32,128]{4,3,2,1,0:T(8,128)S(1)}, f32[1,8,16,32,128]{4,3,2,1,0:T(8,128)}, u32[]{:S(2)}) %copy-start) | copy-done | bytes 2097176
  1.6 0.1 share.1
  1.7 0.7 %collective-permute-start = (f32[3,16,8,128]{3,2,1,0:T(8,128)S(1)}, f32[3,16,8,128]{3,2,1,0:T(8,128)S(1)}, u32[]{:S(2)}, u32[]{:S(2)}) collective-permute-start(f32[3,16,8,128]{3,2,1,0:T(8,128)S(1)} %get-tuple-element.34), channel_id=1, source_target_pairs={{0,1},{1,0},{2,3},{3,2},{4,5},{5,4},{6,7},{7,6},{8,9},{9,8},{10,11... | collective-permute-start | bytes 589832 | tf_op jit(solution)/shard_map/ppermute | solution.py:691
  2.4 0.9 %collective-permute-start.6 = (f32[512,128]{1,0:T(8,128)S(1)}, f32[512,128]{1,0:T(8,128)S(1)}, u32[]{:S(2)}, u32[]{:S(2)}) collective-permute-start(f32[512,128]{1,0:T(8,128)S(1)} %gather.1.after), channel_id=1, source_target_pairs={{0,16},{16,0},{1,17},{17,1},{2,18},{18,2},{3,19},{19,3},{4,20},{20... | collective-permute-start | bytes 786440 | tf_op jit(solution)/shard_map/ppermute | solution.py:695
  3.3 0.1 collective-permute-done.side_ref
  3.5 0.4 %collective-permute-start.4 = (f32[168,128]{1,0:T(8,128)S(1)}, f32[168,128]{1,0:T(8,128)S(1)}, u32[]{:S(2)}, u32[]{:S(2)}) collective-permute-start(f32[168,128]{1,0:T(8,128)S(1)} %get-tuple-element.42), channel_id=1, source_target_pairs={{0,2},{1,3},{2,4},{3,5},{4,6},{5,7},{6,8},{7,9},{8,10},{9,11},{10,... | collective-permute-start | bytes 258056 | tf_op jit(solution)/shard_map/ppermute | solution.py:707
  4.0 0.1 collective-permute-start.5
  4.1 0.0 collective-permute-done.1.ten_ref
  4.1 0.1 copy-done.3
  4.2 0.4 %message_mechanic.1 = (f32[232,128]{1,0:T(8,128)S(1)}, f32[232,128]{1,0:T(8,128)S(1)}, f32[3,18,48,128]{3,2,1,0:T(8,128)S(1)}) custom-call(f32[3,18,48,128]{3,2,1,0:T(8,128)S(1)} %get-tuple-element.37.pad_in, f32[8,16,32,128]{3,2,1,0:T(8,128)S(1)} %bitcast.11, f32[3,16,8,128]{3,2,1,0:T(8,128)S(1)} %collective-permute-done.side_ref, ...), custom_call_target="tpu_custom_call", output_to_operand_aliasing={{2}: (0, {})} | custom-call | flops 10000000000 | bytes 10000000 | tf_op jit(solution)/shard_map/message_mechanic/pallas_call | solution.py:633
  4.5 2.2 %collective-permute-start.2 = (f32[232,128]{1,0:T(8,128)S(1)}, f32[232,128]{1,0:T(8,128)S(1)}, u32[]{:S(2)}, u32[]{:S(2)}) collective-permute-start(f32[232,128]{1,0:T(8,128)S(1)} %get-tuple-element.39), channel_id=1, source_target_pairs={{16,18},{17,19},{18,20},{19,21},{20,22},{21,23},{22,24},{23,25},{2... | collective-permute-start | bytes 356360 | tf_op jit(solution)/shard_map/ppermute | solution.py:719
  6.7 3.1 %collective-permute-start.3 = (f32[232,128]{1,0:T(8,128)S(1)}, f32[232,128]{1,0:T(8,128)S(1)}, u32[]{:S(2)}, u32[]{:S(2)}) collective-permute-start(f32[232,128]{1,0:T(8,128)S(1)} %get-tuple-element.40), channel_id=1, source_target_pairs={{16,30},{17,31},{18,16},{19,17},{20,18},{21,19},{22,20},{23,21},{2... | collective-permute-start | bytes 356360 | tf_op jit(solution)/shard_map/ppermute | solution.py:720
  9.8 0.1 inner_electric.1
  10.0 0.2 %collective-permute-done.6.ten_ref = f32[512,128]{1,0:T(8,128)S(1)} collective-permute-done((f32[512,128]{1,0:T(8,128)S(1)}, f32[512,128]{1,0:T(8,128)S(1)}, u32[]{:S(2)}, u32[]{:S(2)}) %collective-permute-start.6) | collective-permute-done | bytes 262176 | tf_op jit(solution)/shard_map/ppermute | solution.py:695
  10.2 1.6 %inner_mechanic.1 = (f32[3,18,48,128]{3,2,1,0:T(8,128)S(1)}, f32[3,18,8,128]{3,2,1,0:T(8,128)S(1)}, f32[4,16,32,128]{3,2,1,0:T(8,128)S(1)}) custom-call(f32[3,18,48,128]{3,2,1,0:T(8,128)S(1)} %get-tuple-element.41.pad, f32[8,16,32,128]{3,2,1,0:T(8,128)S(1)} %bitcast.13, ...), custom_call_target="tpu_custom_call", output_to_operand_aliasing={{0}: (5, {}), {1}: (6, {}), {2}: (7, {})} | custom-call | flops 60000002048 | bytes 60000000 | tf_op jit(solution)/shard_map/inner_mechanic/pallas_call | solution.py:633
  11.8 1.0 %collective-permute-start.7 = (f32[3,18,8,128]{3,2,1,0:T(8,128)S(1)}, f32[3,18,8,128]{3,2,1,0:T(8,128)S(1)}, u32[]{:S(2)}, u32[]{:S(2)}) collective-permute-start(f32[3,18,8,128]{3,2,1,0:T(8,128)S(1)} %get-tuple-element.51), channel_id=1, source_target_pairs={{0,1},{1,0},{2,3},{3,2},{4,5},{5,4},{6,7},{7,6},{8,9},{9,8},{10,11... | collective-permute-start | bytes 663560 | tf_op jit(solution)/shard_map/ppermute | solution.py:739
  12.9 0.2 %collective-permute-done.2.got_low = f32[232,128]{1,0:T(8,128)S(1)} collective-permute-done((f32[232,128]{1,0:T(8,128)S(1)}, f32[232,128]{1,0:T(8,128)S(1)}, u32[]{:S(2)}, u32[]{:S(2)}) %collective-permute-start.2) | collective-permute-done | bytes 118816 | tf_op jit(solution)/shard_map/ppermute | solution.py:719
  13.1 0.0 collective-permute-done.3.got_high
  13.1 0.3 %outer_mechanic.1 = (f32[3,18,48,128]{3,2,1,0:T(8,128)S(1)}, f32[3,4,8,128]{3,2,1,0:T(8,128)S(1)}) custom-call(f32[3,18,48,128]{3,2,1,0:T(8,128)S(1)} %get-tuple-element.41.pad, f32[8,16,32,128]{3,2,1,0:T(8,128)S(1)} %bitcast.15, s32[2,1,32]{2,1,0:T(1,128)S(1)} %bitcast.24, ...), custom_call_target="tpu_custom_call", output_to_operand_aliasing={{0}: (5, {}), {1}: (6, {})} | custom-call | flops 10000000000 | bytes 10000000 | tf_op jit(solution)/shard_map/outer_mechanic/pallas_call | solution.py:633
  13.3 1.9 %collective-permute-start.8 = (f32[3,4,8,128]{3,2,1,0:T(8,128)S(1)}, f32[3,4,8,128]{3,2,1,0:T(8,128)S(1)}, u32[]{:S(2)}, u32[]{:S(2)}) collective-permute-start(f32[3,4,8,128]{3,2,1,0:T(8,128)S(1)} %get-tuple-element.55), channel_id=1, source_target_pairs={{0,1},{1,0},{2,3},{3,2},{4,5},{5,4},{6,7},{7,6},{8,9},{9,8},{10,11... | collective-permute-start | bytes 147464 | tf_op jit(solution)/shard_map/ppermute | solution.py:759
  15.2 1.3 %middle.1 = (f32[1,4,16,32,128]{4,3,2,1,0:T(8,128)}, f32[3,18,48,128]{3,2,1,0:T(8,128)S(1)}, f32[6,32,128]{2,1,0:T(8,128)S(1)}) custom-call(f32[3,512,128]{2,1,0:T(8,128)S(1)} %get-tuple-element.36.fib_ref, f32[8,16,32,128]{3,2,1,0:T(8,128)S(1)} %bitcast.16, s32[2,1,32]{2,1,0:T(1,128)S(1)} %bitcast.25, ...), custom_call_target="tpu_custom_call", output_to_operand_aliasing={{1}: (5, {}), {0}: (8, {})} | custom-call | flops 60000002048 | bytes 60000000 | tf_op jit(solution)/shard_map/middle/pallas_call | solution.py:633
  16.6 0.9 %last.1 = (f32[1,4,16,32,128]{4,3,2,1,0:T(8,128)}, f32[3,18,48,128]{3,2,1,0:T(8,128)S(1)}) custom-call(f32[3,512,128]{2,1,0:T(8,128)S(1)} %get-tuple-element.36.fib_ref, f32[3,18,48,128]{3,2,1,0:T(8,128)S(1)} %get-tuple-element.54.next_in, f32[3,4,8,128]{3,2,1,0:T(8,128)S(1)} %collective-permute-done.8.side_ref, ...), custom_call_target="tpu_custom_call", output_to_operand_aliasing={{1}: (1, {}), {0}: (5, {})} | custom-call | flops 10000000000 | bytes 10000000 | tf_op jit(solution)/shard_map/last/pallas_call | solution.py:633
  (13 shorter events, 0.1 us)
Async XLA Ops:
  0.0 1.6 %copy-start = (f32[1,8,16,32,128]{4,3,2,1,0:T(8,128)S(1)}, f32[1,8,16,32,128]{4,3,2,1,0:T(8,128)}, u32[]{:S(2)}) copy-start(f32[1,8,16,32,128]{4,3,2,1,0:T(8,128)} %param.5) | copy-start | bytes 6291460
  0.1 4.0 %collective-permute-start.1 = (f32[2,32,128]{2,1,0:T(8,128)S(1)}, f32[2,32,128]{2,1,0:T(8,128)S(1)}, u32[]{:S(2)}, u32[]{:S(2)}) collective-permute-start(f32[2,32,128]{2,1,0:T(8,128)S(1)} %get-tuple-element.38), channel_id=1, source_target_pairs={{0,16},{16,0},{1,17},{17,1},{2,18},{18,2},{3,19},{19,3},{4,20},{20... | collective-permute-start | bytes 98312 | tf_op jit(solution)/shard_map/ppermute | solution.py:689
  1.7 1.8 %collective-permute-start = (f32[3,16,8,128]{3,2,1,0:T(8,128)S(1)}, f32[3,16,8,128]{3,2,1,0:T(8,128)S(1)}, u32[]{:S(2)}, u32[]{:S(2)}) collective-permute-start(f32[3,16,8,128]{3,2,1,0:T(8,128)S(1)} %get-tuple-element.34), channel_id=1, source_target_pairs={{0,1},{1,0},{2,3},{3,2},{4,5},{5,4},{6,7},{7,6},{8,9},{9,8},{10,11... | collective-permute-start | bytes 589832 | tf_op jit(solution)/shard_map/ppermute | solution.py:691
  2.4 1.1 %copy-start.1 = (s32[16,32,8]{1,2,0:T(8,128)S(1)}, s32[16,32,8]{1,2,0:T(8,128)}, u32[]{:S(2)}) copy-start(s32[16,32,8]{1,2,0:T(8,128)} %param.7) | copy-start | bytes 49156
  2.4 1.1 %copy-start.2 = (f32[8,2]{0,1:T(2,128)S(1)}, f32[8,2]{0,1:T(2,128)}, u32[]{:S(2)}) copy-start(f32[8,2]{0,1:T(2,128)} %param.6) | copy-start | bytes 196
  2.4 7.8 %collective-permute-start.6 = (f32[512,128]{1,0:T(8,128)S(1)}, f32[512,128]{1,0:T(8,128)S(1)}, u32[]{:S(2)}, u32[]{:S(2)}) collective-permute-start(f32[512,128]{1,0:T(8,128)S(1)} %gather.1.after), channel_id=1, source_target_pairs={{0,16},{16,0},{1,17},{17,1},{2,18},{18,2},{3,19},{19,3},{4,20},{20... | collective-permute-start | bytes 786440 | tf_op jit(solution)/shard_map/ppermute | solution.py:695
  3.5 0.7 %copy-start.3 = (s32[2,1,1,32]{3,2,1,0:T(1,128)S(1)}, s32[2,1,1,32]{3,2,1,0:T(1,128)}, u32[]{:S(2)}) copy-start(s32[2,1,1,32]{3,2,1,0:T(1,128)} %param.9) | copy-start | bytes 772
  3.5 9.3 %collective-permute-start.4 = (f32[168,128]{1,0:T(8,128)S(1)}, f32[168,128]{1,0:T(8,128)S(1)}, u32[]{:S(2)}, u32[]{:S(2)}) collective-permute-start(f32[168,128]{1,0:T(8,128)S(1)} %get-tuple-element.42), channel_id=1, source_target_pairs={{0,2},{1,3},{2,4},{3,5},{4,6},{5,7},{6,8},{7,9},{8,10},{9,11},{10,... | collective-permute-start | bytes 258056 | tf_op jit(solution)/shard_map/ppermute | solution.py:707
  4.0 8.9 %collective-permute-start.5 = (f32[168,128]{1,0:T(8,128)S(1)}, f32[168,128]{1,0:T(8,128)S(1)}, u32[]{:S(2)}, u32[]{:S(2)}) collective-permute-start(f32[168,128]{1,0:T(8,128)S(1)} %get-tuple-element.43), channel_id=1, source_target_pairs={{0,14},{1,15},{2,0},{3,1},{4,2},{5,3},{6,4},{7,5},{8,6},{9,7},{10,... | collective-permute-start | bytes 258056 | tf_op jit(solution)/shard_map/ppermute | solution.py:708
  4.5 8.5 %collective-permute-start.2 = (f32[232,128]{1,0:T(8,128)S(1)}, f32[232,128]{1,0:T(8,128)S(1)}, u32[]{:S(2)}, u32[]{:S(2)}) collective-permute-start(f32[232,128]{1,0:T(8,128)S(1)} %get-tuple-element.39), channel_id=1, source_target_pairs={{16,18},{17,19},{18,20},{19,21},{20,22},{21,23},{22,24},{23,25},{2... | collective-permute-start | bytes 356360 | tf_op jit(solution)/shard_map/ppermute | solution.py:719
  6.7 6.3 %collective-permute-start.3 = (f32[232,128]{1,0:T(8,128)S(1)}, f32[232,128]{1,0:T(8,128)S(1)}, u32[]{:S(2)}, u32[]{:S(2)}) collective-permute-start(f32[232,128]{1,0:T(8,128)S(1)} %get-tuple-element.40), channel_id=1, source_target_pairs={{16,30},{17,31},{18,16},{19,17},{20,18},{21,19},{22,20},{23,21},{2... | collective-permute-start | bytes 356360 | tf_op jit(solution)/shard_map/ppermute | solution.py:720
  11.8 3.4 %collective-permute-start.7 = (f32[3,18,8,128]{3,2,1,0:T(8,128)S(1)}, f32[3,18,8,128]{3,2,1,0:T(8,128)S(1)}, u32[]{:S(2)}, u32[]{:S(2)}) collective-permute-start(f32[3,18,8,128]{3,2,1,0:T(8,128)S(1)} %get-tuple-element.51), channel_id=1, source_target_pairs={{0,1},{1,0},{2,3},{3,2},{4,5},{5,4},{6,7},{7,6},{8,9},{9,8},{10,11... | collective-permute-start | bytes 663560 | tf_op jit(solution)/shard_map/ppermute | solution.py:739
  13.3 3.3 %collective-permute-start.8 = (f32[3,4,8,128]{3,2,1,0:T(8,128)S(1)}, f32[3,4,8,128]{3,2,1,0:T(8,128)S(1)}, u32[]{:S(2)}, u32[]{:S(2)}) collective-permute-start(f32[3,4,8,128]{3,2,1,0:T(8,128)S(1)} %get-tuple-element.55), channel_id=1, source_target_pairs={{0,1},{1,0},{2,3},{3,2},{4,5},{5,4},{6,7},{7,6},{8,9},{9,8},{10,11... | collective-permute-start | bytes 147464 | tf_op jit(solution)/shard_map/ppermute | solution.py:759

commit v9 on v8

--- a/solution.py
+++ b/solution.py
@@ -13,6 +13,7 @@
     "tension": 0.001,
     "share": 0.001,
     "gather": 6,
+    "edge": 1,
     "message_electric": 1,
     "message_mechanic": 1,
     "inner_electric": 6,
@@ -173,44 +174,47 @@
     return lax.axis_index("sec") == 0
 
 
-def fiber_fields(angles, cls):
-    blocks, classes = cls.shape[0], angles.shape[1]
-    depth = CELLS * blocks
+def fiber_table(angles, blocks):
+    classes, depth = angles.shape[1], CELLS * blocks
     azimuth, elevation = angles[0:1, :], angles[1:2, :]
     flat_part = jnp.cos(elevation)
     fib = [jnp.cos(azimuth) * flat_part, jnp.sin(azimuth) * flat_part, jnp.sin(elevation)]
     own = lax.broadcasted_iota(jnp.int32, (blocks, depth), 1) // CELLS
     own = own == lax.broadcasted_iota(jnp.int32, (blocks, depth), 0)
-    hits = jnp.concatenate([(cls == k).astype(F32) for k in range(classes)], axis=0)
-    table = jnp.concatenate(
-        [
-            jnp.concatenate(
-                [jnp.where(own, jnp.broadcast_to(w[:, k : k + 1], own.shape), 0.0) for w in fib], axis=1
-            )
-            for k in range(classes)
-        ],
-        axis=0,
-    )
-    return lax.dot_general(
-        jnp.concatenate([hits] * 3, axis=0), in_three(table), (((0,), (0,)), ((), ())), preferred_element_type=F32
-    )
-
-
-def all_fibers(ang_ref, cls_ref, flat, fib_ref):
+    return in_three(
+        jnp.concatenate(
+            [
+                jnp.concatenate(
+                    [jnp.where(own, jnp.broadcast_to(w[:, k : k + 1], own.shape), 0.0) for w in fib], axis=1
+                )
+                for k in range(classes)
+            ],
+            axis=0,
+        )
+    )
+
+
+def fiber_fields(table, cls):
+    classes = table.shape[0] // (3 * cls.shape[0])
+    hits = jnp.concatenate([(cls == k).astype(F32) for k in range(classes)] * 3, axis=0)
+    return lax.dot_general(hits, table, (((0,), (0,)), ((), ())), preferred_element_type=F32)
+
+
+def all_fibers(table_ref, cls_ref, flat, fib_ref):
     size_x, _, size_y = cls_ref.shape
     depth = fib_ref.shape[2]
     for x in range(size_x):
         flat[:, x * size_y : (x + 1) * size_y] = cls_ref[x]
-    found = fiber_fields(ang_ref[...], flat[...])
+    found = fiber_fields(table_ref[...], flat[...])
     for a in range(3):
         fib_ref[a] = found[:, a * depth : (a + 1) * depth]
 
 
 def tension_kernel(
-    sec_hbm, map_hbm, list_hbm, plain, edge_ten, list_ref, main, gate, late, map_ref, sems
+    sec_hbm, map_hbm, list_hbm, ang_hbm, plain, edge_ten, list_ref, table_ref, main, gate, late, ang_ref, map_ref, sems
 ):
     size_x, size_y = sec_hbm.shape[1], sec_hbm.shape[2]
-    pieces = (sems.shape[0] - 2) // 3
+    pieces = (sems.shape[0] - 3) // 3
     chunk = size_x // pieces
 
     def plane(x, carry):
@@ -226,14 +230,15 @@
     def _():
         small = [
             pltpu.make_async_copy(src, dst, sems.at[i])
-            for i, (src, dst) in enumerate(((map_hbm, map_ref), (list_hbm, list_ref)))
+            for i, (src, dst) in enumerate(((ang_hbm, ang_ref), (map_hbm, map_ref), (list_hbm, list_ref)))
         ]
+        small[0].start()
         copies = []
         for i in range(pieces):
             here = pl.ds(i * chunk, chunk)
             copies.append(
                 [
-                    pltpu.make_async_copy(sec_hbm.at[src, here], dst.at[:, here], sems.at[2 + 3 * i + k])
+                    pltpu.make_async_copy(sec_hbm.at[src, here], dst.at[:, here], sems.at[3 + 3 * i + k])
                     for k, (src, dst) in enumerate(
                         ((pl.ds(0, 3), main), (pl.ds(3, 1), gate), (pl.ds(6, 2), late))
                     )
@@ -241,13 +246,15 @@
             )
             for copy in copies[-1]:
                 copy.start()
-        for copy in small:
+        for copy in small[1:]:
             copy.start()
+        small[0].wait()
+        table_ref[...] = fiber_table(ang_ref[...], main.shape[3] // CELLS)
         for i in range(pieces):
             for copy in copies[i]:
                 copy.wait()
             lax.fori_loop(i * chunk, (i + 1) * chunk, plane, 0, unroll=2)
-        for copy in small:
+        for copy in small[1:]:
             copy.wait()
         last = (size_x - 1) * size_y
         for p in range(size_y):
@@ -272,7 +279,7 @@
     lax.fori_loop(0, size_x, plane, 0, unroll=4)
 
 
-def gather_kernel(plain, list_ref, all_ref):
+def gather_kernel(plain, list_ref, after, all_ref):
     @pl.when(electric())
     def _():
         columns, depth = plain.shape
@@ -289,7 +296,19 @@
         all_ref[...] = moved[:, :depth] + moved[:, depth : 2 * depth] + moved[:, 2 * depth :]
 
 
-def message_electric(pad_in, own, side_ref, cls_ref, ang_ref, after, high_ref, low_ref, pad, fib_ref, flat):
+def edge_kernel(table_in, cls_ref, ang_ref, after, list_ref, edge_fib, table_ref, flat):
+    size_x, blocks, size_y = cls_ref.shape
+
+    @pl.when(jnp.logical_not(electric()))
+    def _():
+        table_ref[...] = fiber_table(ang_ref[...], blocks)
+
+    for which, (_, edge, _) in enumerate(sides(size_x)):
+        flat[:, which * size_y : (which + 1) * size_y] = cls_ref[edge]
+    edge_fib[...] = fiber_fields(table_ref[...], flat[...])
+
+
+def message_electric(pad_in, own, side_ref, edge_fib, high_ref, low_ref, pad):
     size_x, size_y = own.shape[1], own.shape[2]
 
     def fill(x, carry):
@@ -301,11 +320,11 @@
 
     @pl.when(electric())
     def _():
-        all_fibers(ang_ref, cls_ref, flat, fib_ref)
         for which, ((_, edge, _), out) in enumerate(zip(sides(size_x), (low_ref, high_ref))):
             out[ROW_VOLT_SIDE : ROW_VOLT_SIDE + 1, :] = side_ref[0, edge, 7:8, :]
             out[ROW_VOLT_SIDE + 1 : ROW_VOLT_SIDE + 2, :] = side_ref[0, edge, 0:1, :]
-            fib = [fib_ref[a, place_of(edge, size_y), :] for a in range(3)]
+            rows, depth = slice(which * size_y, (which + 1) * size_y), own.shape[3]
+            fib = [edge_fib[rows, a * depth : (a + 1) * depth] for a in range(3)]
             v, c, d = [rows_of(pad, a, edge + 1, size_y) for a in range(3)]
             f, n, r = [own[k, edge] for k in range(3, 6)]
             rate = volt_rate(pad, edge + 1, fib, size_y)
@@ -315,17 +334,12 @@
             for k, value in enumerate(couplings(fib)):
                 out[ROW_COUPLED + k * size_y : ROW_COUPLED + (k + 1) * size_y, :] = value
 
-def message_mechanic(
-    pad_in, own, side_ref, cls_ref, ang_ref, ten_ref, list_ref, high_ref, low_ref, pad, flat
-):
+def message_mechanic(pad_in, own, side_ref, edge_fib, ten_ref, list_ref, high_ref, low_ref, pad):
     size_x, size_y = own.shape[1], own.shape[2]
 
     @pl.when(jnp.logical_not(electric()))
     def _():
         depth = own.shape[3]
-        for which, (_, edge, _) in enumerate(sides(size_x)):
-            flat[:, which * size_y : (which + 1) * size_y] = cls_ref[edge]
-        fibers = fiber_fields(ang_ref[...], flat[...])
         for which, ((_, edge, _), out) in enumerate(zip(sides(size_x), (low_ref, high_ref))):
             out[ROW_LIST : ROW_LIST + 1, 0:size_y] = list_ref[which].astype(F32)
             rate = motion_rate(pad, edge + 1, size_y)
@@ -339,7 +353,7 @@
                 out[row + 1 : row + 2, :] = side_ref[a, edge, 0:1, :]
                 u = rows_of(pad, a, edge + 1, size_y)
                 out[ROW_NOW + a * size_y : ROW_NOW + (a + 1) * size_y, :] = u
-                drive = own[3 + a, edge] + act * fibers[which * size_y : (which + 1) * size_y, a * depth : (a + 1) * depth]
+                drive = own[3 + a, edge] + act * edge_fib[which * size_y : (which + 1) * size_y, a * depth : (a + 1) * depth]
                 out[ROW_NEXT + a * size_y : ROW_NEXT + (a + 1) * size_y, :] = (
                     0.28 * u + beta * drive + OMEGA * rate[a]
                 )
@@ -350,8 +364,12 @@
     share[a, x] = edges_tile(value)
 
 
-def inner_electric(pad, own, fib_ref, plain, next_pad, share, keep, out_hbm, sems):
+def inner_electric(
+    pad, own, plain, cls_ref, table_ref, next_pad, share, keep, out_hbm, fib_ref, flat, sems
+):
     size_x, size_y = own.shape[1], own.shape[2]
+
+    all_fibers(table_ref, cls_ref, flat, fib_ref)
 
     @pl.when(electric())
     def _():
@@ -389,15 +407,11 @@
             copy.wait()
 
 
-def inner_mechanic(
-    pad, own, cls_ref, ang_ref, ten_ref, next_in, share_in, keep_in, next_pad, share, keep, fib_ref, flat
-):
+def inner_mechanic(pad, own, fib_ref, ten_ref, next_in, share_in, keep_in, next_pad, share, keep):
     size_x, size_y = own.shape[1], own.shape[2]
 
     @pl.when(jnp.logical_not(electric()))
     def _():
-        all_fibers(ang_ref, cls_ref, flat, fib_ref)
-
         def plane(x, carry):
             place = place_of(x, size_y)
             rate = motion_rate(pad, x + 1, size_y)
@@ -507,21 +521,21 @@
     out[2, x] = (1.0 - DT) * n + (0.5 * DT) * (1.0 + jnp.tanh(v))
 
 
-def mechanic_end(x, next_pad, keep, out, size_y, ties=None):
+def mechanic_end(x, next_pad, keep, size_y):
     rate = motion_rate(next_pad, x + 1, size_y)
-    for a in range(3):
-        u = rows_of(next_pad, a, x + 1, size_y)
-        value = 0.4 * u + keep[a, x] + OMEGA * rate[a]
-        out[a, x] = value if ties is None else value + ties[a]
+    return [
+        0.4 * rows_of(next_pad, a, x + 1, size_y) + keep[a, x] + OMEGA * rate[a] for a in range(3)
+    ]
 
 
 def middle_kernel(
-    fib_ref, own, list_ref, got_low, got_high, next_in, side_ref, keep, out_in, out_hbm, next_pad, held, out, sems
+    fib_ref, own, list_ref, got_low, got_high, next_in, side_ref, keep, out_in,
+    out_hbm, next_pad, held, final, out, sems
 ):
     size_x = keep.shape[1]
     size_y = fib_ref.shape[1] // size_x
-    pieces = sems.shape[0] - 1
-    chunk = (size_x - 4) // pieces
+    pieces = sems.shape[0]
+    chunk = final.shape[1]
 
     def copy_out(i, fields):
         here = pl.ds(2 + i * chunk, chunk)
@@ -544,7 +558,7 @@
             return carry
 
         lax.fori_loop(0, size_x, rest, 0, unroll=2)
-        copy = pltpu.make_async_copy(out.at[1:3], out_hbm.at[0, 1:3], sems.at[pieces])
+        copy = pltpu.make_async_copy(out.at[1:3], out_hbm.at[0, 1:3], sems.at[pieces - 1])
         copy.start()
         for i, x in enumerate((0, 1, size_x - 2, size_x - 1)):
             held[i] = out[0, x]
@@ -556,24 +570,29 @@
             copy_out(i, 1).start()
             return carry
 
-        lax.fori_loop(0, pieces, step, 0)
+        lax.fori_loop(0, pieces - 1, step, 0)
+        for k in range(chunk):
+            x = size_x - 2 - chunk + k
+            final[0, k] = out[0, x] + electric_end(x, next_pad, fib_ref)
         copy.wait()
-        for i in range(pieces):
+        for i in range(pieces - 1):
             copy_out(i, 1).wait()
 
     @pl.when(jnp.logical_not(electric()))
     def _():
         fill(3)
-        copy = pltpu.make_async_copy(keep.at[3:4], out_hbm.at[0, 3:4], sems.at[pieces])
+        copy = pltpu.make_async_copy(keep.at[3:4], out_hbm.at[0, 3:4], sems.at[pieces - 1])
         copy.start()
 
         def sweep(i, carry):
             for k in range(chunk):
-                mechanic_end(2 + i * chunk + k, next_pad, keep, out, size_y)
+                x = 2 + i * chunk + k
+                for a, value in enumerate(mechanic_end(x, next_pad, keep, size_y)):
+                    out[a, x] = value
             copy_out(i, 3).start()
             return carry
 
-        lax.fori_loop(0, pieces, sweep, 0)
+        lax.fori_loop(0, pieces - 1, sweep, 0)
         for which, ((halo, edge, _), got) in enumerate(zip(sides(size_x), (got_low, got_high))):
             beta = OMEGA * inverse(own[6, edge])
             ties = tie_rows(
@@ -583,13 +602,16 @@
             )
             for a in range(3):
                 held[3 * which + a] = beta * ties[a] - 0.12 * rows_of(next_pad, a, edge + 1, size_y)
+        for k in range(chunk):
+            for a, value in enumerate(mechanic_end(size_x - 2 - chunk + k, next_pad, keep, size_y)):
+                final[a, k] = value
         copy.wait()
-        for i in range(pieces):
+        for i in range(pieces - 1):
             copy_out(i, 3).wait()
 
 
 def last_kernel(
-    fib_ref, next_in, side_ref, keep, held, out_in, out_hbm, next_pad, out, sems
+    fib_ref, next_in, side_ref, keep, held, final, out_in, out_hbm, next_pad, out, sems
 ):
     size_x = keep.shape[1]
     size_y = fib_ref.shape[1] // size_x
@@ -597,6 +619,10 @@
     def copy_out(which, first, fields):
         here = pl.ds(first, 2)
         return pltpu.make_async_copy(out.at[0:fields, here], out_hbm.at[0, 0:fields, here], sems.at[which])
+
+    def copy_final(fields):
+        here = pl.ds(size_x - 2 - final.shape[1], final.shape[1])
+        return pltpu.make_async_copy(final.at[0:fields], out_hbm.at[0, 0:fields, here], sems.at[2])
 
     work = []
     for which, (halo, edge, _) in enumerate(sides(size_x)):
@@ -605,6 +631,7 @@
 
     @pl.when(electric())
     def _():
+        copy_final(1).start()
         for halo, edge, near, which, first in work:
             fill_sides(next_pad, 0, halo, side_ref[0, 3 * which], size_y)
             fill_sides(next_pad, 0, edge + 1, side_ref[0, 1 + which], size_y)
@@ -613,18 +640,23 @@
             copy_out(which, first, 1).start()
         for item in work:
             copy_out(item[3], item[-1], 1).wait()
+        copy_final(1).wait()
 
     @pl.when(jnp.logical_not(electric()))
     def _():
+        copy_final(3).start()
         for halo, edge, near, which, first in work:
             for a in range(3):
                 fill_sides(next_pad, a, halo, side_ref[a, 3 * which], size_y)
                 fill_sides(next_pad, a, edge + 1, side_ref[a, 1 + which], size_y)
-            mechanic_end(near, next_pad, keep, out, size_y)
-            mechanic_end(edge, next_pad, keep, out, size_y, [held[3 * which + a] for a in range(3)])
+            for a, value in enumerate(mechanic_end(near, next_pad, keep, size_y)):
+                out[a, near] = value
+            for a, value in enumerate(mechanic_end(edge, next_pad, keep, size_y)):
+                out[a, edge] = value + held[3 * which + a]
             copy_out(which, first, 3).start()
         for item in work:
             copy_out(item[3], item[-1], 3).wait()
+        copy_final(3).wait()
 
 
 def call(kernel, name, out_shape, operands, spaces, scratch=(), out_spaces=None, aliases=()):
@@ -671,37 +703,51 @@
     places = row_map.reshape(-1)
 
     field = lambda n: pltpu.VMEM((n, size_x, size_y, depth), F32)
+    flat = lambda count: pltpu.VMEM((classes.shape[1], count), jnp.int32)
     angles = fiber_angles.T
-    plain, edge_ten, own_list = call(
+    plain, edge_ten, own_list, table = call(
         tension_kernel,
         "tension",
-        (f32(columns, depth), f32(2, size_y, depth), jax.ShapeDtypeStruct((1, columns), jnp.int32)),
-        (hbm(own), hbm(places), hbm(row_map.reshape(1, columns))),
-        (H,) * 3,
+        (
+            f32(columns, depth),
+            f32(2, size_y, depth),
+            jax.ShapeDtypeStruct((1, columns), jnp.int32),
+            f32(3 * fiber_angles.shape[0] * classes.shape[1], 3 * depth),
+        ),
+        (hbm(own), hbm(places), hbm(row_map.reshape(1, columns)), hbm(angles)),
+        (H,) * 4,
         [
             field(3),
             field(1),
             field(2),
+            pltpu.VMEM(angles.shape, F32),
             pltpu.SMEM((columns,), jnp.int32),
-            pltpu.SemaphoreType.DMA((2 + 3 * 4,)),
+            pltpu.SemaphoreType.DMA((3 + 3 * 4,)),
         ],
     )
     edge_ten = lax.ppermute(edge_ten, "sec", both)
     pad, share = call(share_kernel, "share", (padded, f32(3, size_x, 8, depth)), (own, plain), (V, V))
     side = lax.ppermute(share, "gy", both)
     result = f32(1, 4, size_x, size_y, depth)
-    flat = lambda count: pltpu.VMEM((classes.shape[1], count), jnp.int32)
-    (gathered,) = call(gather_kernel, "gather", (f32(columns, depth),), (plain, own_list), (V, V))
+    (gathered,) = call(gather_kernel, "gather", (f32(columns, depth),), (plain, own_list, share), (V,) * 3)
+    edge_fib, table = call(
+        edge_kernel,
+        "edge",
+        (f32(2 * size_y, 3 * depth), f32(*table.shape)),
+        (table, classes, angles, gathered, lists),
+        (V,) * 5,
+        [flat(2 * size_y)],
+        aliases={0: 1},
+    )
     tension = lax.ppermute(gathered, "sec", both)
     assert depth == CELLS * classes.shape[1]
     message = f32(VOLT_ROWS, depth)
-    high, low, pad, fib = call(
+    high, low, pad = call(
         message_electric,
         "message_electric",
-        (message, message, padded, f32(3, columns, depth)),
-        (pad, own, side, classes, angles, gathered),
-        (V,) * 6,
-        [flat(columns)],
+        (message, message, padded),
+        (pad, own, side, edge_fib),
+        (V,) * 4,
         aliases={0: 2},
     )
     volt_low = lax.ppermute(high, axes, ring(0, 1))
@@ -711,30 +757,28 @@
         message_mechanic,
         "message_mechanic",
         (message, message, padded),
-        (pad, own, side, classes, angles, edge_ten, lists),
-        (V,) * 7,
-        [flat(2 * size_y)],
+        (pad, own, side, edge_fib, edge_ten, lists),
+        (V,) * 6,
         aliases={0: 2},
     )
     got_low = lax.ppermute(high, axes, ring(1, 1))
     got_high = lax.ppermute(low, axes, ring(1, -1))
-    moved, share, keep, result = call(
+    moved, share, keep, result, fib = call(
         inner_electric,
         "inner_electric",
-        (padded, f32(3, size_x + 2, 8, depth), f32(4, size_x, size_y, depth), result),
-        (pad, own, fib, plain),
-        (V,) * 4,
-        [pltpu.SemaphoreType.DMA((size_x,))],
-        out_spaces=(V, V, V, H),
+        (padded, f32(3, size_x + 2, 8, depth), f32(4, size_x, size_y, depth), result, f32(3, columns, depth)),
+        (pad, own, plain, classes, table),
+        (V,) * 5,
+        [flat(columns), pltpu.SemaphoreType.DMA((size_x,))],
+        out_spaces=(V, V, V, H, V),
     )
     moved, share, keep = call(
         inner_mechanic,
         "inner_mechanic",
         (padded, f32(3, size_x + 2, 8, depth), f32(4, size_x, size_y, depth)),
-        (pad, own, classes, angles, tension, moved, share, keep),
-        (V,) * 8,
-        [pltpu.VMEM((3, columns, depth), F32), flat(columns)],
-        aliases={5: 0, 6: 1, 7: 2},
+        (pad, own, fib, tension, moved, share, keep),
+        (V,) * 7,
+        aliases={4: 0, 5: 1, 6: 2},
     )
     side = lax.ppermute(share, "gy", both)
     wide = pltpu.VMEM((3, 2) + padded.shape[2:], F32)
@@ -758,25 +802,27 @@
     )
     end_side = lax.ppermute(share, "gy", both)
     fields = pltpu.VMEM((3, size_x, size_y, depth), F32)
-    result, moved, held = call(
+    pieces = 3
+    chunk = (size_x - 4) // pieces
+    result, moved, held, final = call(
         middle_kernel,
         "middle",
-        (f32(1, 4, size_x, size_y, depth), padded, f32(6, size_y, depth)),
+        (f32(1, 4, size_x, size_y, depth), padded, f32(6, size_y, depth), f32(3, chunk, size_y, depth)),
         (fib, own, lists, got_low, got_high, moved, side, keep, result),
         (V,) * 8 + (H,),
-        [fields, pltpu.SemaphoreType.DMA((4,))],
-        out_spaces=(H, V, V),
+        [fields, pltpu.SemaphoreType.DMA((pieces,))],
+        out_spaces=(H, V, V, V),
         aliases={5: 1, 8: 0},
     )
     return call(
         last_kernel,
         "last",
         (f32(1, 4, size_x, size_y, depth), padded),
-        (fib, moved, end_side, keep, held, result),
-        (V,) * 5 + (H,),
-        [fields, pltpu.SemaphoreType.DMA((2,))],
+        (fib, moved, end_side, keep, held, final, result),
+        (V,) * 6 + (H,),
+        [fields, pltpu.SemaphoreType.DMA((3,))],
         out_spaces=(H, V),
-        aliases={1: 1, 5: 0},
+        aliases={1: 1, 6: 0},
     )[0]
 
 

time: 17.6 us -> 17.4 us (0.989)
  starting transfers between devices: 11.6 us -> 10.7 us
  waiting for transfers between devices: 0.59 us -> 1.46 us
    ppermute x1, waiting for transfers between devices: 0.2 us -> 0.94 us  [local(): got_low = lax.ppermute(high, axes, ring(1, 1))]
    ppermute x1, starting transfers between devices: 1.91 us -> 1.26 us  [local(): end_side = lax.ppermute(share, 'gy', both)]
    ppermute x1, waiting for transfers between devices: 0.01 us -> 0.5 us  [local(): got_high = lax.ppermute(low, axes, ring(1, -1))]
    ppermute x2, starting transfers between devices: 1.75 us -> 1.5 us  [local(): side = lax.ppermute(share, 'gy', both)]
    ppermute x1, waiting for transfers between devices: 0.23 us -> 0.01 us  [local(): tension = lax.ppermute(gathered, 'sec', both)]
    pallas_call x11 -> x12, Pallas kernels: 4.84 us -> 4.8 us  [call(): pl.pallas_call(kernel, name=name, out_shape=tuple(out_shape), in_specs=[p...]
  transfers between devices with their start and end apart: 9 -> 9, of which waited for: 3 -> 2; matrix products, arithmetic and copies ran while one was open for 0% -> 0% of each run, Pallas kernels for 22% -> 22%
where the time goes in v9:
time: 17.4 us; the launch traced here: 17.3 us
  starting transfers between devices  10.7 us (61%)
  Pallas kernels  4.8 us (28%)
  waiting for transfers between devices  1.46 us (8%)
  local copies, waits for them, and re-layouts  0.22 us (1%)
    pallas_call x12, Pallas kernels, call(): pl.pallas_call(kernel, name=name, out_shape=tuple(out_shape), in_specs=[p...  4.8 us
    ppermute x1, starting transfers between devices, local(): got_high = lax.ppermute(low, axes, ring(1, -1))  3.1 us
    ppermute x1, starting transfers between devices, local(): got_low = lax.ppermute(high, axes, ring(1, 1))  2.14 us
    ppermute x2, starting transfers between devices, local(): side = lax.ppermute(share, 'gy', both)  1.5 us
    ppermute x1, starting transfers between devices, local(): end_side = lax.ppermute(share, 'gy', both)  1.26 us
    ppermute x1, starting transfers between devices, local(): edge_ten = lax.ppermute(edge_ten, 'sec', both)  1.24 us
    ppermute x1, waiting for transfers between devices, local(): got_low = lax.ppermute(high, axes, ring(1, 1))  0.94 us
    ppermute x1, starting transfers between devices, local(): tension = lax.ppermute(gathered, 'sec', both)  0.93 us
  transfers between devices with their start and end apart: 9, of which 2 were waited for; matrix products, arithmetic and copies ran while one was open for 0% of the time, Pallas kernels for 22%

profile of v9, /device:TPU:3, one launch (start us, length us, event | category | flops | bytes accessed | tf_op | source)
XLA Modules:
  0.0 17.3 jit_solution(11791394973326181519)
XLA Ops:
  0.0 0.1 tension.1
  0.1 1.2 %collective-permute-start.1 = (f32[2,32,128]{2,1,0:T(8,128)S(1)}, f32[2,32,128]{2,1,0:T(8,128)S(1)}, u32[]{:S(2)}, u32[]{:S(2)}) collective-permute-start(f32[2,32,128]{2,1,0:T(8,128)S(1)} %get-tuple-element.43), channel_id=1, source_target_pairs={{0,16},{16,0},{1,17},{17,1},{2,18},{18,2},{3,19},{19,3},{4,20},{20... | collective-permute-start | bytes 98312 | tf_op jit(solution)/shard_map/ppermute | solution.py:728
  1.4 0.2 %copy-done = f32[1,8,16,32,128]{4,3,2,1,0:T(8,128)S(1)} copy-done((f32[1,8,16,32,128]{4,3,2,1,0:T(8,128)S(1)}, f32[1,8,16,32,128]{4,3,2,1,0:T(8,128)}, u32[]{:S(2)}) %copy-start) | copy-done | bytes 2097176
  1.6 0.1 share.1
  1.7 0.7 %collective-permute-start = (f32[3,16,8,128]{3,2,1,0:T(8,128)S(1)}, f32[3,16,8,128]{3,2,1,0:T(8,128)S(1)}, u32[]{:S(2)}, u32[]{:S(2)}) collective-permute-start(f32[3,16,8,128]{3,2,1,0:T(8,128)S(1)} %get-tuple-element.38.after), channel_id=1, source_target_pairs={{0,1},{1,0},{2,3},{3,2},{4,5},{5,4},{6,7},{7,6},{8,9},{9,8},{10,11... | collective-permute-start | bytes 589832 | tf_op jit(solution)/shard_map/ppermute | solution.py:730
  2.4 0.9 %collective-permute-start.6 = (f32[512,128]{1,0:T(8,128)S(1)}, f32[512,128]{1,0:T(8,128)S(1)}, u32[]{:S(2)}, u32[]{:S(2)}) collective-permute-start(f32[512,128]{1,0:T(8,128)S(1)} %gather.1.after), channel_id=1, source_target_pairs={{0,16},{16,0},{1,17},{17,1},{2,18},{18,2},{3,19},{19,3},{4,20},{20... | collective-permute-start | bytes 786440 | tf_op jit(solution)/shard_map/ppermute | solution.py:742
  3.4 0.5 %edge.1 = (f32[64,384]{1,0:T(8,128)S(1)}, f32[192,384]{1,0:T(8,128)S(1)}) custom-call(f32[192,384]{1,0:T(8,128)S(1)} %get-tuple-element.39.table_in, s32[16,8,32]{2,1,0:T(8,128)S(1)} %bitcast.19, f32[2,8]{1,0:T(2,128)S(1)} %bitcast.18, f32[512,128]{1,0:T(8,128)S(1)} %gather.1.after, s32[2,1,32]{2,1,0:T(1,128)S(1)} %bitcast.21), custom_call_target="tpu_custom_call", output_to_operand_aliasing={{1}: (0, {})} | custom-call | flops 10000000000 | bytes 10000000 | tf_op jit(solution)/shard_map/edge/pallas_call | solution.py:665
  3.9 0.4 %collective-permute-start.4 = (f32[168,128]{1,0:T(8,128)S(1)}, f32[168,128]{1,0:T(8,128)S(1)}, u32[]{:S(2)}, u32[]{:S(2)}) collective-permute-start(f32[168,128]{1,0:T(8,128)S(1)} %get-tuple-element.49), channel_id=1, source_target_pairs={{0,2},{1,3},{2,4},{3,5},{4,6},{5,7},{6,8},{7,9},{8,10},{9,11},{10,... | collective-permute-start | bytes 258056 | tf_op jit(solution)/shard_map/ppermute | solution.py:753
  4.3 0.2 %collective-permute-start.5 = (f32[168,128]{1,0:T(8,128)S(1)}, f32[168,128]{1,0:T(8,128)S(1)}, u32[]{:S(2)}, u32[]{:S(2)}) collective-permute-start(f32[168,128]{1,0:T(8,128)S(1)} %get-tuple-element.50), channel_id=1, source_target_pairs={{0,14},{1,15},{2,0},{3,1},{4,2},{5,3},{6,4},{7,5},{8,6},{9,7},{10,... | collective-permute-start | bytes 258056 | tf_op jit(solution)/shard_map/ppermute | solution.py:754
  4.4 0.0 collective-permute-done.1.ten_ref
  4.4 0.1 message_mechanic.1
  4.6 2.1 %collective-permute-start.2 = (f32[232,128]{1,0:T(8,128)S(1)}, f32[232,128]{1,0:T(8,128)S(1)}, u32[]{:S(2)}, u32[]{:S(2)}) collective-permute-start(f32[232,128]{1,0:T(8,128)S(1)} %get-tuple-element.47), channel_id=1, source_target_pairs={{16,18},{17,19},{18,20},{19,21},{20,22},{21,23},{22,24},{23,25},{2... | collective-permute-start | bytes 356360 | tf_op jit(solution)/shard_map/ppermute | solution.py:764
  6.7 3.1 %collective-permute-start.3 = (f32[232,128]{1,0:T(8,128)S(1)}, f32[232,128]{1,0:T(8,128)S(1)}, u32[]{:S(2)}, u32[]{:S(2)}) collective-permute-start(f32[232,128]{1,0:T(8,128)S(1)} %get-tuple-element.48), channel_id=1, source_target_pairs={{16,30},{17,31},{18,16},{19,17},{20,18},{21,19},{22,20},{23,21},{2... | collective-permute-start | bytes 356360 | tf_op jit(solution)/shard_map/ppermute | solution.py:765
  9.8 0.6 %inner_electric.1 = (f32[3,18,48,128]{3,2,1,0:T(8,128)S(1)}, f32[3,18,8,128]{3,2,1,0:T(8,128)S(1)}, f32[4,16,32,128]{3,2,1,0:T(8,128)S(1)}, f32[1,4,16,32,128]{4,3,2,1,0:T(8,128)}, f32[3,512,128]{2,1,0:T(8,128)S(1)}) custom-call(f32[3,18,48,128]{3,2,1,0:T(8,128)S(1)} %get-tuple-element.44.pad, f32[8,16,32,128]{3,2,1,0:T(8,128)S(1)} %bitcast.12, ...), custom_call_target="tpu_custom_call" | custom-call | flops 60000002048 | bytes 60000000 | tf_op jit(solution)/shard_map/inner_electric/pallas_call | solution.py:665
  10.4 1.1 %inner_mechanic.1 = (f32[3,18,48,128]{3,2,1,0:T(8,128)S(1)}, f32[3,18,8,128]{3,2,1,0:T(8,128)S(1)}, f32[4,16,32,128]{3,2,1,0:T(8,128)S(1)}) custom-call(f32[3,18,48,128]{3,2,1,0:T(8,128)S(1)} %get-tuple-element.44.pad, f32[8,16,32,128]{3,2,1,0:T(8,128)S(1)} %bitcast.13, ...), custom_call_target="tpu_custom_call", output_to_operand_aliasing={{0}: (4, {}), {1}: (5, {}), {2}: (6, {})} | custom-call | flops 60000002048 | bytes 60000000 | tf_op jit(solution)/shard_map/inner_mechanic/pallas_call | solution.py:665
  11.5 0.8 %collective-permute-start.7 = (f32[3,18,8,128]{3,2,1,0:T(8,128)S(1)}, f32[3,18,8,128]{3,2,1,0:T(8,128)S(1)}, u32[]{:S(2)}, u32[]{:S(2)}) collective-permute-start(f32[3,18,8,128]{3,2,1,0:T(8,128)S(1)} %get-tuple-element.58), channel_id=1, source_target_pairs={{0,1},{1,0},{2,3},{3,2},{4,5},{5,4},{6,7},{7,6},{8,9},{9,8},{10,11... | collective-permute-start | bytes 663560 | tf_op jit(solution)/shard_map/ppermute | solution.py:783
  12.3 0.0 collective-permute-done.4.volt_low
  12.3 0.0 collective-permute-done.5.volt_high
  12.3 0.9 %collective-permute-done.2.got_low = f32[232,128]{1,0:T(8,128)S(1)} collective-permute-done((f32[232,128]{1,0:T(8,128)S(1)}, f32[232,128]{1,0:T(8,128)S(1)}, u32[]{:S(2)}, u32[]{:S(2)}) %collective-permute-start.2) | collective-permute-done | bytes 118816 | tf_op jit(solution)/shard_map/ppermute | solution.py:764
  13.2 0.5 %collective-permute-done.3.got_high = f32[232,128]{1,0:T(8,128)S(1)} collective-permute-done((f32[232,128]{1,0:T(8,128)S(1)}, f32[232,128]{1,0:T(8,128)S(1)}, u32[]{:S(2)}, u32[]{:S(2)}) %collective-permute-start.3) | collective-permute-done | bytes 118816 | tf_op jit(solution)/shard_map/ppermute | solution.py:765
  13.7 0.3 %outer_mechanic.1 = (f32[3,18,48,128]{3,2,1,0:T(8,128)S(1)}, f32[3,4,8,128]{3,2,1,0:T(8,128)S(1)}) custom-call(f32[3,18,48,128]{3,2,1,0:T(8,128)S(1)} %get-tuple-element.44.pad, f32[8,16,32,128]{3,2,1,0:T(8,128)S(1)} %bitcast.15, s32[2,1,32]{2,1,0:T(1,128)S(1)} %bitcast.23, ...), custom_call_target="tpu_custom_call", output_to_operand_aliasing={{0}: (5, {}), {1}: (6, {})} | custom-call | flops 10000000000 | bytes 10000000 | tf_op jit(solution)/shard_map/outer_mechanic/pallas_call | solution.py:665
  14.0 1.3 %collective-permute-start.8 = (f32[3,4,8,128]{3,2,1,0:T(8,128)S(1)}, f32[3,4,8,128]{3,2,1,0:T(8,128)S(1)}, u32[]{:S(2)}, u32[]{:S(2)}) collective-permute-start(f32[3,4,8,128]{3,2,1,0:T(8,128)S(1)} %get-tuple-element.62), channel_id=1, source_target_pairs={{0,1},{1,0},{2,3},{3,2},{4,5},{5,4},{6,7},{7,6},{8,9},{9,8},{10,11... | collective-permute-start | bytes 147464 | tf_op jit(solution)/shard_map/ppermute | solution.py:803
  15.2 1.1 %middle.1 = (f32[1,4,16,32,128]{4,3,2,1,0:T(8,128)}, f32[3,18,48,128]{3,2,1,0:T(8,128)S(1)}, f32[6,32,128]{2,1,0:T(8,128)S(1)}, f32[3,4,32,128]{3,2,1,0:T(8,128)S(1)}) custom-call(f32[3,512,128]{2,1,0:T(8,128)S(1)} %get-tuple-element.46.fib_ref, f32[8,16,32,128]{3,2,1,0:T(8,128)S(1)} %bitcast.16, ...), custom_call_target="tpu_custom_call", output_to_operand_aliasing={{1}: (5, {}), {0}: (8, {})} | custom-call | flops 60000002048 | bytes 60000000 | tf_op jit(solution)/shard_map/middle/pallas_call | solution.py:665
  16.4 0.9 %last.1 = (f32[1,4,16,32,128]{4,3,2,1,0:T(8,128)}, f32[3,18,48,128]{3,2,1,0:T(8,128)S(1)}) custom-call(f32[3,512,128]{2,1,0:T(8,128)S(1)} %get-tuple-element.46.fib_ref, f32[3,18,48,128]{3,2,1,0:T(8,128)S(1)} %get-tuple-element.61.next_in, f32[3,4,8,128]{3,2,1,0:T(8,128)S(1)} %collective-permute-done.8.side_ref, ...), custom_call_target="tpu_custom_call", output_to_operand_aliasing={{1}: (1, {}), {0}: (6, {})} | custom-call | flops 10000000000 | bytes 10000000 | tf_op jit(solution)/shard_map/last/pallas_call | solution.py:665
  (14 shorter events, 0.1 us)
Async XLA Ops:
  0.0 1.6 %copy-start = (f32[1,8,16,32,128]{4,3,2,1,0:T(8,128)S(1)}, f32[1,8,16,32,128]{4,3,2,1,0:T(8,128)}, u32[]{:S(2)}) copy-start(f32[1,8,16,32,128]{4,3,2,1,0:T(8,128)} %param.5) | copy-start | bytes 6291460
  0.1 4.3 %collective-permute-start.1 = (f32[2,32,128]{2,1,0:T(8,128)S(1)}, f32[2,32,128]{2,1,0:T(8,128)S(1)}, u32[]{:S(2)}, u32[]{:S(2)}) collective-permute-start(f32[2,32,128]{2,1,0:T(8,128)S(1)} %get-tuple-element.43), channel_id=1, source_target_pairs={{0,16},{16,0},{1,17},{17,1},{2,18},{18,2},{3,19},{19,3},{4,20},{20... | collective-permute-start | bytes 98312 | tf_op jit(solution)/shard_map/ppermute | solution.py:728
  1.7 2.1 %collective-permute-start = (f32[3,16,8,128]{3,2,1,0:T(8,128)S(1)}, f32[3,16,8,128]{3,2,1,0:T(8,128)S(1)}, u32[]{:S(2)}, u32[]{:S(2)}) collective-permute-start(f32[3,16,8,128]{3,2,1,0:T(8,128)S(1)} %get-tuple-element.38.after), channel_id=1, source_target_pairs={{0,1},{1,0},{2,3},{3,2},{4,5},{5,4},{6,7},{7,6},{8,9},{9,8},{10,11... | collective-permute-start | bytes 589832 | tf_op jit(solution)/shard_map/ppermute | solution.py:730
  2.4 0.9 %copy-start.1 = (f32[8,2]{0,1:T(2,128)S(1)}, f32[8,2]{0,1:T(2,128)}, u32[]{:S(2)}) copy-start(f32[8,2]{0,1:T(2,128)} %param.6) | copy-start | bytes 196
  2.4 0.9 %copy-start.2 = (s32[16,32,8]{1,2,0:T(8,128)S(1)}, s32[16,32,8]{1,2,0:T(8,128)}, u32[]{:S(2)}) copy-start(s32[16,32,8]{1,2,0:T(8,128)} %param.7) | copy-start | bytes 49156
  2.4 0.9 %copy-start.3 = (s32[2,1,1,32]{3,2,1,0:T(1,128)S(1)}, s32[2,1,1,32]{3,2,1,0:T(1,128)}, u32[]{:S(2)}) copy-start(s32[2,1,1,32]{3,2,1,0:T(1,128)} %param.9) | copy-start | bytes 772
  2.4 8.0 %collective-permute-start.6 = (f32[512,128]{1,0:T(8,128)S(1)}, f32[512,128]{1,0:T(8,128)S(1)}, u32[]{:S(2)}, u32[]{:S(2)}) collective-permute-start(f32[512,128]{1,0:T(8,128)S(1)} %gather.1.after), channel_id=1, source_target_pairs={{0,16},{16,0},{1,17},{17,1},{2,18},{18,2},{3,19},{19,3},{4,20},{20... | collective-permute-start | bytes 786440 | tf_op jit(solution)/shard_map/ppermute | solution.py:742
  3.9 8.4 %collective-permute-start.4 = (f32[168,128]{1,0:T(8,128)S(1)}, f32[168,128]{1,0:T(8,128)S(1)}, u32[]{:S(2)}, u32[]{:S(2)}) collective-permute-start(f32[168,128]{1,0:T(8,128)S(1)} %get-tuple-element.49), channel_id=1, source_target_pairs={{0,2},{1,3},{2,4},{3,5},{4,6},{5,7},{6,8},{7,9},{8,10},{9,11},{10,... | collective-permute-start | bytes 258056 | tf_op jit(solution)/shard_map/ppermute | solution.py:753
  4.3 8.0 %collective-permute-start.5 = (f32[168,128]{1,0:T(8,128)S(1)}, f32[168,128]{1,0:T(8,128)S(1)}, u32[]{:S(2)}, u32[]{:S(2)}) collective-permute-start(f32[168,128]{1,0:T(8,128)S(1)} %get-tuple-element.50), channel_id=1, source_target_pairs={{0,14},{1,15},{2,0},{3,1},{4,2},{5,3},{6,4},{7,5},{8,6},{9,7},{10,... | collective-permute-start | bytes 258056 | tf_op jit(solution)/shard_map/ppermute | solution.py:754
  4.6 8.6 %collective-permute-start.2 = (f32[232,128]{1,0:T(8,128)S(1)}, f32[232,128]{1,0:T(8,128)S(1)}, u32[]{:S(2)}, u32[]{:S(2)}) collective-permute-start(f32[232,128]{1,0:T(8,128)S(1)} %get-tuple-element.47), channel_id=1, source_target_pairs={{16,18},{17,19},{18,20},{19,21},{20,22},{21,23},{22,24},{23,25},{2... | collective-permute-start | bytes 356360 | tf_op jit(solution)/shard_map/ppermute | solution.py:764
  6.7 7.0 %collective-permute-start.3 = (f32[232,128]{1,0:T(8,128)S(1)}, f32[232,128]{1,0:T(8,128)S(1)}, u32[]{:S(2)}, u32[]{:S(2)}) collective-permute-start(f32[232,128]{1,0:T(8,128)S(1)} %get-tuple-element.48), channel_id=1, source_target_pairs={{16,30},{17,31},{18,16},{19,17},{20,18},{21,19},{22,20},{23,21},{2... | collective-permute-start | bytes 356360 | tf_op jit(solution)/shard_map/ppermute | solution.py:765
  11.5 3.7 %collective-permute-start.7 = (f32[3,18,8,128]{3,2,1,0:T(8,128)S(1)}, f32[3,18,8,128]{3,2,1,0:T(8,128)S(1)}, u32[]{:S(2)}, u32[]{:S(2)}) collective-permute-start(f32[3,18,8,128]{3,2,1,0:T(8,128)S(1)} %get-tuple-element.58), channel_id=1, source_target_pairs={{0,1},{1,0},{2,3},{3,2},{4,5},{5,4},{6,7},{7,6},{8,9},{9,8},{10,11... | collective-permute-start | bytes 663560 | tf_op jit(solution)/shard_map/ppermute | solution.py:783
  14.0 2.4 %collective-permute-start.8 = (f32[3,4,8,128]{3,2,1,0:T(8,128)S(1)}, f32[3,4,8,128]{3,2,1,0:T(8,128)S(1)}, u32[]{:S(2)}, u32[]{:S(2)}) collective-permute-start(f32[3,4,8,128]{3,2,1,0:T(8,128)S(1)} %get-tuple-element.62), channel_id=1, source_target_pairs={{0,1},{1,0},{2,3},{3,2},{4,5},{5,4},{6,7},{7,6},{8,9},{9,8},{10,11... | collective-permute-start | bytes 147464 | tf_op jit(solution)/shard_map/ppermute | solution.py:803

commit v10 on v9

--- a/solution.py
+++ b/solution.py
@@ -1,3 +1,5 @@
+import functools
+
 import jax
 import jax.numpy as jnp
 from jax import lax
@@ -19,7 +21,8 @@
     "inner_electric": 6,
     "inner_mechanic": 6,
     "outer_electric": 1,
-    "outer_mechanic": 1,
+    "outer_low": 0.01,
+    "outer_high": 1,
     "middle": 6,
     "last": 1,
 }
@@ -151,15 +154,21 @@
     return [moved[:, a * depth : (a + 1) * depth] for a in range(3)]
 
 
-def edges_tile(value):
-    rows = value.shape[0]
-    last = lax.broadcasted_iota(jnp.int32, (8, value.shape[1]), 0) == 7
-    return jnp.where(last, value[rows - 8 :], value[:8])
-
-
-def fill_sides(pad, a, x, tile, size_y):
-    pad[a, x, 0:PAD, :] = tile
-    pad[a, x, PAD + size_y :, :] = tile
+def put_ends(ends, a, x, value):
+    rows, row = value.shape[0], 2 * (a * (ends.shape[0] // 6) + x)
+    ends[pl.ds(row, 1), :] = value[0:1]
+    ends[pl.ds(row + 1, 1), :] = value[rows - 1 : rows]
+
+
+def fill_sides(pad, a, x, ends, k, size_y):
+    row = 2 * (a * (ends.shape[0] // 6) + k)
+    pad[a, x, PAD - 1 : PAD, :] = ends[pl.ds(row + 1, 1), :]
+    pad[a, x, PAD + size_y : PAD + size_y + 1, :] = ends[pl.ds(row, 1), :]
+
+
+def side_rows(ends, a, x):
+    row = 2 * (a * (ends.shape[0] // 6) + x)
+    return ends[row + 1 : row + 2, :], ends[row : row + 1, :]
 
 
 def sides(size_x):
@@ -273,7 +282,7 @@
         for a in range(3):
             value = own[a, x]
             pad[a, x + 1, PAD : PAD + size_y, :] = value
-            share[a, x] = edges_tile(value)
+            put_ends(share, a, x, value)
         return carry
 
     lax.fori_loop(0, size_x, plane, 0, unroll=4)
@@ -313,7 +322,7 @@
 
     def fill(x, carry):
         for a in range(3):
-            fill_sides(pad, a, x + 1, side_ref[a, x], size_y)
+            fill_sides(pad, a, x + 1, side_ref, x, size_y)
         return carry
 
     lax.fori_loop(0, size_x, fill, 0, unroll=4)
@@ -321,8 +330,9 @@
     @pl.when(electric())
     def _():
         for which, ((_, edge, _), out) in enumerate(zip(sides(size_x), (low_ref, high_ref))):
-            out[ROW_VOLT_SIDE : ROW_VOLT_SIDE + 1, :] = side_ref[0, edge, 7:8, :]
-            out[ROW_VOLT_SIDE + 1 : ROW_VOLT_SIDE + 2, :] = side_ref[0, edge, 0:1, :]
+            below, above = side_rows(side_ref, 0, edge)
+            out[ROW_VOLT_SIDE : ROW_VOLT_SIDE + 1, :] = below
+            out[ROW_VOLT_SIDE + 1 : ROW_VOLT_SIDE + 2, :] = above
             rows, depth = slice(which * size_y, (which + 1) * size_y), own.shape[3]
             fib = [edge_fib[rows, a * depth : (a + 1) * depth] for a in range(3)]
             v, c, d = [rows_of(pad, a, edge + 1, size_y) for a in range(3)]
@@ -349,8 +359,7 @@
             out[ROW_STIFF : ROW_STIFF + size_y, :] = stiff
             for a in range(3):
                 row = ROW_SIDE + 2 * a
-                out[row : row + 1, :] = side_ref[a, edge, 7:8, :]
-                out[row + 1 : row + 2, :] = side_ref[a, edge, 0:1, :]
+                out[row : row + 1, :], out[row + 1 : row + 2, :] = side_rows(side_ref, a, edge)
                 u = rows_of(pad, a, edge + 1, size_y)
                 out[ROW_NOW + a * size_y : ROW_NOW + (a + 1) * size_y, :] = u
                 drive = own[3 + a, edge] + act * edge_fib[which * size_y : (which + 1) * size_y, a * depth : (a + 1) * depth]
@@ -361,7 +370,7 @@
 
 def put_inner(next_pad, share, a, x, value):
     next_pad[a, x, PAD : PAD + value.shape[0], :] = value
-    share[a, x] = edges_tile(value)
+    put_ends(share, a, x, value)
 
 
 def inner_electric(
@@ -432,7 +441,7 @@
     size_x, size_y = own.shape[1], own.shape[2]
     def put(a, x, slot, value):
         next_pad[a, x, PAD : PAD + size_y, :] = value
-        share[a, slot] = edges_tile(value)
+        put_ends(share, a, slot, value)
 
     def put_side(a, which, low, high):
         wide[a, which, PAD - 1 : PAD, :] = low
@@ -460,11 +469,11 @@
             )
 
 
-def outer_mechanic(pad, own, list_ref, got_low, got_high, next_in, share_in, next_pad, share, wide):
+def outer_mechanic(which, pad, own, list_ref, got, next_in, share_in, next_pad, share, wide):
     size_x, size_y = own.shape[1], own.shape[2]
     def put(a, x, slot, value):
         next_pad[a, x, PAD : PAD + size_y, :] = value
-        share[a, slot] = edges_tile(value)
+        put_ends(share, a, slot, value)
 
     def put_side(a, which, low, high):
         wide[a, which, PAD - 1 : PAD, :] = low
@@ -472,35 +481,35 @@
 
     @pl.when(jnp.logical_not(electric()))
     def _():
-        for which, ((halo, edge, sign), got) in enumerate(zip(sides(size_x), (got_low, got_high))):
-            for a in range(3):
-                wide[a, which, PAD : PAD + size_y, :] = got[ROW_NOW + a * size_y : ROW_NOW + (a + 1) * size_y, :]
-                row = ROW_SIDE + 2 * a
-                put_side(a, which, got[row : row + 1, :], got[row + 1 : row + 2, :])
-            stiff = got[ROW_STIFF : ROW_STIFF + size_y, :]
-            stiff_own = own[6, edge]
-            now = [rows_of(pad, a, edge + 1, size_y) for a in range(3)]
-            theirs = [rows_of(wide, a, which, size_y) for a in range(3)]
-            ties = tie_rows(list_ref[which].astype(F32), stiff, theirs)
-            rate = motion_from(wide, which, sign, size_y)
-            beta = OMEGA * inverse(stiff_own)
-            for a in range(3):
-                put(
-                    a,
-                    edge + 1,
-                    1 + which,
-                    rows_of(next_pad, a, edge + 1, size_y) + OMEGA * rate[a] + beta * ties[a] - 0.12 * now[a],
-                )
-            ties = tie_rows(got[ROW_LIST : ROW_LIST + 1, 0:size_y], stiff_own, now)
-            rate = motion_from(pad, edge + 1, -sign, size_y)
-            beta = OMEGA * inverse(stiff)
-            for a in range(3):
-                put(
-                    a,
-                    halo,
-                    3 * which,
-                    got[ROW_NEXT + a * size_y : ROW_NEXT + (a + 1) * size_y, :] + OMEGA * rate[a] + beta * ties[a],
-                )
+        halo, edge, sign = sides(size_x)[which]
+        for a in range(3):
+            wide[a, which, PAD : PAD + size_y, :] = got[ROW_NOW + a * size_y : ROW_NOW + (a + 1) * size_y, :]
+            row = ROW_SIDE + 2 * a
+            put_side(a, which, got[row : row + 1, :], got[row + 1 : row + 2, :])
+        stiff = got[ROW_STIFF : ROW_STIFF + size_y, :]
+        stiff_own = own[6, edge]
+        now = [rows_of(pad, a, edge + 1, size_y) for a in range(3)]
+        theirs = [rows_of(wide, a, which, size_y) for a in range(3)]
+        ties = tie_rows(list_ref[which].astype(F32), stiff, theirs)
+        rate = motion_from(wide, which, sign, size_y)
+        beta = OMEGA * inverse(stiff_own)
+        for a in range(3):
+            put(
+                a,
+                edge + 1,
+                1 + which,
+                rows_of(next_pad, a, edge + 1, size_y) + OMEGA * rate[a] + beta * ties[a] - 0.12 * now[a],
+            )
+        ties = tie_rows(got[ROW_LIST : ROW_LIST + 1, 0:size_y], stiff_own, now)
+        rate = motion_from(pad, edge + 1, -sign, size_y)
+        beta = OMEGA * inverse(stiff)
+        for a in range(3):
+            put(
+                a,
+                halo,
+                3 * which,
+                got[ROW_NEXT + a * size_y : ROW_NEXT + (a + 1) * size_y, :] + OMEGA * rate[a] + beta * ties[a],
+            )
 
 
 def electric_end(x, next_pad, fib_ref):
@@ -544,7 +553,7 @@
     def fill(count):
         def one(x, carry):
             for a in range(count):
-                fill_sides(next_pad, a, x, side_ref[a, x], size_y)
+                fill_sides(next_pad, a, x, side_ref, x, size_y)
             return carry
 
         lax.fori_loop(2, size_x, one, 0, unroll=2)
@@ -633,8 +642,8 @@
     def _():
         copy_final(1).start()
         for halo, edge, near, which, first in work:
-            fill_sides(next_pad, 0, halo, side_ref[0, 3 * which], size_y)
-            fill_sides(next_pad, 0, edge + 1, side_ref[0, 1 + which], size_y)
+            fill_sides(next_pad, 0, halo, side_ref, 3 * which, size_y)
+            fill_sides(next_pad, 0, edge + 1, side_ref, 1 + which, size_y)
             for x in (near, edge):
                 out[0, x] = held[2 * which + x - first] + electric_end(x, next_pad, fib_ref)
             copy_out(which, first, 1).start()
@@ -647,8 +656,8 @@
         copy_final(3).start()
         for halo, edge, near, which, first in work:
             for a in range(3):
-                fill_sides(next_pad, a, halo, side_ref[a, 3 * which], size_y)
-                fill_sides(next_pad, a, edge + 1, side_ref[a, 1 + which], size_y)
+                fill_sides(next_pad, a, halo, side_ref, 3 * which, size_y)
+                fill_sides(next_pad, a, edge + 1, side_ref, 1 + which, size_y)
             for a, value in enumerate(mechanic_end(near, next_pad, keep, size_y)):
                 out[a, near] = value
             for a, value in enumerate(mechanic_end(edge, next_pad, keep, size_y)):
@@ -697,6 +706,7 @@
     f32 = lambda *shape: jax.ShapeDtypeStruct(shape, F32)
     hbm = lambda w: pltpu.with_memory_space_constraint(w, H)
     columns = size_x * size_y
+    ends = lambda planes: f32(6 * planes, depth)
     padded = f32(3, size_x + 2, size_y + 2 * PAD, depth)
     classes = fiber_class.transpose(0, 2, 1)
     lists = interface_rows.reshape(2, 1, size_y)
@@ -726,7 +736,7 @@
         ],
     )
     edge_ten = lax.ppermute(edge_ten, "sec", both)
-    pad, share = call(share_kernel, "share", (padded, f32(3, size_x, 8, depth)), (own, plain), (V, V))
+    pad, share = call(share_kernel, "share", (padded, ends(size_x)), (own, plain), (V, V))
     side = lax.ppermute(share, "gy", both)
     result = f32(1, 4, size_x, size_y, depth)
     (gathered,) = call(gather_kernel, "gather", (f32(columns, depth),), (plain, own_list, share), (V,) * 3)
@@ -766,7 +776,7 @@
     moved, share, keep, result, fib = call(
         inner_electric,
         "inner_electric",
-        (padded, f32(3, size_x + 2, 8, depth), f32(4, size_x, size_y, depth), result, f32(3, columns, depth)),
+        (padded, ends(size_x + 2), f32(4, size_x, size_y, depth), result, f32(3, columns, depth)),
         (pad, own, plain, classes, table),
         (V,) * 5,
         [flat(columns), pltpu.SemaphoreType.DMA((size_x,))],
@@ -775,7 +785,7 @@
     moved, share, keep = call(
         inner_mechanic,
         "inner_mechanic",
-        (padded, f32(3, size_x + 2, 8, depth), f32(4, size_x, size_y, depth)),
+        (padded, ends(size_x + 2), f32(4, size_x, size_y, depth)),
         (pad, own, fib, tension, moved, share, keep),
         (V,) * 7,
         aliases={4: 0, 5: 1, 6: 2},
@@ -785,21 +795,22 @@
     moved, share = call(
         outer_electric,
         "outer_electric",
-        (padded, f32(3, 4, 8, depth)),
+        (padded, ends(4)),
         (pad, own, fib, volt_low, volt_high, moved),
         (V,) * 6,
         [wide],
         aliases={5: 0},
     )
-    moved, share = call(
-        outer_mechanic,
-        "outer_mechanic",
-        (padded, f32(3, 4, 8, depth)),
-        (pad, own, lists, got_low, got_high, moved, share),
-        (V,) * 7,
-        [wide],
-        aliases={5: 0, 6: 1},
-    )
+    for which, got in enumerate((got_low, got_high)):
+        moved, share = call(
+            functools.partial(outer_mechanic, which),
+            ("outer_low", "outer_high")[which],
+            (padded, ends(4)),
+            (pad, own, lists, got, moved, share),
+            (V,) * 6,
+            [wide],
+            aliases={4: 0, 5: 1},
+        )
     end_side = lax.ppermute(share, "gy", both)
     fields = pltpu.VMEM((3, size_x, size_y, depth), F32)
     pieces = 3

time: 17.4 us -> 17.4 us (level)
  waiting for transfers between devices: 1.46 us -> 1.24 us
  Pallas kernels: 4.8 us -> 5.02 us
    ppermute x1, waiting for transfers between devices: 0.5 us -> 0.22 us  [local(): got_high = lax.ppermute(low, axes, ring(1, -1))]
    pallas_call x12 -> x13, Pallas kernels: 4.8 us -> 5.02 us  [call(): pl.pallas_call(kernel, name=name, out_shape=tuple(out_shape), in_specs=[p...]
  transfers between devices with their start and end apart: 9 -> 9, of which waited for: 2 -> 2; matrix products, arithmetic and copies ran while one was open for 0% -> 0% of each run, Pallas kernels for 22% -> 23%
where the time goes in v10:
time: 17.4 us; the launch traced here: 17.3 us
  starting transfers between devices  10.7 us (61%)
  Pallas kernels  5.02 us (29%)
  waiting for transfers between devices  1.24 us (7%)
  local copies, waits for them, and re-layouts  0.22 us (1%)
    pallas_call x13, Pallas kernels, call(): pl.pallas_call(kernel, name=name, out_shape=tuple(out_shape), in_specs=[p...  5.02 us
    ppermute x1, starting transfers between devices, local(): got_high = lax.ppermute(low, axes, ring(1, -1))  3.1 us
    ppermute x1, starting transfers between devices, local(): got_low = lax.ppermute(high, axes, ring(1, 1))  2.12 us
    ppermute x2, starting transfers between devices, local(): side = lax.ppermute(share, 'gy', both)  1.49 us
    ppermute x1, starting transfers between devices, local(): edge_ten = lax.ppermute(edge_ten, 'sec', both)  1.24 us
    ppermute x1, starting transfers between devices, local(): end_side = lax.ppermute(share, 'gy', both)  1.24 us
    ppermute x1, waiting for transfers between devices, local(): got_low = lax.ppermute(high, axes, ring(1, 1))  1 us
    ppermute x1, starting transfers between devices, local(): tension = lax.ppermute(gathered, 'sec', both)  0.93 us
  transfers between devices with their start and end apart: 9, of which 2 were waited for; matrix products, arithmetic and copies ran while one was open for 0% of the time, Pallas kernels for 23%

profile of v10, /device:TPU:3, one launch (start us, length us, event | category | flops | bytes accessed | tf_op | source)
XLA Modules:
  0.0 17.3 jit_solution(3463714757905579259)
XLA Ops:
  0.0 0.1 tension.1
  0.1 1.2 %collective-permute-start.1 = (f32[2,32,128]{2,1,0:T(8,128)S(1)}, f32[2,32,128]{2,1,0:T(8,128)S(1)}, u32[]{:S(2)}, u32[]{:S(2)}) collective-permute-start(f32[2,32,128]{2,1,0:T(8,128)S(1)} %get-tuple-element.45), channel_id=1, source_target_pairs={{0,16},{16,0},{1,17},{17,1},{2,18},{18,2},{3,19},{19,3},{4,20},{20... | collective-permute-start | bytes 98312 | tf_op jit(solution)/shard_map/ppermute | solution.py:738
  1.4 0.2 %copy-done = f32[1,8,16,32,128]{4,3,2,1,0:T(8,128)S(1)} copy-done((f32[1,8,16,32,128]{4,3,2,1,0:T(8,128)S(1)}, f32[1,8,16,32,128]{4,3,2,1,0:T(8,128)}, u32[]{:S(2)}) %copy-start) | copy-done | bytes 2097176
  1.6 0.1 share.1
  1.7 0.7 %collective-permute-start = (f32[96,128]{1,0:T(8,128)S(1)}, f32[96,128]{1,0:T(8,128)S(1)}, u32[]{:S(2)}, u32[]{:S(2)}) collective-permute-start(f32[96,128]{1,0:T(8,128)S(1)} %get-tuple-element.40.after), channel_id=1, source_target_pairs={{0,1},{1,0},{2,3},{3,2},{4,5},{5,4},{6,7},{7,6},{8,9},{9,8},{10,11... | collective-permute-start | bytes 147464 | tf_op jit(solution)/shard_map/ppermute | solution.py:740
  2.4 0.9 %collective-permute-start.6 = (f32[512,128]{1,0:T(8,128)S(1)}, f32[512,128]{1,0:T(8,128)S(1)}, u32[]{:S(2)}, u32[]{:S(2)}) collective-permute-start(f32[512,128]{1,0:T(8,128)S(1)} %gather.1.after), channel_id=1, source_target_pairs={{0,16},{16,0},{1,17},{17,1},{2,18},{18,2},{3,19},{19,3},{4,20},{20... | collective-permute-start | bytes 786440 | tf_op jit(solution)/shard_map/ppermute | solution.py:752
  3.4 0.5 %edge.1 = (f32[64,384]{1,0:T(8,128)S(1)}, f32[192,384]{1,0:T(8,128)S(1)}) custom-call(f32[192,384]{1,0:T(8,128)S(1)} %get-tuple-element.41.table_in, s32[16,8,32]{2,1,0:T(8,128)S(1)} %bitcast.25, f32[2,8]{1,0:T(2,128)S(1)} %bitcast.19, f32[512,128]{1,0:T(8,128)S(1)} %gather.1.after, s32[2,1,32]{2,1,0:T(1,128)S(1)} %bitcast.20), custom_call_target="tpu_custom_call", output_to_operand_aliasing={{1}: (0, {})} | custom-call | flops 10000000000 | bytes 10000000 | tf_op jit(solution)/shard_map/edge/pallas_call | solution.py:674
  3.8 0.1 message_electric.1
  3.9 0.4 %collective-permute-start.4 = (f32[168,128]{1,0:T(8,128)S(1)}, f32[168,128]{1,0:T(8,128)S(1)}, u32[]{:S(2)}, u32[]{:S(2)}) collective-permute-start(f32[168,128]{1,0:T(8,128)S(1)} %get-tuple-element.51), channel_id=1, source_target_pairs={{0,2},{1,3},{2,4},{3,5},{4,6},{5,7},{6,8},{7,9},{8,10},{9,11},{10,... | collective-permute-start | bytes 258056 | tf_op jit(solution)/shard_map/ppermute | solution.py:763
  4.3 0.2 collective-permute-start.5
  4.5 0.0 collective-permute-done.1.ten_ref
  4.5 0.1 message_mechanic.1
  4.6 2.1 %collective-permute-start.2 = (f32[232,128]{1,0:T(8,128)S(1)}, f32[232,128]{1,0:T(8,128)S(1)}, u32[]{:S(2)}, u32[]{:S(2)}) collective-permute-start(f32[232,128]{1,0:T(8,128)S(1)} %get-tuple-element.49), channel_id=1, source_target_pairs={{16,18},{17,19},{18,20},{19,21},{20,22},{21,23},{22,24},{23,25},{2... | collective-permute-start | bytes 356360 | tf_op jit(solution)/shard_map/ppermute | solution.py:774
  6.7 3.1 %collective-permute-start.3 = (f32[232,128]{1,0:T(8,128)S(1)}, f32[232,128]{1,0:T(8,128)S(1)}, u32[]{:S(2)}, u32[]{:S(2)}) collective-permute-start(f32[232,128]{1,0:T(8,128)S(1)} %get-tuple-element.50), channel_id=1, source_target_pairs={{16,30},{17,31},{18,16},{19,17},{20,18},{21,19},{22,20},{23,21},{2... | collective-permute-start | bytes 356360 | tf_op jit(solution)/shard_map/ppermute | solution.py:775
  9.8 0.6 %inner_electric.1 = (f32[3,18,48,128]{3,2,1,0:T(8,128)S(1)}, f32[108,128]{1,0:T(8,128)S(1)}, f32[4,16,32,128]{3,2,1,0:T(8,128)S(1)}, f32[1,4,16,32,128]{4,3,2,1,0:T(8,128)}, f32[3,512,128]{2,1,0:T(8,128)S(1)}) custom-call(f32[3,18,48,128]{3,2,1,0:T(8,128)S(1)} %get-tuple-element.46.pad, f32[8,16,32,128]{3,2,1,0:T(8,128)S(1)} %bitcast.12, ...), custom_call_target="tpu_custom_call" | custom-call | flops 60000002048 | bytes 60000000 | tf_op jit(solution)/shard_map/inner_electric/pallas_call | solution.py:674
  10.5 1.1 %inner_mechanic.1 = (f32[3,18,48,128]{3,2,1,0:T(8,128)S(1)}, f32[108,128]{1,0:T(8,128)S(1)}, f32[4,16,32,128]{3,2,1,0:T(8,128)S(1)}) custom-call(f32[3,18,48,128]{3,2,1,0:T(8,128)S(1)} %get-tuple-element.46.pad, f32[8,16,32,128]{3,2,1,0:T(8,128)S(1)} %bitcast.13, ...), custom_call_target="tpu_custom_call", output_to_operand_aliasing={{0}: (4, {}), {1}: (5, {}), {2}: (6, {})} | custom-call | flops 60000002048 | bytes 60000000 | tf_op jit(solution)/shard_map/inner_mechanic/pallas_call | solution.py:674
  11.6 0.8 %collective-permute-start.7 = (f32[108,128]{1,0:T(8,128)S(1)}, f32[108,128]{1,0:T(8,128)S(1)}, u32[]{:S(2)}, u32[]{:S(2)}) collective-permute-start(f32[108,128]{1,0:T(8,128)S(1)} %get-tuple-element.62), channel_id=1, source_target_pairs={{0,1},{1,0},{2,3},{3,2},{4,5},{5,4},{6,7},{7,6},{8,9},{9,8},{10,11... | collective-permute-start | bytes 165896 | tf_op jit(solution)/shard_map/ppermute | solution.py:793
  12.3 1.0 %collective-permute-done.2.got.got_low = f32[232,128]{1,0:T(8,128)S(1)} collective-permute-done((f32[232,128]{1,0:T(8,128)S(1)}, f32[232,128]{1,0:T(8,128)S(1)}, u32[]{:S(2)}, u32[]{:S(2)}) %collective-permute-start.2) | collective-permute-done | bytes 118816 | tf_op jit(solution)/shard_map/ppermute | solution.py:774
  13.3 0.2 %outer_low.1 = (f32[3,18,48,128]{3,2,1,0:T(8,128)S(1)}, f32[24,128]{1,0:T(8,128)S(1)}) custom-call(f32[3,18,48,128]{3,2,1,0:T(8,128)S(1)} %get-tuple-element.46.pad, f32[8,16,32,128]{3,2,1,0:T(8,128)S(1)} %bitcast.15, s32[2,1,32]{2,1,0:T(1,128)S(1)} %bitcast.22, ...), custom_call_target="tpu_custom_call", output_to_operand_aliasing={{0}: (4, {}), {1}: (5, {})} | custom-call | flops 100000000 | bytes 100000 | tf_op jit(solution)/shard_map/outer_low/pallas_call | solution.py:674
  13.5 0.2 %collective-permute-done.3.got.got_high = f32[232,128]{1,0:T(8,128)S(1)} collective-permute-done((f32[232,128]{1,0:T(8,128)S(1)}, f32[232,128]{1,0:T(8,128)S(1)}, u32[]{:S(2)}, u32[]{:S(2)}) %collective-permute-start.3) | collective-permute-done | bytes 118816 | tf_op jit(solution)/shard_map/ppermute | solution.py:775
  13.8 0.2 %outer_high.1 = (f32[3,18,48,128]{3,2,1,0:T(8,128)S(1)}, f32[24,128]{1,0:T(8,128)S(1)}) custom-call(f32[3,18,48,128]{3,2,1,0:T(8,128)S(1)} %get-tuple-element.46.pad, f32[8,16,32,128]{3,2,1,0:T(8,128)S(1)} %bitcast.16, s32[2,1,32]{2,1,0:T(1,128)S(1)} %bitcast.23, ...), custom_call_target="tpu_custom_call", output_to_operand_aliasing={{0}: (4, {}), {1}: (5, {})} | custom-call | flops 10000000000 | bytes 10000000 | tf_op jit(solution)/shard_map/outer_high/pallas_call | solution.py:674
  14.0 1.2 %collective-permute-start.8 = (f32[24,128]{1,0:T(8,128)S(1)}, f32[24,128]{1,0:T(8,128)S(1)}, u32[]{:S(2)}, u32[]{:S(2)}) collective-permute-start(f32[24,128]{1,0:T(8,128)S(1)} %get-tuple-element.66), channel_id=1, source_target_pairs={{0,1},{1,0},{2,3},{3,2},{4,5},{5,4},{6,7},{7,6},{8,9},{9,8},{10,11... | collective-permute-start | bytes 36872 | tf_op jit(solution)/shard_map/ppermute | solution.py:814
  15.2 1.2 %middle.1 = (f32[1,4,16,32,128]{4,3,2,1,0:T(8,128)}, f32[3,18,48,128]{3,2,1,0:T(8,128)S(1)}, f32[6,32,128]{2,1,0:T(8,128)S(1)}, f32[3,4,32,128]{3,2,1,0:T(8,128)S(1)}) custom-call(f32[3,512,128]{2,1,0:T(8,128)S(1)} %get-tuple-element.48.fib_ref, f32[8,16,32,128]{3,2,1,0:T(8,128)S(1)} %bitcast.17, ...), custom_call_target="tpu_custom_call", output_to_operand_aliasing={{1}: (5, {}), {0}: (8, {})} | custom-call | flops 60000002048 | bytes 60000000 | tf_op jit(solution)/shard_map/middle/pallas_call | solution.py:674
  16.4 0.9 %last.1 = (f32[1,4,16,32,128]{4,3,2,1,0:T(8,128)}, f32[3,18,48,128]{3,2,1,0:T(8,128)S(1)}) custom-call(f32[3,512,128]{2,1,0:T(8,128)S(1)} %get-tuple-element.48.fib_ref, f32[3,18,48,128]{3,2,1,0:T(8,128)S(1)} %get-tuple-element.65.next_in, f32[24,128]{1,0:T(8,128)S(1)} %collective-permute-done.8.side_ref, ...), custom_call_target="tpu_custom_call", output_to_operand_aliasing={{1}: (1, {}), {0}: (6, {})} | custom-call | flops 10000000000 | bytes 10000000 | tf_op jit(solution)/shard_map/last/pallas_call | solution.py:674
  (15 shorter events, 0.0 us)
Async XLA Ops:
  0.0 1.6 %copy-start = (f32[1,8,16,32,128]{4,3,2,1,0:T(8,128)S(1)}, f32[1,8,16,32,128]{4,3,2,1,0:T(8,128)}, u32[]{:S(2)}) copy-start(f32[1,8,16,32,128]{4,3,2,1,0:T(8,128)} %param.5) | copy-start | bytes 6291460
  0.1 4.3 %collective-permute-start.1 = (f32[2,32,128]{2,1,0:T(8,128)S(1)}, f32[2,32,128]{2,1,0:T(8,128)S(1)}, u32[]{:S(2)}, u32[]{:S(2)}) collective-permute-start(f32[2,32,128]{2,1,0:T(8,128)S(1)} %get-tuple-element.45), channel_id=1, source_target_pairs={{0,16},{16,0},{1,17},{17,1},{2,18},{18,2},{3,19},{19,3},{4,20},{20... | collective-permute-start | bytes 98312 | tf_op jit(solution)/shard_map/ppermute | solution.py:738
  1.7 2.1 %collective-permute-start = (f32[96,128]{1,0:T(8,128)S(1)}, f32[96,128]{1,0:T(8,128)S(1)}, u32[]{:S(2)}, u32[]{:S(2)}) collective-permute-start(f32[96,128]{1,0:T(8,128)S(1)} %get-tuple-element.40.after), channel_id=1, source_target_pairs={{0,1},{1,0},{2,3},{3,2},{4,5},{5,4},{6,7},{7,6},{8,9},{9,8},{10,11... | collective-permute-start | bytes 147464 | tf_op jit(solution)/shard_map/ppermute | solution.py:740
  2.4 0.9 %copy-start.1 = (f32[8,2]{0,1:T(2,128)S(1)}, f32[8,2]{0,1:T(2,128)}, u32[]{:S(2)}) copy-start(f32[8,2]{0,1:T(2,128)} %param.6) | copy-start | bytes 196
  2.4 0.9 %copy-start.2 = (s32[2,1,1,32]{3,2,1,0:T(1,128)S(1)}, s32[2,1,1,32]{3,2,1,0:T(1,128)}, u32[]{:S(2)}) copy-start(s32[2,1,1,32]{3,2,1,0:T(1,128)} %param.9) | copy-start | bytes 772
  2.4 0.9 %copy-start.3 = (s32[16,32,8]{1,2,0:T(8,128)S(1)}, s32[16,32,8]{1,2,0:T(8,128)}, u32[]{:S(2)}) copy-start(s32[16,32,8]{1,2,0:T(8,128)} %param.7) | copy-start | bytes 49156
  2.4 8.0 %collective-permute-start.6 = (f32[512,128]{1,0:T(8,128)S(1)}, f32[512,128]{1,0:T(8,128)S(1)}, u32[]{:S(2)}, u32[]{:S(2)}) collective-permute-start(f32[512,128]{1,0:T(8,128)S(1)} %gather.1.after), channel_id=1, source_target_pairs={{0,16},{16,0},{1,17},{17,1},{2,18},{18,2},{3,19},{19,3},{4,20},{20... | collective-permute-start | bytes 786440 | tf_op jit(solution)/shard_map/ppermute | solution.py:752
  3.9 8.4 %collective-permute-start.4 = (f32[168,128]{1,0:T(8,128)S(1)}, f32[168,128]{1,0:T(8,128)S(1)}, u32[]{:S(2)}, u32[]{:S(2)}) collective-permute-start(f32[168,128]{1,0:T(8,128)S(1)} %get-tuple-element.51), channel_id=1, source_target_pairs={{0,2},{1,3},{2,4},{3,5},{4,6},{5,7},{6,8},{7,9},{8,10},{9,11},{10,... | collective-permute-start | bytes 258056 | tf_op jit(solution)/shard_map/ppermute | solution.py:763
  4.3 8.0 %collective-permute-start.5 = (f32[168,128]{1,0:T(8,128)S(1)}, f32[168,128]{1,0:T(8,128)S(1)}, u32[]{:S(2)}, u32[]{:S(2)}) collective-permute-start(f32[168,128]{1,0:T(8,128)S(1)} %get-tuple-element.52), channel_id=1, source_target_pairs={{0,14},{1,15},{2,0},{3,1},{4,2},{5,3},{6,4},{7,5},{8,6},{9,7},{10,... | collective-permute-start | bytes 258056 | tf_op jit(solution)/shard_map/ppermute | solution.py:764
  4.6 8.7 %collective-permute-start.2 = (f32[232,128]{1,0:T(8,128)S(1)}, f32[232,128]{1,0:T(8,128)S(1)}, u32[]{:S(2)}, u32[]{:S(2)}) collective-permute-start(f32[232,128]{1,0:T(8,128)S(1)} %get-tuple-element.49), channel_id=1, source_target_pairs={{16,18},{17,19},{18,20},{19,21},{20,22},{21,23},{22,24},{23,25},{2... | collective-permute-start | bytes 356360 | tf_op jit(solution)/shard_map/ppermute | solution.py:774
  6.7 7.0 %collective-permute-start.3 = (f32[232,128]{1,0:T(8,128)S(1)}, f32[232,128]{1,0:T(8,128)S(1)}, u32[]{:S(2)}, u32[]{:S(2)}) collective-permute-start(f32[232,128]{1,0:T(8,128)S(1)} %get-tuple-element.50), channel_id=1, source_target_pairs={{16,30},{17,31},{18,16},{19,17},{20,18},{21,19},{22,20},{23,21},{2... | collective-permute-start | bytes 356360 | tf_op jit(solution)/shard_map/ppermute | solution.py:775
  11.6 3.7 %collective-permute-start.7 = (f32[108,128]{1,0:T(8,128)S(1)}, f32[108,128]{1,0:T(8,128)S(1)}, u32[]{:S(2)}, u32[]{:S(2)}) collective-permute-start(f32[108,128]{1,0:T(8,128)S(1)} %get-tuple-element.62), channel_id=1, source_target_pairs={{0,1},{1,0},{2,3},{3,2},{4,5},{5,4},{6,7},{7,6},{8,9},{9,8},{10,11... | collective-permute-start | bytes 165896 | tf_op jit(solution)/shard_map/ppermute | solution.py:793
  14.0 2.4 %collective-permute-start.8 = (f32[24,128]{1,0:T(8,128)S(1)}, f32[24,128]{1,0:T(8,128)S(1)}, u32[]{:S(2)}, u32[]{:S(2)}) collective-permute-start(f32[24,128]{1,0:T(8,128)S(1)} %get-tuple-element.66), channel_id=1, source_target_pairs={{0,1},{1,0},{2,3},{3,2},{4,5},{5,4},{6,7},{7,6},{8,9},{9,8},{10,11... | collective-permute-start | bytes 36872 | tf_op jit(solution)/shard_map/ppermute | solution.py:814

commit v11 on v10

--- a/solution.py
+++ b/solution.py
@@ -416,7 +416,9 @@
             copy.wait()
 
 
-def inner_mechanic(pad, own, fib_ref, ten_ref, next_in, share_in, keep_in, next_pad, share, keep):
+def inner_mechanic(
+    pad, own, fib_ref, ten_ref, next_in, share_in, keep_in, out_in, next_pad, share, keep, out_hbm, sems
+):
     size_x, size_y = own.shape[1], own.shape[2]
 
     @pl.when(jnp.logical_not(electric()))
@@ -435,6 +437,9 @@
             return carry
 
         lax.fori_loop(0, size_x, plane, 0, unroll=2)
+        copy = pltpu.make_async_copy(keep.at[3:4], out_hbm.at[0, 3:4], sems.at[0])
+        copy.start()
+        copy.wait()
 
 
 def outer_electric(pad, own, fib_ref, volt_low, volt_high, next_in, next_pad, share, wide):
@@ -543,12 +548,11 @@
 ):
     size_x = keep.shape[1]
     size_y = fib_ref.shape[1] // size_x
-    pieces = sems.shape[0]
-    chunk = final.shape[1]
-
-    def copy_out(i, fields):
-        here = pl.ds(2 + i * chunk, chunk)
-        return pltpu.make_async_copy(out.at[0:fields, here], out_hbm.at[0, 0:fields, here], sems.at[i])
+    lead = size_x - 4 - final.shape[1]
+
+    def copy_out(fields):
+        here = pl.ds(2, lead)
+        return pltpu.make_async_copy(out.at[0:fields, here], out_hbm.at[0, 0:fields, here], sems.at[0])
 
     def fill(count):
         def one(x, carry):
@@ -567,41 +571,26 @@
             return carry
 
         lax.fori_loop(0, size_x, rest, 0, unroll=2)
-        copy = pltpu.make_async_copy(out.at[1:3], out_hbm.at[0, 1:3], sems.at[pieces - 1])
+        copy = pltpu.make_async_copy(out.at[1:3], out_hbm.at[0, 1:3], sems.at[1])
         copy.start()
         for i, x in enumerate((0, 1, size_x - 2, size_x - 1)):
             held[i] = out[0, x]
 
-        def step(i, carry):
-            for k in range(chunk):
-                x = 2 + i * chunk + k
-                out[0, x] = out[0, x] + electric_end(x, next_pad, fib_ref)
-            copy_out(i, 1).start()
-            return carry
-
-        lax.fori_loop(0, pieces - 1, step, 0)
-        for k in range(chunk):
-            x = size_x - 2 - chunk + k
-            final[0, k] = out[0, x] + electric_end(x, next_pad, fib_ref)
+        for x in range(2, 2 + lead):
+            out[0, x] = out[0, x] + electric_end(x, next_pad, fib_ref)
+        copy_out(1).start()
+        for x in range(2 + lead, size_x - 2):
+            final[0, x - 2 - lead] = out[0, x] + electric_end(x, next_pad, fib_ref)
         copy.wait()
-        for i in range(pieces - 1):
-            copy_out(i, 1).wait()
+        copy_out(1).wait()
 
     @pl.when(jnp.logical_not(electric()))
     def _():
         fill(3)
-        copy = pltpu.make_async_copy(keep.at[3:4], out_hbm.at[0, 3:4], sems.at[pieces - 1])
-        copy.start()
-
-        def sweep(i, carry):
-            for k in range(chunk):
-                x = 2 + i * chunk + k
-                for a, value in enumerate(mechanic_end(x, next_pad, keep, size_y)):
-                    out[a, x] = value
-            copy_out(i, 3).start()
-            return carry
-
-        lax.fori_loop(0, pieces - 1, sweep, 0)
+        for x in range(2, 2 + lead):
+            for a, value in enumerate(mechanic_end(x, next_pad, keep, size_y)):
+                out[a, x] = value
+        copy_out(3).start()
         for which, ((halo, edge, _), got) in enumerate(zip(sides(size_x), (got_low, got_high))):
             beta = OMEGA * inverse(own[6, edge])
             ties = tie_rows(
@@ -611,12 +600,10 @@
             )
             for a in range(3):
                 held[3 * which + a] = beta * ties[a] - 0.12 * rows_of(next_pad, a, edge + 1, size_y)
-        for k in range(chunk):
-            for a, value in enumerate(mechanic_end(size_x - 2 - chunk + k, next_pad, keep, size_y)):
-                final[a, k] = value
-        copy.wait()
-        for i in range(pieces - 1):
-            copy_out(i, 3).wait()
+        for x in range(2 + lead, size_x - 2):
+            for a, value in enumerate(mechanic_end(x, next_pad, keep, size_y)):
+                final[a, x - 2 - lead] = value
+        copy_out(3).wait()
 
 
 def last_kernel(
@@ -782,13 +769,15 @@
         [flat(columns), pltpu.SemaphoreType.DMA((size_x,))],
         out_spaces=(V, V, V, H, V),
     )
-    moved, share, keep = call(
+    moved, share, keep, result = call(
         inner_mechanic,
         "inner_mechanic",
-        (padded, ends(size_x + 2), f32(4, size_x, size_y, depth)),
-        (pad, own, fib, tension, moved, share, keep),
-        (V,) * 7,
-        aliases={4: 0, 5: 1, 6: 2},
+        (padded, ends(size_x + 2), f32(4, size_x, size_y, depth), f32(1, 4, size_x, size_y, depth)),
+        (pad, own, fib, tension, moved, share, keep, result),
+        (V,) * 7 + (H,),
+        [pltpu.SemaphoreType.DMA((1,))],
+        out_spaces=(V, V, V, H),
+        aliases={4: 0, 5: 1, 6: 2, 7: 3},
     )
     side = lax.ppermute(share, "gy", both)
     wide = pltpu.VMEM((3, 2) + padded.shape[2:], F32)
@@ -813,15 +802,14 @@
         )
     end_side = lax.ppermute(share, "gy", both)
     fields = pltpu.VMEM((3, size_x, size_y, depth), F32)
-    pieces = 3
-    chunk = (size_x - 4) // pieces
+    held_back = 10
     result, moved, held, final = call(
         middle_kernel,
         "middle",
-        (f32(1, 4, size_x, size_y, depth), padded, f32(6, size_y, depth), f32(3, chunk, size_y, depth)),
+        (f32(1, 4, size_x, size_y, depth), padded, f32(6, size_y, depth), f32(3, held_back, size_y, depth)),
         (fib, own, lists, got_low, got_high, moved, side, keep, result),
         (V,) * 8 + (H,),
-        [fields, pltpu.SemaphoreType.DMA((pieces,))],
+        [fields, pltpu.SemaphoreType.DMA((2,))],
         out_spaces=(H, V, V, V),
         aliases={5: 1, 8: 0},
     )

time: 17.4 us -> 17.2 us (0.989)
  waiting for transfers between devices: 1.24 us -> 0.6 us
  Pallas kernels: 5.02 us -> 5.5 us
    ppermute x1, waiting for transfers between devices: 1 us -> 0.36 us  [local(): got_low = lax.ppermute(high, axes, ring(1, 1))]
    pallas_call x13, Pallas kernels: 5.02 us -> 5.5 us  [call(): pl.pallas_call(kernel, name=name, out_shape=tuple(out_shape), in_specs=[p...]
  transfers between devices with their start and end apart: 9 -> 9, of which waited for: 2 -> 2; matrix products, arithmetic and copies ran while one was open for 0% -> 0% of each run, Pallas kernels for 23% -> 26%
where the time goes in v11:
time: 17.2 us; the launch traced here: 17.1 us
  starting transfers between devices  10.7 us (62%)
  Pallas kernels  5.5 us (32%)
  waiting for transfers between devices  0.6 us (3%)
  local copies, waits for them, and re-layouts  0.22 us (1%)
    pallas_call x13, Pallas kernels, call(): pl.pallas_call(kernel, name=name, out_shape=tuple(out_shape), in_specs=[p...  5.5 us
    ppermute x1, starting transfers between devices, local(): got_high = lax.ppermute(low, axes, ring(1, -1))  3.1 us
    ppermute x1, starting transfers between devices, local(): got_low = lax.ppermute(high, axes, ring(1, 1))  2.12 us
    ppermute x2, starting transfers between devices, local(): side = lax.ppermute(share, 'gy', both)  1.49 us
    ppermute x1, starting transfers between devices, local(): edge_ten = lax.ppermute(edge_ten, 'sec', both)  1.24 us
    ppermute x1, starting transfers between devices, local(): end_side = lax.ppermute(share, 'gy', both)  1.24 us
    ppermute x1, starting transfers between devices, local(): tension = lax.ppermute(gathered, 'sec', both)  0.93 us
    ppermute x1, starting transfers between devices, local(): volt_low = lax.ppermute(high, axes, ring(0, 1))  0.39 us
  transfers between devices with their start and end apart: 9, of which 2 were waited for; matrix products, arithmetic and copies ran while one was open for 0% of the time, Pallas kernels for 26%

profile of v11, /device:TPU:3, one launch (start us, length us, event | category | flops | bytes accessed | tf_op | source)
XLA Modules:
  0.0 17.1 jit_solution(12988694830360476601)
XLA Ops:
  0.0 0.1 tension.1
  0.1 1.2 %collective-permute-start.1 = (f32[2,32,128]{2,1,0:T(8,128)S(1)}, f32[2,32,128]{2,1,0:T(8,128)S(1)}, u32[]{:S(2)}, u32[]{:S(2)}) collective-permute-start(f32[2,32,128]{2,1,0:T(8,128)S(1)} %get-tuple-element.46), channel_id=1, source_target_pairs={{0,16},{16,0},{1,17},{17,1},{2,18},{18,2},{3,19},{19,3},{4,20},{20... | collective-permute-start | bytes 98312 | tf_op jit(solution)/shard_map/ppermute | solution.py:725
  1.4 0.2 %copy-done = f32[1,8,16,32,128]{4,3,2,1,0:T(8,128)S(1)} copy-done((f32[1,8,16,32,128]{4,3,2,1,0:T(8,128)S(1)}, f32[1,8,16,32,128]{4,3,2,1,0:T(8,128)}, u32[]{:S(2)}) %copy-start) | copy-done | bytes 2097176
  1.6 0.1 share.1
  1.7 0.7 %collective-permute-start = (f32[96,128]{1,0:T(8,128)S(1)}, f32[96,128]{1,0:T(8,128)S(1)}, u32[]{:S(2)}, u32[]{:S(2)}) collective-permute-start(f32[96,128]{1,0:T(8,128)S(1)} %get-tuple-element.41.after), channel_id=1, source_target_pairs={{0,1},{1,0},{2,3},{3,2},{4,5},{5,4},{6,7},{7,6},{8,9},{9,8},{10,11... | collective-permute-start | bytes 147464 | tf_op jit(solution)/shard_map/ppermute | solution.py:727
  2.4 0.9 %collective-permute-start.6 = (f32[512,128]{1,0:T(8,128)S(1)}, f32[512,128]{1,0:T(8,128)S(1)}, u32[]{:S(2)}, u32[]{:S(2)}) collective-permute-start(f32[512,128]{1,0:T(8,128)S(1)} %gather.1.after), channel_id=1, source_target_pairs={{0,16},{16,0},{1,17},{17,1},{2,18},{18,2},{3,19},{19,3},{4,20},{20... | collective-permute-start | bytes 786440 | tf_op jit(solution)/shard_map/ppermute | solution.py:739
  3.4 0.5 %edge.1 = (f32[64,384]{1,0:T(8,128)S(1)}, f32[192,384]{1,0:T(8,128)S(1)}) custom-call(f32[192,384]{1,0:T(8,128)S(1)} %get-tuple-element.42.table_in, s32[16,8,32]{2,1,0:T(8,128)S(1)} %bitcast.25, f32[2,8]{1,0:T(2,128)S(1)} %bitcast.19, f32[512,128]{1,0:T(8,128)S(1)} %gather.1.after, s32[2,1,32]{2,1,0:T(1,128)S(1)} %bitcast.20), custom_call_target="tpu_custom_call", output_to_operand_aliasing={{1}: (0, {})} | custom-call | flops 10000000000 | bytes 10000000 | tf_op jit(solution)/shard_map/edge/pallas_call | solution.py:661
  3.8 0.0 collective-permute-done.side_ref
  3.8 0.1 message_electric.1
  3.9 0.4 %collective-permute-start.4 = (f32[168,128]{1,0:T(8,128)S(1)}, f32[168,128]{1,0:T(8,128)S(1)}, u32[]{:S(2)}, u32[]{:S(2)}) collective-permute-start(f32[168,128]{1,0:T(8,128)S(1)} %get-tuple-element.52), channel_id=1, source_target_pairs={{0,2},{1,3},{2,4},{3,5},{4,6},{5,7},{6,8},{7,9},{8,10},{9,11},{10,... | collective-permute-start | bytes 258056 | tf_op jit(solution)/shard_map/ppermute | solution.py:750
  4.3 0.2 %collective-permute-start.5 = (f32[168,128]{1,0:T(8,128)S(1)}, f32[168,128]{1,0:T(8,128)S(1)}, u32[]{:S(2)}, u32[]{:S(2)}) collective-permute-start(f32[168,128]{1,0:T(8,128)S(1)} %get-tuple-element.53), channel_id=1, source_target_pairs={{0,14},{1,15},{2,0},{3,1},{4,2},{5,3},{6,4},{7,5},{8,6},{9,7},{10,... | collective-permute-start | bytes 258056 | tf_op jit(solution)/shard_map/ppermute | solution.py:751
  4.5 0.1 message_mechanic.1
  4.6 2.1 %collective-permute-start.2 = (f32[232,128]{1,0:T(8,128)S(1)}, f32[232,128]{1,0:T(8,128)S(1)}, u32[]{:S(2)}, u32[]{:S(2)}) collective-permute-start(f32[232,128]{1,0:T(8,128)S(1)} %get-tuple-element.50), channel_id=1, source_target_pairs={{16,18},{17,19},{18,20},{19,21},{20,22},{21,23},{22,24},{23,25},{2... | collective-permute-start | bytes 356360 | tf_op jit(solution)/shard_map/ppermute | solution.py:761
  6.7 3.1 %collective-permute-start.3 = (f32[232,128]{1,0:T(8,128)S(1)}, f32[232,128]{1,0:T(8,128)S(1)}, u32[]{:S(2)}, u32[]{:S(2)}) collective-permute-start(f32[232,128]{1,0:T(8,128)S(1)} %get-tuple-element.51), channel_id=1, source_target_pairs={{16,30},{17,31},{18,16},{19,17},{20,18},{21,19},{22,20},{23,21},{2... | collective-permute-start | bytes 356360 | tf_op jit(solution)/shard_map/ppermute | solution.py:762
  9.8 0.6 %inner_electric.1 = (f32[3,18,48,128]{3,2,1,0:T(8,128)S(1)}, f32[108,128]{1,0:T(8,128)S(1)}, f32[4,16,32,128]{3,2,1,0:T(8,128)S(1)}, f32[1,4,16,32,128]{4,3,2,1,0:T(8,128)}, f32[3,512,128]{2,1,0:T(8,128)S(1)}) custom-call(f32[3,18,48,128]{3,2,1,0:T(8,128)S(1)} %get-tuple-element.47.pad, f32[8,16,32,128]{3,2,1,0:T(8,128)S(1)} %bitcast.12, ...), custom_call_target="tpu_custom_call" | custom-call | flops 60000002048 | bytes 60000000 | tf_op jit(solution)/shard_map/inner_electric/pallas_call | solution.py:661
  10.5 1.7 %inner_mechanic.1 = (f32[3,18,48,128]{3,2,1,0:T(8,128)S(1)}, f32[108,128]{1,0:T(8,128)S(1)}, f32[4,16,32,128]{3,2,1,0:T(8,128)S(1)}, f32[1,4,16,32,128]{4,3,2,1,0:T(8,128)}) custom-call(f32[3,18,48,128]{3,2,1,0:T(8,128)S(1)} %get-tuple-element.47.pad, ...), custom_call_target="tpu_custom_call", output_to_operand_aliasing={{0}: (4, {}), {1}: (5, {}), {2}: (6, {}), {3}: (7, {})} | custom-call | flops 60000002048 | bytes 60000000 | tf_op jit(solution)/shard_map/inner_mechanic/pallas_call | solution.py:661
  12.2 0.8 %collective-permute-start.7 = (f32[108,128]{1,0:T(8,128)S(1)}, f32[108,128]{1,0:T(8,128)S(1)}, u32[]{:S(2)}, u32[]{:S(2)}) collective-permute-start(f32[108,128]{1,0:T(8,128)S(1)} %get-tuple-element.64), channel_id=1, source_target_pairs={{0,1},{1,0},{2,3},{3,2},{4,5},{5,4},{6,7},{7,6},{8,9},{9,8},{10,11... | collective-permute-start | bytes 165896 | tf_op jit(solution)/shard_map/ppermute | solution.py:782
  13.0 0.4 %collective-permute-done.2.got.got_low = f32[232,128]{1,0:T(8,128)S(1)} collective-permute-done((f32[232,128]{1,0:T(8,128)S(1)}, f32[232,128]{1,0:T(8,128)S(1)}, u32[]{:S(2)}, u32[]{:S(2)}) %collective-permute-start.2) | collective-permute-done | bytes 118816 | tf_op jit(solution)/shard_map/ppermute | solution.py:761
  13.3 0.2 %outer_low.1 = (f32[3,18,48,128]{3,2,1,0:T(8,128)S(1)}, f32[24,128]{1,0:T(8,128)S(1)}) custom-call(f32[3,18,48,128]{3,2,1,0:T(8,128)S(1)} %get-tuple-element.47.pad, f32[8,16,32,128]{3,2,1,0:T(8,128)S(1)} %bitcast.15, s32[2,1,32]{2,1,0:T(1,128)S(1)} %bitcast.22, ...), custom_call_target="tpu_custom_call", output_to_operand_aliasing={{0}: (4, {}), {1}: (5, {})} | custom-call | flops 100000000 | bytes 100000 | tf_op jit(solution)/shard_map/outer_low/pallas_call | solution.py:661
  13.5 0.2 %collective-permute-done.3.got.got_high = f32[232,128]{1,0:T(8,128)S(1)} collective-permute-done((f32[232,128]{1,0:T(8,128)S(1)}, f32[232,128]{1,0:T(8,128)S(1)}, u32[]{:S(2)}, u32[]{:S(2)}) %collective-permute-start.3) | collective-permute-done | bytes 118816 | tf_op jit(solution)/shard_map/ppermute | solution.py:762
  13.8 0.2 %outer_high.1 = (f32[3,18,48,128]{3,2,1,0:T(8,128)S(1)}, f32[24,128]{1,0:T(8,128)S(1)}) custom-call(f32[3,18,48,128]{3,2,1,0:T(8,128)S(1)} %get-tuple-element.47.pad, f32[8,16,32,128]{3,2,1,0:T(8,128)S(1)} %bitcast.16, s32[2,1,32]{2,1,0:T(1,128)S(1)} %bitcast.23, ...), custom_call_target="tpu_custom_call", output_to_operand_aliasing={{0}: (4, {}), {1}: (5, {})} | custom-call | flops 10000000000 | bytes 10000000 | tf_op jit(solution)/shard_map/outer_high/pallas_call | solution.py:661
  14.0 1.2 %collective-permute-start.8 = (f32[24,128]{1,0:T(8,128)S(1)}, f32[24,128]{1,0:T(8,128)S(1)}, u32[]{:S(2)}, u32[]{:S(2)}) collective-permute-start(f32[24,128]{1,0:T(8,128)S(1)} %get-tuple-element.68), channel_id=1, source_target_pairs={{0,1},{1,0},{2,3},{3,2},{4,5},{5,4},{6,7},{7,6},{8,9},{9,8},{10,11... | collective-permute-start | bytes 36872 | tf_op jit(solution)/shard_map/ppermute | solution.py:803
  15.2 1.0 %middle.1 = (f32[1,4,16,32,128]{4,3,2,1,0:T(8,128)}, f32[3,18,48,128]{3,2,1,0:T(8,128)S(1)}, f32[6,32,128]{2,1,0:T(8,128)S(1)}, f32[3,10,32,128]{3,2,1,0:T(8,128)S(1)}) custom-call(f32[3,512,128]{2,1,0:T(8,128)S(1)} %get-tuple-element.49.fib_ref, f32[8,16,32,128]{3,2,1,0:T(8,128)S(1)} %bitcast.17, ...), custom_call_target="tpu_custom_call", output_to_operand_aliasing={{1}: (5, {}), {0}: (8, {})} | custom-call | flops 60000002048 | bytes 60000000 | tf_op jit(solution)/shard_map/middle/pallas_call | solution.py:661
  16.2 0.9 %last.1 = (f32[1,4,16,32,128]{4,3,2,1,0:T(8,128)}, f32[3,18,48,128]{3,2,1,0:T(8,128)S(1)}) custom-call(f32[3,512,128]{2,1,0:T(8,128)S(1)} %get-tuple-element.49.fib_ref, f32[3,18,48,128]{3,2,1,0:T(8,128)S(1)} %get-tuple-element.67.next_in, f32[24,128]{1,0:T(8,128)S(1)} %collective-permute-done.8.side_ref, ...), custom_call_target="tpu_custom_call", output_to_operand_aliasing={{1}: (1, {}), {0}: (6, {})} | custom-call | flops 10000000000 | bytes 10000000 | tf_op jit(solution)/shard_map/last/pallas_call | solution.py:661
  (15 shorter events, 0.0 us)
Async XLA Ops:
  0.0 1.6 %copy-start = (f32[1,8,16,32,128]{4,3,2,1,0:T(8,128)S(1)}, f32[1,8,16,32,128]{4,3,2,1,0:T(8,128)}, u32[]{:S(2)}) copy-start(f32[1,8,16,32,128]{4,3,2,1,0:T(8,128)} %param.5) | copy-start | bytes 6291460
  0.1 4.3 %collective-permute-start.1 = (f32[2,32,128]{2,1,0:T(8,128)S(1)}, f32[2,32,128]{2,1,0:T(8,128)S(1)}, u32[]{:S(2)}, u32[]{:S(2)}) collective-permute-start(f32[2,32,128]{2,1,0:T(8,128)S(1)} %get-tuple-element.46), channel_id=1, source_target_pairs={{0,16},{16,0},{1,17},{17,1},{2,18},{18,2},{3,19},{19,3},{4,20},{20... | collective-permute-start | bytes 98312 | tf_op jit(solution)/shard_map/ppermute | solution.py:725
  1.7 2.1 %collective-permute-start = (f32[96,128]{1,0:T(8,128)S(1)}, f32[96,128]{1,0:T(8,128)S(1)}, u32[]{:S(2)}, u32[]{:S(2)}) collective-permute-start(f32[96,128]{1,0:T(8,128)S(1)} %get-tuple-element.41.after), channel_id=1, source_target_pairs={{0,1},{1,0},{2,3},{3,2},{4,5},{5,4},{6,7},{7,6},{8,9},{9,8},{10,11... | collective-permute-start | bytes 147464 | tf_op jit(solution)/shard_map/ppermute | solution.py:727
  2.4 0.9 %copy-start.1 = (f32[8,2]{0,1:T(2,128)S(1)}, f32[8,2]{0,1:T(2,128)}, u32[]{:S(2)}) copy-start(f32[8,2]{0,1:T(2,128)} %param.6) | copy-start | bytes 196
  2.4 0.9 %copy-start.2 = (s32[2,1,1,32]{3,2,1,0:T(1,128)S(1)}, s32[2,1,1,32]{3,2,1,0:T(1,128)}, u32[]{:S(2)}) copy-start(s32[2,1,1,32]{3,2,1,0:T(1,128)} %param.9) | copy-start | bytes 772
  2.4 0.9 %copy-start.3 = (s32[16,32,8]{1,2,0:T(8,128)S(1)}, s32[16,32,8]{1,2,0:T(8,128)}, u32[]{:S(2)}) copy-start(s32[16,32,8]{1,2,0:T(8,128)} %param.7) | copy-start | bytes 49156
  2.4 8.0 %collective-permute-start.6 = (f32[512,128]{1,0:T(8,128)S(1)}, f32[512,128]{1,0:T(8,128)S(1)}, u32[]{:S(2)}, u32[]{:S(2)}) collective-permute-start(f32[512,128]{1,0:T(8,128)S(1)} %gather.1.after), channel_id=1, source_target_pairs={{0,16},{16,0},{1,17},{17,1},{2,18},{18,2},{3,19},{19,3},{4,20},{20... | collective-permute-start | bytes 786440 | tf_op jit(solution)/shard_map/ppermute | solution.py:739
  3.9 9.0 %collective-permute-start.4 = (f32[168,128]{1,0:T(8,128)S(1)}, f32[168,128]{1,0:T(8,128)S(1)}, u32[]{:S(2)}, u32[]{:S(2)}) collective-permute-start(f32[168,128]{1,0:T(8,128)S(1)} %get-tuple-element.52), channel_id=1, source_target_pairs={{0,2},{1,3},{2,4},{3,5},{4,6},{5,7},{6,8},{7,9},{8,10},{9,11},{10,... | collective-permute-start | bytes 258056 | tf_op jit(solution)/shard_map/ppermute | solution.py:750
  4.3 8.7 %collective-permute-start.5 = (f32[168,128]{1,0:T(8,128)S(1)}, f32[168,128]{1,0:T(8,128)S(1)}, u32[]{:S(2)}, u32[]{:S(2)}) collective-permute-start(f32[168,128]{1,0:T(8,128)S(1)} %get-tuple-element.53), channel_id=1, source_target_pairs={{0,14},{1,15},{2,0},{3,1},{4,2},{5,3},{6,4},{7,5},{8,6},{9,7},{10,... | collective-permute-start | bytes 258056 | tf_op jit(solution)/shard_map/ppermute | solution.py:751
  4.6 8.7 %collective-permute-start.2 = (f32[232,128]{1,0:T(8,128)S(1)}, f32[232,128]{1,0:T(8,128)S(1)}, u32[]{:S(2)}, u32[]{:S(2)}) collective-permute-start(f32[232,128]{1,0:T(8,128)S(1)} %get-tuple-element.50), channel_id=1, source_target_pairs={{16,18},{17,19},{18,20},{19,21},{20,22},{21,23},{22,24},{23,25},{2... | collective-permute-start | bytes 356360 | tf_op jit(solution)/shard_map/ppermute | solution.py:761
  6.7 7.0 %collective-permute-start.3 = (f32[232,128]{1,0:T(8,128)S(1)}, f32[232,128]{1,0:T(8,128)S(1)}, u32[]{:S(2)}, u32[]{:S(2)}) collective-permute-start(f32[232,128]{1,0:T(8,128)S(1)} %get-tuple-element.51), channel_id=1, source_target_pairs={{16,30},{17,31},{18,16},{19,17},{20,18},{21,19},{22,20},{23,21},{2... | collective-permute-start | bytes 356360 | tf_op jit(solution)/shard_map/ppermute | solution.py:762
  12.2 3.0 %collective-permute-start.7 = (f32[108,128]{1,0:T(8,128)S(1)}, f32[108,128]{1,0:T(8,128)S(1)}, u32[]{:S(2)}, u32[]{:S(2)}) collective-permute-start(f32[108,128]{1,0:T(8,128)S(1)} %get-tuple-element.64), channel_id=1, source_target_pairs={{0,1},{1,0},{2,3},{3,2},{4,5},{5,4},{6,7},{7,6},{8,9},{9,8},{10,11... | collective-permute-start | bytes 165896 | tf_op jit(solution)/shard_map/ppermute | solution.py:782
  14.0 2.2 %collective-permute-start.8 = (f32[24,128]{1,0:T(8,128)S(1)}, f32[24,128]{1,0:T(8,128)S(1)}, u32[]{:S(2)}, u32[]{:S(2)}) collective-permute-start(f32[24,128]{1,0:T(8,128)S(1)} %get-tuple-element.68), channel_id=1, source_target_pairs={{0,1},{1,0},{2,3},{3,2},{4,5},{5,4},{6,7},{7,6},{8,9},{9,8},{10,11... | collective-permute-start | bytes 36872 | tf_op jit(solution)/shard_map/ppermute | solution.py:803

commit v12 on v11

--- a/solution.py
+++ b/solution.py
@@ -411,7 +411,7 @@
             keep[3, x] = c1 - DT * (0.5 * c1 + flow1)
             return carry
 
-        lax.fori_loop(0, size_x, plane, 0, unroll=2)
+        lax.fori_loop(0, size_x, plane, 0, unroll=8)
         for copy in copies:
             copy.wait()
 
@@ -436,7 +436,7 @@
                 put_inner(next_pad, share, a, x + 1, value)
             return carry
 
-        lax.fori_loop(0, size_x, plane, 0, unroll=2)
+        lax.fori_loop(0, size_x, plane, 0, unroll=8)
         copy = pltpu.make_async_copy(keep.at[3:4], out_hbm.at[0, 3:4], sems.at[0])
         copy.start()
         copy.wait()
@@ -802,7 +802,7 @@
         )
     end_side = lax.ppermute(share, "gy", both)
     fields = pltpu.VMEM((3, size_x, size_y, depth), F32)
-    held_back = 10
+    held_back = 11
     result, moved, held, final = call(
         middle_kernel,
         "middle",

time: 17.2 us -> 17.2 us (level)
  transfers between devices with their start and end apart: 9 -> 9, of which waited for: 2 -> 2; matrix products, arithmetic and copies ran while one was open for 0% -> 0% of each run, Pallas kernels for 26% -> 25%
where the time goes in v12:
time: 17.2 us; the launch traced here: 17.1 us
  starting transfers between devices  10.7 us (62%)
  Pallas kernels  5.34 us (31%)
  waiting for transfers between devices  0.71 us (4%)
  local copies, waits for them, and re-layouts  0.22 us (1%)
    pallas_call x13, Pallas kernels, call(): pl.pallas_call(kernel, name=name, out_shape=tuple(out_shape), in_specs=[p...  5.34 us
    ppermute x1, starting transfers between devices, local(): got_high = lax.ppermute(low, axes, ring(1, -1))  3.1 us
    ppermute x1, starting transfers between devices, local(): got_low = lax.ppermute(high, axes, ring(1, 1))  2.12 us
    ppermute x2, starting transfers between devices, local(): side = lax.ppermute(share, 'gy', both)  1.49 us
    ppermute x1, starting transfers between devices, local(): edge_ten = lax.ppermute(edge_ten, 'sec', both)  1.24 us
    ppermute x1, starting transfers between devices, local(): end_side = lax.ppermute(share, 'gy', both)  1.24 us
    ppermute x1, starting transfers between devices, local(): tension = lax.ppermute(gathered, 'sec', both)  0.93 us
    ppermute x1, waiting for transfers between devices, local(): got_low = lax.ppermute(high, axes, ring(1, 1))  0.47 us
  transfers between devices with their start and end apart: 9, of which 2 were waited for; matrix products, arithmetic and copies ran while one was open for 0% of the time, Pallas kernels for 25%

profile of v12, /device:TPU:3, one launch (start us, length us, event | category | flops | bytes accessed | tf_op | source)
XLA Modules:
  0.0 17.1 jit_solution(15169660447452299632)
XLA Ops:
  0.0 0.1 tension.1
  0.1 1.2 %collective-permute-start.1 = (f32[2,32,128]{2,1,0:T(8,128)S(1)}, f32[2,32,128]{2,1,0:T(8,128)S(1)}, u32[]{:S(2)}, u32[]{:S(2)}) collective-permute-start(f32[2,32,128]{2,1,0:T(8,128)S(1)} %get-tuple-element.46), channel_id=1, source_target_pairs={{0,16},{16,0},{1,17},{17,1},{2,18},{18,2},{3,19},{19,3},{4,20},{20... | collective-permute-start | bytes 98312 | tf_op jit(solution)/shard_map/ppermute | solution.py:725
  1.4 0.2 %copy-done = f32[1,8,16,32,128]{4,3,2,1,0:T(8,128)S(1)} copy-done((f32[1,8,16,32,128]{4,3,2,1,0:T(8,128)S(1)}, f32[1,8,16,32,128]{4,3,2,1,0:T(8,128)}, u32[]{:S(2)}) %copy-start) | copy-done | bytes 2097176
  1.6 0.1 share.1
  1.7 0.7 %collective-permute-start = (f32[96,128]{1,0:T(8,128)S(1)}, f32[96,128]{1,0:T(8,128)S(1)}, u32[]{:S(2)}, u32[]{:S(2)}) collective-permute-start(f32[96,128]{1,0:T(8,128)S(1)} %get-tuple-element.41.after), channel_id=1, source_target_pairs={{0,1},{1,0},{2,3},{3,2},{4,5},{5,4},{6,7},{7,6},{8,9},{9,8},{10,11... | collective-permute-start | bytes 147464 | tf_op jit(solution)/shard_map/ppermute | solution.py:727
  2.4 0.9 %collective-permute-start.6 = (f32[512,128]{1,0:T(8,128)S(1)}, f32[512,128]{1,0:T(8,128)S(1)}, u32[]{:S(2)}, u32[]{:S(2)}) collective-permute-start(f32[512,128]{1,0:T(8,128)S(1)} %gather.1.after), channel_id=1, source_target_pairs={{0,16},{16,0},{1,17},{17,1},{2,18},{18,2},{3,19},{19,3},{4,20},{20... | collective-permute-start | bytes 786440 | tf_op jit(solution)/shard_map/ppermute | solution.py:739
  3.4 0.5 %edge.1 = (f32[64,384]{1,0:T(8,128)S(1)}, f32[192,384]{1,0:T(8,128)S(1)}) custom-call(f32[192,384]{1,0:T(8,128)S(1)} %get-tuple-element.42.table_in, s32[16,8,32]{2,1,0:T(8,128)S(1)} %bitcast.25, f32[2,8]{1,0:T(2,128)S(1)} %bitcast.19, f32[512,128]{1,0:T(8,128)S(1)} %gather.1.after, s32[2,1,32]{2,1,0:T(1,128)S(1)} %bitcast.20), custom_call_target="tpu_custom_call", output_to_operand_aliasing={{1}: (0, {})} | custom-call | flops 10000000000 | bytes 10000000 | tf_op jit(solution)/shard_map/edge/pallas_call | solution.py:661
  3.8 0.0 collective-permute-done.side_ref
  3.8 0.1 message_electric.1
  3.9 0.4 %collective-permute-start.4 = (f32[168,128]{1,0:T(8,128)S(1)}, f32[168,128]{1,0:T(8,128)S(1)}, u32[]{:S(2)}, u32[]{:S(2)}) collective-permute-start(f32[168,128]{1,0:T(8,128)S(1)} %get-tuple-element.52), channel_id=1, source_target_pairs={{0,2},{1,3},{2,4},{3,5},{4,6},{5,7},{6,8},{7,9},{8,10},{9,11},{10,... | collective-permute-start | bytes 258056 | tf_op jit(solution)/shard_map/ppermute | solution.py:750
  4.3 0.2 %collective-permute-start.5 = (f32[168,128]{1,0:T(8,128)S(1)}, f32[168,128]{1,0:T(8,128)S(1)}, u32[]{:S(2)}, u32[]{:S(2)}) collective-permute-start(f32[168,128]{1,0:T(8,128)S(1)} %get-tuple-element.53), channel_id=1, source_target_pairs={{0,14},{1,15},{2,0},{3,1},{4,2},{5,3},{6,4},{7,5},{8,6},{9,7},{10,... | collective-permute-start | bytes 258056 | tf_op jit(solution)/shard_map/ppermute | solution.py:751
  4.5 0.1 message_mechanic.1
  4.6 2.1 %collective-permute-start.2 = (f32[232,128]{1,0:T(8,128)S(1)}, f32[232,128]{1,0:T(8,128)S(1)}, u32[]{:S(2)}, u32[]{:S(2)}) collective-permute-start(f32[232,128]{1,0:T(8,128)S(1)} %get-tuple-element.50), channel_id=1, source_target_pairs={{16,18},{17,19},{18,20},{19,21},{20,22},{21,23},{22,24},{23,25},{2... | collective-permute-start | bytes 356360 | tf_op jit(solution)/shard_map/ppermute | solution.py:761
  6.7 3.1 %collective-permute-start.3 = (f32[232,128]{1,0:T(8,128)S(1)}, f32[232,128]{1,0:T(8,128)S(1)}, u32[]{:S(2)}, u32[]{:S(2)}) collective-permute-start(f32[232,128]{1,0:T(8,128)S(1)} %get-tuple-element.51), channel_id=1, source_target_pairs={{16,30},{17,31},{18,16},{19,17},{20,18},{21,19},{22,20},{23,21},{2... | collective-permute-start | bytes 356360 | tf_op jit(solution)/shard_map/ppermute | solution.py:762
  9.8 0.6 %inner_electric.1 = (f32[3,18,48,128]{3,2,1,0:T(8,128)S(1)}, f32[108,128]{1,0:T(8,128)S(1)}, f32[4,16,32,128]{3,2,1,0:T(8,128)S(1)}, f32[1,4,16,32,128]{4,3,2,1,0:T(8,128)}, f32[3,512,128]{2,1,0:T(8,128)S(1)}) custom-call(f32[3,18,48,128]{3,2,1,0:T(8,128)S(1)} %get-tuple-element.47.pad, f32[8,16,32,128]{3,2,1,0:T(8,128)S(1)} %bitcast.12, ...), custom_call_target="tpu_custom_call" | custom-call | flops 60000002048 | bytes 60000000 | tf_op jit(solution)/shard_map/inner_electric/pallas_call | solution.py:661
  10.5 1.6 %inner_mechanic.1 = (f32[3,18,48,128]{3,2,1,0:T(8,128)S(1)}, f32[108,128]{1,0:T(8,128)S(1)}, f32[4,16,32,128]{3,2,1,0:T(8,128)S(1)}, f32[1,4,16,32,128]{4,3,2,1,0:T(8,128)}) custom-call(f32[3,18,48,128]{3,2,1,0:T(8,128)S(1)} %get-tuple-element.47.pad, ...), custom_call_target="tpu_custom_call", output_to_operand_aliasing={{0}: (4, {}), {1}: (5, {}), {2}: (6, {}), {3}: (7, {})} | custom-call | flops 60000002048 | bytes 60000000 | tf_op jit(solution)/shard_map/inner_mechanic/pallas_call | solution.py:661
  12.1 0.8 %collective-permute-start.7 = (f32[108,128]{1,0:T(8,128)S(1)}, f32[108,128]{1,0:T(8,128)S(1)}, u32[]{:S(2)}, u32[]{:S(2)}) collective-permute-start(f32[108,128]{1,0:T(8,128)S(1)} %get-tuple-element.64), channel_id=1, source_target_pairs={{0,1},{1,0},{2,3},{3,2},{4,5},{5,4},{6,7},{7,6},{8,9},{9,8},{10,11... | collective-permute-start | bytes 165896 | tf_op jit(solution)/shard_map/ppermute | solution.py:782
  12.9 0.5 %collective-permute-done.2.got.got_low = f32[232,128]{1,0:T(8,128)S(1)} collective-permute-done((f32[232,128]{1,0:T(8,128)S(1)}, f32[232,128]{1,0:T(8,128)S(1)}, u32[]{:S(2)}, u32[]{:S(2)}) %collective-permute-start.2) | collective-permute-done | bytes 118816 | tf_op jit(solution)/shard_map/ppermute | solution.py:761
  13.3 0.2 %outer_low.1 = (f32[3,18,48,128]{3,2,1,0:T(8,128)S(1)}, f32[24,128]{1,0:T(8,128)S(1)}) custom-call(f32[3,18,48,128]{3,2,1,0:T(8,128)S(1)} %get-tuple-element.47.pad, f32[8,16,32,128]{3,2,1,0:T(8,128)S(1)} %bitcast.15, s32[2,1,32]{2,1,0:T(1,128)S(1)} %bitcast.22, ...), custom_call_target="tpu_custom_call", output_to_operand_aliasing={{0}: (4, {}), {1}: (5, {})} | custom-call | flops 100000000 | bytes 100000 | tf_op jit(solution)/shard_map/outer_low/pallas_call | solution.py:661
  13.5 0.2 %collective-permute-done.3.got.got_high = f32[232,128]{1,0:T(8,128)S(1)} collective-permute-done((f32[232,128]{1,0:T(8,128)S(1)}, f32[232,128]{1,0:T(8,128)S(1)}, u32[]{:S(2)}, u32[]{:S(2)}) %collective-permute-start.3) | collective-permute-done | bytes 118816 | tf_op jit(solution)/shard_map/ppermute | solution.py:762
  13.8 0.2 %outer_high.1 = (f32[3,18,48,128]{3,2,1,0:T(8,128)S(1)}, f32[24,128]{1,0:T(8,128)S(1)}) custom-call(f32[3,18,48,128]{3,2,1,0:T(8,128)S(1)} %get-tuple-element.47.pad, f32[8,16,32,128]{3,2,1,0:T(8,128)S(1)} %bitcast.16, s32[2,1,32]{2,1,0:T(1,128)S(1)} %bitcast.23, ...), custom_call_target="tpu_custom_call", output_to_operand_aliasing={{0}: (4, {}), {1}: (5, {})} | custom-call | flops 10000000000 | bytes 10000000 | tf_op jit(solution)/shard_map/outer_high/pallas_call | solution.py:661
  14.0 1.2 %collective-permute-start.8 = (f32[24,128]{1,0:T(8,128)S(1)}, f32[24,128]{1,0:T(8,128)S(1)}, u32[]{:S(2)}, u32[]{:S(2)}) collective-permute-start(f32[24,128]{1,0:T(8,128)S(1)} %get-tuple-element.68), channel_id=1, source_target_pairs={{0,1},{1,0},{2,3},{3,2},{4,5},{5,4},{6,7},{7,6},{8,9},{9,8},{10,11... | collective-permute-start | bytes 36872 | tf_op jit(solution)/shard_map/ppermute | solution.py:803
  15.2 0.9 %middle.1 = (f32[1,4,16,32,128]{4,3,2,1,0:T(8,128)}, f32[3,18,48,128]{3,2,1,0:T(8,128)S(1)}, f32[6,32,128]{2,1,0:T(8,128)S(1)}, f32[3,11,32,128]{3,2,1,0:T(8,128)S(1)}) custom-call(f32[3,512,128]{2,1,0:T(8,128)S(1)} %get-tuple-element.49.fib_ref, f32[8,16,32,128]{3,2,1,0:T(8,128)S(1)} %bitcast.17, ...), custom_call_target="tpu_custom_call", output_to_operand_aliasing={{1}: (5, {}), {0}: (8, {})} | custom-call | flops 60000002048 | bytes 60000000 | tf_op jit(solution)/shard_map/middle/pallas_call | solution.py:661
  16.1 0.9 %last.1 = (f32[1,4,16,32,128]{4,3,2,1,0:T(8,128)}, f32[3,18,48,128]{3,2,1,0:T(8,128)S(1)}) custom-call(f32[3,512,128]{2,1,0:T(8,128)S(1)} %get-tuple-element.49.fib_ref, f32[3,18,48,128]{3,2,1,0:T(8,128)S(1)} %get-tuple-element.67.next_in, f32[24,128]{1,0:T(8,128)S(1)} %collective-permute-done.8.side_ref, ...), custom_call_target="tpu_custom_call", output_to_operand_aliasing={{1}: (1, {}), {0}: (6, {})} | custom-call | flops 10000000000 | bytes 10000000 | tf_op jit(solution)/shard_map/last/pallas_call | solution.py:661
  (15 shorter events, 0.0 us)
Async XLA Ops:
  0.0 1.6 %copy-start = (f32[1,8,16,32,128]{4,3,2,1,0:T(8,128)S(1)}, f32[1,8,16,32,128]{4,3,2,1,0:T(8,128)}, u32[]{:S(2)}) copy-start(f32[1,8,16,32,128]{4,3,2,1,0:T(8,128)} %param.5) | copy-start | bytes 6291460
  0.1 4.3 %collective-permute-start.1 = (f32[2,32,128]{2,1,0:T(8,128)S(1)}, f32[2,32,128]{2,1,0:T(8,128)S(1)}, u32[]{:S(2)}, u32[]{:S(2)}) collective-permute-start(f32[2,32,128]{2,1,0:T(8,128)S(1)} %get-tuple-element.46), channel_id=1, source_target_pairs={{0,16},{16,0},{1,17},{17,1},{2,18},{18,2},{3,19},{19,3},{4,20},{20... | collective-permute-start | bytes 98312 | tf_op jit(solution)/shard_map/ppermute | solution.py:725
  1.7 2.1 %collective-permute-start = (f32[96,128]{1,0:T(8,128)S(1)}, f32[96,128]{1,0:T(8,128)S(1)}, u32[]{:S(2)}, u32[]{:S(2)}) collective-permute-start(f32[96,128]{1,0:T(8,128)S(1)} %get-tuple-element.41.after), channel_id=1, source_target_pairs={{0,1},{1,0},{2,3},{3,2},{4,5},{5,4},{6,7},{7,6},{8,9},{9,8},{10,11... | collective-permute-start | bytes 147464 | tf_op jit(solution)/shard_map/ppermute | solution.py:727
  2.4 0.9 %copy-start.1 = (f32[8,2]{0,1:T(2,128)S(1)}, f32[8,2]{0,1:T(2,128)}, u32[]{:S(2)}) copy-start(f32[8,2]{0,1:T(2,128)} %param.6) | copy-start | bytes 196
  2.4 0.9 %copy-start.2 = (s32[2,1,1,32]{3,2,1,0:T(1,128)S(1)}, s32[2,1,1,32]{3,2,1,0:T(1,128)}, u32[]{:S(2)}) copy-start(s32[2,1,1,32]{3,2,1,0:T(1,128)} %param.9) | copy-start | bytes 772
  2.4 0.9 %copy-start.3 = (s32[16,32,8]{1,2,0:T(8,128)S(1)}, s32[16,32,8]{1,2,0:T(8,128)}, u32[]{:S(2)}) copy-start(s32[16,32,8]{1,2,0:T(8,128)} %param.7) | copy-start | bytes 49156
  2.4 8.0 %collective-permute-start.6 = (f32[512,128]{1,0:T(8,128)S(1)}, f32[512,128]{1,0:T(8,128)S(1)}, u32[]{:S(2)}, u32[]{:S(2)}) collective-permute-start(f32[512,128]{1,0:T(8,128)S(1)} %gather.1.after), channel_id=1, source_target_pairs={{0,16},{16,0},{1,17},{17,1},{2,18},{18,2},{3,19},{19,3},{4,20},{20... | collective-permute-start | bytes 786440 | tf_op jit(solution)/shard_map/ppermute | solution.py:739
  3.9 8.9 %collective-permute-start.4 = (f32[168,128]{1,0:T(8,128)S(1)}, f32[168,128]{1,0:T(8,128)S(1)}, u32[]{:S(2)}, u32[]{:S(2)}) collective-permute-start(f32[168,128]{1,0:T(8,128)S(1)} %get-tuple-element.52), channel_id=1, source_target_pairs={{0,2},{1,3},{2,4},{3,5},{4,6},{5,7},{6,8},{7,9},{8,10},{9,11},{10,... | collective-permute-start | bytes 258056 | tf_op jit(solution)/shard_map/ppermute | solution.py:750
  4.3 8.5 %collective-permute-start.5 = (f32[168,128]{1,0:T(8,128)S(1)}, f32[168,128]{1,0:T(8,128)S(1)}, u32[]{:S(2)}, u32[]{:S(2)}) collective-permute-start(f32[168,128]{1,0:T(8,128)S(1)} %get-tuple-element.53), channel_id=1, source_target_pairs={{0,14},{1,15},{2,0},{3,1},{4,2},{5,3},{6,4},{7,5},{8,6},{9,7},{10,... | collective-permute-start | bytes 258056 | tf_op jit(solution)/shard_map/ppermute | solution.py:751
  4.6 8.7 %collective-permute-start.2 = (f32[232,128]{1,0:T(8,128)S(1)}, f32[232,128]{1,0:T(8,128)S(1)}, u32[]{:S(2)}, u32[]{:S(2)}) collective-permute-start(f32[232,128]{1,0:T(8,128)S(1)} %get-tuple-element.50), channel_id=1, source_target_pairs={{16,18},{17,19},{18,20},{19,21},{20,22},{21,23},{22,24},{23,25},{2... | collective-permute-start | bytes 356360 | tf_op jit(solution)/shard_map/ppermute | solution.py:761
  6.7 7.0 %collective-permute-start.3 = (f32[232,128]{1,0:T(8,128)S(1)}, f32[232,128]{1,0:T(8,128)S(1)}, u32[]{:S(2)}, u32[]{:S(2)}) collective-permute-start(f32[232,128]{1,0:T(8,128)S(1)} %get-tuple-element.51), channel_id=1, source_target_pairs={{16,30},{17,31},{18,16},{19,17},{20,18},{21,19},{22,20},{23,21},{2... | collective-permute-start | bytes 356360 | tf_op jit(solution)/shard_map/ppermute | solution.py:762
  12.1 3.1 %collective-permute-start.7 = (f32[108,128]{1,0:T(8,128)S(1)}, f32[108,128]{1,0:T(8,128)S(1)}, u32[]{:S(2)}, u32[]{:S(2)}) collective-permute-start(f32[108,128]{1,0:T(8,128)S(1)} %get-tuple-element.64), channel_id=1, source_target_pairs={{0,1},{1,0},{2,3},{3,2},{4,5},{5,4},{6,7},{7,6},{8,9},{9,8},{10,11... | collective-permute-start | bytes 165896 | tf_op jit(solution)/shard_map/ppermute | solution.py:782
  14.0 2.2 %collective-permute-start.8 = (f32[24,128]{1,0:T(8,128)S(1)}, f32[24,128]{1,0:T(8,128)S(1)}, u32[]{:S(2)}, u32[]{:S(2)}) collective-permute-start(f32[24,128]{1,0:T(8,128)S(1)} %get-tuple-element.68), channel_id=1, source_target_pairs={{0,1},{1,0},{2,3},{3,2},{4,5},{5,4},{6,7},{7,6},{8,9},{9,8},{10,11... | collective-permute-start | bytes 36872 | tf_op jit(solution)/shard_map/ppermute | solution.py:803
